TPU v7x, 32 devices: a whole 2x2x4 slice. The times are simulated.
32 devices in a mesh: scen: 2 (over x), tm: 16 (over z, y, core).
Axes of the slice: x: 2, y: 2, z: 4, core: 2. Of those that a mesh axis runs over, the one named last changes fastest.
Arguments:
- base_injection: bfloat16 [32, 36864], P(('scen', 'tm')), parts along dimension 0, may hold values from -6 to 6
- ptdf_tiles: bfloat16 [128, 80, 128, 128], P(None, 'tm'), may hold values from -0.0625 to 0.0625
- tile_block: int32 [128, 80], P(None, 'tm'), may hold values from 0 to 17
- limits: float32 [16384], replicated, may hold values from 0.5 to 2
- stor_bus: int32 [2048], replicated, may hold values from 0 to 36863
- stor_gain: float32 [2048], replicated, may hold values from 0.5 to 4
- soc_init: float32 [32, 2048], P(('scen', 'tm')), parts along dimension 0, may hold values from 0 to 1
Outputs:
- injection: float32 [32, 36864], P(('scen', 'tm')), parts along dimension 0
- line_dual: float32 [32, 16384], P(('scen', 'tm')), parts along dimension 0
- level: float32 [32, 2048], P(('scen', 'tm')), parts along dimension 0
There are 2 independent parts, one for each index of `scen`. A program takes and returns all parts, laid end to end along the dimension named above; an argument that names none is the same for every part. Nothing has to cross between parts.
All inputs are finite; a program needn't handle non-finite values.
Results may differ from a plain program's by a relative error of at most 0.012.
The roundings to bfloat16 on the way count: a program that leaves them out, or rounds other values in their place, can miss the bound.
Values may be sent and summed in bfloat16 or wider, within the bound.
No kernel may reach another device: no remote copies, remote signals or barrier semaphores. Data moves between devices by JAX's collectives and lax.ppermute only.
A program may use at most 128 MiB of HBM per device.

v0:
```python
import jax
import jax.numpy as jnp
from jax import lax
from jax.sharding import PartitionSpec as P

ITERS = 2


step_size = 0.5
penalty = 4.0
ramp_weight = 0.5


def padded_2(block, sides, width):
    for axis, dim in sides:
        count = lax.axis_size(axis)
        forward = [(i, i + 1) for i in range(count - 1)]
        forward.append((count - 1, 0))
        backward = [(target, source) for source, target in forward]
        low = lax.ppermute(
            lax.slice_in_dim(block, block.shape[dim] - width, None, axis=dim), axis, forward
        )
        high = lax.ppermute(lax.slice_in_dim(block, 0, width, axis=dim), axis, backward)
        block = jnp.concatenate([low, block, high], axis=dim)
    return block


def shards(base_injection, ptdf_tiles, tile_block, limits, stor_bus, stor_gain, soc_init):
    hour_rows = base_injection.shape[0]
    bus_count = base_injection.shape[1]
    line_count = limits.shape[0]
    groups = ptdf_tiles.shape[0]
    tile_width = ptdf_tiles.shape[2]
    devices = lax.axis_size("tm")
    bus_blocks = bus_count // (devices * tile_width)
    total_hours = hour_rows * devices
    base_full = base_injection.astype(jnp.float32)
    inject = base_full
    level = soc_init
    line_dual = jnp.zeros((total_hours, line_count), jnp.float32)
    for iteration in range(ITERS):
        joined = jnp.concatenate([inject, level], axis=1)
        padded = padded_2(joined.astype(jnp.bfloat16), (("tm", 0),), 1).astype(joined.dtype)
        sent_rows = inject.astype(jnp.bfloat16)
        columns = lax.all_to_all(sent_rows, "tm", split_axis=1, concat_axis=0, tiled=True)
        columns = columns.reshape(total_hours, bus_blocks, tile_width)
        picked = columns[:, tile_block]
        partial_flow = jnp.einsum(
            "hgkb,gklb->hgl", picked, ptdf_tiles, preferred_element_type=jnp.float32
        )
        line_flows = lax.psum(partial_flow.reshape(total_hours, line_count), "tm")
        shifted = line_flows + line_dual
        clipped = jnp.clip(shifted, -limits, limits)
        line_dual = shifted - clipped
        dual_piece = line_dual.astype(jnp.bfloat16)
        piece_rows = dual_piece.shape[0]
        folded = dual_piece.reshape(piece_rows, groups, tile_width)
        contrib = jnp.einsum(
            "hgl,gklb->hgkb", folded, ptdf_tiles, preferred_element_type=jnp.float32
        )
        summed = (
            jnp.zeros((piece_rows, bus_blocks, tile_width), jnp.float32)
            .at[:, tile_block]
            .add(contrib)
        )
        price_cols = summed.reshape(piece_rows, bus_blocks * tile_width)
        bus_price = lax.all_to_all(price_cols, "tm", split_axis=0, concat_axis=1, tiled=True)
        prev_inj = padded[:-2, :bus_count]
        next_inj = padded[2:, :bus_count]
        prev_level = padded[:-2, bus_count:]
        store_price = bus_price[:, stor_bus]
        charge = level - prev_level
        updated = inject - step_size * (
            inject
            - base_full
            + penalty * bus_price
            + ramp_weight * (2.0 * inject - prev_inj - next_inj)
        )
        updated = updated.at[:, stor_bus].add(-step_size * charge)
        level = 0.5 * (level + prev_level) - stor_gain * store_price
        inject = updated
    own_dual = lax.dynamic_slice_in_dim(line_dual, lax.axis_index("tm") * hour_rows, hour_rows, 0)
    return (inject, own_dual, level)


def solution(mesh):
    in_specs = (
        P(("scen", "tm"), None),
        P(None, "tm", None, None),
        P(None, "tm"),
        P(),
        P(),
        P(),
        P(("scen", "tm"), None),
    )
    out_specs = (P(("scen", "tm"), None), P(("scen", "tm"), None), P(("scen", "tm"), None))
    return jax.shard_map(shards, mesh=mesh, in_specs=in_specs, out_specs=out_specs, check_vma=False)
```

profile of v0, /device:TPU:0, one launch (start us, length us, event | category | flops | bytes accessed | tf_op | source)
XLA Modules:
  0.0 460.1 jit_solution(3896762354028429285)
XLA Ops:
  7.7 2.0 reduce.4
  10.3 7.4 %all-to-all-start = ((bf16[16,2,1152]{2,1,0:T(2,128)(2,1)}), bf16[16,2,1152]{2,1,0:T(2,128)(2,1)S(1)}, u32[]{:S(2)}, u32[]{:S(2)}) async-start(bf16[16,2,1152]{2,1,0:T(2,128)(2,1)} %reshape.246), calls=%async_computation | async-start | bytes 147456 | tf_op jit(solution)/shard_map/all_to_all | solution.py:45
  18.8 5.9 %all-to-all-done = bf16[16,2,1152]{2,1,0:T(2,128)(2,1)S(1)} async-done(((bf16[16,2,1152]{2,1,0:T(2,128)(2,1)}), bf16[16,2,1152]{2,1,0:T(2,128)(2,1)S(1)}, u32[]{:S(2)}, u32[]{:S(2)}) %all-to-all-start) | async-done | bytes 73760 | tf_op jit(solution)/shard_map/all_to_all | solution.py:45
  25.2 2.6 gather_fusion
  27.9 10.8 %convolution_bitcast_fusion.1 = f32[128,2,8,128]{3,2,1,0:T(8,128)S(1)} fusion(bf16[16,128,5,128]{3,0,2,1:T(8,128)(2,1)S(1)} %bitcast.86, bf16[128,5,128,128]{3,2,1,0:T(8,128)(2,1)} %param.8), kind=kOutput, calls=%fused_computation.9 | convolution fusion | flops 335544320 | bytes 24641536 | tf_op jit(solution)/shard_map/hgkb,gklb->hgl/dot_general | solution.py:48
  38.6 1.1 copy.55
  39.8 90.6 %all-reduce.3.cloned.1.call-done = f32[16,16384]{1,0:T(8,128)} async-done(((f32[16,16384]{1,0:T(8,128)}), f32[16,16384]{1,0:T(8,128)}) %all-reduce.3.cloned.1.call-update) | async-done | bytes 1048592 | tf_op jit(solution)/shard_map/psum | solution.py:51
  130.3 1.4 fusion.1
  131.8 10.7 %fusion.4 = f32[128,16,5,128]{3,1,2,0:T(8,128)} fusion(bf16[128,5,128,128]{3,2,1,0:T(8,128)(2,1)} %param.8, bf16[16,128,128,1]{2,1,0,3:T(8,128)(2,1)S(1)} %bitcast.91), kind=kOutput, calls=%fused_computation.18 | convolution fusion | flops 335544320 | bytes 26738688 | tf_op jit(solution)/shard_map/hgl,gklb->hgkb/dot_general | solution.py:58
  142.5 50.9 %scatter_fusion = f32[16,18,128]{2,0,1:T(8,128)S(1)} fusion(f32[16,18,128]{2,0,1:T(8,128)S(1)} %broadcast.48.clone, s32[640]{0:T(1024)S(1)} %reshape.186, f32[640,16,128]{2,1,0:T(8,128)} %bitcast.84), kind=kCustom, calls=%fused_computation.4 | custom fusion | flops 1310720 | bytes 15731200 | tf_op jit(solution)/shard_map/scatter-add | solution.py:64
  194.4 4.0 all-to-all-start.1
  199.0 4.0 collective-permute-start.1
  203.0 4.0 all-to-all-done.1
  207.0 11.8 %gather_fusion.2 = f32[2048]{0:T(1024)S(1)} fusion(f32[36864]{0:T(1024)S(1)} %bitcast.79, s32[2048]{0:T(1024)S(1)} %get-tuple-element.10), kind=kCustom, calls=%fused_computation.2 | custom fusion | bytes 24576 | tf_op jit(solution)/shard_map/gather | solution.py:71
  219.1 1.3 multiply_subtract_fusion.1
  220.4 11.5 %scatter_fusion.1 = f32[36864]{0:T(1024)S(1)} fusion(f32[36864]{0:T(1024)S(1)} %bitcast.76, s32[2048]{0:T(1024)S(1)} %get-tuple-element.11, f32[2048]{0:T(1024)S(1)} %bitcast.96), kind=kCustom, calls=%fused_computation.5 | custom fusion | flops 2048 | bytes 32768 | tf_op jit(solution)/shard_map/scatter-add | solution.py:79
  232.0 1.1 reduce.5
  233.7 3.5 all-to-all-start.2
  237.5 6.7 %all-to-all-done.2 = bf16[16,2,1152]{2,1,0:T(2,128)(2,1)S(1)} async-done(((bf16[16,2,1152]{2,1,0:T(2,128)(2,1)}), bf16[16,2,1152]{2,1,0:T(2,128)(2,1)S(1)}, u32[]{:S(2)}, u32[]{:S(2)}) %all-to-all-start.2) | async-done | bytes 73760 | tf_op jit(solution)/shard_map/all_to_all | solution.py:45
  244.7 2.6 gather_fusion.1
  247.4 10.7 %convolution_bitcast_fusion = f32[128,2,8,128]{3,2,1,0:T(8,128)S(1)} fusion(bf16[16,128,5,128]{3,0,2,1:T(8,128)(2,1)S(1)} %bitcast.85, bf16[128,5,128,128]{3,2,1,0:T(8,128)(2,1)} %param.8), kind=kOutput, calls=%fused_computation.8 | convolution fusion | flops 335544320 | bytes 24641536 | tf_op jit(solution)/shard_map/hgkb,gklb->hgl/dot_general | solution.py:48
  258.1 1.1 copy.54
  259.5 4.4 collective-permute-start.3
  263.9 86.5 %all-reduce.5.cloned.1.call-done = f32[16,16384]{1,0:T(8,128)} async-done(((f32[16,16384]{1,0:T(8,128)}), f32[16,16384]{1,0:T(8,128)}) %all-reduce.5.cloned.1.call-update) | async-done | bytes 1048592 | tf_op jit(solution)/shard_map/psum | solution.py:51
  350.4 1.8 convert_bitcast_fusion
  352.4 10.7 %fusion.2 = f32[128,16,5,128]{3,1,2,0:T(8,128)} fusion(bf16[128,5,128,128]{3,2,1,0:T(8,128)(2,1)} %param.8, bf16[16,128,128,1]{2,1,0,3:T(8,128)(2,1)S(1)} %bitcast.92), kind=kOutput, calls=%fused_computation.16 | convolution fusion | flops 335544320 | bytes 26738688 | tf_op jit(solution)/shard_map/hgl,gklb->hgkb/dot_general | solution.py:58
  363.1 50.9 %scatter_fusion.2 = f32[16,18,128]{2,0,1:T(8,128)S(1)} fusion(f32[16,18,128]{2,0,1:T(8,128)S(1)} %broadcast.48, s32[640]{0:T(1024)S(1)} %reshape.186, f32[640,16,128]{2,1,0:T(8,128)} %bitcast.83), kind=kCustom, calls=%fused_computation.6 | custom fusion | flops 1310720 | bytes 15731200 | tf_op jit(solution)/shard_map/scatter-add | solution.py:64
  414.9 4.0 all-to-all-start.3
  419.6 7.5 %all-to-all-done.3 = f32[16,1,2304]{2,1,0:T(1,128)S(1)} async-done(((f32[16,1,2304]{2,1,0:T(1,128)}), f32[16,1,2304]{2,1,0:T(1,128)S(1)}, u32[]{:S(2)}, u32[]{:S(2)}) %all-to-all-start.3) | async-done | bytes 147488 | tf_op jit(solution)/shard_map/all_to_all | solution.py:67
  427.1 11.8 %gather_fusion.3 = f32[2048]{0:T(1024)S(1)} fusion(f32[36864]{0:T(1024)S(1)} %bitcast.80, s32[2048]{0:T(1024)S(1)} %get-tuple-element.10), kind=kCustom, calls=%fused_computation.3 | custom fusion | bytes 24576 | tf_op jit(solution)/shard_map/gather | solution.py:71
  439.7 1.3 multiply_subtract_fusion
  441.0 11.5 %scatter_fusion.3 = f32[36864]{0:T(1024)S(1)} fusion(f32[36864]{0:T(1024)S(1)} %bitcast.81, s32[2048]{0:T(1024)S(1)} %get-tuple-element.11, f32[2048]{0:T(1024)S(1)} %bitcast.95), kind=kCustom, calls=%fused_computation.7 | custom fusion | flops 2048 | bytes 32768 | tf_op jit(solution)/shard_map/scatter-add | solution.py:79
  (58 shorter events, 9.3 us)
Async XLA Ops:
  10.3 14.4 %all-to-all-start = ((bf16[16,2,1152]{2,1,0:T(2,128)(2,1)}), bf16[16,2,1152]{2,1,0:T(2,128)(2,1)S(1)}, u32[]{:S(2)}, u32[]{:S(2)}) async-start(bf16[16,2,1152]{2,1,0:T(2,128)(2,1)} %reshape.246), calls=%async_computation | async-start | bytes 147456 | tf_op jit(solution)/shard_map/all_to_all | solution.py:45
  17.7 112.6 %all-reduce.3.cloned.1.call-start = ((), (), s32[]{:S(2)}) async-start(), calls=%async_computation.4 | async-start | bytes 2097152 | tf_op jit(solution)/shard_map/psum | solution.py:51
  27.8 11.9 %copy-start.2 = (f32[16384]{0:T(1024)S(1)}, f32[16384]{0:T(1024)}, u32[]{:S(2)}) copy-start(f32[16384]{0:T(1024)} %param.10) | copy-start | bytes 196612
  27.9 11.9 %copy-start.3 = (f32[1,2048]{1,0:T(1,128)S(1)}, f32[1,2048]{1,0:T(1,128)}, u32[]{:S(2)}) copy-start(f32[1,2048]{1,0:T(1,128)} %param.13) | copy-start | bytes 24580
  142.5 55.8 %copy-start.1 = (bf16[1,36864]{1,0:T(2,128)(2,1)S(1)}, bf16[1,36864]{1,0:T(2,128)(2,1)}, u32[]{:S(2)}) copy-start(bf16[1,36864]{1,0:T(2,128)(2,1)} %param.7) | copy-start | bytes 221188
  142.5 60.5 %copy-start.5 = (s32[2048]{0:T(1024)S(1)}, s32[2048]{0:T(1024)}, u32[]{:S(2)}) copy-start(s32[2048]{0:T(1024)} %param.11) | copy-start | bytes 24580
  193.5 25.3 %copy-start.4 = (f32[2048]{0:T(1024)S(1)}, f32[2048]{0:T(1024)}, u32[]{:S(2)}) copy-start(f32[2048]{0:T(1024)} %param.12) | copy-start | bytes 24580
  194.4 12.6 %all-to-all-start.1 = ((f32[16,1,2304]{2,1,0:T(1,128)}), f32[16,1,2304]{2,1,0:T(1,128)S(1)}, u32[]{:S(2)}, u32[]{:S(2)}) async-start(f32[16,1,2304]{2,1,0:T(1,128)} %all_to_all.54), calls=%async_computation.1 | async-start | bytes 294912 | tf_op jit(solution)/shard_map/all_to_all | solution.py:67
  198.5 20.3 %collective-permute-start = (bf16[1,38912]{1,0:T(2,128)(2,1)S(1)}, bf16[1,38912]{1,0:T(2,128)(2,1)S(1)}, u32[]{:S(2)}, u32[]{:S(2)}) collective-permute-start(bf16[1,38912]{1,0:T(2,128)(2,1)S(1)} %pad_maximum_fusion), channel_id=1, source_target_pairs={{0,1},{1,2},{2,3},{3,4},{4,5},{5,6},{6,7},{7,8},{8,9},{9,10},{10,1... | collective-permute-start | bytes 233480 | tf_op jit(solution)/shard_map/ppermute | solution.py:20
  199.0 19.8 %collective-permute-start.1 = (bf16[1,38912]{1,0:T(2,128)(2,1)S(1)}, bf16[1,38912]{1,0:T(2,128)(2,1)S(1)}, u32[]{:S(2)}, u32[]{:S(2)}) collective-permute-start(bf16[1,38912]{1,0:T(2,128)(2,1)S(1)} %pad_maximum_fusion), channel_id=1, source_target_pairs={{1,0},{2,1},{3,2},{4,3},{5,4},{6,5},{7,6},{8,7},{9,8},{10,9},{11,1... | collective-permute-start | bytes 233480 | tf_op jit(solution)/shard_map/ppermute | solution.py:23
  233.7 10.5 %all-to-all-start.2 = ((bf16[16,2,1152]{2,1,0:T(2,128)(2,1)}), bf16[16,2,1152]{2,1,0:T(2,128)(2,1)S(1)}, u32[]{:S(2)}, u32[]{:S(2)}) async-start(bf16[16,2,1152]{2,1,0:T(2,128)(2,1)} %reshape.248), calls=%async_computation.2 | async-start | bytes 147456 | tf_op jit(solution)/shard_map/all_to_all | solution.py:45
  237.2 113.2 %all-reduce.5.cloned.1.call-start = ((), (), s32[]{:S(2)}) async-start(), calls=%async_computation.5 | async-start | bytes 2097152 | tf_op jit(solution)/shard_map/psum | solution.py:51
  259.4 179.5 %collective-permute-start.2 = (bf16[1,38912]{1,0:T(2,128)(2,1)S(1)}, bf16[1,38912]{1,0:T(2,128)(2,1)S(1)}, u32[]{:S(2)}, u32[]{:S(2)}) collective-permute-start(bf16[1,38912]{1,0:T(2,128)(2,1)S(1)} %pad_maximum_fusion.1), channel_id=1, source_target_pairs={{0,1},{1,2},{2,3},{3,4},{4,5},{5,6},{6,7},{7,8},{8,9},{9,10},{10,1... | collective-permute-start | bytes 233480 | tf_op jit(solution)/shard_map/ppermute | solution.py:20
  259.5 179.4 %collective-permute-start.3 = (bf16[1,38912]{1,0:T(2,128)(2,1)S(1)}, bf16[1,38912]{1,0:T(2,128)(2,1)S(1)}, u32[]{:S(2)}, u32[]{:S(2)}) collective-permute-start(bf16[1,38912]{1,0:T(2,128)(2,1)S(1)} %pad_maximum_fusion.1), channel_id=1, source_target_pairs={{1,0},{2,1},{3,2},{4,3},{5,4},{6,5},{7,6},{8,7},{9,8},{10,9},{11,1... | collective-permute-start | bytes 233480 | tf_op jit(solution)/shard_map/ppermute | solution.py:23
  414.9 12.2 %all-to-all-start.3 = ((f32[16,1,2304]{2,1,0:T(1,128)}), f32[16,1,2304]{2,1,0:T(1,128)S(1)}, u32[]{:S(2)}, u32[]{:S(2)}) async-start(f32[16,1,2304]{2,1,0:T(1,128)} %all_to_all.55), calls=%async_computation.3 | async-start | bytes 294912 | tf_op jit(solution)/shard_map/all_to_all | solution.py:67
  452.6 0.7 copy-start
Sparse Core Ops, SparseCore 0:
  39.8 90.4 all-reduce.2
  259.4 91.0 all-reduce.4
where the time goes:
time: 462 us; the launch traced here: 460 us
  waiting for transfers between devices  201 us (44%)
  other arithmetic  136 us (29%)
  matrix products  42.9 us (9%)
  local copies, waits for them, and re-layouts  37.4 us (8%)
  starting transfers between devices  28.1 us (6%)
  between operations  14.5 us (3%)
    psum x2, waiting for transfers between devices, shards(): line_flows = lax.psum(partial_flow.reshape(total_hours, line_count), 'tm')  177 us
    scatter-add x2, other arithmetic, shards(): summed = jnp.zeros((piece_rows, bus_blocks, tile_width), jnp.float32).at[...  102 us
    gather x2, local copies, waits for them, and re-layouts, shards(): store_price = bus_price[:, stor_bus]  23.5 us
    scatter-add x2, other arithmetic, shards(): updated = updated.at[:, stor_bus].add(-step_size * charge)  23.1 us
    dot_general x2, matrix products, shards(): jnp.einsum('hgkb,gklb->hgl', picked, ptdf_tiles, preferred_element_type=j...  21.5 us
    dot_general x2, matrix products, shards(): jnp.einsum('hgl,gklb->hgkb', folded, ptdf_tiles, preferred_element_type=j...  21.4 us
    all_to_all x2, waiting for transfers between devices, shards(): lax.all_to_all(sent_rows, 'tm', split_axis=1, concat_axis=0, tiled=True)  12.7 us
    all_to_all x2, waiting for transfers between devices, shards(): lax.all_to_all(price_cols, 'tm', split_axis=0, concat_axis=1, tiled=True)  11.5 us
  transfers between devices with their start and end apart: 10, of which 6 were waited for; matrix products, arithmetic and copies ran while one was open for 19% of the time, Pallas kernels for 0%

commit v1 on v0

v1 whole, which is shorter than its diff:
```python
import functools

import jax
import jax.numpy as jnp
from jax import lax
from jax.experimental import pallas as pl
from jax.experimental.pallas import tpu as pltpu
from jax.sharding import PartitionSpec as P

ITERS = 2


step_size = 0.5
penalty = 4.0
ramp_weight = 0.5

NT = (((1,), (1,)), ((), ()))
VMEM = pl.BlockSpec(memory_space=pltpu.VMEM)
SMEM = pl.BlockSpec(memory_space=pltpu.SMEM)
HBM = pl.BlockSpec(memory_space=pl.ANY)
UNROLL = 4
CHUNKS = 16


def fetch(tiles_hbm, tiles, sems, chunk):
    size = tiles.shape[0] // sems.shape[0]
    part = pl.ds(chunk * size, size)
    return pltpu.make_async_copy(tiles_hbm.at[part], tiles.at[part], sems.at[chunk])


def fetch_all(tiles_hbm, tiles, sems):
    for chunk in range(sems.shape[0]):
        fetch(tiles_hbm, tiles, sems, chunk).start()


def flow_pass(picked, blocks, tiles, flows, ready):
    groups, depth = tiles.shape[0], tiles.shape[1]
    size = groups // CHUNKS

    def chunk_body(chunk, carry):
        ready(chunk)

        def body(step, inner):
            for u in range(UNROLL):
                g = chunk * size + step * UNROLL + u
                total = None
                for k in range(depth):
                    rows = picked[blocks[g * depth + k]]
                    part = lax.dot_general(rows, tiles[g, k], NT, preferred_element_type=jnp.float32)
                    total = part if total is None else total + part
                flows[g] = total.astype(flows.dtype)
            return inner

        return lax.fori_loop(0, size // UNROLL, body, carry)

    lax.fori_loop(0, CHUNKS, chunk_body, 0)


def price_pass(dual, blocks, tiles, sums, ready):
    groups, depth = tiles.shape[0], tiles.shape[1]
    size = groups // CHUNKS
    for ref in sums:
        ref[...] = jnp.zeros_like(ref)

    def chunk_body(chunk, carry):
        ready(chunk)

        def body(step, inner):
            for u in range(UNROLL):
                g = chunk * size + step * UNROLL + u
                rows = dual[g]
                for k in range(depth):
                    part = jnp.dot(rows, tiles[g, k], preferred_element_type=jnp.float32)
                    at = blocks[g * depth + k]
                    sums[k][at] = sums[k][at] + part
            return inner

        return lax.fori_loop(0, size // UNROLL, body, carry)

    lax.fori_loop(0, CHUNKS, chunk_body, 0)


def earlier(values):
    return jnp.concatenate([values[-1:], values[:-1]], axis=0)


def later(values):
    return jnp.concatenate([values[1:], values[:1]], axis=0)


def update_pass(sums, inject, base, delta, out, sent):
    for block in range(sums[0].shape[0]):
        price = sums[0][block]
        for ref in sums[1:]:
            price = price + ref[block]
        sums[0][block] = price
        now = inject(block)
        new = now - step_size * (
            (now - base(block))
            + penalty * price
            + ramp_weight * (2.0 * now - earlier(now) - later(now))
        )
        new = new - delta[block]
        out(block, new)
        if sent is not None:
            sent[block] = new.astype(jnp.bfloat16)


def level_pass(price, level, unit_block, unit_lane, gain, out, mine):
    count, hours, width = price.shape

    def body(c, carry):
        cols = pl.ds(pl.multiple_of(c * width, width), width)
        block = jnp.broadcast_to(unit_block[:, cols], (hours, width))
        lane = jnp.broadcast_to(unit_lane[:, cols], (hours, width))
        found = jnp.zeros((hours, width), jnp.float32)
        for b in range(count):
            found = jnp.where(block == b, jnp.take_along_axis(price[b], lane, axis=1), found)
        now = level[:, cols]
        new = 0.5 * (now + earlier(now)) - gain[:, cols] * found
        if mine:
            new = jnp.where((block >= 0) & (block < count), new, 0.0)
        out[:, cols] = new
        return carry

    lax.fori_loop(0, level.shape[1] // width, body, 0)


def first_flow_kernel(blocks, base, tiles_hbm, flows, tiles, picked, sems):
    fetch_all(tiles_hbm, tiles, sems)
    width = tiles.shape[3]
    for b in range(picked.shape[0]):
        picked[b] = base[:, b * width : (b + 1) * width]
    flow_pass(picked, blocks, tiles, flows, lambda c: fetch(tiles_hbm, tiles, sems, c).wait())


def middle_kernel(
    blocks, dual, base, delta, level, unit_block, unit_lane, gain, tiles_hbm,
    inject_out, level_out, flows, tiles, picked, sems, *sums
):
    fetch_all(tiles_hbm, tiles, sems)
    width = tiles.shape[3]
    price_pass(dual, blocks, tiles, sums, lambda c: fetch(tiles_hbm, tiles, sems, c).wait())

    def start(b):
        return base[:, b * width : (b + 1) * width].astype(jnp.float32)

    def write(b, new):
        inject_out[b] = new

    update_pass(sums, start, start, delta, write, picked)
    flow_pass(picked, blocks, tiles, flows, lambda c: None)
    level_pass(sums[0], level, unit_block, unit_lane, gain, level_out, False)


def last_kernel(
    blocks, dual, base, inject, delta, level, unit_block, unit_lane, gain, tiles_hbm,
    inject_out, level_out, tiles, sems, *sums
):
    fetch_all(tiles_hbm, tiles, sems)
    width = tiles.shape[3]
    price_pass(dual, blocks, tiles, sums, lambda c: fetch(tiles_hbm, tiles, sems, c).wait())

    def start(b):
        return base[:, b * width : (b + 1) * width].astype(jnp.float32)

    def write(b, new):
        inject_out[:, b * width : (b + 1) * width] = new

    update_pass(sums, lambda b: inject[b], start, delta, write, None)
    level_pass(sums[0], level, unit_block, unit_lane, gain, level_out, True)


def storage_kernel(level, unit_block, unit_lane, delta):
    count, hours, width = delta.shape
    units = level.shape[1]
    span = 2 * width
    delta[...] = jnp.zeros_like(delta)

    def body(c, carry):
        cols = pl.ds(pl.multiple_of(c * span, span), span)
        now = level[:, cols]
        charge = step_size * (now - earlier(now))
        high = charge.astype(jnp.bfloat16).astype(jnp.float32)
        low = charge - high
        lane = jnp.broadcast_to(unit_lane[:, cols], (width, span))
        hot = (lane == lax.broadcasted_iota(jnp.int32, (width, span), 0)).astype(jnp.bfloat16)
        block = jnp.broadcast_to(unit_block[:, cols], (hours, span))
        for b in range(count):
            held = block == b
            both = jnp.concatenate([jnp.where(held, high, 0.0), jnp.where(held, low, 0.0)], axis=0)
            part = lax.dot_general(both.astype(jnp.bfloat16), hot, NT, preferred_element_type=jnp.float32)
            delta[b] = delta[b] + (part[:hours] + part[hours:])
        return carry

    lax.fori_loop(0, units // span, body, 0)


def shards(base_injection, ptdf_tiles, tile_block, limits, stor_bus, stor_gain, soc_init):
    hour_rows = base_injection.shape[0]
    bus_count = base_injection.shape[1]
    line_count = limits.shape[0]
    groups, depth, lines, width = ptdf_tiles.shape
    units = stor_bus.shape[0]
    devices = lax.axis_size("tm")
    me = lax.axis_index("tm")
    buses = bus_count // devices
    bus_blocks = buses // width
    hours = hour_rows * devices
    own_groups = groups // devices
    blocks = tile_block.reshape(groups * depth)
    unit_block = (stor_bus // width - me * bus_blocks).reshape(1, units)
    unit_lane = (stor_bus % width).reshape(1, units)
    gain = stor_gain.reshape(1, units)
    own_limits = lax.dynamic_slice_in_dim(limits.reshape(groups, 1, lines), me * own_groups, own_groups, 0)

    tile_bytes = ptdf_tiles.size * 2
    held = [
        pltpu.VMEM(ptdf_tiles.shape, ptdf_tiles.dtype),
        pltpu.VMEM((bus_blocks, hours, width), jnp.bfloat16),
        pltpu.SemaphoreType.DMA((CHUNKS,)),
    ]
    sums = [pltpu.VMEM((bus_blocks, hours, width), jnp.float32)] * depth
    params = pltpu.CompilerParams(vmem_limit_bytes=tile_bytes + (16 << 20))
    pass_flops = 2 * hours * ptdf_tiles.size
    flow_shape = jax.ShapeDtypeStruct((groups, hours, lines), jnp.bfloat16)
    block_shape = jax.ShapeDtypeStruct((bus_blocks, hours, width), jnp.float32)
    level_shape = jax.ShapeDtypeStruct((hours, units), jnp.float32)

    level = lax.all_gather(soc_init, "tm", axis=0, tiled=True)
    base = lax.all_to_all(base_injection, "tm", split_axis=1, concat_axis=0, tiled=True)

    flows = pl.pallas_call(
        first_flow_kernel,
        out_shape=flow_shape,
        in_specs=[SMEM, VMEM, HBM],
        out_specs=VMEM,
        scratch_shapes=held,
        compiler_params=params,
        cost_estimate=pl.CostEstimate(flops=pass_flops, bytes_accessed=tile_bytes, transcendentals=0),
        name="first_flow",
    )(blocks, base, ptdf_tiles)

    line_dual = jnp.zeros((own_groups, hours, lines), jnp.float32)
    inject = None
    for iteration in range(ITERS):
        delta = pl.pallas_call(
            storage_kernel,
            out_shape=block_shape,
            in_specs=[VMEM] * 3,
            out_specs=VMEM,
            cost_estimate=pl.CostEstimate(flops=pass_flops, bytes_accessed=units * hours * 4, transcendentals=0),
            name="storage",
        )(level, unit_block, unit_lane)
        parts = lax.all_to_all(
            flows.reshape(devices, own_groups, hours, lines), "tm", split_axis=0, concat_axis=0, tiled=True
        )
        shifted = jnp.sum(parts.astype(jnp.float32), axis=0) + line_dual
        clipped = jnp.clip(shifted, -own_limits, own_limits)
        line_dual = shifted - clipped
        dual = lax.all_gather(line_dual.astype(jnp.bfloat16), "tm", axis=0, tiled=True)
        if iteration < ITERS - 1:
            inject, level, flows = pl.pallas_call(
                middle_kernel,
                out_shape=[block_shape, level_shape, flow_shape],
                in_specs=[SMEM] + [VMEM] * 7 + [HBM],
                out_specs=[VMEM] * 3,
                scratch_shapes=held + sums,
                compiler_params=params,
                cost_estimate=pl.CostEstimate(
                    flops=2 * pass_flops, bytes_accessed=tile_bytes, transcendentals=0
                ),
                name="price_then_flow",
            )(blocks, dual, base, delta, level, unit_block, unit_lane, gain, ptdf_tiles)
        else:
            inject, level = pl.pallas_call(
                last_kernel,
                out_shape=[jax.ShapeDtypeStruct((hours, buses), jnp.float32), level_shape],
                in_specs=[SMEM] + [VMEM] * 8 + [HBM],
                out_specs=[VMEM] * 2,
                scratch_shapes=[held[0], held[2]] + sums,
                compiler_params=params,
                cost_estimate=pl.CostEstimate(flops=pass_flops, bytes_accessed=tile_bytes, transcendentals=0),
                name="last_price",
            )(blocks, dual, base, inject, delta, level, unit_block, unit_lane, gain, ptdf_tiles)

    own_dual = lax.all_to_all(
        jnp.swapaxes(line_dual, 0, 1).reshape(hours, own_groups * lines), "tm", split_axis=0, concat_axis=1, tiled=True
    )
    joined = jnp.concatenate([inject, level], axis=1)
    back = lax.all_to_all(
        joined.reshape(devices, hour_rows, buses + units), "tm", split_axis=0, concat_axis=0, tiled=True
    )
    inject = jnp.swapaxes(back[:, :, :buses], 0, 1).reshape(hour_rows, bus_count)
    level = jnp.sum(back[:, :, buses:], axis=0)
    return (inject, own_dual, level)


def solution(mesh):
    in_specs = (
        P(("scen", "tm"), None),
        P(None, "tm", None, None),
        P(None, "tm"),
        P(),
        P(),
        P(),
        P(("scen", "tm"), None),
    )
    out_specs = (P(("scen", "tm"), None), P(("scen", "tm"), None), P(("scen", "tm"), None))
    return jax.shard_map(shards, mesh=mesh, in_specs=in_specs, out_specs=out_specs, check_vma=False)
```

time: 462 us -> 204 us (0.44)
  waiting for transfers between devices: 201 us -> 25.1 us
  other arithmetic: 136 us -> 4.15 us
  Pallas kernels: 0 us -> 70.5 us
  blocking collectives: 0 us -> 68.8 us
  matrix products: 42.9 us -> 0 us
  local copies, waits for them, and re-layouts: 37.4 us -> 11.6 us
  between operations: 14.5 us -> 0.81 us
  starting transfers between devices: 28.1 us -> 22.1 us
    psum x2 -> x0, waiting for transfers between devices: 177 us -> none  [shards(): line_flows = lax.psum(partial_flow.reshape(total_hours, line_count), 'tm')]
    scatter-add x4 -> x0, other arithmetic: 125 us -> none  [the longest x2 102 us: shards(): summed = jnp.zeros((piece_rows, bus_blocks, tile_width), jnp.float32).at[...]
    pallas_call x0 -> x5, Pallas kernels: none -> 70.5 us  [the longest x1 28.5 us: shards(): pl.pallas_call(middle_kernel, out_shape=[block_shape, level_shape, flow_s...]
    all_gather x0 -> x3, blocking collectives: none -> 68.8 us  [the longest x2 43.6 us: shards(): lax.all_gather(line_dual.astype(jnp.bfloat16), 'tm', axis=0, tiled=True)]
    dot_general x4 -> x0, matrix products: 42.9 us -> none  [the longest x2 21.5 us: shards(): jnp.einsum('hgkb,gklb->hgl', picked, ptdf_tiles, preferred_element_type=j...]
    gather x4 -> x0, local copies, waits for them, and re-layouts: 28.8 us -> none  [the longest x2 23.5 us: shards(): store_price = bus_price[:, stor_bus]]
    ppermute x4 -> x0, starting transfers between devices: 8.98 us -> none  [the longest x2 8.47 us: padded_2(): lax.ppermute(lax.slice_in_dim(block, 0, width, axis=dim), axis, backward)]
    unnamed x19 -> x31, local copies, waits for them, and re-layouts: 2.81 us -> 9.04 us
  transfers between devices with their start and end apart: 10 -> 5, of which waited for: 6 -> 3; matrix products, arithmetic and copies ran while one was open for 19% -> 2% of each run, Pallas kernels for 0% -> 12%
where the time goes in v1:
time: 204 us; the launch traced here: 203 us
  Pallas kernels  70.5 us (35%)
  blocking collectives  68.8 us (34%)
  waiting for transfers between devices  25.1 us (12%)
  starting transfers between devices  22.1 us (11%)
  local copies, waits for them, and re-layouts  11.6 us (6%)
  other arithmetic  4.15 us (2%)
    all_gather x2, blocking collectives, shards(): lax.all_gather(line_dual.astype(jnp.bfloat16), 'tm', axis=0, tiled=True)  43.6 us
    pallas_call x1, Pallas kernels, shards(): pl.pallas_call(middle_kernel, out_shape=[block_shape, level_shape, flow_s...  28.5 us
    all_gather x1, blocking collectives, shards(): level = lax.all_gather(soc_init, 'tm', axis=0, tiled=True)  25.3 us
    pallas_call x1, Pallas kernels, shards(): pl.pallas_call(first_flow_kernel, out_shape=flow_shape, in_specs=[SMEM, V...  17.5 us
    pallas_call x1, Pallas kernels, shards(): pl.pallas_call(last_kernel, out_shape=[jax.ShapeDtypeStruct((hours, buses...  13.2 us
    pallas_call x2, Pallas kernels, shards(): pl.pallas_call(storage_kernel, out_shape=block_shape, in_specs=[VMEM] * 3...  11.3 us
    all_to_all x1, waiting for transfers between devices, shards(): lax.all_to_all(joined.reshape(devices, hour_rows, buses + units), 'tm', s...  10.3 us
    unnamed x31, local copies, waits for them, and re-layouts  9.04 us
  transfers between devices with their start and end apart: 5, of which 3 were waited for; matrix products, arithmetic and copies ran while one was open for 2% of the time, Pallas kernels for 12%

profile of v1, /device:TPU:0, one launch (start us, length us, event | category | flops | bytes accessed | tf_op | source)
XLA Modules:
  0.0 203.0 jit_solution(2614245594261997039)
XLA Ops:
  1.2 2.0 reduce.1
  3.1 0.7 reshape.55
  3.8 7.4 %all-to-all-start = ((bf16[16,2,1152]{2,1,0:T(2,128)(2,1)}), bf16[16,2,1152]{2,1,0:T(2,128)(2,1)S(1)}, u32[]{:S(2)}, u32[]{:S(2)}) async-start(bf16[16,2,1152]{2,1,0:T(2,128)(2,1)} %reshape.55), calls=%async_computation | async-start | bytes 147456 | tf_op jit(solution)/shard_map/all_to_all | solution.py:231
  11.2 0.8 copy.16
  12.2 6.0 %all-to-all-done = bf16[16,2,1152]{2,1,0:T(2,128)(2,1)S(1)} async-done(((bf16[16,2,1152]{2,1,0:T(2,128)(2,1)}), bf16[16,2,1152]{2,1,0:T(2,128)(2,1)S(1)}, u32[]{:S(2)}, u32[]{:S(2)}) %all-to-all-start) | async-done | bytes 73760 | tf_op jit(solution)/shard_map/all_to_all | solution.py:231
  18.3 17.5 %first_flow.1 = bf16[128,16,128]{2,1,0:T(8,128)(2,1)} custom-call(s32[640]{0:T(1024)S(1)} %reshape.45.blocks, bf16[16,2304]{1,0:T(8,128)(2,1)S(1)} %bitcast.41, bf16[128,5,128,128]{3,2,1,0:T(8,128)(2,1)} %tiles_hbm.5), custom_call_target="tpu_custom_call" | custom-call | flops 335544320 | bytes 20971520 | tf_op jit(solution)/shard_map/first_flow/pallas_call | solution.py:233
  35.8 3.6 %all-to-all-start.1 = ((bf16[16,8,16,128]{3,2,1,0:T(8,128)(2,1)}), bf16[16,8,16,128]{3,2,1,0:T(8,128)(2,1)S(1)}, u32[]{:S(2)}, u32[]{:S(2)}) async-start(bf16[16,8,16,128]{3,2,1,0:T(8,128)(2,1)} %bitcast.1), calls=%async_computation.1 | async-start | bytes 1048576 | tf_op jit(solution)/shard_map/all_to_all | solution.py:255
  39.4 25.3 %all-gather = f32[16,1,2048]{2,1,0:T(1,128)S(1)} all-gather(f32[1,1,2048]{2,1,0:T(1,128)S(1)} %bitcast.60), channel_id=1, replica_groups=mesh['scen'=2,'tm'=16] {'tm'}, dimensions={0}, use_global_device_ids=true | all-gather | bytes 139264 | tf_op jit(solution)/shard_map/all_gather | solution.py:230
  64.6 0.7 copy.24
  66.0 5.7 %storage.2.delta = f32[18,16,128]{2,1,0:T(8,128)} custom-call(f32[16,2048]{1,0:T(8,128)} %bitcast.44, s32[1,2048]{1,0:T(1,128)} %bitcast.50, s32[1,2048]{1,0:T(1,128)} %bitcast.46), custom_call_target="tpu_custom_call" | custom-call | flops 335544320 | bytes 131072 | tf_op jit(solution)/shard_map/storage/pallas_call | solution.py:247
  71.6 0.7 dynamic-slice_bitcast_fusion
  72.4 20.3 %all_gather.9.dual = bf16[128,16,128]{2,1,0:T(8,128)(2,1)S(1)} all-gather(bf16[8,16,128]{2,1,0:T(8,128)(2,1)S(1)} %fusion.2), channel_id=1, replica_groups=mesh['scen'=2,'tm'=16] {'tm'}, dimensions={0}, use_global_device_ids=true | all-gather | bytes 557056 | tf_op jit(solution)/shard_map/all_gather | solution.py:261
  92.8 0.9 copy-done
  93.7 0.9 copy-done.1
  94.6 0.7 copy-done.5
  95.3 0.7 copy-done.7
  96.0 28.5 %price_then_flow.1 = (f32[18,16,128]{2,1,0:T(8,128)S(1)}, f32[16,2048]{1,0:T(8,128)S(1)}, bf16[128,16,128]{2,1,0:T(8,128)(2,1)}) custom-call(s32[640]{0:T(1024)S(1)} %reshape.45.blocks, bf16[128,16,128]{2,1,0:T(8,128)(2,1)S(1)} %all_gather.9.dual, bf16[16,2304]{1,0:T(8,128)(2,1)S(1)} %bitcast.42, f32[18,16,128]{2,1,0:T(8,128)S(1)} %copy-done.1, ...), custom_call_target="tpu_custom_call" | custom-call | flops 671088640 | bytes 20971520 | tf_op jit(solution)/shard_map/price_then_flow/pallas_call | solution.py:263
  124.5 0.6 copy-done.3
  125.1 3.6 %all-to-all-start.2 = ((bf16[16,8,16,128]{3,2,1,0:T(8,128)(2,1)}), bf16[16,8,16,128]{3,2,1,0:T(8,128)(2,1)S(1)}, u32[]{:S(2)}, u32[]{:S(2)}) async-start(bf16[16,8,16,128]{3,2,1,0:T(8,128)(2,1)} %bitcast.9), calls=%async_computation.2 | async-start | bytes 1048576 | tf_op jit(solution)/shard_map/all_to_all | solution.py:255
  128.7 5.6 %storage.3.delta = f32[18,16,128]{2,1,0:T(8,128)} custom-call(f32[16,2048]{1,0:T(8,128)} %copy-done.3, s32[1,2048]{1,0:T(1,128)} %bitcast.51, s32[1,2048]{1,0:T(1,128)} %bitcast.47), custom_call_target="tpu_custom_call" | custom-call | flops 335544320 | bytes 131072 | tf_op jit(solution)/shard_map/storage/pallas_call | solution.py:247
  134.4 8.8 %all-to-all-done.2 = bf16[16,8,16,128]{3,2,1,0:T(8,128)(2,1)S(1)} async-done(((bf16[16,8,16,128]{3,2,1,0:T(8,128)(2,1)}), bf16[16,8,16,128]{3,2,1,0:T(8,128)(2,1)S(1)}, u32[]{:S(2)}, u32[]{:S(2)}) %all-to-all-start.2) | async-done | bytes 524320 | tf_op jit(solution)/shard_map/all_to_all | solution.py:255
  143.3 0.7 copy.18
  143.9 4.0 %all-to-all-start.4 = ((f32[16,1,1024]{2,1,0:T(1,128)}), f32[16,1,1024]{2,1,0:T(1,128)S(1)}, u32[]{:S(2)}, u32[]{:S(2)}) async-start(f32[16,1,1024]{2,1,0:T(1,128)} %bitcast.14), calls=%async_computation.4 | async-start | bytes 131072 | tf_op jit(solution)/shard_map/all_to_all | solution.py:287
  148.0 23.2 %all_gather.11.dual = bf16[128,16,128]{2,1,0:T(8,128)(2,1)S(1)} all-gather(bf16[8,16,128]{2,1,0:T(8,128)(2,1)S(1)} %subtract_convert_fusion), channel_id=1, replica_groups=mesh['scen'=2,'tm'=16] {'tm'}, dimensions={0}, use_global_device_ids=true | all-gather | bytes 557056 | tf_op jit(solution)/shard_map/all_gather | solution.py:261
  171.2 0.9 copy-done.2
  172.1 0.9 copy-done.4
  173.0 13.2 %last_price.1 = (f32[16,2304]{1,0:T(8,128)S(1)}, f32[16,2048]{1,0:T(8,128)S(1)}) custom-call(s32[640]{0:T(1024)S(1)} %reshape.45.blocks, bf16[128,16,128]{2,1,0:T(8,128)(2,1)S(1)} %all_gather.11.dual, bf16[16,2304]{1,0:T(8,128)(2,1)S(1)} %bitcast.43, f32[18,16,128]{2,1,0:T(8,128)S(1)} %get-tuple-element.9.inject, f32[18,16,128]{2,1,0:T(8,128)S(1)} %copy-done.2, ...), custom_call_target="tpu_custom_call" | custom-call | flops 335544320 | bytes 20971520 | tf_op jit(solution)/shard_map/last_price/pallas_call | solution.py:276
  186.3 1.0 copy.17
  187.3 3.5 %all-to-all-start.3 = ((f32[16,1,4352]{2,1,0:T(1,128)}), f32[16,1,4352]{2,1,0:T(1,128)S(1)}, u32[]{:S(2)}, u32[]{:S(2)}) async-start(f32[16,1,4352]{2,1,0:T(1,128)} %copy.17), calls=%async_computation.3 | async-start | bytes 557056 | tf_op jit(solution)/shard_map/all_to_all | solution.py:291
  190.8 10.3 %all-to-all-done.3 = f32[16,1,4352]{2,1,0:T(1,128)S(1)} async-done(((f32[16,1,4352]{2,1,0:T(1,128)}), f32[16,1,4352]{2,1,0:T(1,128)S(1)}, u32[]{:S(2)}, u32[]{:S(2)}) %all-to-all-start.3) | async-done | bytes 278560 | tf_op jit(solution)/shard_map/all_to_all | solution.py:291
  201.1 0.7 slice_reduce_fusion
  201.7 0.7 slice.8
  (31 shorter events, 2.3 us)
Async XLA Ops:
  0.6 38.7 %copy-start.10 = (f32[1,2048]{1,0:T(1,128)S(1)}, f32[1,2048]{1,0:T(1,128)}, u32[]{:S(2)}) copy-start(f32[1,2048]{1,0:T(1,128)} %param.13) | copy-start | bytes 24580
  0.6 64.7 %copy-start.11 = (s32[2048]{0:T(1024)S(1)}, s32[2048]{0:T(1024)}, u32[]{:S(2)}) copy-start(s32[2048]{0:T(1024)} %param.11) | copy-start | bytes 24580
  0.7 92.1 %copy-start.9 = (f32[2048]{0:T(1024)S(1)}, f32[2048]{0:T(1024)}, u32[]{:S(2)}) copy-start(f32[2048]{0:T(1024)} %param.12) | copy-start | bytes 24580
  3.8 14.4 %all-to-all-start = ((bf16[16,2,1152]{2,1,0:T(2,128)(2,1)}), bf16[16,2,1152]{2,1,0:T(2,128)(2,1)S(1)}, u32[]{:S(2)}, u32[]{:S(2)}) async-start(bf16[16,2,1152]{2,1,0:T(2,128)(2,1)} %reshape.55), calls=%async_computation | async-start | bytes 147456 | tf_op jit(solution)/shard_map/all_to_all | solution.py:231
  35.8 36.5 %all-to-all-start.1 = ((bf16[16,8,16,128]{3,2,1,0:T(8,128)(2,1)}), bf16[16,8,16,128]{3,2,1,0:T(8,128)(2,1)S(1)}, u32[]{:S(2)}, u32[]{:S(2)}) async-start(bf16[16,8,16,128]{3,2,1,0:T(8,128)(2,1)} %bitcast.1), calls=%async_computation.1 | async-start | bytes 1048576 | tf_op jit(solution)/shard_map/all_to_all | solution.py:255
  65.9 105.3 %copy-start.6 = (s32[2048]{0:T(1024)S(1)}, s32[2048]{0:T(1024)}, u32[]{:S(2)}) copy-start(s32[2048]{0:T(1024)} %get-tuple-element.15) | copy-start | bytes 24580
  66.0 105.3 %copy-start.8 = (s32[2048]{0:T(1024)S(1)}, s32[2048]{0:T(1024)}, u32[]{:S(2)}) copy-start(s32[2048]{0:T(1024)} %get-tuple-element.16) | copy-start | bytes 24580
  92.8 0.9 copy-start
  93.7 0.9 copy-start.1
  94.6 0.7 copy-start.5
  95.3 0.7 copy-start.7
  124.5 0.7 copy-start.3
  125.1 18.0 %all-to-all-start.2 = ((bf16[16,8,16,128]{3,2,1,0:T(8,128)(2,1)}), bf16[16,8,16,128]{3,2,1,0:T(8,128)(2,1)S(1)}, u32[]{:S(2)}, u32[]{:S(2)}) async-start(bf16[16,8,16,128]{3,2,1,0:T(8,128)(2,1)} %bitcast.9), calls=%async_computation.2 | async-start | bytes 1048576 | tf_op jit(solution)/shard_map/all_to_all | solution.py:255
  143.9 43.3 %all-to-all-start.4 = ((f32[16,1,1024]{2,1,0:T(1,128)}), f32[16,1,1024]{2,1,0:T(1,128)S(1)}, u32[]{:S(2)}, u32[]{:S(2)}) async-start(f32[16,1,1024]{2,1,0:T(1,128)} %bitcast.14), calls=%async_computation.4 | async-start | bytes 131072 | tf_op jit(solution)/shard_map/all_to_all | solution.py:287
  171.2 0.9 copy-start.2
  172.1 0.9 copy-start.4
  187.3 13.8 %all-to-all-start.3 = ((f32[16,1,4352]{2,1,0:T(1,128)}), f32[16,1,4352]{2,1,0:T(1,128)S(1)}, u32[]{:S(2)}, u32[]{:S(2)}) async-start(f32[16,1,4352]{2,1,0:T(1,128)} %copy.17), calls=%async_computation.3 | async-start | bytes 557056 | tf_op jit(solution)/shard_map/all_to_all | solution.py:291

commit v2 on v1

--- a/solution.py
+++ b/solution.py
@@ -17,67 +17,84 @@
 NT = (((1,), (1,)), ((), ()))
 VMEM = pl.BlockSpec(memory_space=pltpu.VMEM)
 SMEM = pl.BlockSpec(memory_space=pltpu.SMEM)
-HBM = pl.BlockSpec(memory_space=pl.ANY)
-UNROLL = 4
-CHUNKS = 16
-
-
-def fetch(tiles_hbm, tiles, sems, chunk):
-    size = tiles.shape[0] // sems.shape[0]
-    part = pl.ds(chunk * size, size)
-    return pltpu.make_async_copy(tiles_hbm.at[part], tiles.at[part], sems.at[chunk])
-
-
-def fetch_all(tiles_hbm, tiles, sems):
-    for chunk in range(sems.shape[0]):
-        fetch(tiles_hbm, tiles, sems, chunk).start()
-
-
-def flow_pass(picked, blocks, tiles, flows, ready):
-    groups, depth = tiles.shape[0], tiles.shape[1]
-    size = groups // CHUNKS
-
-    def chunk_body(chunk, carry):
-        ready(chunk)
-
-        def body(step, inner):
-            for u in range(UNROLL):
-                g = chunk * size + step * UNROLL + u
-                total = None
-                for k in range(depth):
-                    rows = picked[blocks[g * depth + k]]
-                    part = lax.dot_general(rows, tiles[g, k], NT, preferred_element_type=jnp.float32)
-                    total = part if total is None else total + part
-                flows[g] = total.astype(flows.dtype)
-            return inner
-
-        return lax.fori_loop(0, size // UNROLL, body, carry)
-
-    lax.fori_loop(0, CHUNKS, chunk_body, 0)
-
-
-def price_pass(dual, blocks, tiles, sums, ready):
-    groups, depth = tiles.shape[0], tiles.shape[1]
-    size = groups // CHUNKS
+PARAMS = pltpu.CompilerParams(vmem_limit_bytes=12 << 20)
+
+
+def flow_pass(picked, blocks, tiles, flows):
+    groups, depth, lines = tiles.shape[0], tiles.shape[1], tiles.shape[2]
+    hours = picked.shape[1]
+
+    def body(step, carry):
+        base = step * 4
+        rows = [[picked[blocks[(base + u) * depth + k]] for k in range(depth)] for u in range(4)]
+        zero = jnp.zeros_like(rows[0][0])
+        totals = [None] * 4
+
+        def add(u, part):
+            totals[u] = part if totals[u] is None else totals[u] + part
+
+        for first in (0, 2):
+            for k in range(0, depth - 1, 2):
+                left = wide([[rows[first][k], rows[first][k + 1]], [rows[first + 1][k], rows[first + 1][k + 1]]])
+                g = base + first
+                right = wide([[tiles[g, k], tiles[g, k + 1]], [tiles[g + 1, k], tiles[g + 1, k + 1]]])
+                part = lax.dot_general(left, right, NT, preferred_element_type=jnp.float32)
+                add(first, part[:hours, :lines])
+                add(first + 1, part[hours:, lines:])
+        if depth % 2:
+            k = depth - 1
+            left = wide([[rows[0][k], zero], [rows[1][k], zero], [zero, rows[2][k]], [zero, rows[3][k]]])
+            right = wide([[tiles[base, k], tiles[base + 2, k]], [tiles[base + 1, k], tiles[base + 3, k]]])
+            part = lax.dot_general(left, right, NT, preferred_element_type=jnp.float32)
+            for u in range(4):
+                at = (u % 2) * lines
+                add(u, part[u * hours : (u + 1) * hours, at : at + lines])
+        for u in range(4):
+            flows[base + u] = totals[u].astype(flows.dtype)
+        return carry
+
+    lax.fori_loop(0, groups // 4, body, 0)
+
+
+def wide(parts):
+    return jnp.concatenate([jnp.concatenate(row, axis=1) for row in parts], axis=0)
+
+
+def price_pass(dual, blocks, tiles, sums):
+    groups, depth, width = tiles.shape[0], tiles.shape[1], tiles.shape[3]
+    hours = dual.shape[1]
     for ref in sums:
         ref[...] = jnp.zeros_like(ref)
 
-    def chunk_body(chunk, carry):
-        ready(chunk)
-
-        def body(step, inner):
-            for u in range(UNROLL):
-                g = chunk * size + step * UNROLL + u
-                rows = dual[g]
-                for k in range(depth):
-                    part = jnp.dot(rows, tiles[g, k], preferred_element_type=jnp.float32)
-                    at = blocks[g * depth + k]
-                    sums[k][at] = sums[k][at] + part
-            return inner
-
-        return lax.fori_loop(0, size // UNROLL, body, carry)
-
-    lax.fori_loop(0, CHUNKS, chunk_body, 0)
+    def body(step, carry):
+        base = step * 4
+        rows = [dual[base + u] for u in range(4)]
+        zero = jnp.zeros_like(rows[0])
+        parts = []
+        for first in (0, 2):
+            left = wide([[rows[first], zero], [zero, rows[first + 1]]])
+            for k in range(0, depth - 1, 2):
+                g = base + first
+                right = wide([[tiles[g, k], tiles[g, k + 1]], [tiles[g + 1, k], tiles[g + 1, k + 1]]])
+                part = jnp.dot(left, right, preferred_element_type=jnp.float32)
+                for u in range(2):
+                    for j in range(2):
+                        block = part[u * hours : (u + 1) * hours, j * width : (j + 1) * width]
+                        parts.append((first + u, k + j, block))
+        if depth % 2:
+            k = depth - 1
+            left = wide([[rows[0], zero], [zero, rows[1]], [rows[2], zero], [zero, rows[3]]])
+            right = wide([[tiles[base, k], tiles[base + 2, k]], [tiles[base + 1, k], tiles[base + 3, k]]])
+            part = jnp.dot(left, right, preferred_element_type=jnp.float32)
+            for u in range(4):
+                at = (u // 2) * width
+                parts.append((u, k, part[u * hours : (u + 1) * hours, at : at + width]))
+        for u, k, part in parts:
+            at = blocks[(base + u) * depth + k]
+            sums[k][at] = sums[k][at] + part
+        return carry
+
+    lax.fori_loop(0, groups // 4, body, 0)
 
 
 def earlier(values):
@@ -126,21 +143,30 @@
     lax.fori_loop(0, level.shape[1] // width, body, 0)
 
 
-def first_flow_kernel(blocks, base, tiles_hbm, flows, tiles, picked, sems):
-    fetch_all(tiles_hbm, tiles, sems)
+def hold_kernel(tiles_hbm, tiles, sems):
+    size = tiles.shape[0] // sems.shape[0]
+    copies = []
+    for chunk in range(sems.shape[0]):
+        part = pl.ds(chunk * size, size)
+        copies.append(pltpu.make_async_copy(tiles_hbm.at[part], tiles.at[part], sems.at[chunk]))
+        copies[-1].start()
+    for copy in copies:
+        copy.wait()
+
+
+def first_flow_kernel(blocks, base, tiles, flows, picked):
     width = tiles.shape[3]
     for b in range(picked.shape[0]):
         picked[b] = base[:, b * width : (b + 1) * width]
-    flow_pass(picked, blocks, tiles, flows, lambda c: fetch(tiles_hbm, tiles, sems, c).wait())
+    flow_pass(picked, blocks, tiles, flows)
 
 
 def middle_kernel(
-    blocks, dual, base, delta, level, unit_block, unit_lane, gain, tiles_hbm,
-    inject_out, level_out, flows, tiles, picked, sems, *sums
+    blocks, dual, base, delta, level, unit_block, unit_lane, gain, tiles,
+    inject_out, level_out, flows, picked, *sums
 ):
-    fetch_all(tiles_hbm, tiles, sems)
     width = tiles.shape[3]
-    price_pass(dual, blocks, tiles, sums, lambda c: fetch(tiles_hbm, tiles, sems, c).wait())
+    price_pass(dual, blocks, tiles, sums)
 
     def start(b):
         return base[:, b * width : (b + 1) * width].astype(jnp.float32)
@@ -149,17 +175,16 @@
         inject_out[b] = new
 
     update_pass(sums, start, start, delta, write, picked)
-    flow_pass(picked, blocks, tiles, flows, lambda c: None)
+    flow_pass(picked, blocks, tiles, flows)
     level_pass(sums[0], level, unit_block, unit_lane, gain, level_out, False)
 
 
 def last_kernel(
-    blocks, dual, base, inject, delta, level, unit_block, unit_lane, gain, tiles_hbm,
-    inject_out, level_out, tiles, sems, *sums
+    blocks, dual, base, inject, delta, level, unit_block, unit_lane, gain, tiles,
+    inject_out, level_out, *sums
 ):
-    fetch_all(tiles_hbm, tiles, sems)
     width = tiles.shape[3]
-    price_pass(dual, blocks, tiles, sums, lambda c: fetch(tiles_hbm, tiles, sems, c).wait())
+    price_pass(dual, blocks, tiles, sums)
 
     def start(b):
         return base[:, b * width : (b + 1) * width].astype(jnp.float32)
@@ -215,31 +240,44 @@
     own_limits = lax.dynamic_slice_in_dim(limits.reshape(groups, 1, lines), me * own_groups, own_groups, 0)
 
     tile_bytes = ptdf_tiles.size * 2
-    held = [
-        pltpu.VMEM(ptdf_tiles.shape, ptdf_tiles.dtype),
-        pltpu.VMEM((bus_blocks, hours, width), jnp.bfloat16),
-        pltpu.SemaphoreType.DMA((CHUNKS,)),
-    ]
+    held = [pltpu.VMEM((bus_blocks, hours, width), jnp.bfloat16)]
     sums = [pltpu.VMEM((bus_blocks, hours, width), jnp.float32)] * depth
-    params = pltpu.CompilerParams(vmem_limit_bytes=tile_bytes + (16 << 20))
     pass_flops = 2 * hours * ptdf_tiles.size
     flow_shape = jax.ShapeDtypeStruct((groups, hours, lines), jnp.bfloat16)
     block_shape = jax.ShapeDtypeStruct((bus_blocks, hours, width), jnp.float32)
     level_shape = jax.ShapeDtypeStruct((hours, units), jnp.float32)
 
-    level = lax.all_gather(soc_init, "tm", axis=0, tiled=True)
-    base = lax.all_to_all(base_injection, "tm", split_axis=1, concat_axis=0, tiled=True)
-
+    high = soc_init.astype(jnp.bfloat16)
+    low = (soc_init - high.astype(jnp.float32)).astype(jnp.bfloat16)
+    own = jnp.concatenate([high, low], axis=1)[:, None, :]
+    sent = jnp.concatenate(
+        [base_injection.reshape(hour_rows, devices, buses), jnp.broadcast_to(own, (hour_rows, devices, 2 * units))], axis=2
+    )
+    came = lax.all_to_all(jnp.swapaxes(sent, 0, 1), "tm", split_axis=0, concat_axis=0, tiled=True)
+    came = came.reshape(hours, buses + 2 * units)
+    base = came[:, :buses]
+    level = came[:, buses : buses + units].astype(jnp.float32) + came[:, buses + units :].astype(jnp.float32)
+
+    tiles = pl.pallas_call(
+        hold_kernel,
+        out_shape=jax.ShapeDtypeStruct(ptdf_tiles.shape, ptdf_tiles.dtype),
+        in_specs=[pl.BlockSpec(memory_space=pltpu.HBM)],
+        out_specs=VMEM,
+        scratch_shapes=[pltpu.SemaphoreType.DMA((16,))],
+        compiler_params=PARAMS,
+        cost_estimate=pl.CostEstimate(flops=0, bytes_accessed=2 * tile_bytes, transcendentals=0),
+        name="hold_tiles",
+    )(ptdf_tiles)
     flows = pl.pallas_call(
         first_flow_kernel,
         out_shape=flow_shape,
-        in_specs=[SMEM, VMEM, HBM],
+        in_specs=[SMEM, VMEM, VMEM],
         out_specs=VMEM,
         scratch_shapes=held,
-        compiler_params=params,
+        compiler_params=PARAMS,
         cost_estimate=pl.CostEstimate(flops=pass_flops, bytes_accessed=tile_bytes, transcendentals=0),
         name="first_flow",
-    )(blocks, base, ptdf_tiles)
+    )(blocks, base, tiles)
 
     line_dual = jnp.zeros((own_groups, hours, lines), jnp.float32)
     inject = None
@@ -249,6 +287,7 @@
             out_shape=block_shape,
             in_specs=[VMEM] * 3,
             out_specs=VMEM,
+            compiler_params=PARAMS,
             cost_estimate=pl.CostEstimate(flops=pass_flops, bytes_accessed=units * hours * 4, transcendentals=0),
             name="storage",
         )(level, unit_block, unit_lane)
@@ -263,26 +302,26 @@
             inject, level, flows = pl.pallas_call(
                 middle_kernel,
                 out_shape=[block_shape, level_shape, flow_shape],
-                in_specs=[SMEM] + [VMEM] * 7 + [HBM],
+                in_specs=[SMEM] + [VMEM] * 8,
                 out_specs=[VMEM] * 3,
                 scratch_shapes=held + sums,
-                compiler_params=params,
+                compiler_params=PARAMS,
                 cost_estimate=pl.CostEstimate(
                     flops=2 * pass_flops, bytes_accessed=tile_bytes, transcendentals=0
                 ),
                 name="price_then_flow",
-            )(blocks, dual, base, delta, level, unit_block, unit_lane, gain, ptdf_tiles)
+            )(blocks, dual, base, delta, level, unit_block, unit_lane, gain, tiles)
         else:
             inject, level = pl.pallas_call(
                 last_kernel,
                 out_shape=[jax.ShapeDtypeStruct((hours, buses), jnp.float32), level_shape],
-                in_specs=[SMEM] + [VMEM] * 8 + [HBM],
+                in_specs=[SMEM] + [VMEM] * 9,
                 out_specs=[VMEM] * 2,
-                scratch_shapes=[held[0], held[2]] + sums,
-                compiler_params=params,
+                scratch_shapes=sums,
+                compiler_params=PARAMS,
                 cost_estimate=pl.CostEstimate(flops=pass_flops, bytes_accessed=tile_bytes, transcendentals=0),
                 name="last_price",
-            )(blocks, dual, base, inject, delta, level, unit_block, unit_lane, gain, ptdf_tiles)
+            )(blocks, dual, base, inject, delta, level, unit_block, unit_lane, gain, tiles)
 
     own_dual = lax.all_to_all(
         jnp.swapaxes(line_dual, 0, 1).reshape(hours, own_groups * lines), "tm", split_axis=0, concat_axis=1, tiled=True

time: 204 us -> 200 us (0.980)
  local copies, waits for them, and re-layouts: 11.6 us -> 40.3 us
  blocking collectives: 68.8 us -> 44.5 us
  Pallas kernels: 70.5 us -> 54.2 us
  waiting for transfers between devices: 25.1 us -> 30.4 us
  starting transfers between devices: 22.1 us -> 24.5 us
    unnamed x31 -> x19, local copies, waits for them, and re-layouts: 9.04 us -> 37.1 us
    all_gather x1 -> x0, blocking collectives: 25.3 us -> none  [shards(): level = lax.all_gather(soc_init, 'tm', axis=0, tiled=True)]
    all_to_all x2, waiting for transfers between devices: 8.79 us -> 20.1 us  [shards(): lax.all_to_all(flows.reshape(devices, own_groups, hours, lines), 'tm', sp...]
    pallas_call x1, Pallas kernels: 28.5 us -> 22 us  [shards(): pl.pallas_call(middle_kernel, out_shape=[block_shape, level_shape, flow_s...]
    all_to_all x1, waiting for transfers between devices: 6.01 us -> 0.01 us  [shards(): lax.all_to_all(jnp.swapaxes(sent, 0, 1), 'tm', split_axis=0, concat_axis=...]
    pallas_call x1, Pallas kernels: 17.5 us -> 12.3 us  [shards(): pl.pallas_call(first_flow_kernel, out_shape=flow_shape, in_specs=[SMEM, V...]
    pallas_call x2, Pallas kernels: 11.3 us -> 8.05 us  [shards(): pl.pallas_call(storage_kernel, out_shape=block_shape, in_specs=[VMEM] * 3...]
    pallas_call x1, Pallas kernels: 13.2 us -> 10.3 us  [shards(): pl.pallas_call(last_kernel, out_shape=[jax.ShapeDtypeStruct((hours, buses...]
  transfers between devices with their start and end apart: 5 -> 5, of which waited for: 3 -> 3; matrix products, arithmetic and copies ran while one was open for 2% -> 1% of each run, Pallas kernels for 12% -> 10%
where the time goes in v2:
time: 200 us; the launch traced here: 199 us
  Pallas kernels  54.2 us (27%)
  blocking collectives  44.5 us (22%)
  local copies, waits for them, and re-layouts  40.3 us (20%)
  waiting for transfers between devices  30.4 us (15%)
  starting transfers between devices  24.5 us (12%)
  other arithmetic  4.55 us (2%)
    all_gather x2, blocking collectives, shards(): lax.all_gather(line_dual.astype(jnp.bfloat16), 'tm', axis=0, tiled=True)  44.5 us
    unnamed x19, local copies, waits for them, and re-layouts  37.1 us
    pallas_call x1, Pallas kernels, shards(): pl.pallas_call(middle_kernel, out_shape=[block_shape, level_shape, flow_s...  22 us
    all_to_all x2, waiting for transfers between devices, shards(): lax.all_to_all(flows.reshape(devices, own_groups, hours, lines), 'tm', sp...  20.1 us
    pallas_call x1, Pallas kernels, shards(): pl.pallas_call(first_flow_kernel, out_shape=flow_shape, in_specs=[SMEM, V...  12.3 us
    pallas_call x1, Pallas kernels, shards(): pl.pallas_call(last_kernel, out_shape=[jax.ShapeDtypeStruct((hours, buses...  10.3 us
    all_to_all x1, waiting for transfers between devices, shards(): lax.all_to_all(joined.reshape(devices, hour_rows, buses + units), 'tm', s...  10.3 us
    all_to_all x2, starting transfers between devices, shards(): lax.all_to_all(flows.reshape(devices, own_groups, hours, lines), 'tm', sp...  9.58 us
  transfers between devices with their start and end apart: 5, of which 3 were waited for; matrix products, arithmetic and copies ran while one was open for 1% of the time, Pallas kernels for 10%

profile of v2, /device:TPU:0, one launch (start us, length us, event | category | flops | bytes accessed | tf_op | source)
XLA Modules:
  0.0 199.3 jit_solution(7202903672105981853)
XLA Ops:
  0.6 0.8 fusion.6
  1.4 1.3 reduce.1
  3.5 0.7 reduce.4
  4.2 0.7 reshape.61
  4.9 7.4 %all-to-all-start = ((bf16[16,2,3200]{2,1,0:T(2,128)(2,1)}), bf16[16,2,3200]{2,1,0:T(2,128)(2,1)S(1)}, u32[]{:S(2)}, u32[]{:S(2)}) async-start(bf16[16,2,3200]{2,1,0:T(2,128)(2,1)} %reshape.61), calls=%async_computation | async-start | bytes 409600 | tf_op jit(solution)/shard_map/all_to_all | solution.py:256
  12.3 0.8 copy.16
  13.4 7.0 %copy-done.4 = bf16[128,5,128,128]{3,2,1,0:T(8,128)(2,1)S(1)} copy-done((bf16[128,5,128,128]{3,2,1,0:T(8,128)(2,1)S(1)}, bf16[128,5,128,128]{3,2,1,0:T(8,128)(2,1)}, u32[]{:S(2)}) %copy-start.4) | copy-done | bytes 20971544
  20.3 1.6 hold_tiles.1.tiles
  21.9 7.0 %copy-done = bf16[128,5,128,128]{3,2,1,0:T(8,128)(2,1)} copy-done((bf16[128,5,128,128]{3,2,1,0:T(8,128)(2,1)}, bf16[128,5,128,128]{3,2,1,0:T(8,128)(2,1)S(1)}, u32[]{:S(2)}) %copy-start) | copy-done | bytes 20971544
  29.1 7.0 %copy-done.1 = bf16[128,5,128,128]{3,2,1,0:T(8,128)(2,1)S(1)} copy-done((bf16[128,5,128,128]{3,2,1,0:T(8,128)(2,1)S(1)}, bf16[128,5,128,128]{3,2,1,0:T(8,128)(2,1)}, u32[]{:S(2)}) %copy-start.1) | copy-done | bytes 20971544
  36.0 12.3 %first_flow.1 = bf16[128,16,128]{2,1,0:T(8,128)(2,1)} custom-call(s32[640]{0:T(1024)S(1)} %reshape.48.blocks, bf16[16,2304]{1,0:T(8,128)(2,1)S(1)} %slice.20.base, bf16[128,5,128,128]{3,2,1,0:T(8,128)(2,1)S(1)} %copy-done.1), custom_call_target="tpu_custom_call" | custom-call | flops 335544320 | bytes 20971520 | tf_op jit(solution)/shard_map/first_flow/pallas_call | solution.py:271
  48.3 6.0 %all-to-all-start.1 = ((bf16[16,8,16,128]{3,2,1,0:T(8,128)(2,1)}), bf16[16,8,16,128]{3,2,1,0:T(8,128)(2,1)S(1)}, u32[]{:S(2)}, u32[]{:S(2)}) async-start(bf16[16,8,16,128]{3,2,1,0:T(8,128)(2,1)} %bitcast.1), calls=%async_computation.1 | async-start | bytes 1048576 | tf_op jit(solution)/shard_map/all_to_all | solution.py:294
  54.4 0.7 dynamic-slice_bitcast_fusion
  55.1 4.0 %storage.2.delta = f32[18,16,128]{2,1,0:T(8,128)S(1)} custom-call(f32[16,2048]{1,0:T(8,128)S(1)} %convert_add_fusion.level, s32[1,2048]{1,0:T(1,128)S(1)} %bitcast.40, s32[1,2048]{1,0:T(1,128)S(1)} %bitcast.36), custom_call_target="tpu_custom_call" | custom-call | flops 335544320 | bytes 131072 | tf_op jit(solution)/shard_map/storage/pallas_call | solution.py:285
  59.1 9.7 %all-to-all-done.1 = bf16[16,8,16,128]{3,2,1,0:T(8,128)(2,1)S(1)} async-done(((bf16[16,8,16,128]{3,2,1,0:T(8,128)(2,1)}), bf16[16,8,16,128]{3,2,1,0:T(8,128)(2,1)S(1)}, u32[]{:S(2)}, u32[]{:S(2)}) %all-to-all-start.1) | async-done | bytes 524320 | tf_op jit(solution)/shard_map/all_to_all | solution.py:294
  68.9 21.3 %all_gather.6.dual = bf16[128,16,128]{2,1,0:T(8,128)(2,1)S(1)} all-gather(bf16[8,16,128]{2,1,0:T(8,128)(2,1)S(1)} %fusion.2), channel_id=1, replica_groups=mesh['scen'=2,'tm'=16] {'tm'}, dimensions={0}, use_global_device_ids=true | all-gather | bytes 557056 | tf_op jit(solution)/shard_map/all_gather | solution.py:300
  90.2 7.0 %copy-done.2 = bf16[128,5,128,128]{3,2,1,0:T(8,128)(2,1)S(1)} copy-done((bf16[128,5,128,128]{3,2,1,0:T(8,128)(2,1)S(1)}, bf16[128,5,128,128]{3,2,1,0:T(8,128)(2,1)}, u32[]{:S(2)}) %copy-start.2) | copy-done | bytes 20971544
  97.2 22.0 %price_then_flow.1 = (f32[18,16,128]{2,1,0:T(8,128)S(1)}, f32[16,2048]{1,0:T(8,128)S(1)}, bf16[128,16,128]{2,1,0:T(8,128)(2,1)}) custom-call(s32[640]{0:T(1024)S(1)} %reshape.48.blocks, bf16[128,16,128]{2,1,0:T(8,128)(2,1)S(1)} %all_gather.6.dual, bf16[16,2304]{1,0:T(8,128)(2,1)S(1)} %slice.20.base, f32[18,16,128]{2,1,0:T(8,128)S(1)} %storage.2.delta, ...), custom_call_target="tpu_custom_call" | custom-call | flops 671088640 | bytes 20971520 | tf_op jit(solution)/shard_map/price_then_flow/pallas_call | solution.py:302
  119.1 3.6 %all-to-all-start.2 = ((bf16[16,8,16,128]{3,2,1,0:T(8,128)(2,1)}), bf16[16,8,16,128]{3,2,1,0:T(8,128)(2,1)S(1)}, u32[]{:S(2)}, u32[]{:S(2)}) async-start(bf16[16,8,16,128]{3,2,1,0:T(8,128)(2,1)} %bitcast.8), calls=%async_computation.2 | async-start | bytes 1048576 | tf_op jit(solution)/shard_map/all_to_all | solution.py:294
  122.7 4.0 %storage.3.delta = f32[18,16,128]{2,1,0:T(8,128)S(1)} custom-call(f32[16,2048]{1,0:T(8,128)S(1)} %get-tuple-element.10.level, s32[1,2048]{1,0:T(1,128)S(1)} %bitcast.42, s32[1,2048]{1,0:T(1,128)S(1)} %bitcast.38), custom_call_target="tpu_custom_call" | custom-call | flops 335544320 | bytes 131072 | tf_op jit(solution)/shard_map/storage/pallas_call | solution.py:285
  126.7 10.4 %all-to-all-done.2 = bf16[16,8,16,128]{3,2,1,0:T(8,128)(2,1)S(1)} async-done(((bf16[16,8,16,128]{3,2,1,0:T(8,128)(2,1)}), bf16[16,8,16,128]{3,2,1,0:T(8,128)(2,1)S(1)}, u32[]{:S(2)}, u32[]{:S(2)}) %all-to-all-start.2) | async-done | bytes 524320 | tf_op jit(solution)/shard_map/all_to_all | solution.py:294
  137.3 0.7 copy.19
  137.9 4.0 %all-to-all-start.4 = ((f32[16,1,1024]{2,1,0:T(1,128)}), f32[16,1,1024]{2,1,0:T(1,128)S(1)}, u32[]{:S(2)}, u32[]{:S(2)}) async-start(f32[16,1,1024]{2,1,0:T(1,128)} %bitcast.13), calls=%async_computation.4 | async-start | bytes 131072 | tf_op jit(solution)/shard_map/all_to_all | solution.py:326
  142.0 23.2 %all_gather.7.dual = bf16[128,16,128]{2,1,0:T(8,128)(2,1)S(1)} all-gather(bf16[8,16,128]{2,1,0:T(8,128)(2,1)S(1)} %subtract_convert_fusion), channel_id=1, replica_groups=mesh['scen'=2,'tm'=16] {'tm'}, dimensions={0}, use_global_device_ids=true | all-gather | bytes 557056 | tf_op jit(solution)/shard_map/all_gather | solution.py:300
  165.2 7.0 %copy-done.3 = bf16[128,5,128,128]{3,2,1,0:T(8,128)(2,1)S(1)} copy-done((bf16[128,5,128,128]{3,2,1,0:T(8,128)(2,1)S(1)}, bf16[128,5,128,128]{3,2,1,0:T(8,128)(2,1)}, u32[]{:S(2)}) %copy-start.3) | copy-done | bytes 20971544
  172.2 10.3 %last_price.1 = (f32[16,2304]{1,0:T(8,128)S(1)}, f32[16,2048]{1,0:T(8,128)S(1)}) custom-call(s32[640]{0:T(1024)S(1)} %reshape.48.blocks, bf16[128,16,128]{2,1,0:T(8,128)(2,1)S(1)} %all_gather.7.dual, bf16[16,2304]{1,0:T(8,128)(2,1)S(1)} %slice.20.base, f32[18,16,128]{2,1,0:T(8,128)S(1)} %get-tuple-element.9.inject, f32[18,16,128]{2,1,0:T(8,128)S(1)} %storage.3.delta, ...), custom_call_target="tpu_custom_call" | custom-call | flops 335544320 | bytes 20971520 | tf_op jit(solution)/shard_map/last_price/pallas_call | solution.py:315
  182.5 1.0 copy.18
  183.5 3.5 %all-to-all-start.3 = ((f32[16,1,4352]{2,1,0:T(1,128)}), f32[16,1,4352]{2,1,0:T(1,128)S(1)}, u32[]{:S(2)}, u32[]{:S(2)}) async-start(f32[16,1,4352]{2,1,0:T(1,128)} %copy.18), calls=%async_computation.3 | async-start | bytes 557056 | tf_op jit(solution)/shard_map/all_to_all | solution.py:330
  187.1 10.3 %all-to-all-done.3 = f32[16,1,4352]{2,1,0:T(1,128)S(1)} async-done(((f32[16,1,4352]{2,1,0:T(1,128)}), f32[16,1,4352]{2,1,0:T(1,128)S(1)}, u32[]{:S(2)}, u32[]{:S(2)}) %all-to-all-start.3) | async-done | bytes 278560 | tf_op jit(solution)/shard_map/all_to_all | solution.py:330
  197.4 0.7 slice_reduce_fusion
  198.0 0.7 slice.23
  198.7 0.6 copy.26
  (28 shorter events, 1.4 us)
Async XLA Ops:
  4.9 23.9 %all-to-all-start = ((bf16[16,2,3200]{2,1,0:T(2,128)(2,1)}), bf16[16,2,3200]{2,1,0:T(2,128)(2,1)S(1)}, u32[]{:S(2)}, u32[]{:S(2)}) async-start(bf16[16,2,3200]{2,1,0:T(2,128)(2,1)} %reshape.61), calls=%async_computation | async-start | bytes 409600 | tf_op jit(solution)/shard_map/all_to_all | solution.py:256
  13.3 7.0 %copy-start.4 = (bf16[128,5,128,128]{3,2,1,0:T(8,128)(2,1)S(1)}, bf16[128,5,128,128]{3,2,1,0:T(8,128)(2,1)}, u32[]{:S(2)}) copy-start(bf16[128,5,128,128]{3,2,1,0:T(8,128)(2,1)} %tiles_hbm.1) | copy-start | bytes 62914564
  21.9 7.0 %copy-start = (bf16[128,5,128,128]{3,2,1,0:T(8,128)(2,1)}, bf16[128,5,128,128]{3,2,1,0:T(8,128)(2,1)S(1)}, u32[]{:S(2)}) copy-start(bf16[128,5,128,128]{3,2,1,0:T(8,128)(2,1)S(1)} %hold_tiles.1.tiles) | copy-start | bytes 62914564
  28.9 26.2 %copy-start.6 = (s32[2048]{0:T(1024)S(1)}, s32[2048]{0:T(1024)}, u32[]{:S(2)}) copy-start(s32[2048]{0:T(1024)} %param.11) | copy-start | bytes 24580
  28.9 61.3 %copy-start.5 = (f32[2048]{0:T(1024)S(1)}, f32[2048]{0:T(1024)}, u32[]{:S(2)}) copy-start(f32[2048]{0:T(1024)} %param.12) | copy-start | bytes 24580
  29.1 7.0 %copy-start.1 = (bf16[128,5,128,128]{3,2,1,0:T(8,128)(2,1)S(1)}, bf16[128,5,128,128]{3,2,1,0:T(8,128)(2,1)}, u32[]{:S(2)}) copy-start(bf16[128,5,128,128]{3,2,1,0:T(8,128)(2,1)} %copy-done) | copy-start | bytes 62914564
  48.3 20.5 %all-to-all-start.1 = ((bf16[16,8,16,128]{3,2,1,0:T(8,128)(2,1)}), bf16[16,8,16,128]{3,2,1,0:T(8,128)(2,1)S(1)}, u32[]{:S(2)}, u32[]{:S(2)}) async-start(bf16[16,8,16,128]{3,2,1,0:T(8,128)(2,1)} %bitcast.1), calls=%async_computation.1 | async-start | bytes 1048576 | tf_op jit(solution)/shard_map/all_to_all | solution.py:294
  90.2 7.0 %copy-start.2 = (bf16[128,5,128,128]{3,2,1,0:T(8,128)(2,1)S(1)}, bf16[128,5,128,128]{3,2,1,0:T(8,128)(2,1)}, u32[]{:S(2)}) copy-start(bf16[128,5,128,128]{3,2,1,0:T(8,128)(2,1)} %copy-done) | copy-start | bytes 62914564
  119.1 18.0 %all-to-all-start.2 = ((bf16[16,8,16,128]{3,2,1,0:T(8,128)(2,1)}), bf16[16,8,16,128]{3,2,1,0:T(8,128)(2,1)S(1)}, u32[]{:S(2)}, u32[]{:S(2)}) async-start(bf16[16,8,16,128]{3,2,1,0:T(8,128)(2,1)} %bitcast.8), calls=%async_computation.2 | async-start | bytes 1048576 | tf_op jit(solution)/shard_map/all_to_all | solution.py:294
  137.9 45.6 %all-to-all-start.4 = ((f32[16,1,1024]{2,1,0:T(1,128)}), f32[16,1,1024]{2,1,0:T(1,128)S(1)}, u32[]{:S(2)}, u32[]{:S(2)}) async-start(f32[16,1,1024]{2,1,0:T(1,128)} %bitcast.13), calls=%async_computation.4 | async-start | bytes 131072 | tf_op jit(solution)/shard_map/all_to_all | solution.py:326
  165.2 7.0 %copy-start.3 = (bf16[128,5,128,128]{3,2,1,0:T(8,128)(2,1)S(1)}, bf16[128,5,128,128]{3,2,1,0:T(8,128)(2,1)}, u32[]{:S(2)}) copy-start(bf16[128,5,128,128]{3,2,1,0:T(8,128)(2,1)} %copy-done) | copy-start | bytes 62914564
  183.5 13.8 %all-to-all-start.3 = ((f32[16,1,4352]{2,1,0:T(1,128)}), f32[16,1,4352]{2,1,0:T(1,128)S(1)}, u32[]{:S(2)}, u32[]{:S(2)}) async-start(f32[16,1,4352]{2,1,0:T(1,128)} %copy.18), calls=%async_computation.3 | async-start | bytes 557056 | tf_op jit(solution)/shard_map/all_to_all | solution.py:330

commit v3 on v2

--- a/solution.py
+++ b/solution.py
@@ -17,15 +17,39 @@
 NT = (((1,), (1,)), ((), ()))
 VMEM = pl.BlockSpec(memory_space=pltpu.VMEM)
 SMEM = pl.BlockSpec(memory_space=pltpu.SMEM)
-PARAMS = pltpu.CompilerParams(vmem_limit_bytes=12 << 20)
-
-
-def flow_pass(picked, blocks, tiles, flows):
+HBM = pl.BlockSpec(memory_space=pl.ANY)
+SMALL = pltpu.CompilerParams(vmem_limit_bytes=12 << 20)
+CHUNKS = 8
+
+
+def fetch(tiles_hbm, tiles, sems, chunk):
+    size = tiles.shape[0] // sems.shape[0]
+    part = pl.ds(chunk * size, size)
+    return pltpu.make_async_copy(tiles_hbm.at[part], tiles.at[part], sems.at[chunk])
+
+
+def fetch_all(tiles_hbm, tiles, sems):
+    for chunk in range(sems.shape[0]):
+        fetch(tiles_hbm, tiles, sems, chunk).start()
+
+
+def over_groups(groups, ready, four):
+    size = groups // CHUNKS
+
+    def body(chunk, carry):
+        ready(chunk)
+        for sub in range(0, size, 4):
+            four(chunk * size + sub)
+        return carry
+
+    lax.fori_loop(0, CHUNKS, body, 0)
+
+
+def flow_pass(picked, blocks, tiles, flows, ready):
     groups, depth, lines = tiles.shape[0], tiles.shape[1], tiles.shape[2]
     hours = picked.shape[1]
 
-    def body(step, carry):
-        base = step * 4
+    def four(base):
         rows = [[picked[blocks[(base + u) * depth + k]] for k in range(depth)] for u in range(4)]
         zero = jnp.zeros_like(rows[0][0])
         totals = [None] * 4
@@ -51,23 +75,21 @@
                 add(u, part[u * hours : (u + 1) * hours, at : at + lines])
         for u in range(4):
             flows[base + u] = totals[u].astype(flows.dtype)
-        return carry
-
-    lax.fori_loop(0, groups // 4, body, 0)
+
+    over_groups(groups, ready, four)
 
 
 def wide(parts):
     return jnp.concatenate([jnp.concatenate(row, axis=1) for row in parts], axis=0)
 
 
-def price_pass(dual, blocks, tiles, sums):
+def price_pass(dual, blocks, tiles, sums, ready):
     groups, depth, width = tiles.shape[0], tiles.shape[1], tiles.shape[3]
     hours = dual.shape[1]
     for ref in sums:
         ref[...] = jnp.zeros_like(ref)
 
-    def body(step, carry):
-        base = step * 4
+    def four(base):
         rows = [dual[base + u] for u in range(4)]
         zero = jnp.zeros_like(rows[0])
         parts = []
@@ -92,9 +114,8 @@
         for u, k, part in parts:
             at = blocks[(base + u) * depth + k]
             sums[k][at] = sums[k][at] + part
-        return carry
-
-    lax.fori_loop(0, groups // 4, body, 0)
+
+    over_groups(groups, ready, four)
 
 
 def earlier(values):
@@ -143,30 +164,21 @@
     lax.fori_loop(0, level.shape[1] // width, body, 0)
 
 
-def hold_kernel(tiles_hbm, tiles, sems):
-    size = tiles.shape[0] // sems.shape[0]
-    copies = []
-    for chunk in range(sems.shape[0]):
-        part = pl.ds(chunk * size, size)
-        copies.append(pltpu.make_async_copy(tiles_hbm.at[part], tiles.at[part], sems.at[chunk]))
-        copies[-1].start()
-    for copy in copies:
-        copy.wait()
-
-
-def first_flow_kernel(blocks, base, tiles, flows, picked):
+def first_flow_kernel(blocks, base, tiles_hbm, flows, tiles, sems, picked):
+    fetch_all(tiles_hbm, tiles, sems)
     width = tiles.shape[3]
     for b in range(picked.shape[0]):
         picked[b] = base[:, b * width : (b + 1) * width]
-    flow_pass(picked, blocks, tiles, flows)
+    flow_pass(picked, blocks, tiles, flows, lambda c: fetch(tiles_hbm, tiles, sems, c).wait())
 
 
 def middle_kernel(
-    blocks, dual, base, delta, level, unit_block, unit_lane, gain, tiles,
-    inject_out, level_out, flows, picked, *sums
+    blocks, dual, base, delta, level, unit_block, unit_lane, gain, tiles_hbm,
+    inject_out, level_out, flows, tiles, sems, picked, *sums
 ):
+    fetch_all(tiles_hbm, tiles, sems)
     width = tiles.shape[3]
-    price_pass(dual, blocks, tiles, sums)
+    price_pass(dual, blocks, tiles, sums, lambda c: fetch(tiles_hbm, tiles, sems, c).wait())
 
     def start(b):
         return base[:, b * width : (b + 1) * width].astype(jnp.float32)
@@ -175,16 +187,17 @@
         inject_out[b] = new
 
     update_pass(sums, start, start, delta, write, picked)
-    flow_pass(picked, blocks, tiles, flows)
+    flow_pass(picked, blocks, tiles, flows, lambda c: None)
     level_pass(sums[0], level, unit_block, unit_lane, gain, level_out, False)
 
 
 def last_kernel(
-    blocks, dual, base, inject, delta, level, unit_block, unit_lane, gain, tiles,
-    inject_out, level_out, *sums
+    blocks, dual, base, inject, delta, level, unit_block, unit_lane, gain, tiles_hbm,
+    inject_out, level_out, tiles, sems, *sums
 ):
+    fetch_all(tiles_hbm, tiles, sems)
     width = tiles.shape[3]
-    price_pass(dual, blocks, tiles, sums)
+    price_pass(dual, blocks, tiles, sums, lambda c: fetch(tiles_hbm, tiles, sems, c).wait())
 
     def start(b):
         return base[:, b * width : (b + 1) * width].astype(jnp.float32)
@@ -240,7 +253,9 @@
     own_limits = lax.dynamic_slice_in_dim(limits.reshape(groups, 1, lines), me * own_groups, own_groups, 0)
 
     tile_bytes = ptdf_tiles.size * 2
-    held = [pltpu.VMEM((bus_blocks, hours, width), jnp.bfloat16)]
+    stream = [pltpu.VMEM(ptdf_tiles.shape, ptdf_tiles.dtype), pltpu.SemaphoreType.DMA((CHUNKS,))]
+    held = stream + [pltpu.VMEM((bus_blocks, hours, width), jnp.bfloat16)]
+    large = pltpu.CompilerParams(vmem_limit_bytes=tile_bytes + (16 << 20))
     sums = [pltpu.VMEM((bus_blocks, hours, width), jnp.float32)] * depth
     pass_flops = 2 * hours * ptdf_tiles.size
     flow_shape = jax.ShapeDtypeStruct((groups, hours, lines), jnp.bfloat16)
@@ -258,26 +273,16 @@
     base = came[:, :buses]
     level = came[:, buses : buses + units].astype(jnp.float32) + came[:, buses + units :].astype(jnp.float32)
 
-    tiles = pl.pallas_call(
-        hold_kernel,
-        out_shape=jax.ShapeDtypeStruct(ptdf_tiles.shape, ptdf_tiles.dtype),
-        in_specs=[pl.BlockSpec(memory_space=pltpu.HBM)],
-        out_specs=VMEM,
-        scratch_shapes=[pltpu.SemaphoreType.DMA((16,))],
-        compiler_params=PARAMS,
-        cost_estimate=pl.CostEstimate(flops=0, bytes_accessed=2 * tile_bytes, transcendentals=0),
-        name="hold_tiles",
-    )(ptdf_tiles)
     flows = pl.pallas_call(
         first_flow_kernel,
         out_shape=flow_shape,
-        in_specs=[SMEM, VMEM, VMEM],
+        in_specs=[SMEM, VMEM, HBM],
         out_specs=VMEM,
         scratch_shapes=held,
-        compiler_params=PARAMS,
+        compiler_params=large,
         cost_estimate=pl.CostEstimate(flops=pass_flops, bytes_accessed=tile_bytes, transcendentals=0),
         name="first_flow",
-    )(blocks, base, tiles)
+    )(blocks, base, ptdf_tiles)
 
     line_dual = jnp.zeros((own_groups, hours, lines), jnp.float32)
     inject = None
@@ -287,7 +292,7 @@
             out_shape=block_shape,
             in_specs=[VMEM] * 3,
             out_specs=VMEM,
-            compiler_params=PARAMS,
+            compiler_params=SMALL,
             cost_estimate=pl.CostEstimate(flops=pass_flops, bytes_accessed=units * hours * 4, transcendentals=0),
             name="storage",
         )(level, unit_block, unit_lane)
@@ -302,36 +307,35 @@
             inject, level, flows = pl.pallas_call(
                 middle_kernel,
                 out_shape=[block_shape, level_shape, flow_shape],
-                in_specs=[SMEM] + [VMEM] * 8,
+                in_specs=[SMEM] + [VMEM] * 7 + [HBM],
                 out_specs=[VMEM] * 3,
                 scratch_shapes=held + sums,
-                compiler_params=PARAMS,
+                compiler_params=large,
                 cost_estimate=pl.CostEstimate(
                     flops=2 * pass_flops, bytes_accessed=tile_bytes, transcendentals=0
                 ),
                 name="price_then_flow",
-            )(blocks, dual, base, delta, level, unit_block, unit_lane, gain, tiles)
+            )(blocks, dual, base, delta, level, unit_block, unit_lane, gain, ptdf_tiles)
         else:
             inject, level = pl.pallas_call(
                 last_kernel,
                 out_shape=[jax.ShapeDtypeStruct((hours, buses), jnp.float32), level_shape],
-                in_specs=[SMEM] + [VMEM] * 9,
+                in_specs=[SMEM] + [VMEM] * 8 + [HBM],
                 out_specs=[VMEM] * 2,
-                scratch_shapes=sums,
-                compiler_params=PARAMS,
+                scratch_shapes=stream + sums,
+                compiler_params=large,
                 cost_estimate=pl.CostEstimate(flops=pass_flops, bytes_accessed=tile_bytes, transcendentals=0),
                 name="last_price",
-            )(blocks, dual, base, inject, delta, level, unit_block, unit_lane, gain, tiles)
-
-    own_dual = lax.all_to_all(
-        jnp.swapaxes(line_dual, 0, 1).reshape(hours, own_groups * lines), "tm", split_axis=0, concat_axis=1, tiled=True
-    )
-    joined = jnp.concatenate([inject, level], axis=1)
+            )(blocks, dual, base, inject, delta, level, unit_block, unit_lane, gain, ptdf_tiles)
+
+    duals = own_groups * lines
+    joined = jnp.concatenate([inject, level, jnp.swapaxes(line_dual, 0, 1).reshape(hours, duals)], axis=1)
     back = lax.all_to_all(
-        joined.reshape(devices, hour_rows, buses + units), "tm", split_axis=0, concat_axis=0, tiled=True
+        joined.reshape(devices, hour_rows, buses + units + duals), "tm", split_axis=0, concat_axis=0, tiled=True
     )
     inject = jnp.swapaxes(back[:, :, :buses], 0, 1).reshape(hour_rows, bus_count)
-    level = jnp.sum(back[:, :, buses:], axis=0)
+    level = jnp.sum(back[:, :, buses : buses + units], axis=0)
+    own_dual = jnp.swapaxes(back[:, :, buses + units :], 0, 1).reshape(hour_rows, line_count)
     return (inject, own_dual, level)
 
 

time: 200 us -> 156 us (0.78)
  local copies, waits for them, and re-layouts: 40.3 us -> 4.21 us
  blocking collectives: 44.5 us -> 56.4 us
  starting transfers between devices: 24.5 us -> 14.6 us
  Pallas kernels: 54.2 us -> 46.4 us
  waiting for transfers between devices: 30.4 us -> 28.2 us
    unnamed x19 -> x8, local copies, waits for them, and re-layouts: 37.1 us -> 1.71 us
    all_to_all x0 -> x1, blocking collectives: none -> 14 us  [shards(): lax.all_to_all(joined.reshape(devices, hour_rows, buses + units + duals),...]
    all_to_all x2 -> x0, waiting for transfers between devices: 10.3 us -> none  [the longest x1 10.3 us: shards(): lax.all_to_all(joined.reshape(devices, hour_rows, buses + units), 'tm', s...]
    all_to_all x1, waiting for transfers between devices: 0.01 us -> 8.12 us  [shards(): lax.all_to_all(jnp.swapaxes(sent, 0, 1), 'tm', split_axis=0, concat_axis=...]
    all_to_all x2 -> x0, starting transfers between devices: 7.56 us -> none  [the longest x1 4.02 us: shards(): lax.all_to_all(jnp.swapaxes(line_dual, 0, 1).reshape(hours, own_groups *...]
    pallas_call x1, Pallas kernels: 22 us -> 17.9 us  [shards(): pl.pallas_call(middle_kernel, out_shape=[block_shape, level_shape, flow_s...]
    all_to_all x2, starting transfers between devices: 9.58 us -> 7.17 us  [shards(): lax.all_to_all(flows.reshape(devices, own_groups, hours, lines), 'tm', sp...]
    all_gather x2, blocking collectives: 44.5 us -> 42.4 us  [shards(): lax.all_gather(line_dual.astype(jnp.bfloat16), 'tm', axis=0, tiled=True)]
  transfers between devices with their start and end apart: 5 -> 3, of which waited for: 3 -> 3; matrix products, arithmetic and copies ran while one was open for 1% -> 1% of each run, Pallas kernels for 10% -> 5%
where the time goes in v3:
time: 156 us; the launch traced here: 155 us
  blocking collectives  56.4 us (36%)
  Pallas kernels  46.4 us (30%)
  waiting for transfers between devices  28.2 us (18%)
  starting transfers between devices  14.6 us (9%)
  other arithmetic  4.55 us (3%)
  local copies, waits for them, and re-layouts  4.21 us (3%)
    all_gather x2, blocking collectives, shards(): lax.all_gather(line_dual.astype(jnp.bfloat16), 'tm', axis=0, tiled=True)  42.4 us
    all_to_all x2, waiting for transfers between devices, shards(): lax.all_to_all(flows.reshape(devices, own_groups, hours, lines), 'tm', sp...  20.1 us
    pallas_call x1, Pallas kernels, shards(): pl.pallas_call(middle_kernel, out_shape=[block_shape, level_shape, flow_s...  17.9 us
    all_to_all x1, blocking collectives, shards(): lax.all_to_all(joined.reshape(devices, hour_rows, buses + units + duals),...  14 us
    pallas_call x1, Pallas kernels, shards(): pl.pallas_call(first_flow_kernel, out_shape=flow_shape, in_specs=[SMEM, V...  10.3 us
    pallas_call x1, Pallas kernels, shards(): pl.pallas_call(last_kernel, out_shape=[jax.ShapeDtypeStruct((hours, buses...  10.2 us
    all_to_all x1, waiting for transfers between devices, shards(): lax.all_to_all(jnp.swapaxes(sent, 0, 1), 'tm', split_axis=0, concat_axis=...  8.12 us
    pallas_call x2, Pallas kernels, shards(): pl.pallas_call(storage_kernel, out_shape=block_shape, in_specs=[VMEM] * 3...  8.05 us
  transfers between devices with their start and end apart: 3, of which 3 were waited for; matrix products, arithmetic and copies ran while one was open for 1% of the time, Pallas kernels for 5%

profile of v3, /device:TPU:0, one launch (start us, length us, event | category | flops | bytes accessed | tf_op | source)
XLA Modules:
  0.0 155.1 jit_solution(16733148622648617118)
XLA Ops:
  0.6 0.0 copy-start.1
  0.7 0.8 fusion.6
  1.4 1.3 reduce.1
  2.8 0.1 reshape.44
  2.9 0.1 maximum_reduce_fusion
  3.0 0.5 broadcast.21
  3.5 0.7 reduce.4
  4.2 0.7 reshape.57
  5.0 7.4 %all-to-all-start = ((bf16[16,2,3200]{2,1,0:T(2,128)(2,1)}), bf16[16,2,3200]{2,1,0:T(2,128)(2,1)S(1)}, u32[]{:S(2)}, u32[]{:S(2)}) async-start(bf16[16,2,3200]{2,1,0:T(2,128)(2,1)} %reshape.57), calls=%async_computation | async-start | bytes 409600 | tf_op jit(solution)/shard_map/all_to_all | solution.py:271
  12.4 0.8 copy.15
  13.2 0.2 reshape.43.blocks
  13.4 8.1 %all-to-all-done = bf16[16,2,3200]{2,1,0:T(2,128)(2,1)S(1)} async-done(((bf16[16,2,3200]{2,1,0:T(2,128)(2,1)}), bf16[16,2,3200]{2,1,0:T(2,128)(2,1)S(1)}, u32[]{:S(2)}, u32[]{:S(2)}) %all-to-all-start) | async-done | bytes 204832 | tf_op jit(solution)/shard_map/all_to_all | solution.py:271
  21.5 0.2 reshape.58
  21.7 10.3 %first_flow.1 = bf16[128,16,128]{2,1,0:T(8,128)(2,1)} custom-call(s32[640]{0:T(1024)S(1)} %reshape.43.blocks, bf16[16,2304]{1,0:T(8,128)(2,1)S(1)} %slice.24.base, bf16[128,5,128,128]{3,2,1,0:T(8,128)(2,1)} %tiles_hbm.5), custom_call_target="tpu_custom_call" | custom-call | flops 335544320 | bytes 20971520 | tf_op jit(solution)/shard_map/first_flow/pallas_call | solution.py:276
  31.9 3.6 %all-to-all-start.1 = ((bf16[16,8,16,128]{3,2,1,0:T(8,128)(2,1)}), bf16[16,8,16,128]{3,2,1,0:T(8,128)(2,1)S(1)}, u32[]{:S(2)}, u32[]{:S(2)}) async-start(bf16[16,8,16,128]{3,2,1,0:T(8,128)(2,1)} %bitcast.1), calls=%async_computation.1 | async-start | bytes 1048576 | tf_op jit(solution)/shard_map/all_to_all | solution.py:299
  35.5 0.7 dynamic-slice_bitcast_fusion
  36.3 4.0 %storage.2.delta = f32[18,16,128]{2,1,0:T(8,128)S(1)} custom-call(f32[16,2048]{1,0:T(8,128)S(1)} %convert_add_fusion.level, s32[1,2048]{1,0:T(1,128)S(1)} %bitcast.46, s32[1,2048]{1,0:T(1,128)S(1)} %bitcast.42), custom_call_target="tpu_custom_call" | custom-call | flops 335544320 | bytes 131072 | tf_op jit(solution)/shard_map/storage/pallas_call | solution.py:290
  40.3 9.7 %all-to-all-done.1 = bf16[16,8,16,128]{3,2,1,0:T(8,128)(2,1)S(1)} async-done(((bf16[16,8,16,128]{3,2,1,0:T(8,128)(2,1)}), bf16[16,8,16,128]{3,2,1,0:T(8,128)(2,1)S(1)}, u32[]{:S(2)}, u32[]{:S(2)}) %all-to-all-start.1) | async-done | bytes 524320 | tf_op jit(solution)/shard_map/all_to_all | solution.py:299
  50.0 0.1 convert_reduce_fusion.1
  50.1 21.2 %all_gather.6.dual = bf16[128,16,128]{2,1,0:T(8,128)(2,1)S(1)} all-gather(bf16[8,16,128]{2,1,0:T(8,128)(2,1)S(1)} %fusion.2), channel_id=1, replica_groups=mesh['scen'=2,'tm'=16] {'tm'}, dimensions={0}, use_global_device_ids=true | all-gather | bytes 557056 | tf_op jit(solution)/shard_map/all_gather | solution.py:305
  71.3 17.9 %price_then_flow.1 = (f32[18,16,128]{2,1,0:T(8,128)S(1)}, f32[16,2048]{1,0:T(8,128)S(1)}, bf16[128,16,128]{2,1,0:T(8,128)(2,1)}) custom-call(s32[640]{0:T(1024)S(1)} %reshape.43.blocks, bf16[128,16,128]{2,1,0:T(8,128)(2,1)S(1)} %all_gather.6.dual, bf16[16,2304]{1,0:T(8,128)(2,1)S(1)} %slice.24.base, f32[18,16,128]{2,1,0:T(8,128)S(1)} %storage.2.delta, ...), custom_call_target="tpu_custom_call" | custom-call | flops 671088640 | bytes 20971520 | tf_op jit(solution)/shard_map/price_then_flow/pallas_call | solution.py:307
  89.2 3.6 %all-to-all-start.2 = ((bf16[16,8,16,128]{3,2,1,0:T(8,128)(2,1)}), bf16[16,8,16,128]{3,2,1,0:T(8,128)(2,1)S(1)}, u32[]{:S(2)}, u32[]{:S(2)}) async-start(bf16[16,8,16,128]{3,2,1,0:T(8,128)(2,1)} %bitcast.8), calls=%async_computation.2 | async-start | bytes 1048576 | tf_op jit(solution)/shard_map/all_to_all | solution.py:299
  92.8 4.0 %storage.3.delta = f32[18,16,128]{2,1,0:T(8,128)S(1)} custom-call(f32[16,2048]{1,0:T(8,128)S(1)} %get-tuple-element.10.level, s32[1,2048]{1,0:T(1,128)S(1)} %bitcast.48, s32[1,2048]{1,0:T(1,128)S(1)} %bitcast.44), custom_call_target="tpu_custom_call" | custom-call | flops 335544320 | bytes 131072 | tf_op jit(solution)/shard_map/storage/pallas_call | solution.py:290
  96.8 10.4 %all-to-all-done.2 = bf16[16,8,16,128]{3,2,1,0:T(8,128)(2,1)S(1)} async-done(((bf16[16,8,16,128]{3,2,1,0:T(8,128)(2,1)}), bf16[16,8,16,128]{3,2,1,0:T(8,128)(2,1)S(1)}, u32[]{:S(2)}, u32[]{:S(2)}) %all-to-all-start.2) | async-done | bytes 524320 | tf_op jit(solution)/shard_map/all_to_all | solution.py:299
  107.2 0.1 convert_reduce_fusion
  107.4 21.2 %all_gather.7.dual = bf16[128,16,128]{2,1,0:T(8,128)(2,1)S(1)} all-gather(bf16[8,16,128]{2,1,0:T(8,128)(2,1)S(1)} %subtract_convert_fusion), channel_id=1, replica_groups=mesh['scen'=2,'tm'=16] {'tm'}, dimensions={0}, use_global_device_ids=true | all-gather | bytes 557056 | tf_op jit(solution)/shard_map/all_gather | solution.py:305
  128.6 10.2 %last_price.1 = (f32[16,2304]{1,0:T(8,128)S(1)}, f32[16,2048]{1,0:T(8,128)S(1)}) custom-call(s32[640]{0:T(1024)S(1)} %reshape.43.blocks, bf16[128,16,128]{2,1,0:T(8,128)(2,1)S(1)} %all_gather.7.dual, bf16[16,2304]{1,0:T(8,128)(2,1)S(1)} %slice.24.base, f32[18,16,128]{2,1,0:T(8,128)S(1)} %get-tuple-element.9.inject, f32[18,16,128]{2,1,0:T(8,128)S(1)} %storage.3.delta, ...), custom_call_target="tpu_custom_call" | custom-call | flops 335544320 | bytes 20971520 | tf_op jit(solution)/shard_map/last_price/pallas_call | solution.py:320
  138.8 0.4 copy.18
  139.1 14.0 %all_to_all.20 = f32[16,1,5376]{2,1,0:T(1,128)S(1)} all-to-all(f32[16,1,5376]{2,1,0:T(1,128)S(1)} %copy.18), channel_id=1, replica_groups=mesh['scen'=2,'tm'=16] {'tm'}, dimensions={0} | all-to-all | bytes 688128 | tf_op jit(solution)/shard_map/all_to_all | solution.py:333
  153.1 0.7 slice_reduce_fusion
  153.7 0.6 slice.28
  154.4 0.7 slice.27
  (13 shorter events, 0.2 us)
Async XLA Ops:
  0.6 35.6 %copy-start.1 = (s32[2048]{0:T(1024)S(1)}, s32[2048]{0:T(1024)}, u32[]{:S(2)}) copy-start(s32[2048]{0:T(1024)} %param.11) | copy-start | bytes 24580
  0.6 70.6 %copy-start = (f32[2048]{0:T(1024)S(1)}, f32[2048]{0:T(1024)}, u32[]{:S(2)}) copy-start(f32[2048]{0:T(1024)} %param.12) | copy-start | bytes 24580
  5.0 16.5 %all-to-all-start = ((bf16[16,2,3200]{2,1,0:T(2,128)(2,1)}), bf16[16,2,3200]{2,1,0:T(2,128)(2,1)S(1)}, u32[]{:S(2)}, u32[]{:S(2)}) async-start(bf16[16,2,3200]{2,1,0:T(2,128)(2,1)} %reshape.57), calls=%async_computation | async-start | bytes 409600 | tf_op jit(solution)/shard_map/all_to_all | solution.py:271
  31.9 18.0 %all-to-all-start.1 = ((bf16[16,8,16,128]{3,2,1,0:T(8,128)(2,1)}), bf16[16,8,16,128]{3,2,1,0:T(8,128)(2,1)S(1)}, u32[]{:S(2)}, u32[]{:S(2)}) async-start(bf16[16,8,16,128]{3,2,1,0:T(8,128)(2,1)} %bitcast.1), calls=%async_computation.1 | async-start | bytes 1048576 | tf_op jit(solution)/shard_map/all_to_all | solution.py:299
  89.2 18.0 %all-to-all-start.2 = ((bf16[16,8,16,128]{3,2,1,0:T(8,128)(2,1)}), bf16[16,8,16,128]{3,2,1,0:T(8,128)(2,1)S(1)}, u32[]{:S(2)}, u32[]{:S(2)}) async-start(bf16[16,8,16,128]{3,2,1,0:T(8,128)(2,1)} %bitcast.8), calls=%async_computation.2 | async-start | bytes 1048576 | tf_op jit(solution)/shard_map/all_to_all | solution.py:299

commit v4 on v3

v4 whole, which is shorter than its diff:
```python
import functools

import jax
import jax.numpy as jnp
from jax import lax
from jax.experimental import pallas as pl
from jax.experimental.pallas import tpu as pltpu
from jax.sharding import PartitionSpec as P

ITERS = 2


step_size = 0.5
penalty = 4.0
ramp_weight = 0.5

NT = (((1,), (1,)), ((), ()))
VMEM = pl.BlockSpec(memory_space=pltpu.VMEM)
SMEM = pl.BlockSpec(memory_space=pltpu.SMEM)
HBM = pl.BlockSpec(memory_space=pl.ANY)
SMALL = pltpu.CompilerParams(vmem_limit_bytes=12 << 20)
STRAIGHT = 16


class Half:
    def __init__(self, core, blocks, tiles_hbm, tiles, sems):
        self.core, self.blocks, self.tiles_hbm, self.tiles, self.sems = core, blocks, tiles_hbm, tiles, sems
        self.chunks = sems.shape[0]
        self.own = tiles.shape[0] // self.chunks

    def fetch(self, chunk):
        there = pl.ds((2 * chunk + self.core) * self.own, self.own)
        here = pl.ds(chunk * self.own, self.own)
        return pltpu.make_async_copy(self.tiles_hbm.at[there], self.tiles.at[here], self.sems.at[chunk])

    def start(self):
        for chunk in range(self.chunks):
            self.fetch(chunk).start()

    def each_four(self, wait, four):
        depth = self.tiles.shape[1]
        per = max(1, STRAIGHT // self.own)

        def body(step, carry):
            for c in range(per):
                chunk = step * per + c
                if wait:
                    self.fetch(chunk).wait()
                for sub in range(0, self.own, 4):
                    first = ((2 * chunk + self.core) * self.own + sub) * depth
                    four(chunk * self.own + sub, lambda u, k: self.blocks[first + u * depth + k])
            return carry

        lax.fori_loop(0, self.chunks // per, body, 0)


def wide(parts):
    return jnp.concatenate([jnp.concatenate(row, axis=1) for row in parts], axis=0)


def flow_pass(picked, half, flows, wait):
    tiles = half.tiles
    depth, lines = tiles.shape[1], tiles.shape[2]
    hours = picked.shape[1]

    def four(base, block):
        rows = [[picked[block(u, k)] for k in range(depth)] for u in range(4)]
        zero = jnp.zeros_like(rows[0][0])
        totals = [None] * 4

        def add(u, part):
            totals[u] = part if totals[u] is None else totals[u] + part

        for first in (0, 2):
            for k in range(0, depth - 1, 2):
                left = wide([[rows[first][k], rows[first][k + 1]], [rows[first + 1][k], rows[first + 1][k + 1]]])
                g = base + first
                right = wide([[tiles[g, k], tiles[g, k + 1]], [tiles[g + 1, k], tiles[g + 1, k + 1]]])
                part = lax.dot_general(left, right, NT, preferred_element_type=jnp.float32)
                add(first, part[:hours, :lines])
                add(first + 1, part[hours:, lines:])
        if depth % 2:
            k = depth - 1
            left = wide([[rows[0][k], zero], [rows[1][k], zero], [zero, rows[2][k]], [zero, rows[3][k]]])
            right = wide([[tiles[base, k], tiles[base + 2, k]], [tiles[base + 1, k], tiles[base + 3, k]]])
            part = lax.dot_general(left, right, NT, preferred_element_type=jnp.float32)
            for u in range(4):
                at = (u % 2) * lines
                add(u, part[u * hours : (u + 1) * hours, at : at + lines])
        for u in range(4):
            flows[base + u] = totals[u].astype(flows.dtype)

    half.each_four(wait, four)


def price_pass(dual, half, sums, wait):
    tiles = half.tiles
    depth, width = tiles.shape[1], tiles.shape[3]
    hours = dual.shape[1]
    for ref in sums:
        ref[...] = jnp.zeros_like(ref)

    def four(base, block):
        rows = [dual[base + u] for u in range(4)]
        zero = jnp.zeros_like(rows[0])
        parts = []
        for first in (0, 2):
            left = wide([[rows[first], zero], [zero, rows[first + 1]]])
            for k in range(0, depth - 1, 2):
                g = base + first
                right = wide([[tiles[g, k], tiles[g, k + 1]], [tiles[g + 1, k], tiles[g + 1, k + 1]]])
                part = jnp.dot(left, right, preferred_element_type=jnp.float32)
                for u in range(2):
                    for j in range(2):
                        piece = part[u * hours : (u + 1) * hours, j * width : (j + 1) * width]
                        parts.append((first + u, k + j, piece))
        if depth % 2:
            k = depth - 1
            left = wide([[rows[0], zero], [zero, rows[1]], [rows[2], zero], [zero, rows[3]]])
            right = wide([[tiles[base, k], tiles[base + 2, k]], [tiles[base + 1, k], tiles[base + 3, k]]])
            part = jnp.dot(left, right, preferred_element_type=jnp.float32)
            for u in range(4):
                at = (u // 2) * width
                parts.append((u, k, part[u * hours : (u + 1) * hours, at : at + width]))
        for u, k, part in parts:
            at = block(u, k)
            sums[k][at] = sums[k][at] + part

    half.each_four(wait, four)


def earlier(values):
    return jnp.concatenate([values[-1:], values[:-1]], axis=0)


def later(values):
    return jnp.concatenate([values[1:], values[:1]], axis=0)


def total(sums, block):
    price = sums[0][block]
    for ref in sums[1:]:
        price = price + ref[block]
    return price


def update_pass(sums, before, inject, base, delta, price_out, out):
    for block in range(sums[0].shape[0]):
        price = before[block] + total(sums, block)
        price_out[block] = price
        now = inject(block)
        new = now - step_size * (
            (now - base(block))
            + penalty * price
            + ramp_weight * (2.0 * now - earlier(now) - later(now))
        )
        out(block, new - delta[block])


def level_pass(price, level, unit_block, unit_lane, gain, out, mine):
    count, hours, width = price.shape

    def body(c, carry):
        cols = pl.ds(pl.multiple_of(c * width, width), width)
        block = jnp.broadcast_to(unit_block[:, cols], (hours, width))
        lane = jnp.broadcast_to(unit_lane[:, cols], (hours, width))
        found = jnp.zeros((hours, width), jnp.float32)
        for b in range(count):
            found = jnp.where(block == b, jnp.take_along_axis(price[b], lane, axis=1), found)
        now = level[:, cols]
        new = 0.5 * (now + earlier(now)) - gain[:, cols] * found
        if mine:
            new = jnp.where((block >= 0) & (block < count), new, 0.0)
        out[:, cols] = new
        return carry

    lax.fori_loop(0, level.shape[1] // width, body, 0)


def first_flow_kernel(core, blocks, base, tiles_hbm, flows, picked, tiles, sems):
    half = Half(1 - core[0], blocks, tiles_hbm, tiles, sems)
    half.start()
    width = tiles.shape[3]
    for b in range(picked.shape[0]):
        picked[b] = base[:, b * width : (b + 1) * width]
    flow_pass(picked, half, flows, True)


def own_flow_kernel(core, blocks, picked, tiles_hbm, flows, tiles, sems):
    half = Half(core[0], blocks, tiles_hbm, tiles, sems)
    half.start()
    flow_pass(picked, half, flows, True)


def own_price_kernel(core, blocks, dual, tiles_hbm, price, tiles, sems, *sums):
    half = Half(core[0], blocks, tiles_hbm, tiles, sems)
    half.start()
    price_pass(dual, half, sums, True)
    for b in range(price.shape[0]):
        price[b] = total(sums, b)


def middle_kernel(
    core, blocks, dual, before, base, delta, tiles_hbm,
    price, inject_out, picked, flows, tiles, sems, *sums
):
    half = Half(1 - core[0], blocks, tiles_hbm, tiles, sems)
    half.start()
    width = tiles.shape[3]
    price_pass(dual, half, sums, True)

    def start(b):
        return base[:, b * width : (b + 1) * width].astype(jnp.float32)

    def write(b, new):
        inject_out[b] = new
        picked[b] = new.astype(picked.dtype)

    update_pass(sums, before, start, start, delta, price, write)
    flow_pass(picked, half, flows, False)


def last_kernel(
    core, blocks, dual, before, base, inject, delta, level, unit_block, unit_lane, gain, tiles_hbm,
    inject_out, level_out, tiles, sems, price, *sums
):
    half = Half(1 - core[0], blocks, tiles_hbm, tiles, sems)
    half.start()
    width = tiles.shape[3]
    price_pass(dual, half, sums, True)

    def start(b):
        return base[:, b * width : (b + 1) * width].astype(jnp.float32)

    def write(b, new):
        inject_out[:, b * width : (b + 1) * width] = new

    update_pass(sums, before, lambda b: inject[b], start, delta, price, write)
    level_pass(price, level, unit_block, unit_lane, gain, level_out, True)


def storage_pass(level, unit_block, unit_lane, delta):
    count, hours, width = delta.shape
    units = level.shape[1]
    span = 2 * width
    delta[...] = jnp.zeros_like(delta)

    def body(c, carry):
        cols = pl.ds(pl.multiple_of(c * span, span), span)
        now = level[:, cols]
        charge = step_size * (now - earlier(now))
        high = charge.astype(jnp.bfloat16).astype(jnp.float32)
        low = charge - high
        lane = jnp.broadcast_to(unit_lane[:, cols], (width, span))
        hot = (lane == lax.broadcasted_iota(jnp.int32, (width, span), 0)).astype(jnp.bfloat16)
        block = jnp.broadcast_to(unit_block[:, cols], (hours, span))
        for b in range(count):
            held = block == b
            both = jnp.concatenate([jnp.where(held, high, 0.0), jnp.where(held, low, 0.0)], axis=0)
            part = lax.dot_general(both.astype(jnp.bfloat16), hot, NT, preferred_element_type=jnp.float32)
            delta[b] = delta[b] + (part[:hours] + part[hours:])
        return carry

    lax.fori_loop(0, units // span, body, 0)


def storage_kernel(level, unit_block, unit_lane, delta):
    storage_pass(level, unit_block, unit_lane, delta)


def level_kernel(price, level, unit_block, unit_lane, gain, level_out, delta):
    level_pass(price, level, unit_block, unit_lane, gain, level_out, False)
    storage_pass(level_out, unit_block, unit_lane, delta)


def shards(base_injection, ptdf_tiles, tile_block, limits, stor_bus, stor_gain, soc_init):
    hour_rows = base_injection.shape[0]
    bus_count = base_injection.shape[1]
    line_count = limits.shape[0]
    groups, depth, lines, width = ptdf_tiles.shape
    units = stor_bus.shape[0]
    devices = lax.axis_size("tm")
    me = lax.axis_index("tm")
    buses = bus_count // devices
    bus_blocks = buses // width
    hours = hour_rows * devices
    own_groups = groups // devices
    blocks = tile_block.reshape(groups * depth)
    unit_block = (stor_bus // width - me * bus_blocks).reshape(1, units)
    unit_lane = (stor_bus % width).reshape(1, units)
    gain = stor_gain.reshape(1, units)
    own_limits = lax.dynamic_slice_in_dim(limits.reshape(groups, 1, lines), me * own_groups, own_groups, 0)

    chips = devices // 2
    half_groups = chips * own_groups
    core = (me % 2).reshape(1)
    same_core = [[2 * chip + c for chip in range(chips)] for c in range(2)]
    sibling = [(d, d + 1 - 2 * (d % 2)) for d in range(devices)]

    half_bytes = ptdf_tiles.size
    half_flops = hours * ptdf_tiles.size
    stream = [pltpu.VMEM((half_groups, *ptdf_tiles.shape[1:]), ptdf_tiles.dtype), pltpu.SemaphoreType.DMA((chips,))]
    sums = [pltpu.VMEM((bus_blocks, hours, width), jnp.float32)] * depth
    large = pltpu.CompilerParams(vmem_limit_bytes=half_bytes + (16 << 20))
    picked_shape = jax.ShapeDtypeStruct((bus_blocks, hours, width), jnp.bfloat16)
    block_shape = jax.ShapeDtypeStruct((bus_blocks, hours, width), jnp.float32)
    level_shape = jax.ShapeDtypeStruct((hours, units), jnp.float32)
    flow_shape = jax.ShapeDtypeStruct((half_groups, hours, lines), jnp.float32)

    def product(kernel, name, outs, operands, scratch, passes=1):
        return pl.pallas_call(
            kernel,
            out_shape=outs,
            in_specs=[SMEM] * 2 + [VMEM] * len(operands) + [HBM],
            out_specs=[VMEM] * len(outs),
            scratch_shapes=stream + scratch,
            compiler_params=large,
            cost_estimate=pl.CostEstimate(
                flops=passes * half_flops, bytes_accessed=passes * half_bytes, transcendentals=0
            ),
            name=name,
        )(core, blocks, *operands, ptdf_tiles)

    def small(kernel, name, outs, operands):
        return pl.pallas_call(
            kernel,
            out_shape=outs,
            in_specs=[VMEM] * len(operands),
            out_specs=[VMEM] * len(outs),
            compiler_params=SMALL,
            cost_estimate=pl.CostEstimate(flops=half_flops, bytes_accessed=4 << 20, transcendentals=0),
            name=name,
        )(*operands)

    high = soc_init.astype(jnp.bfloat16)
    low = (soc_init - high.astype(jnp.float32)).astype(jnp.bfloat16)
    own = jnp.concatenate([high, low], axis=1)[:, None, :]
    sent = jnp.concatenate(
        [base_injection.reshape(hour_rows, devices, buses), jnp.broadcast_to(own, (hour_rows, devices, 2 * units))], axis=2
    )
    came = lax.all_to_all(jnp.swapaxes(sent, 0, 1), "tm", split_axis=0, concat_axis=0, tiled=True)
    came = came.reshape(hours, buses + 2 * units)
    base = came[:, :buses]
    level = came[:, buses : buses + units].astype(jnp.float32) + came[:, buses + units :].astype(jnp.float32)

    away, picked = product(first_flow_kernel, "first_flow", [flow_shape, picked_shape], [base], [])
    (delta,) = small(storage_kernel, "storage", [block_shape], [level, unit_block, unit_lane])
    line_dual = jnp.zeros((own_groups, hours, lines), jnp.float32)
    inject = None
    for iteration in range(ITERS):
        arrived = lax.ppermute(away, "tm", sibling)
        (flows,) = product(own_flow_kernel, "own_flow", [flow_shape], [picked], [])
        pair = (flows + arrived).astype(jnp.bfloat16).reshape(chips, own_groups, hours, lines)
        parts = lax.all_to_all(pair, "tm", split_axis=0, concat_axis=0, axis_index_groups=same_core, tiled=True)
        shifted = jnp.sum(parts.astype(jnp.float32), axis=0) + line_dual
        clipped = jnp.clip(shifted, -own_limits, own_limits)
        line_dual = shifted - clipped
        dual = jnp.broadcast_to(line_dual.astype(jnp.bfloat16)[None], (chips, own_groups, hours, lines))
        dual = lax.all_to_all(dual, "tm", split_axis=0, concat_axis=0, axis_index_groups=same_core, tiled=True)
        dual = dual.reshape(half_groups, hours, lines)
        other = lax.ppermute(dual, "tm", sibling)
        (before,) = product(own_price_kernel, "own_price", [block_shape], [dual], sums)
        if iteration < ITERS - 1:
            price, inject, picked, away = product(
                middle_kernel,
                "price_then_flow",
                [block_shape, block_shape, picked_shape, flow_shape],
                [other, before, base, delta],
                sums,
                2,
            )
            level, delta = small(
                level_kernel, "storage", [level_shape, block_shape], [price, level, unit_block, unit_lane, gain]
            )
        else:
            inject, level = product(
                last_kernel,
                "last_price",
                [jax.ShapeDtypeStruct((hours, buses), jnp.float32), level_shape],
                [other, before, base, inject, delta, level, unit_block, unit_lane, gain],
                [pltpu.VMEM(block_shape.shape, block_shape.dtype)] + sums,
            )

    duals = own_groups * lines
    joined = jnp.concatenate([inject, level, jnp.swapaxes(line_dual, 0, 1).reshape(hours, duals)], axis=1)
    back = lax.all_to_all(
        joined.reshape(devices, hour_rows, buses + units + duals), "tm", split_axis=0, concat_axis=0, tiled=True
    )
    inject = jnp.swapaxes(back[:, :, :buses], 0, 1).reshape(hour_rows, bus_count)
    level = jnp.sum(back[:, :, buses : buses + units], axis=0)
    own_dual = jnp.swapaxes(back[:, :, buses + units :], 0, 1).reshape(hour_rows, line_count)
    return (inject, own_dual, level)


def solution(mesh):
    in_specs = (
        P(("scen", "tm"), None),
        P(None, "tm", None, None),
        P(None, "tm"),
        P(),
        P(),
        P(),
        P(("scen", "tm"), None),
    )
    out_specs = (P(("scen", "tm"), None), P(("scen", "tm"), None), P(("scen", "tm"), None))
    return jax.shard_map(shards, mesh=mesh, in_specs=in_specs, out_specs=out_specs, check_vma=False)
```

time: 156 us -> 183 us (1.17)
  local copies, waits for them, and re-layouts: 4.21 us -> 46.8 us
  blocking collectives: 56.4 us -> 39.4 us
  Pallas kernels: 46.4 us -> 48.6 us
  waiting for transfers between devices: 28.2 us -> 26.3 us
    all_gather x2 -> x0, blocking collectives: 42.4 us -> none  [shards(): lax.all_gather(line_dual.astype(jnp.bfloat16), 'tm', axis=0, tiled=True)]
    unnamed x8 -> x20, local copies, waits for them, and re-layouts: 1.71 us -> 43.5 us
    all_to_all x0 -> x2, blocking collectives: none -> 24.4 us  [the longest x1 12.5 us: shards(): lax.all_to_all(pair, 'tm', split_axis=0, concat_axis=0, axis_index_groups...]
    pallas_call x5 -> x9, Pallas kernels: 46.4 us -> 48.6 us  [the longest x7 38.8 us: product(): pl.pallas_call(kernel, out_shape=outs, in_specs=[SMEM] * 2 + [VMEM] * len...]
    all_to_all x2, waiting for transfers between devices: 20.1 us -> 18.2 us  [the longest x1 9.13 us: shards(): lax.all_to_all(dual, 'tm', split_axis=0, concat_axis=0, axis_index_groups...]
  transfers between devices with their start and end apart: 3 -> 7, of which waited for: 3 -> 3; matrix products, arithmetic and copies ran while one was open for 1% -> 1% of each run, Pallas kernels for 5% -> 16%
where the time goes in v4:
time: 183 us; the launch traced here: 182 us
  Pallas kernels  48.6 us (27%)
  local copies, waits for them, and re-layouts  46.8 us (26%)
  blocking collectives  39.4 us (22%)
  waiting for transfers between devices  26.3 us (14%)
  starting transfers between devices  15 us (8%)
  other arithmetic  5.34 us (3%)
    unnamed x20, local copies, waits for them, and re-layouts  43.5 us
    pallas_call x7, Pallas kernels, product(): pl.pallas_call(kernel, out_shape=outs, in_specs=[SMEM] * 2 + [VMEM] * len...  38.8 us
    all_to_all x1, blocking collectives, shards(): lax.all_to_all(joined.reshape(devices, hour_rows, buses + units + duals),...  15 us
    all_to_all x1, blocking collectives, shards(): lax.all_to_all(pair, 'tm', split_axis=0, concat_axis=0, axis_index_groups...  12.5 us
    all_to_all x1, blocking collectives, shards(): lax.all_to_all(dual, 'tm', split_axis=0, concat_axis=0, axis_index_groups...  12 us
    pallas_call x2, Pallas kernels, small(): pl.pallas_call(kernel, out_shape=outs, in_specs=[VMEM] * len(operands), o...  9.84 us
    all_to_all x1, waiting for transfers between devices, shards(): lax.all_to_all(dual, 'tm', split_axis=0, concat_axis=0, axis_index_groups...  9.13 us
    all_to_all x1, waiting for transfers between devices, shards(): lax.all_to_all(pair, 'tm', split_axis=0, concat_axis=0, axis_index_groups...  9.09 us
  transfers between devices with their start and end apart: 7, of which 3 were waited for; matrix products, arithmetic and copies ran while one was open for 1% of the time, Pallas kernels for 16%

profile of v4, /device:TPU:0, one launch (start us, length us, event | category | flops | bytes accessed | tf_op | source)
XLA Modules:
  0.0 182.4 jit_solution(16217468769277110627)
XLA Ops:
  0.6 0.8 fusion.6
  1.4 1.3 reduce.1
  3.5 0.7 reduce.4
  4.2 0.7 reshape.84
  4.9 7.4 %all-to-all-start = ((bf16[16,2,3200]{2,1,0:T(2,128)(2,1)}), bf16[16,2,3200]{2,1,0:T(2,128)(2,1)S(1)}, u32[]{:S(2)}, u32[]{:S(2)}) async-start(bf16[16,2,3200]{2,1,0:T(2,128)(2,1)} %reshape.84), calls=%async_computation | async-start | bytes 409600 | tf_op jit(solution)/shard_map/all_to_all | solution.py:341
  12.3 0.8 copy.18
  13.4 8.1 %all-to-all-done = bf16[16,2,3200]{2,1,0:T(2,128)(2,1)S(1)} async-done(((bf16[16,2,3200]{2,1,0:T(2,128)(2,1)}), bf16[16,2,3200]{2,1,0:T(2,128)(2,1)S(1)}, u32[]{:S(2)}, u32[]{:S(2)}) %all-to-all-start) | async-done | bytes 204832 | tf_op jit(solution)/shard_map/all_to_all | solution.py:341
  21.7 7.0 %copy-done = bf16[128,5,128,128]{3,2,1,0:T(8,128)(2,1)S(1)} copy-done((bf16[128,5,128,128]{3,2,1,0:T(8,128)(2,1)S(1)}, bf16[128,5,128,128]{3,2,1,0:T(8,128)(2,1)}, u32[]{:S(2)}) %copy-start) | copy-done | bytes 20971544
  28.6 5.4 %first_flow.1 = (f32[64,16,128]{2,1,0:T(8,128)S(1)}, bf16[18,16,128]{2,1,0:T(8,128)(2,1)S(1)}) custom-call(s32[1]{0:T(128)} %bitcast.core, s32[640]{0:T(1024)S(1)} %reshape.68.blocks, bf16[16,2304]{1,0:T(8,128)(2,1)S(1)} %slice.24.base, bf16[128,5,128,128]{3,2,1,0:T(8,128)(2,1)S(1)} %copy-done), custom_call_target="tpu_custom_call" | custom-call | flops 167772160 | bytes 10485760 | tf_op jit(solution)/shard_map/first_flow/pallas_call | solution.py:311
  34.2 7.0 %copy-done.1 = bf16[128,5,128,128]{3,2,1,0:T(8,128)(2,1)S(1)} copy-done((bf16[128,5,128,128]{3,2,1,0:T(8,128)(2,1)S(1)}, bf16[128,5,128,128]{3,2,1,0:T(8,128)(2,1)}, u32[]{:S(2)}) %copy-start.1) | copy-done | bytes 20971544
  41.1 5.4 %own_flow.2 = f32[64,16,128]{2,1,0:T(8,128)S(1)} custom-call(s32[1]{0:T(128)} %bitcast.core, s32[640]{0:T(1024)S(1)} %reshape.68.blocks, bf16[18,16,128]{2,1,0:T(8,128)(2,1)S(1)} %get-tuple-element.13.picked, bf16[128,5,128,128]{3,2,1,0:T(8,128)(2,1)S(1)} %copy-done.1), custom_call_target="tpu_custom_call" | custom-call | flops 167772160 | bytes 10485760 | tf_op jit(solution)/shard_map/own_flow/pallas_call | solution.py:311
  46.5 0.8 add_convert_fusion.1
  47.3 3.4 %all-to-all-start.1 = ((bf16[8,8,16,128]{3,2,1,0:T(8,128)(2,1)}), bf16[8,8,16,128]{3,2,1,0:T(8,128)(2,1)S(1)}, u32[]{:S(2)}, u32[]{:S(2)}) async-start(bf16[8,8,16,128]{3,2,1,0:T(8,128)(2,1)} %bitcast.2), calls=%async_computation.1 | async-start | bytes 524288 | tf_op jit(solution)/shard_map/all_to_all | solution.py:354
  50.7 0.7 dynamic-slice_bitcast_fusion
  51.4 9.1 %all-to-all-done.1 = bf16[8,8,16,128]{3,2,1,0:T(8,128)(2,1)S(1)} async-done(((bf16[8,8,16,128]{3,2,1,0:T(8,128)(2,1)}), bf16[8,8,16,128]{3,2,1,0:T(8,128)(2,1)S(1)}, u32[]{:S(2)}, u32[]{:S(2)}) %all-to-all-start.1) | async-done | bytes 262176 | tf_op jit(solution)/shard_map/all_to_all | solution.py:354
  60.6 0.7 broadcast_in_dim.10
  61.3 3.6 %all-to-all-start.2 = ((bf16[8,8,16,128]{3,2,1,0:T(8,128)(2,1)}), bf16[8,8,16,128]{3,2,1,0:T(8,128)(2,1)S(1)}, u32[]{:S(2)}, u32[]{:S(2)}) async-start(bf16[8,8,16,128]{3,2,1,0:T(8,128)(2,1)} %broadcast_in_dim.10), calls=%async_computation.2 | async-start | bytes 524288 | tf_op jit(solution)/shard_map/all_to_all | solution.py:359
  64.9 9.1 %all-to-all-done.2 = bf16[8,8,16,128]{3,2,1,0:T(8,128)(2,1)S(1)} async-done(((bf16[8,8,16,128]{3,2,1,0:T(8,128)(2,1)}), bf16[8,8,16,128]{3,2,1,0:T(8,128)(2,1)S(1)}, u32[]{:S(2)}, u32[]{:S(2)}) %all-to-all-start.2) | async-done | bytes 262176 | tf_op jit(solution)/shard_map/all_to_all | solution.py:359
  74.0 4.0 %storage.2.delta = f32[18,16,128]{2,1,0:T(8,128)S(1)} custom-call(f32[16,2048]{1,0:T(8,128)S(1)} %convert_add_fusion.level, s32[1,2048]{1,0:T(1,128)S(1)} %bitcast.52, s32[1,2048]{1,0:T(1,128)S(1)} %bitcast.49), custom_call_target="tpu_custom_call" | custom-call | flops 167772160 | bytes 4194304 | tf_op jit(solution)/shard_map/storage/pallas_call | solution.py:325
  78.1 7.0 %copy-done.2 = bf16[128,5,128,128]{3,2,1,0:T(8,128)(2,1)S(1)} copy-done((bf16[128,5,128,128]{3,2,1,0:T(8,128)(2,1)S(1)}, bf16[128,5,128,128]{3,2,1,0:T(8,128)(2,1)}, u32[]{:S(2)}) %copy-start.2) | copy-done | bytes 20971544
  85.0 4.3 %own_price.2.before = f32[18,16,128]{2,1,0:T(8,128)S(1)} custom-call(s32[1]{0:T(128)} %bitcast.core, s32[640]{0:T(1024)S(1)} %reshape.68.blocks, bf16[64,16,128]{2,1,0:T(8,128)(2,1)S(1)} %bitcast.46, bf16[128,5,128,128]{3,2,1,0:T(8,128)(2,1)S(1)} %copy-done.2), custom_call_target="tpu_custom_call" | custom-call | flops 167772160 | bytes 10485760 | tf_op jit(solution)/shard_map/own_price/pallas_call | solution.py:311
  89.3 7.0 %copy-done.3 = bf16[128,5,128,128]{3,2,1,0:T(8,128)(2,1)S(1)} copy-done((bf16[128,5,128,128]{3,2,1,0:T(8,128)(2,1)S(1)}, bf16[128,5,128,128]{3,2,1,0:T(8,128)(2,1)}, u32[]{:S(2)}) %copy-start.3) | copy-done | bytes 20971544
  96.3 7.9 %price_then_flow.1 = (f32[18,16,128]{2,1,0:T(8,128)S(1)}, f32[18,16,128]{2,1,0:T(8,128)S(1)}, bf16[18,16,128]{2,1,0:T(8,128)(2,1)S(1)}, f32[64,16,128]{2,1,0:T(8,128)S(1)}) custom-call(s32[1]{0:T(128)} %bitcast.core, s32[640]{0:T(1024)S(1)} %reshape.68.blocks, bf16[64,16,128]{2,1,0:T(8,128)(2,1)S(1)} %collective-permute-done.1.dual, ...), custom_call_target="tpu_custom_call" | custom-call | flops 335544320 | bytes 20971520 | tf_op jit(solution)/shard_map/price_then_flow/pallas_call | solution.py:311
  104.8 7.0 %copy-done.4 = bf16[128,5,128,128]{3,2,1,0:T(8,128)(2,1)S(1)} copy-done((bf16[128,5,128,128]{3,2,1,0:T(8,128)(2,1)S(1)}, bf16[128,5,128,128]{3,2,1,0:T(8,128)(2,1)}, u32[]{:S(2)}) %copy-start.4) | copy-done | bytes 20971544
  111.7 5.4 %own_flow.3 = f32[64,16,128]{2,1,0:T(8,128)S(1)} custom-call(s32[1]{0:T(128)} %bitcast.core, s32[640]{0:T(1024)S(1)} %reshape.68.blocks, bf16[18,16,128]{2,1,0:T(8,128)(2,1)S(1)} %get-tuple-element.15.picked, bf16[128,5,128,128]{3,2,1,0:T(8,128)(2,1)S(1)} %copy-done.4), custom_call_target="tpu_custom_call" | custom-call | flops 167772160 | bytes 10485760 | tf_op jit(solution)/shard_map/own_flow/pallas_call | solution.py:311
  117.2 12.5 %all_to_all.30 = bf16[8,8,16,128]{3,2,1,0:T(8,128)(2,1)S(1)} all-to-all(bf16[8,8,16,128]{3,2,1,0:T(8,128)(2,1)S(1)} %bitcast.57), channel_id=1, replica_groups={{0,2,4,6,8,10,12,14},{1,3,5,7,9,11,13,15},{16,18,20,22,24,26,28,30},{17..., dimensions={0} | all-to-all | bytes 524288 | tf_op jit(solution)/shard_map/all_to_all | solution.py:354
  129.8 12.0 %all_to_all.31 = bf16[8,8,16,128]{3,2,1,0:T(8,128)(2,1)S(1)} all-to-all(bf16[8,8,16,128]{3,2,1,0:T(8,128)(2,1)S(1)} %broadcast_in_dim.11), channel_id=1, replica_groups={{0,2,4,6,8,10,12,14},{1,3,5,7,9,11,13,15},{16,18,20,22,24,26,28,30},{17..., dimensions={0} | all-to-all | bytes 524288 | tf_op jit(solution)/shard_map/all_to_all | solution.py:359
  141.8 5.8 %storage.3 = (f32[16,2048]{1,0:T(8,128)S(1)}, f32[18,16,128]{2,1,0:T(8,128)S(1)}) custom-call(f32[18,16,128]{2,1,0:T(8,128)S(1)} %get-tuple-element.18.price, f32[16,2048]{1,0:T(8,128)S(1)} %convert_add_fusion.level, s32[1,2048]{1,0:T(1,128)S(1)} %bitcast.53, s32[1,2048]{1,0:T(1,128)S(1)} %bitcast.50, f32[1,2048]{1,0:T(1,128)S(1)} %bitcast.55), custom_call_target="tpu_custom_call" | custom-call | flops 167772160 | bytes 4194304 | tf_op jit(solution)/shard_map/storage/pallas_call | solution.py:325
  147.6 4.3 %own_price.3.before = f32[18,16,128]{2,1,0:T(8,128)S(1)} custom-call(s32[1]{0:T(128)} %bitcast.core, s32[640]{0:T(1024)S(1)} %reshape.68.blocks, bf16[64,16,128]{2,1,0:T(8,128)(2,1)S(1)} %bitcast.48, bf16[128,5,128,128]{3,2,1,0:T(8,128)(2,1)S(1)} %copy-done.4), custom_call_target="tpu_custom_call" | custom-call | flops 167772160 | bytes 10485760 | tf_op jit(solution)/shard_map/own_price/pallas_call | solution.py:311
  151.9 7.0 %copy-done.5 = bf16[128,5,128,128]{3,2,1,0:T(8,128)(2,1)S(1)} copy-done((bf16[128,5,128,128]{3,2,1,0:T(8,128)(2,1)S(1)}, bf16[128,5,128,128]{3,2,1,0:T(8,128)(2,1)}, u32[]{:S(2)}) %copy-start.5) | copy-done | bytes 20971544
  158.9 6.2 %last_price.1 = (f32[16,2304]{1,0:T(8,128)S(1)}, f32[16,2048]{1,0:T(8,128)S(1)}) custom-call(s32[1]{0:T(128)} %bitcast.core, s32[640]{0:T(1024)S(1)} %reshape.68.blocks, bf16[64,16,128]{2,1,0:T(8,128)(2,1)S(1)} %collective-permute-done.3.dual, f32[18,16,128]{2,1,0:T(8,128)S(1)} %own_price.3.before, bf16[16,2304]{1,0:T(8,128)(2,1)S(1)} %slice.24.base, ...), custom_call_target="tpu_custom_call" | custom-call | flops 167772160 | bytes 10485760 | tf_op jit(solution)/shard_map/last_price/pallas_call | solution.py:311
  165.5 15.0 %all_to_all.32 = f32[16,1,5376]{2,1,0:T(1,128)S(1)} all-to-all(f32[16,1,5376]{2,1,0:T(1,128)S(1)} %copy.21), channel_id=1, replica_groups=mesh['scen'=2,'tm'=16] {'tm'}, dimensions={0} | all-to-all | bytes 688128 | tf_op jit(solution)/shard_map/all_to_all | solution.py:386
  (41 shorter events, 4.4 us)
Async XLA Ops:
  4.9 16.5 %all-to-all-start = ((bf16[16,2,3200]{2,1,0:T(2,128)(2,1)}), bf16[16,2,3200]{2,1,0:T(2,128)(2,1)S(1)}, u32[]{:S(2)}, u32[]{:S(2)}) async-start(bf16[16,2,3200]{2,1,0:T(2,128)(2,1)} %reshape.84), calls=%async_computation | async-start | bytes 409600 | tf_op jit(solution)/shard_map/all_to_all | solution.py:341
  21.7 7.0 %copy-start = (bf16[128,5,128,128]{3,2,1,0:T(8,128)(2,1)S(1)}, bf16[128,5,128,128]{3,2,1,0:T(8,128)(2,1)}, u32[]{:S(2)}) copy-start(bf16[128,5,128,128]{3,2,1,0:T(8,128)(2,1)} %tiles_hbm.13) | copy-start | bytes 62914564
  28.6 36.2 %copy-start.7 = (s32[2048]{0:T(1024)S(1)}, s32[2048]{0:T(1024)}, u32[]{:S(2)}) copy-start(s32[2048]{0:T(1024)} %param.11) | copy-start | bytes 24580
  34.1 12.4 %collective-permute-start = (f32[64,16,128]{2,1,0:T(8,128)S(1)}, f32[64,16,128]{2,1,0:T(8,128)S(1)}, u32[]{:S(2)}, u32[]{:S(2)}) collective-permute-start(f32[64,16,128]{2,1,0:T(8,128)S(1)} %get-tuple-element.14), channel_id=1, source_target_pairs={{0,1},{1,0},{2,3},{3,2},{4,5},{5,4},{6,7},{7,6},{8,9},{9,8},{10,11... | collective-permute-start | bytes 1572872 | tf_op jit(solution)/shard_map/ppermute | solution.py:351
  34.1 7.0 %copy-start.1 = (bf16[128,5,128,128]{3,2,1,0:T(8,128)(2,1)S(1)}, bf16[128,5,128,128]{3,2,1,0:T(8,128)(2,1)}, u32[]{:S(2)}) copy-start(bf16[128,5,128,128]{3,2,1,0:T(8,128)(2,1)} %tiles_hbm.13) | copy-start | bytes 62914564
  47.3 13.2 %all-to-all-start.1 = ((bf16[8,8,16,128]{3,2,1,0:T(8,128)(2,1)}), bf16[8,8,16,128]{3,2,1,0:T(8,128)(2,1)S(1)}, u32[]{:S(2)}, u32[]{:S(2)}) async-start(bf16[8,8,16,128]{3,2,1,0:T(8,128)(2,1)} %bitcast.2), calls=%async_computation.1 | async-start | bytes 524288 | tf_op jit(solution)/shard_map/all_to_all | solution.py:354
  61.3 12.7 %all-to-all-start.2 = ((bf16[8,8,16,128]{3,2,1,0:T(8,128)(2,1)}), bf16[8,8,16,128]{3,2,1,0:T(8,128)(2,1)S(1)}, u32[]{:S(2)}, u32[]{:S(2)}) async-start(bf16[8,8,16,128]{3,2,1,0:T(8,128)(2,1)} %broadcast_in_dim.10), calls=%async_computation.2 | async-start | bytes 524288 | tf_op jit(solution)/shard_map/all_to_all | solution.py:359
  74.0 15.3 %collective-permute-start.1 = (bf16[64,16,128]{2,1,0:T(8,128)(2,1)S(1)}, bf16[64,16,128]{2,1,0:T(8,128)(2,1)S(1)}, u32[]{:S(2)}, u32[]{:S(2)}) collective-permute-start(bf16[64,16,128]{2,1,0:T(8,128)(2,1)S(1)} %bitcast.45), channel_id=1, source_target_pairs={{0,1},{1,0},{2,3},{3,2},{4,5},{5,4},{6,7},{7,6},{8,9},{9,8},{10,11... | collective-permute-start | bytes 786440 | tf_op jit(solution)/shard_map/ppermute | solution.py:361
  78.1 7.0 %copy-start.2 = (bf16[128,5,128,128]{3,2,1,0:T(8,128)(2,1)S(1)}, bf16[128,5,128,128]{3,2,1,0:T(8,128)(2,1)}, u32[]{:S(2)}) copy-start(bf16[128,5,128,128]{3,2,1,0:T(8,128)(2,1)} %tiles_hbm.13) | copy-start | bytes 62914564
  89.3 7.0 %copy-start.3 = (bf16[128,5,128,128]{3,2,1,0:T(8,128)(2,1)S(1)}, bf16[128,5,128,128]{3,2,1,0:T(8,128)(2,1)}, u32[]{:S(2)}) copy-start(bf16[128,5,128,128]{3,2,1,0:T(8,128)(2,1)} %tiles_hbm.13) | copy-start | bytes 62914564
  96.3 45.5 %copy-start.6 = (f32[2048]{0:T(1024)S(1)}, f32[2048]{0:T(1024)}, u32[]{:S(2)}) copy-start(f32[2048]{0:T(1024)} %param.12) | copy-start | bytes 24580
  104.2 12.9 %collective-permute-start.2 = (f32[64,16,128]{2,1,0:T(8,128)S(1)}, f32[64,16,128]{2,1,0:T(8,128)S(1)}, u32[]{:S(2)}, u32[]{:S(2)}) collective-permute-start(f32[64,16,128]{2,1,0:T(8,128)S(1)} %get-tuple-element.16), channel_id=1, source_target_pairs={{0,1},{1,0},{2,3},{3,2},{4,5},{5,4},{6,7},{7,6},{8,9},{9,8},{10,11... | collective-permute-start | bytes 1572872 | tf_op jit(solution)/shard_map/ppermute | solution.py:351
  104.7 7.0 %copy-start.4 = (bf16[128,5,128,128]{3,2,1,0:T(8,128)(2,1)S(1)}, bf16[128,5,128,128]{3,2,1,0:T(8,128)(2,1)}, u32[]{:S(2)}) copy-start(bf16[128,5,128,128]{3,2,1,0:T(8,128)(2,1)} %tiles_hbm.13) | copy-start | bytes 62914564
  141.8 10.1 %collective-permute-start.3 = (bf16[64,16,128]{2,1,0:T(8,128)(2,1)S(1)}, bf16[64,16,128]{2,1,0:T(8,128)(2,1)S(1)}, u32[]{:S(2)}, u32[]{:S(2)}) collective-permute-start(bf16[64,16,128]{2,1,0:T(8,128)(2,1)S(1)} %bitcast.47), channel_id=1, source_target_pairs={{0,1},{1,0},{2,3},{3,2},{4,5},{5,4},{6,7},{7,6},{8,9},{9,8},{10,11... | collective-permute-start | bytes 786440 | tf_op jit(solution)/shard_map/ppermute | solution.py:361
  151.9 7.0 %copy-start.5 = (bf16[128,5,128,128]{3,2,1,0:T(8,128)(2,1)S(1)}, bf16[128,5,128,128]{3,2,1,0:T(8,128)(2,1)}, u32[]{:S(2)}) copy-start(bf16[128,5,128,128]{3,2,1,0:T(8,128)(2,1)} %tiles_hbm.13) | copy-start | bytes 62914564

commit v5 on v4

--- a/solution.py
+++ b/solution.py
@@ -22,14 +22,24 @@
 STRAIGHT = 16
 
 
+def partner(chip, slot, chips):
+    if chips & (chips - 1) == 0:
+        return chip ^ slot
+    return (chip + slot) % chips
+
+
 class Half:
-    def __init__(self, core, blocks, tiles_hbm, tiles, sems):
-        self.core, self.blocks, self.tiles_hbm, self.tiles, self.sems = core, blocks, tiles_hbm, tiles, sems
+    def __init__(self, chip, core, blocks, tiles_hbm, tiles, sems):
+        self.chip, self.core = chip, core
+        self.blocks, self.tiles_hbm, self.tiles, self.sems = blocks, tiles_hbm, tiles, sems
         self.chunks = sems.shape[0]
         self.own = tiles.shape[0] // self.chunks
 
+    def first_group(self, chunk):
+        return (2 * partner(self.chip, chunk, self.chunks) + self.core) * self.own
+
     def fetch(self, chunk):
-        there = pl.ds((2 * chunk + self.core) * self.own, self.own)
+        there = pl.ds(self.first_group(chunk), self.own)
         here = pl.ds(chunk * self.own, self.own)
         return pltpu.make_async_copy(self.tiles_hbm.at[there], self.tiles.at[here], self.sems.at[chunk])
 
@@ -47,7 +57,7 @@
                 if wait:
                     self.fetch(chunk).wait()
                 for sub in range(0, self.own, 4):
-                    first = ((2 * chunk + self.core) * self.own + sub) * depth
+                    first = (self.first_group(chunk) + sub) * depth
                     four(chunk * self.own + sub, lambda u, k: self.blocks[first + u * depth + k])
             return carry
 
@@ -177,23 +187,40 @@
     lax.fori_loop(0, level.shape[1] // width, body, 0)
 
 
-def first_flow_kernel(core, blocks, base, tiles_hbm, flows, picked, tiles, sems):
-    half = Half(1 - core[0], blocks, tiles_hbm, tiles, sems)
+def pack_kernel(base, soc, out):
+    devices, rows, width = out.shape
+    hour_rows = soc.shape[0]
+    count = base.shape[1] // devices
+    units = soc.shape[1]
+    pad = jnp.zeros((rows // hour_rows - count - units, width), jnp.float32)
+    for d in range(devices):
+        parts = []
+        for r in range(hour_rows):
+            parts += [base[r, d * count : (d + 1) * count], soc[r], pad]
+        out[d] = jnp.concatenate(parts, axis=0).astype(out.dtype)
+
+
+def first_flow_kernel(place, blocks, came, tiles_hbm, flows, picked, level, tiles, sems, flat):
+    half = Half(place[0], 1 - place[1], blocks, tiles_hbm, tiles, sems)
     half.start()
-    width = tiles.shape[3]
-    for b in range(picked.shape[0]):
-        picked[b] = base[:, b * width : (b + 1) * width]
+    count, hours, width = picked.shape
+    flat[...] = came[...].astype(jnp.float32)
+    rows = flat.shape[0] // hours
+    for b in range(count):
+        picked[b] = flat[pl.ds(b, hours, stride=rows), :].astype(picked.dtype)
+    for c in range(level.shape[1] // width):
+        level[:, c * width : (c + 1) * width] = flat[pl.ds(count + c, hours, stride=rows), :]
     flow_pass(picked, half, flows, True)
 
 
-def own_flow_kernel(core, blocks, picked, tiles_hbm, flows, tiles, sems):
-    half = Half(core[0], blocks, tiles_hbm, tiles, sems)
+def own_flow_kernel(place, blocks, picked, tiles_hbm, flows, tiles, sems):
+    half = Half(place[0], place[1], blocks, tiles_hbm, tiles, sems)
     half.start()
     flow_pass(picked, half, flows, True)
 
 
-def own_price_kernel(core, blocks, dual, tiles_hbm, price, tiles, sems, *sums):
-    half = Half(core[0], blocks, tiles_hbm, tiles, sems)
+def own_price_kernel(place, blocks, dual, tiles_hbm, price, tiles, sems, *sums):
+    half = Half(place[0], place[1], blocks, tiles_hbm, tiles, sems)
     half.start()
     price_pass(dual, half, sums, True)
     for b in range(price.shape[0]):
@@ -201,16 +228,15 @@
 
 
 def middle_kernel(
-    core, blocks, dual, before, base, delta, tiles_hbm,
+    place, blocks, dual, before, base, delta, tiles_hbm,
     price, inject_out, picked, flows, tiles, sems, *sums
 ):
-    half = Half(1 - core[0], blocks, tiles_hbm, tiles, sems)
+    half = Half(place[0], 1 - place[1], blocks, tiles_hbm, tiles, sems)
     half.start()
-    width = tiles.shape[3]
     price_pass(dual, half, sums, True)
 
     def start(b):
-        return base[:, b * width : (b + 1) * width].astype(jnp.float32)
+        return base[b].astype(jnp.float32)
 
     def write(b, new):
         inject_out[b] = new
@@ -221,22 +247,46 @@
 
 
 def last_kernel(
-    core, blocks, dual, before, base, inject, delta, level, unit_block, unit_lane, gain, tiles_hbm,
-    inject_out, level_out, tiles, sems, price, *sums
+    place, blocks, dual, before, base, inject, delta, level, line_dual, unit_block, unit_lane, gain, tiles_hbm,
+    out, tiles, sems, price, level_out, flat, *sums
 ):
-    half = Half(1 - core[0], blocks, tiles_hbm, tiles, sems)
+    half = Half(place[0], 1 - place[1], blocks, tiles_hbm, tiles, sems)
     half.start()
-    width = tiles.shape[3]
+    count, hours, width = price.shape
+    rows = flat.shape[0] // hours
+    flat[...] = jnp.zeros_like(flat)
+    units = level.shape[1] // width
+    for g in range(line_dual.shape[0]):
+        flat[pl.ds(count + units + g, hours, stride=rows), :] = line_dual[g]
     price_pass(dual, half, sums, True)
 
     def start(b):
-        return base[:, b * width : (b + 1) * width].astype(jnp.float32)
+        return base[b].astype(jnp.float32)
 
     def write(b, new):
-        inject_out[:, b * width : (b + 1) * width] = new
+        flat[pl.ds(b, hours, stride=rows), :] = new
 
     update_pass(sums, before, lambda b: inject[b], start, delta, price, write)
     level_pass(price, level, unit_block, unit_lane, gain, level_out, True)
+    for c in range(units):
+        flat[pl.ds(count + c, hours, stride=rows), :] = level_out[:, c * width : (c + 1) * width]
+    out[...] = flat[...].astype(out.dtype)
+
+
+def unpack_kernel(back, inject, line_dual, level):
+    devices = back.shape[0]
+    hour_rows, units = level.shape[0], level.shape[1]
+    count, own = inject.shape[1] // devices, line_dual.shape[1] // devices
+    rows = back.shape[1] // hour_rows
+    for r in range(hour_rows):
+        sum_levels = None
+        for d in range(devices):
+            came = back[d, r * rows : (r + 1) * rows].astype(jnp.float32)
+            inject[r, d * count : (d + 1) * count] = came[:count]
+            line_dual[r, d * own : (d + 1) * own] = came[count + units : count + units + own]
+            part = came[count : count + units]
+            sum_levels = part if sum_levels is None else sum_levels + part
+        level[r] = sum_levels
 
 
 def storage_pass(level, unit_block, unit_lane, delta):
@@ -293,15 +343,20 @@
 
     chips = devices // 2
     half_groups = chips * own_groups
-    core = (me % 2).reshape(1)
-    same_core = [[2 * chip + c for chip in range(chips)] for c in range(2)]
+    place = jnp.stack([me // 2, me % 2])
     sibling = [(d, d + 1 - 2 * (d % 2)) for d in range(devices)]
+
+    def to_partner(slot):
+        return [(d, 2 * partner(d // 2, slot, chips) + d % 2) for d in range(devices)]
+
+    def from_partner(slot):
+        return [(target, source) for source, target in to_partner(slot)]
 
     half_bytes = ptdf_tiles.size
     half_flops = hours * ptdf_tiles.size
     stream = [pltpu.VMEM((half_groups, *ptdf_tiles.shape[1:]), ptdf_tiles.dtype), pltpu.SemaphoreType.DMA((chips,))]
     sums = [pltpu.VMEM((bus_blocks, hours, width), jnp.float32)] * depth
-    large = pltpu.CompilerParams(vmem_limit_bytes=half_bytes + (16 << 20))
+    large = pltpu.CompilerParams(vmem_limit_bytes=48 << 20)
     picked_shape = jax.ShapeDtypeStruct((bus_blocks, hours, width), jnp.bfloat16)
     block_shape = jax.ShapeDtypeStruct((bus_blocks, hours, width), jnp.float32)
     level_shape = jax.ShapeDtypeStruct((hours, units), jnp.float32)
@@ -319,7 +374,7 @@
                 flops=passes * half_flops, bytes_accessed=passes * half_bytes, transcendentals=0
             ),
             name=name,
-        )(core, blocks, *operands, ptdf_tiles)
+        )(place, blocks, *operands, ptdf_tiles)
 
     def small(kernel, name, outs, operands):
         return pl.pallas_call(
@@ -332,32 +387,57 @@
             name=name,
         )(*operands)
 
-    high = soc_init.astype(jnp.bfloat16)
-    low = (soc_init - high.astype(jnp.float32)).astype(jnp.bfloat16)
-    own = jnp.concatenate([high, low], axis=1)[:, None, :]
-    sent = jnp.concatenate(
-        [base_injection.reshape(hour_rows, devices, buses), jnp.broadcast_to(own, (hour_rows, devices, 2 * units))], axis=2
+    unit_rows = units // width
+
+    def whole_tiles(rows):
+        return -(-rows // 16) * 16
+
+    rows_in = whole_tiles(bus_blocks + unit_rows)
+    rows_out = whole_tiles(bus_blocks + unit_rows + own_groups)
+    (sent,) = small(
+        pack_kernel,
+        "pack",
+        [jax.ShapeDtypeStruct((devices, hour_rows * rows_in, width), jnp.bfloat16)],
+        [
+            base_injection.astype(jnp.float32).reshape(hour_rows, bus_count // width, width),
+            soc_init.reshape(hour_rows, unit_rows, width),
+        ],
     )
-    came = lax.all_to_all(jnp.swapaxes(sent, 0, 1), "tm", split_axis=0, concat_axis=0, tiled=True)
-    came = came.reshape(hours, buses + 2 * units)
-    base = came[:, :buses]
-    level = came[:, buses : buses + units].astype(jnp.float32) + came[:, buses + units :].astype(jnp.float32)
-
-    away, picked = product(first_flow_kernel, "first_flow", [flow_shape, picked_shape], [base], [])
-    (delta,) = small(storage_kernel, "storage", [block_shape], [level, unit_block, unit_lane])
+    came = lax.all_to_all(sent, "tm", split_axis=0, concat_axis=0, tiled=True)
+    away, base, level = product(
+        first_flow_kernel,
+        "first_flow",
+        [flow_shape, picked_shape, level_shape],
+        [came.reshape(hours * rows_in, width)],
+        [pltpu.VMEM((hours * rows_in, width), jnp.float32)],
+    )
+    picked = base
+    price = None
     line_dual = jnp.zeros((own_groups, hours, lines), jnp.float32)
-    inject = None
     for iteration in range(ITERS):
-        arrived = lax.ppermute(away, "tm", sibling)
+        arrived = lax.ppermute(away, "tm", sibling).reshape(chips, own_groups, hours, lines)
         (flows,) = product(own_flow_kernel, "own_flow", [flow_shape], [picked], [])
-        pair = (flows + arrived).astype(jnp.bfloat16).reshape(chips, own_groups, hours, lines)
-        parts = lax.all_to_all(pair, "tm", split_axis=0, concat_axis=0, axis_index_groups=same_core, tiled=True)
-        shifted = jnp.sum(parts.astype(jnp.float32), axis=0) + line_dual
+        flows = flows.reshape(chips, own_groups, hours, lines)
+        parts = [
+            lax.ppermute((flows[slot] + arrived[slot]).astype(jnp.bfloat16), "tm", to_partner(slot))
+            for slot in range(1, chips)
+        ]
+        if iteration == 0:
+            (delta,) = small(storage_kernel, "storage", [block_shape], [level, unit_block, unit_lane])
+        else:
+            level, delta = small(
+                level_kernel, "storage", [level_shape, block_shape], [price, level, unit_block, unit_lane, gain]
+            )
+        parts, level, delta = lax.optimization_barrier((parts, level, delta))
+        shifted = flows[0] + arrived[0] + line_dual
+        for part in parts:
+            shifted = shifted + part.astype(jnp.float32)
         clipped = jnp.clip(shifted, -own_limits, own_limits)
         line_dual = shifted - clipped
-        dual = jnp.broadcast_to(line_dual.astype(jnp.bfloat16)[None], (chips, own_groups, hours, lines))
-        dual = lax.all_to_all(dual, "tm", split_axis=0, concat_axis=0, axis_index_groups=same_core, tiled=True)
-        dual = dual.reshape(half_groups, hours, lines)
+        dual = line_dual.astype(jnp.bfloat16)
+        dual = jnp.concatenate(
+            [dual] + [lax.ppermute(dual, "tm", from_partner(slot)) for slot in range(1, chips)], axis=0
+        )
         other = lax.ppermute(dual, "tm", sibling)
         (before,) = product(own_price_kernel, "own_price", [block_shape], [dual], sums)
         if iteration < ITERS - 1:
@@ -369,26 +449,36 @@
                 sums,
                 2,
             )
-            level, delta = small(
-                level_kernel, "storage", [level_shape, block_shape], [price, level, unit_block, unit_lane, gain]
-            )
         else:
-            inject, level = product(
+            (out,) = product(
                 last_kernel,
                 "last_price",
-                [jax.ShapeDtypeStruct((hours, buses), jnp.float32), level_shape],
-                [other, before, base, inject, delta, level, unit_block, unit_lane, gain],
-                [pltpu.VMEM(block_shape.shape, block_shape.dtype)] + sums,
+                [jax.ShapeDtypeStruct((hours * rows_out, width), jnp.bfloat16)],
+                [other, before, base, inject, delta, level, line_dual, unit_block, unit_lane, gain],
+                [
+                    pltpu.VMEM(block_shape.shape, jnp.float32),
+                    pltpu.VMEM(level_shape.shape, jnp.float32),
+                    pltpu.VMEM((hours * rows_out, width), jnp.float32),
+                ]
+                + sums,
             )
 
-    duals = own_groups * lines
-    joined = jnp.concatenate([inject, level, jnp.swapaxes(line_dual, 0, 1).reshape(hours, duals)], axis=1)
     back = lax.all_to_all(
-        joined.reshape(devices, hour_rows, buses + units + duals), "tm", split_axis=0, concat_axis=0, tiled=True
+        out.reshape(devices, hour_rows * rows_out, width), "tm", split_axis=0, concat_axis=0, tiled=True
     )
-    inject = jnp.swapaxes(back[:, :, :buses], 0, 1).reshape(hour_rows, bus_count)
-    level = jnp.sum(back[:, :, buses : buses + units], axis=0)
-    own_dual = jnp.swapaxes(back[:, :, buses + units :], 0, 1).reshape(hour_rows, line_count)
+    inject, own_dual, level = small(
+        unpack_kernel,
+        "unpack",
+        [
+            jax.ShapeDtypeStruct((hour_rows, bus_count // width, width), jnp.float32),
+            jax.ShapeDtypeStruct((hour_rows, line_count // width, width), jnp.float32),
+            jax.ShapeDtypeStruct((hour_rows, unit_rows, width), jnp.float32),
+        ],
+        [back],
+    )
+    inject = inject.reshape(hour_rows, bus_count)
+    own_dual = own_dual.reshape(hour_rows, line_count)
+    level = level.reshape(hour_rows, units)
     return (inject, own_dual, level)
 
 

time: 183 us -> 146 us (0.80)
  local copies, waits for them, and re-layouts: 46.8 us -> 1.83 us
  starting transfers between devices: 15 us -> 49.5 us
  blocking collectives: 39.4 us -> 11.7 us
  Pallas kernels: 48.6 us -> 55.1 us
  other arithmetic: 5.34 us -> 2.1 us
  waiting for transfers between devices: 26.3 us -> 24 us
    unnamed x20 -> x19, local copies, waits for them, and re-layouts: 43.5 us -> 1.61 us
    ppermute x2 -> x30, starting transfers between devices: 0.64 us -> 41.9 us  [the longest x14 22.5 us: shards(): lax.ppermute((flows[slot] + arrived[slot]).astype(jnp.bfloat16), 'tm', to...]
    all_to_all x3 -> x1, blocking collectives: 39.4 us -> 11.7 us  [shards(): lax.all_to_all(out.reshape(devices, hour_rows * rows_out, width), 'tm', s...]
    all_to_all x3 -> x1, waiting for transfers between devices: 26.3 us -> 7.89 us  [shards(): came = lax.all_to_all(sent, 'tm', split_axis=0, concat_axis=0, tiled=True)]
    ppermute x2 -> x30, waiting for transfers between devices: 0.01 us -> 16.1 us  [the longest x14 16.1 us: shards(): lax.ppermute(dual, 'tm', from_partner(slot))]
    all_to_all x3 -> x1, starting transfers between devices: 14.3 us -> 7.39 us  [shards(): came = lax.all_to_all(sent, 'tm', split_axis=0, concat_axis=0, tiled=True)]
    pallas_call x7, Pallas kernels: 38.8 us -> 43.9 us  [product(): pl.pallas_call(kernel, out_shape=outs, in_specs=[SMEM] * 2 + [VMEM] * len...]
    pallas_call x2 -> x4, Pallas kernels: 9.84 us -> 11.2 us  [small(): pl.pallas_call(kernel, out_shape=outs, in_specs=[VMEM] * len(operands), o...]
  transfers between devices with their start and end apart: 7 -> 33, of which waited for: 3 -> 5; matrix products, arithmetic and copies ran while one was open for 1% -> 1% of each run, Pallas kernels for 16% -> 22%
where the time goes in v5:
time: 146 us; the launch traced here: 145 us
  Pallas kernels  55.1 us (38%)
  starting transfers between devices  49.5 us (34%)
  waiting for transfers between devices  24 us (16%)
  blocking collectives  11.7 us (8%)
  other arithmetic  2.1 us (1%)
  local copies, waits for them, and re-layouts  1.83 us (1%)
    pallas_call x7, Pallas kernels, product(): pl.pallas_call(kernel, out_shape=outs, in_specs=[SMEM] * 2 + [VMEM] * len...  43.9 us
    ppermute x14, starting transfers between devices, shards(): lax.ppermute((flows[slot] + arrived[slot]).astype(jnp.bfloat16), 'tm', to...  22.5 us
    ppermute x14, starting transfers between devices, shards(): lax.ppermute(dual, 'tm', from_partner(slot))  18.8 us
    ppermute x14, waiting for transfers between devices, shards(): lax.ppermute(dual, 'tm', from_partner(slot))  16.1 us
    all_to_all x1, blocking collectives, shards(): lax.all_to_all(out.reshape(devices, hour_rows * rows_out, width), 'tm', s...  11.7 us
    pallas_call x4, Pallas kernels, small(): pl.pallas_call(kernel, out_shape=outs, in_specs=[VMEM] * len(operands), o...  11.2 us
    all_to_all x1, waiting for transfers between devices, shards(): came = lax.all_to_all(sent, 'tm', split_axis=0, concat_axis=0, tiled=True)  7.89 us
    all_to_all x1, starting transfers between devices, shards(): came = lax.all_to_all(sent, 'tm', split_axis=0, concat_axis=0, tiled=True)  7.39 us
  transfers between devices with their start and end apart: 33, of which 5 were waited for; matrix products, arithmetic and copies ran while one was open for 1% of the time, Pallas kernels for 22%

profile of v5, /device:TPU:0, one launch (start us, length us, event | category | flops | bytes accessed | tf_op | source)
XLA Modules:
  0.0 145.2 jit_solution(1950275587025705084)
XLA Ops:
  3.1 7.4 %all-to-all-start = ((bf16[16,48,128]{2,1,0:T(8,128)(2,1)}), bf16[16,48,128]{2,1,0:T(8,128)(2,1)S(1)}, u32[]{:S(2)}, u32[]{:S(2)}) async-start(bf16[16,48,128]{2,1,0:T(8,128)(2,1)} %pack.1), calls=%async_computation | async-start | bytes 393216 | tf_op jit(solution)/shard_map/all_to_all | solution.py:406
  11.6 7.9 %all-to-all-done = bf16[16,48,128]{2,1,0:T(8,128)(2,1)S(1)} async-done(((bf16[16,48,128]{2,1,0:T(8,128)(2,1)}), bf16[16,48,128]{2,1,0:T(8,128)(2,1)S(1)}, u32[]{:S(2)}, u32[]{:S(2)}) %all-to-all-start) | async-done | bytes 196640 | tf_op jit(solution)/shard_map/all_to_all | solution.py:406
  19.5 6.0 %first_flow.1 = (f32[64,16,128]{2,1,0:T(8,128)S(1)}, bf16[18,16,128]{2,1,0:T(8,128)(2,1)S(1)}, f32[16,2048]{1,0:T(8,128)S(1)}) custom-call(s32[2]{0:T(128)S(1)} %pad_add_fusion.place, s32[640]{0:T(1024)S(1)} %reshape.112.blocks, bf16[768,128]{1,0:T(8,128)(2,1)S(1)} %bitcast.17, bf16[128,5,128,128]{3,2,1,0:T(8,128)(2,1)} %tiles_hbm.13), custom_call_target="tpu_custom_call" | custom-call | flops 167772160 | bytes 10485760 | tf_op jit(solution)/shard_map/first_flow/pallas_call | solution.py:366
  25.6 6.0 %own_flow.2 = f32[64,16,128]{2,1,0:T(8,128)S(1)} custom-call(s32[2]{0:T(128)S(1)} %pad_add_fusion.place, s32[640]{0:T(1024)S(1)} %reshape.112.blocks, bf16[18,16,128]{2,1,0:T(8,128)(2,1)S(1)} %get-tuple-element.33.picked.base, bf16[128,5,128,128]{3,2,1,0:T(8,128)(2,1)} %tiles_hbm.13), custom_call_target="tpu_custom_call" | custom-call | flops 167772160 | bytes 10485760 | tf_op jit(solution)/shard_map/own_flow/pallas_call | solution.py:366
  31.7 1.5 %collective-permute-start.7 = (bf16[8,16,128]{2,1,0:T(8,128)(2,1)S(1)}, bf16[8,16,128]{2,1,0:T(8,128)(2,1)S(1)}, u32[]{:S(2)}, u32[]{:S(2)}) collective-permute-start(bf16[8,16,128]{2,1,0:T(8,128)(2,1)S(1)} %get-tuple-element.76), channel_id=1, source_target_pairs={{0,14},{1,15},{2,12},{3,13},{4,10},{5,11},{6,8},{7,9},{8,6},{9,7},... | collective-permute-start | bytes 98312 | tf_op jit(solution)/shard_map/ppermute | solution.py:422
  33.1 2.1 %collective-permute-start.6 = (bf16[8,16,128]{2,1,0:T(8,128)(2,1)S(1)}, bf16[8,16,128]{2,1,0:T(8,128)(2,1)S(1)}, u32[]{:S(2)}, u32[]{:S(2)}) collective-permute-start(bf16[8,16,128]{2,1,0:T(8,128)(2,1)S(1)} %get-tuple-element.77), channel_id=1, source_target_pairs={{0,12},{1,13},{2,14},{3,15},{4,8},{5,9},{6,10},{7,11},{8,4},{9,5},... | collective-permute-start | bytes 98312 | tf_op jit(solution)/shard_map/ppermute | solution.py:422
  35.5 4.0 %collective-permute-start.4 = (bf16[8,16,128]{2,1,0:T(8,128)(2,1)S(1)}, bf16[8,16,128]{2,1,0:T(8,128)(2,1)S(1)}, u32[]{:S(2)}, u32[]{:S(2)}) collective-permute-start(bf16[8,16,128]{2,1,0:T(8,128)(2,1)S(1)} %get-tuple-element.79), channel_id=1, source_target_pairs={{0,8},{1,9},{2,10},{3,11},{4,12},{5,13},{6,14},{7,15},{8,0},{9,1},... | collective-permute-start | bytes 98312 | tf_op jit(solution)/shard_map/ppermute | solution.py:422
  39.5 1.7 %collective-permute-start.2 = (bf16[8,16,128]{2,1,0:T(8,128)(2,1)S(1)}, bf16[8,16,128]{2,1,0:T(8,128)(2,1)S(1)}, u32[]{:S(2)}, u32[]{:S(2)}) collective-permute-start(bf16[8,16,128]{2,1,0:T(8,128)(2,1)S(1)} %get-tuple-element.81), channel_id=1, source_target_pairs={{0,4},{1,5},{2,6},{3,7},{4,0},{5,1},{6,2},{7,3},{8,12},{9,13},{10,... | collective-permute-start | bytes 98312 | tf_op jit(solution)/shard_map/ppermute | solution.py:422
  41.2 1.8 %collective-permute-start.1 = (bf16[8,16,128]{2,1,0:T(8,128)(2,1)S(1)}, bf16[8,16,128]{2,1,0:T(8,128)(2,1)S(1)}, u32[]{:S(2)}, u32[]{:S(2)}) collective-permute-start(bf16[8,16,128]{2,1,0:T(8,128)(2,1)S(1)} %get-tuple-element.82), channel_id=1, source_target_pairs={{0,2},{1,3},{2,0},{3,1},{4,6},{5,7},{6,4},{7,5},{8,10},{9,11},{10,... | collective-permute-start | bytes 98312 | tf_op jit(solution)/shard_map/ppermute | solution.py:422
  43.7 4.0 %storage.2.delta = f32[18,16,128]{2,1,0:T(8,128)S(1)} custom-call(f32[16,2048]{1,0:T(8,128)S(1)} %get-tuple-element.47.level, s32[1,2048]{1,0:T(1,128)S(1)} %bitcast.23, s32[1,2048]{1,0:T(1,128)S(1)} %bitcast.20), custom_call_target="tpu_custom_call" | custom-call | flops 167772160 | bytes 4194304 | tf_op jit(solution)/shard_map/storage/pallas_call | solution.py:380
  48.1 2.3 %collective-permute-start.14 = (bf16[8,16,128]{2,1,0:T(8,128)(2,1)S(1)}, bf16[8,16,128]{2,1,0:T(8,128)(2,1)S(1)}, u32[]{:S(2)}, u32[]{:S(2)}) collective-permute-start(bf16[8,16,128]{2,1,0:T(8,128)(2,1)S(1)} %get-tuple-element.67), channel_id=1, source_target_pairs={{14,0},{15,1},{12,2},{13,3},{10,4},{11,5},{8,6},{9,7},{6,8},{7,9},... | collective-permute-start | bytes 98312 | tf_op jit(solution)/shard_map/ppermute | solution.py:439
  50.5 2.7 %collective-permute-start.13 = (bf16[8,16,128]{2,1,0:T(8,128)(2,1)S(1)}, bf16[8,16,128]{2,1,0:T(8,128)(2,1)S(1)}, u32[]{:S(2)}, u32[]{:S(2)}) collective-permute-start(bf16[8,16,128]{2,1,0:T(8,128)(2,1)S(1)} %get-tuple-element.67), channel_id=1, source_target_pairs={{12,0},{13,1},{14,2},{15,3},{8,4},{9,5},{10,6},{11,7},{4,8},{5,9},... | collective-permute-start | bytes 98312 | tf_op jit(solution)/shard_map/ppermute | solution.py:439
  53.2 2.6 %collective-permute-start.11 = (bf16[8,16,128]{2,1,0:T(8,128)(2,1)S(1)}, bf16[8,16,128]{2,1,0:T(8,128)(2,1)S(1)}, u32[]{:S(2)}, u32[]{:S(2)}) collective-permute-start(bf16[8,16,128]{2,1,0:T(8,128)(2,1)S(1)} %get-tuple-element.67), channel_id=1, source_target_pairs={{8,0},{9,1},{10,2},{11,3},{12,4},{13,5},{14,6},{15,7},{0,8},{1,9},... | collective-permute-start | bytes 98312 | tf_op jit(solution)/shard_map/ppermute | solution.py:439
  55.8 4.1 %collective-permute-done.9 = bf16[8,16,128]{2,1,0:T(8,128)(2,1)S(1)} collective-permute-done((bf16[8,16,128]{2,1,0:T(8,128)(2,1)S(1)}, bf16[8,16,128]{2,1,0:T(8,128)(2,1)S(1)}, u32[]{:S(2)}, u32[]{:S(2)}) %collective-permute-start.9) | collective-permute-done | bytes 32800 | tf_op jit(solution)/shard_map/ppermute | solution.py:439
  61.3 3.5 %collective-permute-done.10 = bf16[8,16,128]{2,1,0:T(8,128)(2,1)S(1)} collective-permute-done((bf16[8,16,128]{2,1,0:T(8,128)(2,1)S(1)}, bf16[8,16,128]{2,1,0:T(8,128)(2,1)S(1)}, u32[]{:S(2)}, u32[]{:S(2)}) %collective-permute-start.10) | collective-permute-done | bytes 32800 | tf_op jit(solution)/shard_map/ppermute | solution.py:439
  64.9 5.1 %own_price.2.before = f32[18,16,128]{2,1,0:T(8,128)S(1)} custom-call(s32[2]{0:T(128)S(1)} %pad_add_fusion.place, s32[640]{0:T(1024)S(1)} %reshape.112.blocks, bf16[64,16,128]{2,1,0:T(8,128)(2,1)S(1)} %constant_dynamic-update-slice_fusion.dual, bf16[128,5,128,128]{3,2,1,0:T(8,128)(2,1)} %tiles_hbm.13), custom_call_target="tpu_custom_call" | custom-call | flops 167772160 | bytes 10485760 | tf_op jit(solution)/shard_map/own_price/pallas_call | solution.py:366
  70.0 8.7 %price_then_flow.1 = (f32[18,16,128]{2,1,0:T(8,128)S(1)}, f32[18,16,128]{2,1,0:T(8,128)S(1)}, bf16[18,16,128]{2,1,0:T(8,128)(2,1)S(1)}, f32[64,16,128]{2,1,0:T(8,128)S(1)}) custom-call(s32[2]{0:T(128)S(1)} %pad_add_fusion.place, s32[640]{0:T(1024)S(1)} %reshape.112.blocks, bf16[64,16,128]{2,1,0:T(8,128)(2,1)S(1)} %collective-permute-done.15.dual, ...), custom_call_target="tpu_custom_call" | custom-call | flops 335544320 | bytes 20971520 | tf_op jit(solution)/shard_map/price_then_flow/pallas_call | solution.py:366
  79.2 6.0 %own_flow.3 = f32[64,16,128]{2,1,0:T(8,128)S(1)} custom-call(s32[2]{0:T(128)S(1)} %pad_add_fusion.place, s32[640]{0:T(1024)S(1)} %reshape.112.blocks, bf16[18,16,128]{2,1,0:T(8,128)(2,1)S(1)} %get-tuple-element.44.picked, bf16[128,5,128,128]{3,2,1,0:T(8,128)(2,1)} %tiles_hbm.13), custom_call_target="tpu_custom_call" | custom-call | flops 167772160 | bytes 10485760 | tf_op jit(solution)/shard_map/own_flow/pallas_call | solution.py:366
  85.3 2.2 %collective-permute-start.23 = (bf16[8,16,128]{2,1,0:T(8,128)(2,1)S(1)}, bf16[8,16,128]{2,1,0:T(8,128)(2,1)S(1)}, u32[]{:S(2)}, u32[]{:S(2)}) collective-permute-start(bf16[8,16,128]{2,1,0:T(8,128)(2,1)S(1)} %get-tuple-element.69), channel_id=1, source_target_pairs={{0,14},{1,15},{2,12},{3,13},{4,10},{5,11},{6,8},{7,9},{8,6},{9,7},... | collective-permute-start | bytes 98312 | tf_op jit(solution)/shard_map/ppermute | solution.py:422
  87.5 2.7 %collective-permute-start.22 = (bf16[8,16,128]{2,1,0:T(8,128)(2,1)S(1)}, bf16[8,16,128]{2,1,0:T(8,128)(2,1)S(1)}, u32[]{:S(2)}, u32[]{:S(2)}) collective-permute-start(bf16[8,16,128]{2,1,0:T(8,128)(2,1)S(1)} %get-tuple-element.70), channel_id=1, source_target_pairs={{0,12},{1,13},{2,14},{3,15},{4,8},{5,9},{6,10},{7,11},{8,4},{9,5},... | collective-permute-start | bytes 98312 | tf_op jit(solution)/shard_map/ppermute | solution.py:422
  90.2 2.8 %collective-permute-start.20 = (bf16[8,16,128]{2,1,0:T(8,128)(2,1)S(1)}, bf16[8,16,128]{2,1,0:T(8,128)(2,1)S(1)}, u32[]{:S(2)}, u32[]{:S(2)}) collective-permute-start(bf16[8,16,128]{2,1,0:T(8,128)(2,1)S(1)} %get-tuple-element.72), channel_id=1, source_target_pairs={{0,8},{1,9},{2,10},{3,11},{4,12},{5,13},{6,14},{7,15},{8,0},{9,1},... | collective-permute-start | bytes 98312 | tf_op jit(solution)/shard_map/ppermute | solution.py:422
  93.1 3.0 %collective-permute-start.18 = (bf16[8,16,128]{2,1,0:T(8,128)(2,1)S(1)}, bf16[8,16,128]{2,1,0:T(8,128)(2,1)S(1)}, u32[]{:S(2)}, u32[]{:S(2)}) collective-permute-start(bf16[8,16,128]{2,1,0:T(8,128)(2,1)S(1)} %get-tuple-element.74), channel_id=1, source_target_pairs={{0,4},{1,5},{2,6},{3,7},{4,0},{5,1},{6,2},{7,3},{8,12},{9,13},{10,... | collective-permute-start | bytes 98312 | tf_op jit(solution)/shard_map/ppermute | solution.py:422
  96.5 5.8 %storage.3 = (f32[16,2048]{1,0:T(8,128)S(1)}, f32[18,16,128]{2,1,0:T(8,128)S(1)}) custom-call(f32[18,16,128]{2,1,0:T(8,128)S(1)} %get-tuple-element.46.price, f32[16,2048]{1,0:T(8,128)S(1)} %get-tuple-element.47.level, s32[1,2048]{1,0:T(1,128)S(1)} %bitcast.24, s32[1,2048]{1,0:T(1,128)S(1)} %bitcast.21, f32[1,2048]{1,0:T(1,128)S(1)} %bitcast.26), custom_call_target="tpu_custom_call" | custom-call | flops 167772160 | bytes 4194304 | tf_op jit(solution)/shard_map/storage/pallas_call | solution.py:380
  102.5 1.6 %collective-permute-start.24 = (bf16[8,16,128]{2,1,0:T(8,128)(2,1)S(1)}, bf16[8,16,128]{2,1,0:T(8,128)(2,1)S(1)}, u32[]{:S(2)}, u32[]{:S(2)}) collective-permute-start(bf16[8,16,128]{2,1,0:T(8,128)(2,1)S(1)} %get-tuple-element.64), channel_id=1, source_target_pairs={{2,0},{3,1},{0,2},{1,3},{6,4},{7,5},{4,6},{5,7},{10,8},{11,9},{8,1... | collective-permute-start | bytes 98312 | tf_op jit(solution)/shard_map/ppermute | solution.py:439
  104.1 1.4 collective-permute-start.30
  105.5 2.3 %collective-permute-start.29 = (bf16[8,16,128]{2,1,0:T(8,128)(2,1)S(1)}, bf16[8,16,128]{2,1,0:T(8,128)(2,1)S(1)}, u32[]{:S(2)}, u32[]{:S(2)}) collective-permute-start(bf16[8,16,128]{2,1,0:T(8,128)(2,1)S(1)} %get-tuple-element.64), channel_id=1, source_target_pairs={{12,0},{13,1},{14,2},{15,3},{8,4},{9,5},{10,6},{11,7},{4,8},{5,9},... | collective-permute-start | bytes 98312 | tf_op jit(solution)/shard_map/ppermute | solution.py:439
  107.9 3.9 %collective-permute-start.27 = (bf16[8,16,128]{2,1,0:T(8,128)(2,1)S(1)}, bf16[8,16,128]{2,1,0:T(8,128)(2,1)S(1)}, u32[]{:S(2)}, u32[]{:S(2)}) collective-permute-start(bf16[8,16,128]{2,1,0:T(8,128)(2,1)S(1)} %get-tuple-element.64), channel_id=1, source_target_pairs={{8,0},{9,1},{10,2},{11,3},{12,4},{13,5},{14,6},{15,7},{0,8},{1,9},... | collective-permute-start | bytes 98312 | tf_op jit(solution)/shard_map/ppermute | solution.py:439
  111.8 3.9 %collective-permute-done.25 = bf16[8,16,128]{2,1,0:T(8,128)(2,1)S(1)} collective-permute-done((bf16[8,16,128]{2,1,0:T(8,128)(2,1)S(1)}, bf16[8,16,128]{2,1,0:T(8,128)(2,1)S(1)}, u32[]{:S(2)}, u32[]{:S(2)}) %collective-permute-start.25) | collective-permute-done | bytes 32800 | tf_op jit(solution)/shard_map/ppermute | solution.py:439
  116.0 4.6 %collective-permute-done.26 = bf16[8,16,128]{2,1,0:T(8,128)(2,1)S(1)} collective-permute-done((bf16[8,16,128]{2,1,0:T(8,128)(2,1)S(1)}, bf16[8,16,128]{2,1,0:T(8,128)(2,1)S(1)}, u32[]{:S(2)}, u32[]{:S(2)}) %collective-permute-start.26) | collective-permute-done | bytes 32800 | tf_op jit(solution)/shard_map/ppermute | solution.py:439
  120.7 5.0 %own_price.3.before = f32[18,16,128]{2,1,0:T(8,128)S(1)} custom-call(s32[2]{0:T(128)S(1)} %pad_add_fusion.place, s32[640]{0:T(1024)S(1)} %reshape.112.blocks, bf16[64,16,128]{2,1,0:T(8,128)(2,1)S(1)} %constant_dynamic-update-slice_fusion.8.dual, bf16[128,5,128,128]{3,2,1,0:T(8,128)(2,1)} %tiles_hbm.13), custom_call_target="tpu_custom_call" | custom-call | flops 167772160 | bytes 10485760 | tf_op jit(solution)/shard_map/own_price/pallas_call | solution.py:366
  125.8 7.1 %last_price.1 = bf16[768,128]{1,0:T(8,128)(2,1)S(1)} custom-call(s32[2]{0:T(128)S(1)} %pad_add_fusion.place, s32[640]{0:T(1024)S(1)} %reshape.112.blocks, bf16[64,16,128]{2,1,0:T(8,128)(2,1)S(1)} %collective-permute-done.31.dual, f32[18,16,128]{2,1,0:T(8,128)S(1)} %own_price.3.before, bf16[18,16,128]{2,1,0:T(8,128)(2,1)S(1)} %get-tuple-element.33.picked.base, ...), custom_call_target="tpu_custom_call" | custom-call | flops 167772160 | bytes 10485760 | tf_op jit(solution)/shard_map/last_price/pallas_call | solution.py:366
  132.8 11.7 %all_to_all.10.back = bf16[16,48,128]{2,1,0:T(8,128)(2,1)S(1)} all-to-all(bf16[16,48,128]{2,1,0:T(8,128)(2,1)S(1)} %bitcast.18), channel_id=1, replica_groups=mesh['scen'=2,'tm'=16] {'tm'}, dimensions={0} | all-to-all | bytes 393216 | tf_op jit(solution)/shard_map/all_to_all | solution.py:466
  (76 shorter events, 8.8 us)
Async XLA Ops:
  3.1 16.4 %all-to-all-start = ((bf16[16,48,128]{2,1,0:T(8,128)(2,1)}), bf16[16,48,128]{2,1,0:T(8,128)(2,1)S(1)}, u32[]{:S(2)}, u32[]{:S(2)}) async-start(bf16[16,48,128]{2,1,0:T(8,128)(2,1)} %pack.1), calls=%async_computation | async-start | bytes 393216 | tf_op jit(solution)/shard_map/all_to_all | solution.py:406
  25.5 6.1 %collective-permute-start = (f32[64,16,128]{2,1,0:T(8,128)S(1)}, f32[64,16,128]{2,1,0:T(8,128)S(1)}, u32[]{:S(2)}, u32[]{:S(2)}) collective-permute-start(f32[64,16,128]{2,1,0:T(8,128)S(1)} %get-tuple-element.34), channel_id=1, source_target_pairs={{0,1},{1,0},{2,3},{3,2},{4,5},{5,4},{6,7},{7,6},{8,9},{9,8},{10,11... | collective-permute-start | bytes 1572872 | tf_op jit(solution)/shard_map/ppermute | solution.py:418
  31.7 7.8 %collective-permute-start.7 = (bf16[8,16,128]{2,1,0:T(8,128)(2,1)S(1)}, bf16[8,16,128]{2,1,0:T(8,128)(2,1)S(1)}, u32[]{:S(2)}, u32[]{:S(2)}) collective-permute-start(bf16[8,16,128]{2,1,0:T(8,128)(2,1)S(1)} %get-tuple-element.76), channel_id=1, source_target_pairs={{0,14},{1,15},{2,12},{3,13},{4,10},{5,11},{6,8},{7,9},{8,6},{9,7},... | collective-permute-start | bytes 98312 | tf_op jit(solution)/shard_map/ppermute | solution.py:422
  33.1 8.1 %collective-permute-start.6 = (bf16[8,16,128]{2,1,0:T(8,128)(2,1)S(1)}, bf16[8,16,128]{2,1,0:T(8,128)(2,1)S(1)}, u32[]{:S(2)}, u32[]{:S(2)}) collective-permute-start(bf16[8,16,128]{2,1,0:T(8,128)(2,1)S(1)} %get-tuple-element.77), channel_id=1, source_target_pairs={{0,12},{1,13},{2,14},{3,15},{4,8},{5,9},{6,10},{7,11},{8,4},{9,5},... | collective-permute-start | bytes 98312 | tf_op jit(solution)/shard_map/ppermute | solution.py:422
  35.3 12.4 %collective-permute-start.5 = (bf16[8,16,128]{2,1,0:T(8,128)(2,1)S(1)}, bf16[8,16,128]{2,1,0:T(8,128)(2,1)S(1)}, u32[]{:S(2)}, u32[]{:S(2)}) collective-permute-start(bf16[8,16,128]{2,1,0:T(8,128)(2,1)S(1)} %get-tuple-element.78), channel_id=1, source_target_pairs={{0,10},{1,11},{2,8},{3,9},{4,14},{5,15},{6,12},{7,13},{8,2},{9,3},... | collective-permute-start | bytes 98312 | tf_op jit(solution)/shard_map/ppermute | solution.py:422
  35.5 12.3 %collective-permute-start.4 = (bf16[8,16,128]{2,1,0:T(8,128)(2,1)S(1)}, bf16[8,16,128]{2,1,0:T(8,128)(2,1)S(1)}, u32[]{:S(2)}, u32[]{:S(2)}) collective-permute-start(bf16[8,16,128]{2,1,0:T(8,128)(2,1)S(1)} %get-tuple-element.79), channel_id=1, source_target_pairs={{0,8},{1,9},{2,10},{3,11},{4,12},{5,13},{6,14},{7,15},{8,0},{9,1},... | collective-permute-start | bytes 98312 | tf_op jit(solution)/shard_map/ppermute | solution.py:422
  39.5 8.2 %collective-permute-start.3 = (bf16[8,16,128]{2,1,0:T(8,128)(2,1)S(1)}, bf16[8,16,128]{2,1,0:T(8,128)(2,1)S(1)}, u32[]{:S(2)}, u32[]{:S(2)}) collective-permute-start(bf16[8,16,128]{2,1,0:T(8,128)(2,1)S(1)} %get-tuple-element.80), channel_id=1, source_target_pairs={{0,6},{1,7},{2,4},{3,5},{4,2},{5,3},{6,0},{7,1},{8,14},{9,15},{10,... | collective-permute-start | bytes 98312 | tf_op jit(solution)/shard_map/ppermute | solution.py:422
  39.5 8.3 %collective-permute-start.2 = (bf16[8,16,128]{2,1,0:T(8,128)(2,1)S(1)}, bf16[8,16,128]{2,1,0:T(8,128)(2,1)S(1)}, u32[]{:S(2)}, u32[]{:S(2)}) collective-permute-start(bf16[8,16,128]{2,1,0:T(8,128)(2,1)S(1)} %get-tuple-element.81), channel_id=1, source_target_pairs={{0,4},{1,5},{2,6},{3,7},{4,0},{5,1},{6,2},{7,3},{8,12},{9,13},{10,... | collective-permute-start | bytes 98312 | tf_op jit(solution)/shard_map/ppermute | solution.py:422
  41.2 6.5 %collective-permute-start.1 = (bf16[8,16,128]{2,1,0:T(8,128)(2,1)S(1)}, bf16[8,16,128]{2,1,0:T(8,128)(2,1)S(1)}, u32[]{:S(2)}, u32[]{:S(2)}) collective-permute-start(bf16[8,16,128]{2,1,0:T(8,128)(2,1)S(1)} %get-tuple-element.82), channel_id=1, source_target_pairs={{0,2},{1,3},{2,0},{3,1},{4,6},{5,7},{6,4},{7,5},{8,10},{9,11},{10,... | collective-permute-start | bytes 98312 | tf_op jit(solution)/shard_map/ppermute | solution.py:422
  47.8 8.0 %collective-permute-start.8 = (bf16[8,16,128]{2,1,0:T(8,128)(2,1)S(1)}, bf16[8,16,128]{2,1,0:T(8,128)(2,1)S(1)}, u32[]{:S(2)}, u32[]{:S(2)}) collective-permute-start(bf16[8,16,128]{2,1,0:T(8,128)(2,1)S(1)} %get-tuple-element.67), channel_id=1, source_target_pairs={{2,0},{3,1},{0,2},{1,3},{6,4},{7,5},{4,6},{5,7},{10,8},{11,9},{8,1... | collective-permute-start | bytes 98312 | tf_op jit(solution)/shard_map/ppermute | solution.py:439
  48.1 16.7 %collective-permute-start.14 = (bf16[8,16,128]{2,1,0:T(8,128)(2,1)S(1)}, bf16[8,16,128]{2,1,0:T(8,128)(2,1)S(1)}, u32[]{:S(2)}, u32[]{:S(2)}) collective-permute-start(bf16[8,16,128]{2,1,0:T(8,128)(2,1)S(1)} %get-tuple-element.67), channel_id=1, source_target_pairs={{14,0},{15,1},{12,2},{13,3},{10,4},{11,5},{8,6},{9,7},{6,8},{7,9},... | collective-permute-start | bytes 98312 | tf_op jit(solution)/shard_map/ppermute | solution.py:439
  50.5 14.3 %collective-permute-start.13 = (bf16[8,16,128]{2,1,0:T(8,128)(2,1)S(1)}, bf16[8,16,128]{2,1,0:T(8,128)(2,1)S(1)}, u32[]{:S(2)}, u32[]{:S(2)}) collective-permute-start(bf16[8,16,128]{2,1,0:T(8,128)(2,1)S(1)} %get-tuple-element.67), channel_id=1, source_target_pairs={{12,0},{13,1},{14,2},{15,3},{8,4},{9,5},{10,6},{11,7},{4,8},{5,9},... | collective-permute-start | bytes 98312 | tf_op jit(solution)/shard_map/ppermute | solution.py:439
  53.2 11.6 %collective-permute-start.12 = (bf16[8,16,128]{2,1,0:T(8,128)(2,1)S(1)}, bf16[8,16,128]{2,1,0:T(8,128)(2,1)S(1)}, u32[]{:S(2)}, u32[]{:S(2)}) collective-permute-start(bf16[8,16,128]{2,1,0:T(8,128)(2,1)S(1)} %get-tuple-element.67), channel_id=1, source_target_pairs={{10,0},{11,1},{8,2},{9,3},{14,4},{15,5},{12,6},{13,7},{2,8},{3,9},... | collective-permute-start | bytes 98312 | tf_op jit(solution)/shard_map/ppermute | solution.py:439
  53.2 11.6 %collective-permute-start.11 = (bf16[8,16,128]{2,1,0:T(8,128)(2,1)S(1)}, bf16[8,16,128]{2,1,0:T(8,128)(2,1)S(1)}, u32[]{:S(2)}, u32[]{:S(2)}) collective-permute-start(bf16[8,16,128]{2,1,0:T(8,128)(2,1)S(1)} %get-tuple-element.67), channel_id=1, source_target_pairs={{8,0},{9,1},{10,2},{11,3},{12,4},{13,5},{14,6},{15,7},{0,8},{1,9},... | collective-permute-start | bytes 98312 | tf_op jit(solution)/shard_map/ppermute | solution.py:439
  55.8 4.1 %collective-permute-start.9 = (bf16[8,16,128]{2,1,0:T(8,128)(2,1)S(1)}, bf16[8,16,128]{2,1,0:T(8,128)(2,1)S(1)}, u32[]{:S(2)}, u32[]{:S(2)}) collective-permute-start(bf16[8,16,128]{2,1,0:T(8,128)(2,1)S(1)} %get-tuple-element.67), channel_id=1, source_target_pairs={{4,0},{5,1},{6,2},{7,3},{0,4},{1,5},{2,6},{3,7},{12,8},{13,9},{14,... | collective-permute-start | bytes 98312 | tf_op jit(solution)/shard_map/ppermute | solution.py:439
  59.9 4.8 %collective-permute-start.10 = (bf16[8,16,128]{2,1,0:T(8,128)(2,1)S(1)}, bf16[8,16,128]{2,1,0:T(8,128)(2,1)S(1)}, u32[]{:S(2)}, u32[]{:S(2)}) collective-permute-start(bf16[8,16,128]{2,1,0:T(8,128)(2,1)S(1)} %get-tuple-element.67), channel_id=1, source_target_pairs={{6,0},{7,1},{4,2},{5,3},{2,4},{3,5},{0,6},{1,7},{14,8},{15,9},{12,... | collective-permute-start | bytes 98312 | tf_op jit(solution)/shard_map/ppermute | solution.py:439
  64.8 5.2 %collective-permute-start.15 = (bf16[64,16,128]{2,1,0:T(8,128)(2,1)S(1)}, bf16[64,16,128]{2,1,0:T(8,128)(2,1)S(1)}, u32[]{:S(2)}, u32[]{:S(2)}) collective-permute-start(bf16[64,16,128]{2,1,0:T(8,128)(2,1)S(1)} %constant_dynamic-update-slice_fusion.dual), channel_id=1, source_target_pairs={{0,1},{1,0},{2,3},{3,2},{4,5},{5,4},{6,7},{7,6},{8,9},{9,8},{10,11... | collective-permute-start | bytes 786440 | tf_op jit(solution)/shard_map/ppermute | solution.py:441
  78.7 6.6 %collective-permute-start.16 = (f32[64,16,128]{2,1,0:T(8,128)S(1)}, f32[64,16,128]{2,1,0:T(8,128)S(1)}, u32[]{:S(2)}, u32[]{:S(2)}) collective-permute-start(f32[64,16,128]{2,1,0:T(8,128)S(1)} %get-tuple-element.45), channel_id=1, source_target_pairs={{0,1},{1,0},{2,3},{3,2},{4,5},{5,4},{6,7},{7,6},{8,9},{9,8},{10,11... | collective-permute-start | bytes 1572872 | tf_op jit(solution)/shard_map/ppermute | solution.py:418
  85.3 7.7 %collective-permute-start.23 = (bf16[8,16,128]{2,1,0:T(8,128)(2,1)S(1)}, bf16[8,16,128]{2,1,0:T(8,128)(2,1)S(1)}, u32[]{:S(2)}, u32[]{:S(2)}) collective-permute-start(bf16[8,16,128]{2,1,0:T(8,128)(2,1)S(1)} %get-tuple-element.69), channel_id=1, source_target_pairs={{0,14},{1,15},{2,12},{3,13},{4,10},{5,11},{6,8},{7,9},{8,6},{9,7},... | collective-permute-start | bytes 98312 | tf_op jit(solution)/shard_map/ppermute | solution.py:422
  87.5 8.6 %collective-permute-start.22 = (bf16[8,16,128]{2,1,0:T(8,128)(2,1)S(1)}, bf16[8,16,128]{2,1,0:T(8,128)(2,1)S(1)}, u32[]{:S(2)}, u32[]{:S(2)}) collective-permute-start(bf16[8,16,128]{2,1,0:T(8,128)(2,1)S(1)} %get-tuple-element.70), channel_id=1, source_target_pairs={{0,12},{1,13},{2,14},{3,15},{4,8},{5,9},{6,10},{7,11},{8,4},{9,5},... | collective-permute-start | bytes 98312 | tf_op jit(solution)/shard_map/ppermute | solution.py:422
  90.2 12.1 %collective-permute-start.21 = (bf16[8,16,128]{2,1,0:T(8,128)(2,1)S(1)}, bf16[8,16,128]{2,1,0:T(8,128)(2,1)S(1)}, u32[]{:S(2)}, u32[]{:S(2)}) collective-permute-start(bf16[8,16,128]{2,1,0:T(8,128)(2,1)S(1)} %get-tuple-element.71), channel_id=1, source_target_pairs={{0,10},{1,11},{2,8},{3,9},{4,14},{5,15},{6,12},{7,13},{8,2},{9,3},... | collective-permute-start | bytes 98312 | tf_op jit(solution)/shard_map/ppermute | solution.py:422
  90.2 12.2 %collective-permute-start.20 = (bf16[8,16,128]{2,1,0:T(8,128)(2,1)S(1)}, bf16[8,16,128]{2,1,0:T(8,128)(2,1)S(1)}, u32[]{:S(2)}, u32[]{:S(2)}) collective-permute-start(bf16[8,16,128]{2,1,0:T(8,128)(2,1)S(1)} %get-tuple-element.72), channel_id=1, source_target_pairs={{0,8},{1,9},{2,10},{3,11},{4,12},{5,13},{6,14},{7,15},{8,0},{9,1},... | collective-permute-start | bytes 98312 | tf_op jit(solution)/shard_map/ppermute | solution.py:422
  93.0 9.4 %collective-permute-start.19 = (bf16[8,16,128]{2,1,0:T(8,128)(2,1)S(1)}, bf16[8,16,128]{2,1,0:T(8,128)(2,1)S(1)}, u32[]{:S(2)}, u32[]{:S(2)}) collective-permute-start(bf16[8,16,128]{2,1,0:T(8,128)(2,1)S(1)} %get-tuple-element.73), channel_id=1, source_target_pairs={{0,6},{1,7},{2,4},{3,5},{4,2},{5,3},{6,0},{7,1},{8,14},{9,15},{10,... | collective-permute-start | bytes 98312 | tf_op jit(solution)/shard_map/ppermute | solution.py:422
  93.1 9.4 %collective-permute-start.18 = (bf16[8,16,128]{2,1,0:T(8,128)(2,1)S(1)}, bf16[8,16,128]{2,1,0:T(8,128)(2,1)S(1)}, u32[]{:S(2)}, u32[]{:S(2)}) collective-permute-start(bf16[8,16,128]{2,1,0:T(8,128)(2,1)S(1)} %get-tuple-element.74), channel_id=1, source_target_pairs={{0,4},{1,5},{2,6},{3,7},{4,0},{5,1},{6,2},{7,3},{8,12},{9,13},{10,... | collective-permute-start | bytes 98312 | tf_op jit(solution)/shard_map/ppermute | solution.py:422
  96.1 6.3 %collective-permute-start.17 = (bf16[8,16,128]{2,1,0:T(8,128)(2,1)S(1)}, bf16[8,16,128]{2,1,0:T(8,128)(2,1)S(1)}, u32[]{:S(2)}, u32[]{:S(2)}) collective-permute-start(bf16[8,16,128]{2,1,0:T(8,128)(2,1)S(1)} %get-tuple-element.75), channel_id=1, source_target_pairs={{0,2},{1,3},{2,0},{3,1},{4,6},{5,7},{6,4},{7,5},{8,10},{9,11},{10,... | collective-permute-start | bytes 98312 | tf_op jit(solution)/shard_map/ppermute | solution.py:422
  102.5 9.3 %collective-permute-start.24 = (bf16[8,16,128]{2,1,0:T(8,128)(2,1)S(1)}, bf16[8,16,128]{2,1,0:T(8,128)(2,1)S(1)}, u32[]{:S(2)}, u32[]{:S(2)}) collective-permute-start(bf16[8,16,128]{2,1,0:T(8,128)(2,1)S(1)} %get-tuple-element.64), channel_id=1, source_target_pairs={{2,0},{3,1},{0,2},{1,3},{6,4},{7,5},{4,6},{5,7},{10,8},{11,9},{8,1... | collective-permute-start | bytes 98312 | tf_op jit(solution)/shard_map/ppermute | solution.py:439
  104.1 16.5 %collective-permute-start.30 = (bf16[8,16,128]{2,1,0:T(8,128)(2,1)S(1)}, bf16[8,16,128]{2,1,0:T(8,128)(2,1)S(1)}, u32[]{:S(2)}, u32[]{:S(2)}) collective-permute-start(bf16[8,16,128]{2,1,0:T(8,128)(2,1)S(1)} %get-tuple-element.64), channel_id=1, source_target_pairs={{14,0},{15,1},{12,2},{13,3},{10,4},{11,5},{8,6},{9,7},{6,8},{7,9},... | collective-permute-start | bytes 98312 | tf_op jit(solution)/shard_map/ppermute | solution.py:439
  105.5 15.0 %collective-permute-start.29 = (bf16[8,16,128]{2,1,0:T(8,128)(2,1)S(1)}, bf16[8,16,128]{2,1,0:T(8,128)(2,1)S(1)}, u32[]{:S(2)}, u32[]{:S(2)}) collective-permute-start(bf16[8,16,128]{2,1,0:T(8,128)(2,1)S(1)} %get-tuple-element.64), channel_id=1, source_target_pairs={{12,0},{13,1},{14,2},{15,3},{8,4},{9,5},{10,6},{11,7},{4,8},{5,9},... | collective-permute-start | bytes 98312 | tf_op jit(solution)/shard_map/ppermute | solution.py:439
  107.9 12.7 %collective-permute-start.28 = (bf16[8,16,128]{2,1,0:T(8,128)(2,1)S(1)}, bf16[8,16,128]{2,1,0:T(8,128)(2,1)S(1)}, u32[]{:S(2)}, u32[]{:S(2)}) collective-permute-start(bf16[8,16,128]{2,1,0:T(8,128)(2,1)S(1)} %get-tuple-element.64), channel_id=1, source_target_pairs={{10,0},{11,1},{8,2},{9,3},{14,4},{15,5},{12,6},{13,7},{2,8},{3,9},... | collective-permute-start | bytes 98312 | tf_op jit(solution)/shard_map/ppermute | solution.py:439
  107.9 12.7 %collective-permute-start.27 = (bf16[8,16,128]{2,1,0:T(8,128)(2,1)S(1)}, bf16[8,16,128]{2,1,0:T(8,128)(2,1)S(1)}, u32[]{:S(2)}, u32[]{:S(2)}) collective-permute-start(bf16[8,16,128]{2,1,0:T(8,128)(2,1)S(1)} %get-tuple-element.64), channel_id=1, source_target_pairs={{8,0},{9,1},{10,2},{11,3},{12,4},{13,5},{14,6},{15,7},{0,8},{1,9},... | collective-permute-start | bytes 98312 | tf_op jit(solution)/shard_map/ppermute | solution.py:439
  115.7 4.8 %collective-permute-start.26 = (bf16[8,16,128]{2,1,0:T(8,128)(2,1)S(1)}, bf16[8,16,128]{2,1,0:T(8,128)(2,1)S(1)}, u32[]{:S(2)}, u32[]{:S(2)}) collective-permute-start(bf16[8,16,128]{2,1,0:T(8,128)(2,1)S(1)} %get-tuple-element.64), channel_id=1, source_target_pairs={{6,0},{7,1},{4,2},{5,3},{2,4},{3,5},{0,6},{1,7},{14,8},{15,9},{12,... | collective-permute-start | bytes 98312 | tf_op jit(solution)/shard_map/ppermute | solution.py:439
  120.6 5.1 %collective-permute-start.31 = (bf16[64,16,128]{2,1,0:T(8,128)(2,1)S(1)}, bf16[64,16,128]{2,1,0:T(8,128)(2,1)S(1)}, u32[]{:S(2)}, u32[]{:S(2)}) collective-permute-start(bf16[64,16,128]{2,1,0:T(8,128)(2,1)S(1)} %constant_dynamic-update-slice_fusion.8.dual), channel_id=1, source_target_pairs={{0,1},{1,0},{2,3},{3,2},{4,5},{5,4},{6,7},{7,6},{8,9},{9,8},{10,11... | collective-permute-start | bytes 786440 | tf_op jit(solution)/shard_map/ppermute | solution.py:441
  (4 other events, 47.0 us)

commit v6 on v5

--- a/solution.py
+++ b/solution.py
@@ -16,39 +16,35 @@
 
 NT = (((1,), (1,)), ((), ()))
 VMEM = pl.BlockSpec(memory_space=pltpu.VMEM)
-SMEM = pl.BlockSpec(memory_space=pltpu.SMEM)
 HBM = pl.BlockSpec(memory_space=pl.ANY)
 SMALL = pltpu.CompilerParams(vmem_limit_bytes=12 << 20)
 STRAIGHT = 16
 
 
-def partner(chip, slot, chips):
-    if chips & (chips - 1) == 0:
-        return chip ^ slot
-    return (chip + slot) % chips
-
-
 class Half:
-    def __init__(self, chip, core, blocks, tiles_hbm, tiles, sems):
-        self.chip, self.core = chip, core
+    def __init__(self, sibling, blocks_hbm, tiles_hbm, tiles, sems, blocks, block_sem):
+        me = lax.axis_index("tm")
+        self.core = 1 - me % 2 if sibling else me % 2
         self.blocks, self.tiles_hbm, self.tiles, self.sems = blocks, tiles_hbm, tiles, sems
         self.chunks = sems.shape[0]
         self.own = tiles.shape[0] // self.chunks
+        for chunk in range(self.chunks):
+            self.fetch(chunk).start()
+        self.block_copy = pltpu.make_async_copy(blocks_hbm, blocks, block_sem)
+        self.block_copy.start()
 
     def first_group(self, chunk):
-        return (2 * partner(self.chip, chunk, self.chunks) + self.core) * self.own
+        return (2 * chunk + self.core) * self.own
 
     def fetch(self, chunk):
         there = pl.ds(self.first_group(chunk), self.own)
         here = pl.ds(chunk * self.own, self.own)
         return pltpu.make_async_copy(self.tiles_hbm.at[there], self.tiles.at[here], self.sems.at[chunk])
 
-    def start(self):
-        for chunk in range(self.chunks):
-            self.fetch(chunk).start()
-
     def each_four(self, wait, four):
         depth = self.tiles.shape[1]
+        if wait:
+            self.block_copy.wait()
         per = max(1, STRAIGHT // self.own)
 
         def body(step, carry):
@@ -200,9 +196,9 @@
         out[d] = jnp.concatenate(parts, axis=0).astype(out.dtype)
 
 
-def first_flow_kernel(place, blocks, came, tiles_hbm, flows, picked, level, tiles, sems, flat):
-    half = Half(place[0], 1 - place[1], blocks, tiles_hbm, tiles, sems)
-    half.start()
+def first_flow_kernel(blocks_hbm, tiles_hbm, came, flows, picked, level, *scratch):
+    stream, (flat,) = (blocks_hbm, tiles_hbm, *scratch[:4]), scratch[4:]
+    half = Half(True, *stream)
     count, hours, width = picked.shape
     flat[...] = came[...].astype(jnp.float32)
     rows = flat.shape[0] // hours
@@ -213,26 +209,25 @@
     flow_pass(picked, half, flows, True)
 
 
-def own_flow_kernel(place, blocks, picked, tiles_hbm, flows, tiles, sems):
-    half = Half(place[0], place[1], blocks, tiles_hbm, tiles, sems)
-    half.start()
+def own_flow_kernel(blocks_hbm, tiles_hbm, picked, flows, *scratch):
+    stream = (blocks_hbm, tiles_hbm, *scratch)
+    half = Half(False, *stream)
     flow_pass(picked, half, flows, True)
 
 
-def own_price_kernel(place, blocks, dual, tiles_hbm, price, tiles, sems, *sums):
-    half = Half(place[0], place[1], blocks, tiles_hbm, tiles, sems)
-    half.start()
+def own_price_kernel(blocks_hbm, tiles_hbm, dual, price, *scratch):
+    stream, sums = (blocks_hbm, tiles_hbm, *scratch[:4]), scratch[4:]
+    half = Half(False, *stream)
     price_pass(dual, half, sums, True)
     for b in range(price.shape[0]):
         price[b] = total(sums, b)
 
 
 def middle_kernel(
-    place, blocks, dual, before, base, delta, tiles_hbm,
-    price, inject_out, picked, flows, tiles, sems, *sums
+    blocks_hbm, tiles_hbm, dual, before, base, delta, price, inject_out, picked, flows, *scratch
 ):
-    half = Half(place[0], 1 - place[1], blocks, tiles_hbm, tiles, sems)
-    half.start()
+    stream, sums = (blocks_hbm, tiles_hbm, *scratch[:4]), scratch[4:]
+    half = Half(True, *stream)
     price_pass(dual, half, sums, True)
 
     def start(b):
@@ -247,11 +242,11 @@
 
 
 def last_kernel(
-    place, blocks, dual, before, base, inject, delta, level, line_dual, unit_block, unit_lane, gain, tiles_hbm,
-    out, tiles, sems, price, level_out, flat, *sums
+    blocks_hbm, tiles_hbm, dual, before, base, inject, delta, level, line_dual, unit_block, unit_lane, gain,
+    out, *scratch
 ):
-    half = Half(place[0], 1 - place[1], blocks, tiles_hbm, tiles, sems)
-    half.start()
+    stream, (price, level_out, flat, *sums) = (blocks_hbm, tiles_hbm, *scratch[:4]), scratch[4:]
+    half = Half(True, *stream)
     count, hours, width = price.shape
     rows = flat.shape[0] // hours
     flat[...] = jnp.zeros_like(flat)
@@ -343,18 +338,17 @@
 
     chips = devices // 2
     half_groups = chips * own_groups
-    place = jnp.stack([me // 2, me % 2])
     sibling = [(d, d + 1 - 2 * (d % 2)) for d in range(devices)]
 
-    def to_partner(slot):
-        return [(d, 2 * partner(d // 2, slot, chips) + d % 2) for d in range(devices)]
-
-    def from_partner(slot):
-        return [(target, source) for source, target in to_partner(slot)]
+    same_core = [[2 * chip + c for chip in range(chips)] for c in range(2)]
+
+    def exchange(value):
+        return lax.all_to_all(value, "tm", split_axis=0, concat_axis=0, axis_index_groups=same_core, tiled=True)
 
     half_bytes = ptdf_tiles.size
     half_flops = hours * ptdf_tiles.size
     stream = [pltpu.VMEM((half_groups, *ptdf_tiles.shape[1:]), ptdf_tiles.dtype), pltpu.SemaphoreType.DMA((chips,))]
+    stream += [pltpu.SMEM(blocks.shape, blocks.dtype), pltpu.SemaphoreType.DMA]
     sums = [pltpu.VMEM((bus_blocks, hours, width), jnp.float32)] * depth
     large = pltpu.CompilerParams(vmem_limit_bytes=48 << 20)
     picked_shape = jax.ShapeDtypeStruct((bus_blocks, hours, width), jnp.bfloat16)
@@ -366,7 +360,7 @@
         return pl.pallas_call(
             kernel,
             out_shape=outs,
-            in_specs=[SMEM] * 2 + [VMEM] * len(operands) + [HBM],
+            in_specs=[HBM] * 2 + [VMEM] * len(operands),
             out_specs=[VMEM] * len(outs),
             scratch_shapes=stream + scratch,
             compiler_params=large,
@@ -374,7 +368,7 @@
                 flops=passes * half_flops, bytes_accessed=passes * half_bytes, transcendentals=0
             ),
             name=name,
-        )(place, blocks, *operands, ptdf_tiles)
+        )(blocks, ptdf_tiles, *operands)
 
     def small(kernel, name, outs, operands):
         return pl.pallas_call(
@@ -415,13 +409,10 @@
     price = None
     line_dual = jnp.zeros((own_groups, hours, lines), jnp.float32)
     for iteration in range(ITERS):
-        arrived = lax.ppermute(away, "tm", sibling).reshape(chips, own_groups, hours, lines)
+        arrived = lax.ppermute(away, "tm", sibling)
         (flows,) = product(own_flow_kernel, "own_flow", [flow_shape], [picked], [])
-        flows = flows.reshape(chips, own_groups, hours, lines)
-        parts = [
-            lax.ppermute((flows[slot] + arrived[slot]).astype(jnp.bfloat16), "tm", to_partner(slot))
-            for slot in range(1, chips)
-        ]
+        pair = (flows + arrived).astype(jnp.bfloat16).reshape(chips, own_groups, hours, lines)
+        parts = exchange(pair)
         if iteration == 0:
             (delta,) = small(storage_kernel, "storage", [block_shape], [level, unit_block, unit_lane])
         else:
@@ -429,15 +420,11 @@
                 level_kernel, "storage", [level_shape, block_shape], [price, level, unit_block, unit_lane, gain]
             )
         parts, level, delta = lax.optimization_barrier((parts, level, delta))
-        shifted = flows[0] + arrived[0] + line_dual
-        for part in parts:
-            shifted = shifted + part.astype(jnp.float32)
+        shifted = jnp.sum(parts.astype(jnp.float32), axis=0) + line_dual
         clipped = jnp.clip(shifted, -own_limits, own_limits)
         line_dual = shifted - clipped
-        dual = line_dual.astype(jnp.bfloat16)
-        dual = jnp.concatenate(
-            [dual] + [lax.ppermute(dual, "tm", from_partner(slot)) for slot in range(1, chips)], axis=0
-        )
+        dual = exchange(jnp.broadcast_to(line_dual.astype(jnp.bfloat16)[None], (chips, own_groups, hours, lines)))
+        dual = dual.reshape(half_groups, hours, lines)
         other = lax.ppermute(dual, "tm", sibling)
         (before,) = product(own_price_kernel, "own_price", [block_shape], [dual], sums)
         if iteration < ITERS - 1:

time: 146 us -> 126 us (0.86)
  starting transfers between devices: 49.5 us -> 15 us
  blocking collectives: 11.7 us -> 37.1 us
  waiting for transfers between devices: 24 us -> 16.4 us
  Pallas kernels: 55.1 us -> 51.2 us
    ppermute x30 -> x2, starting transfers between devices: 41.9 us -> 0.65 us  [shards(): arrived = lax.ppermute(away, 'tm', sibling)]
    all_to_all x0 -> x2, blocking collectives: none -> 24.5 us  [exchange(): lax.all_to_all(value, 'tm', split_axis=0, concat_axis=0, axis_index_group...]
    ppermute x30 -> x2, waiting for transfers between devices: 16.1 us -> 0.01 us  [shards(): arrived = lax.ppermute(away, 'tm', sibling)]
    all_to_all x0 -> x2, waiting for transfers between devices: none -> 8.38 us  [exchange(): lax.all_to_all(value, 'tm', split_axis=0, concat_axis=0, axis_index_group...]
    all_to_all x0 -> x2, starting transfers between devices: none -> 6.99 us  [exchange(): lax.all_to_all(value, 'tm', split_axis=0, concat_axis=0, axis_index_group...]
    pallas_call x7, Pallas kernels: 43.9 us -> 39.9 us  [product(): pl.pallas_call(kernel, out_shape=outs, in_specs=[HBM] * 2 + [VMEM] * len(...]
    convert_element_type x2 -> x4, other arithmetic: 0.13 us -> 1.62 us  [the longest x2 1.58 us: shards(): (flows + arrived).astype(jnp.bfloat16)]
  transfers between devices with their start and end apart: 33 -> 7, of which waited for: 5 -> 3; matrix products, arithmetic and copies ran while one was open for 1% -> 1% of each run, Pallas kernels for 22% -> 24%
where the time goes in v6:
time: 126 us
  Pallas kernels  51.2 us (41%)
  blocking collectives  37.1 us (29%)
  waiting for transfers between devices  16.4 us (13%)
  starting transfers between devices  15 us (12%)
  other arithmetic  3.46 us (3%)
  local copies, waits for them, and re-layouts  1.77 us (1%)
    pallas_call x7, Pallas kernels, product(): pl.pallas_call(kernel, out_shape=outs, in_specs=[HBM] * 2 + [VMEM] * len(...  39.9 us
    all_to_all x2, blocking collectives, exchange(): lax.all_to_all(value, 'tm', split_axis=0, concat_axis=0, axis_index_group...  24.5 us
    all_to_all x1, blocking collectives, shards(): lax.all_to_all(out.reshape(devices, hour_rows * rows_out, width), 'tm', s...  12.6 us
    pallas_call x4, Pallas kernels, small(): pl.pallas_call(kernel, out_shape=outs, in_specs=[VMEM] * len(operands), o...  11.2 us
    all_to_all x2, waiting for transfers between devices, exchange(): lax.all_to_all(value, 'tm', split_axis=0, concat_axis=0, axis_index_group...  8.38 us
    all_to_all x1, waiting for transfers between devices, shards(): came = lax.all_to_all(sent, 'tm', split_axis=0, concat_axis=0, tiled=True)  7.99 us
    all_to_all x1, starting transfers between devices, shards(): came = lax.all_to_all(sent, 'tm', split_axis=0, concat_axis=0, tiled=True)  7.39 us
    all_to_all x2, starting transfers between devices, exchange(): lax.all_to_all(value, 'tm', split_axis=0, concat_axis=0, axis_index_group...  6.99 us
  transfers between devices with their start and end apart: 7, of which 3 were waited for; matrix products, arithmetic and copies ran while one was open for 1% of the time, Pallas kernels for 24%

profile of v6, /device:TPU:0, one launch (start us, length us, event | category | flops | bytes accessed | tf_op | source)
XLA Modules:
  0.0 125.7 jit_solution(5126326653248650701)
XLA Ops:
  0.6 1.1 reshape.88
  1.7 0.0 copy-start.1
  1.7 0.7 copy-done.1
  2.4 0.7 pack.1
  3.1 7.4 %all-to-all-start = ((bf16[16,48,128]{2,1,0:T(8,128)(2,1)}), bf16[16,48,128]{2,1,0:T(8,128)(2,1)S(1)}, u32[]{:S(2)}, u32[]{:S(2)}) async-start(bf16[16,48,128]{2,1,0:T(8,128)(2,1)} %pack.1), calls=%async_computation | async-start | bytes 393216 | tf_op jit(solution)/shard_map/all_to_all | solution.py:400
  10.5 0.8 copy.10
  11.3 0.2 reshape.71.blocks_hbm
  11.5 8.0 %all-to-all-done = bf16[16,48,128]{2,1,0:T(8,128)(2,1)S(1)} async-done(((bf16[16,48,128]{2,1,0:T(8,128)(2,1)}), bf16[16,48,128]{2,1,0:T(8,128)(2,1)S(1)}, u32[]{:S(2)}, u32[]{:S(2)}) %all-to-all-start) | async-done | bytes 196640 | tf_op jit(solution)/shard_map/all_to_all | solution.py:400
  19.5 5.5 %first_flow.1 = (f32[64,16,128]{2,1,0:T(8,128)S(1)}, bf16[18,16,128]{2,1,0:T(8,128)(2,1)S(1)}, f32[16,2048]{1,0:T(8,128)S(1)}) custom-call(s32[640]{0:T(1024)S(1)} %reshape.71.blocks_hbm, bf16[128,5,128,128]{3,2,1,0:T(8,128)(2,1)} %tiles_hbm.13, bf16[768,128]{1,0:T(8,128)(2,1)S(1)} %bitcast.23), custom_call_target="tpu_custom_call" | custom-call | flops 167772160 | bytes 10485760 | tf_op jit(solution)/shard_map/first_flow/pallas_call | solution.py:360
  24.9 0.1 collective-permute-start
  25.0 5.5 %own_flow.2 = f32[64,16,128]{2,1,0:T(8,128)S(1)} custom-call(s32[640]{0:T(1024)S(1)} %reshape.71.blocks_hbm, bf16[128,5,128,128]{3,2,1,0:T(8,128)(2,1)} %tiles_hbm.13, bf16[18,16,128]{2,1,0:T(8,128)(2,1)S(1)} %get-tuple-element.21.picked.base), custom_call_target="tpu_custom_call" | custom-call | flops 167772160 | bytes 10485760 | tf_op jit(solution)/shard_map/own_flow/pallas_call | solution.py:360
  30.5 0.8 add_convert_fusion.1
  31.3 3.4 %all-to-all-start.1 = ((bf16[8,8,16,128]{3,2,1,0:T(8,128)(2,1)}), bf16[8,8,16,128]{3,2,1,0:T(8,128)(2,1)S(1)}, u32[]{:S(2)}, u32[]{:S(2)}) async-start(bf16[8,8,16,128]{3,2,1,0:T(8,128)(2,1)} %bitcast.3), calls=%async_computation.1 | async-start | bytes 524288 | tf_op jit(solution)/shard_map/all_to_all | solution.py:346
  34.7 0.7 dynamic-slice_bitcast_fusion
  35.4 4.0 %storage.2.delta = f32[18,16,128]{2,1,0:T(8,128)S(1)} custom-call(f32[16,2048]{1,0:T(8,128)S(1)} %get-tuple-element.29.level, s32[1,2048]{1,0:T(1,128)S(1)} %bitcast.29, s32[1,2048]{1,0:T(1,128)S(1)} %bitcast.26), custom_call_target="tpu_custom_call" | custom-call | flops 167772160 | bytes 4194304 | tf_op jit(solution)/shard_map/storage/pallas_call | solution.py:374
  39.4 5.0 %all-to-all-done.1 = bf16[8,8,16,128]{3,2,1,0:T(8,128)(2,1)S(1)} async-done(((bf16[8,8,16,128]{3,2,1,0:T(8,128)(2,1)}), bf16[8,8,16,128]{3,2,1,0:T(8,128)(2,1)S(1)}, u32[]{:S(2)}, u32[]{:S(2)}) %all-to-all-start.1) | async-done | bytes 262176 | tf_op jit(solution)/shard_map/all_to_all | solution.py:346
  44.6 12.5 %all_to_all.30 = bf16[8,8,16,128]{3,2,1,0:T(8,128)(2,1)S(1)} all-to-all(bf16[8,8,16,128]{3,2,1,0:T(8,128)(2,1)S(1)} %broadcast_in_dim.4), channel_id=1, replica_groups={{0,2,4,6,8,10,12,14},{1,3,5,7,9,11,13,15},{16,18,20,22,24,26,28,30},{17..., dimensions={0} | all-to-all | bytes 524288 | tf_op jit(solution)/shard_map/all_to_all | solution.py:346
  57.1 4.5 %own_price.2.before = f32[18,16,128]{2,1,0:T(8,128)S(1)} custom-call(s32[640]{0:T(1024)S(1)} %reshape.71.blocks_hbm, bf16[128,5,128,128]{3,2,1,0:T(8,128)(2,1)} %tiles_hbm.13, bf16[64,16,128]{2,1,0:T(8,128)(2,1)S(1)} %bitcast.20), custom_call_target="tpu_custom_call" | custom-call | flops 167772160 | bytes 10485760 | tf_op jit(solution)/shard_map/own_price/pallas_call | solution.py:360
  61.6 0.0 copy-start
  61.6 0.0 collective-permute-done.1.dual
  61.6 8.1 %price_then_flow.1 = (f32[18,16,128]{2,1,0:T(8,128)S(1)}, f32[18,16,128]{2,1,0:T(8,128)S(1)}, bf16[18,16,128]{2,1,0:T(8,128)(2,1)S(1)}, f32[64,16,128]{2,1,0:T(8,128)S(1)}) custom-call(s32[640]{0:T(1024)S(1)} %reshape.71.blocks_hbm, bf16[128,5,128,128]{3,2,1,0:T(8,128)(2,1)} %tiles_hbm.13, bf16[64,16,128]{2,1,0:T(8,128)(2,1)S(1)} %collective-permute-done.1.dual, ...), custom_call_target="tpu_custom_call" | custom-call | flops 335544320 | bytes 20971520 | tf_op jit(solution)/shard_map/price_then_flow/pallas_call | solution.py:360
  69.7 0.6 collective-permute-start.2
  70.3 5.4 %own_flow.3 = f32[64,16,128]{2,1,0:T(8,128)S(1)} custom-call(s32[640]{0:T(1024)S(1)} %reshape.71.blocks_hbm, bf16[128,5,128,128]{3,2,1,0:T(8,128)(2,1)} %tiles_hbm.13, bf16[18,16,128]{2,1,0:T(8,128)(2,1)S(1)} %get-tuple-element.26.picked), custom_call_target="tpu_custom_call" | custom-call | flops 167772160 | bytes 10485760 | tf_op jit(solution)/shard_map/own_flow/pallas_call | solution.py:360
  75.8 0.8 add_convert_fusion
  76.6 3.6 %all-to-all-start.3 = ((bf16[8,8,16,128]{3,2,1,0:T(8,128)(2,1)}), bf16[8,8,16,128]{3,2,1,0:T(8,128)(2,1)S(1)}, u32[]{:S(2)}, u32[]{:S(2)}) async-start(bf16[8,8,16,128]{3,2,1,0:T(8,128)(2,1)} %bitcast.10), calls=%async_computation.3 | async-start | bytes 524288 | tf_op jit(solution)/shard_map/all_to_all | solution.py:346
  80.1 5.8 %storage.3 = (f32[16,2048]{1,0:T(8,128)S(1)}, f32[18,16,128]{2,1,0:T(8,128)S(1)}) custom-call(f32[18,16,128]{2,1,0:T(8,128)S(1)} %get-tuple-element.28.price, f32[16,2048]{1,0:T(8,128)S(1)} %get-tuple-element.29.level, s32[1,2048]{1,0:T(1,128)S(1)} %bitcast.30, s32[1,2048]{1,0:T(1,128)S(1)} %bitcast.27, f32[1,2048]{1,0:T(1,128)S(1)} %bitcast.32), custom_call_target="tpu_custom_call" | custom-call | flops 167772160 | bytes 4194304 | tf_op jit(solution)/shard_map/storage/pallas_call | solution.py:374
  86.0 3.3 %all-to-all-done.3 = bf16[8,8,16,128]{3,2,1,0:T(8,128)(2,1)S(1)} async-done(((bf16[8,8,16,128]{3,2,1,0:T(8,128)(2,1)}), bf16[8,8,16,128]{3,2,1,0:T(8,128)(2,1)S(1)}, u32[]{:S(2)}, u32[]{:S(2)}) %all-to-all-start.3) | async-done | bytes 262176 | tf_op jit(solution)/shard_map/all_to_all | solution.py:346
  89.4 12.0 %all_to_all.31 = bf16[8,8,16,128]{3,2,1,0:T(8,128)(2,1)S(1)} all-to-all(bf16[8,8,16,128]{3,2,1,0:T(8,128)(2,1)S(1)} %broadcast_in_dim.5), channel_id=1, replica_groups={{0,2,4,6,8,10,12,14},{1,3,5,7,9,11,13,15},{16,18,20,22,24,26,28,30},{17..., dimensions={0} | all-to-all | bytes 524288 | tf_op jit(solution)/shard_map/all_to_all | solution.py:346
  101.4 4.5 %own_price.3.before = f32[18,16,128]{2,1,0:T(8,128)S(1)} custom-call(s32[640]{0:T(1024)S(1)} %reshape.71.blocks_hbm, bf16[128,5,128,128]{3,2,1,0:T(8,128)(2,1)} %tiles_hbm.13, bf16[64,16,128]{2,1,0:T(8,128)(2,1)S(1)} %bitcast.22), custom_call_target="tpu_custom_call" | custom-call | flops 167772160 | bytes 10485760 | tf_op jit(solution)/shard_map/own_price/pallas_call | solution.py:360
  105.9 6.5 %last_price.1 = bf16[768,128]{1,0:T(8,128)(2,1)S(1)} custom-call(s32[640]{0:T(1024)S(1)} %reshape.71.blocks_hbm, bf16[128,5,128,128]{3,2,1,0:T(8,128)(2,1)} %tiles_hbm.13, bf16[64,16,128]{2,1,0:T(8,128)(2,1)S(1)} %collective-permute-done.3.dual, f32[18,16,128]{2,1,0:T(8,128)S(1)} %own_price.3.before, bf16[18,16,128]{2,1,0:T(8,128)(2,1)S(1)} %get-tuple-element.21.picked.base, ...), custom_call_target="tpu_custom_call" | custom-call | flops 167772160 | bytes 10485760 | tf_op jit(solution)/shard_map/last_price/pallas_call | solution.py:360
  112.4 12.6 %all_to_all.32.back = bf16[16,48,128]{2,1,0:T(8,128)(2,1)S(1)} all-to-all(bf16[16,48,128]{2,1,0:T(8,128)(2,1)S(1)} %bitcast.24), channel_id=1, replica_groups=mesh['scen'=2,'tm'=16] {'tm'}, dimensions={0} | all-to-all | bytes 393216 | tf_op jit(solution)/shard_map/all_to_all | solution.py:453
  125.0 0.7 unpack.1
  (15 shorter events, 0.2 us)
Async XLA Ops:
  1.7 0.7 copy-start.1
  3.1 16.4 %all-to-all-start = ((bf16[16,48,128]{2,1,0:T(8,128)(2,1)}), bf16[16,48,128]{2,1,0:T(8,128)(2,1)S(1)}, u32[]{:S(2)}, u32[]{:S(2)}) async-start(bf16[16,48,128]{2,1,0:T(8,128)(2,1)} %pack.1), calls=%async_computation | async-start | bytes 393216 | tf_op jit(solution)/shard_map/all_to_all | solution.py:400
  19.5 15.9 %copy-start.2 = (s32[2048]{0:T(1024)S(1)}, s32[2048]{0:T(1024)}, u32[]{:S(2)}) copy-start(s32[2048]{0:T(1024)} %param.11) | copy-start | bytes 24580
  24.9 5.5 %collective-permute-start = (f32[64,16,128]{2,1,0:T(8,128)S(1)}, f32[64,16,128]{2,1,0:T(8,128)S(1)}, u32[]{:S(2)}, u32[]{:S(2)}) collective-permute-start(f32[64,16,128]{2,1,0:T(8,128)S(1)} %get-tuple-element.22), channel_id=1, source_target_pairs={{0,1},{1,0},{2,3},{3,2},{4,5},{5,4},{6,7},{7,6},{8,9},{9,8},{10,11... | collective-permute-start | bytes 1572872 | tf_op jit(solution)/shard_map/ppermute | solution.py:412
  31.3 13.2 %all-to-all-start.1 = ((bf16[8,8,16,128]{3,2,1,0:T(8,128)(2,1)}), bf16[8,8,16,128]{3,2,1,0:T(8,128)(2,1)S(1)}, u32[]{:S(2)}, u32[]{:S(2)}) async-start(bf16[8,8,16,128]{3,2,1,0:T(8,128)(2,1)} %bitcast.3), calls=%async_computation.1 | async-start | bytes 524288 | tf_op jit(solution)/shard_map/all_to_all | solution.py:346
  57.1 4.5 %collective-permute-start.1 = (bf16[64,16,128]{2,1,0:T(8,128)(2,1)S(1)}, bf16[64,16,128]{2,1,0:T(8,128)(2,1)S(1)}, u32[]{:S(2)}, u32[]{:S(2)}) collective-permute-start(bf16[64,16,128]{2,1,0:T(8,128)(2,1)S(1)} %bitcast.19), channel_id=1, source_target_pairs={{0,1},{1,0},{2,3},{3,2},{4,5},{5,4},{6,7},{7,6},{8,9},{9,8},{10,11... | collective-permute-start | bytes 786440 | tf_op jit(solution)/shard_map/ppermute | solution.py:428
  61.6 18.6 %copy-start = (f32[2048]{0:T(1024)S(1)}, f32[2048]{0:T(1024)}, u32[]{:S(2)}) copy-start(f32[2048]{0:T(1024)} %param.12) | copy-start | bytes 24580
  69.7 6.0 %collective-permute-start.2 = (f32[64,16,128]{2,1,0:T(8,128)S(1)}, f32[64,16,128]{2,1,0:T(8,128)S(1)}, u32[]{:S(2)}, u32[]{:S(2)}) collective-permute-start(f32[64,16,128]{2,1,0:T(8,128)S(1)} %get-tuple-element.27), channel_id=1, source_target_pairs={{0,1},{1,0},{2,3},{3,2},{4,5},{5,4},{6,7},{7,6},{8,9},{9,8},{10,11... | collective-permute-start | bytes 1572872 | tf_op jit(solution)/shard_map/ppermute | solution.py:412
  76.6 12.7 %all-to-all-start.3 = ((bf16[8,8,16,128]{3,2,1,0:T(8,128)(2,1)}), bf16[8,8,16,128]{3,2,1,0:T(8,128)(2,1)S(1)}, u32[]{:S(2)}, u32[]{:S(2)}) async-start(bf16[8,8,16,128]{3,2,1,0:T(8,128)(2,1)} %bitcast.10), calls=%async_computation.3 | async-start | bytes 524288 | tf_op jit(solution)/shard_map/all_to_all | solution.py:346
  101.4 4.5 %collective-permute-start.3 = (bf16[64,16,128]{2,1,0:T(8,128)(2,1)S(1)}, bf16[64,16,128]{2,1,0:T(8,128)(2,1)S(1)}, u32[]{:S(2)}, u32[]{:S(2)}) collective-permute-start(bf16[64,16,128]{2,1,0:T(8,128)(2,1)S(1)} %bitcast.21), channel_id=1, source_target_pairs={{0,1},{1,0},{2,3},{3,2},{4,5},{5,4},{6,7},{7,6},{8,9},{9,8},{10,11... | collective-permute-start | bytes 786440 | tf_op jit(solution)/shard_map/ppermute | solution.py:428

commit v7 on v6

--- a/solution.py
+++ b/solution.py
@@ -18,7 +18,7 @@
 VMEM = pl.BlockSpec(memory_space=pltpu.VMEM)
 HBM = pl.BlockSpec(memory_space=pl.ANY)
 SMALL = pltpu.CompilerParams(vmem_limit_bytes=12 << 20)
-STRAIGHT = 16
+STRAIGHT = 32
 
 
 class Half:
@@ -163,16 +163,30 @@
         out(block, new - delta[block])
 
 
+def one_hot(unit_lane, cols, width):
+    lane = jnp.broadcast_to(unit_lane[:, cols], (width, cols.size))
+    return (lane == lax.broadcasted_iota(jnp.int32, (width, cols.size), 0)).astype(jnp.bfloat16)
+
+
+def high_low(values, axis):
+    high = values.astype(jnp.bfloat16)
+    low = (values - high.astype(jnp.float32)).astype(jnp.bfloat16)
+    return jnp.concatenate([high, low], axis=axis)
+
+
 def level_pass(price, level, unit_block, unit_lane, gain, out, mine):
     count, hours, width = price.shape
+    span = 2 * width
+    prices = high_low(jnp.concatenate([price[b] for b in range(count)], axis=0), 1)
 
     def body(c, carry):
-        cols = pl.ds(pl.multiple_of(c * width, width), width)
-        block = jnp.broadcast_to(unit_block[:, cols], (hours, width))
-        lane = jnp.broadcast_to(unit_lane[:, cols], (hours, width))
-        found = jnp.zeros((hours, width), jnp.float32)
+        cols = pl.ds(pl.multiple_of(c * span, span), span)
+        hot = one_hot(unit_lane, cols, width)
+        picked = jnp.dot(prices, jnp.concatenate([hot, hot], axis=0), preferred_element_type=jnp.float32)
+        block = jnp.broadcast_to(unit_block[:, cols], (hours, span))
+        found = jnp.zeros((hours, span), jnp.float32)
         for b in range(count):
-            found = jnp.where(block == b, jnp.take_along_axis(price[b], lane, axis=1), found)
+            found = jnp.where(block == b, picked[b * hours : (b + 1) * hours], found)
         now = level[:, cols]
         new = 0.5 * (now + earlier(now)) - gain[:, cols] * found
         if mine:
@@ -180,20 +194,31 @@
         out[:, cols] = new
         return carry
 
-    lax.fori_loop(0, level.shape[1] // width, body, 0)
-
-
-def pack_kernel(base, soc, out):
+    lax.fori_loop(0, level.shape[1] // span, body, 0)
+
+
+def pack_kernel(base, soc_hbm, out, flat, soc, sem):
     devices, rows, width = out.shape
     hour_rows = soc.shape[0]
-    count = base.shape[1] // devices
-    units = soc.shape[1]
-    pad = jnp.zeros((rows // hour_rows - count - units, width), jnp.float32)
-    for d in range(devices):
-        parts = []
-        for r in range(hour_rows):
-            parts += [base[r, d * count : (d + 1) * count], soc[r], pad]
-        out[d] = jnp.concatenate(parts, axis=0).astype(out.dtype)
+    rows = rows // hour_rows
+    count = base.shape[1] // (devices * width)
+    units = soc.shape[1] // width
+    copy = pltpu.make_async_copy(soc_hbm, soc, sem)
+    copy.start()
+    flat[...] = jnp.zeros_like(flat)
+    for r in range(hour_rows):
+        for d in range(devices):
+            at = (d * hour_rows + r) * rows
+            for b in range(count):
+                first = (d * count + b) * width
+                flat[at + b : at + b + 1, :] = base[r : r + 1, first : first + width].astype(jnp.float32)
+    copy.wait()
+    for r in range(hour_rows):
+        levels = jnp.concatenate([soc[r : r + 1, c * width : (c + 1) * width] for c in range(units)], axis=0)
+        for d in range(devices):
+            at = (d * hour_rows + r) * rows
+            flat[at + count : at + count + units, :] = levels
+    out[...] = flat[...].reshape(out.shape).astype(out.dtype)
 
 
 def first_flow_kernel(blocks_hbm, tiles_hbm, came, flows, picked, level, *scratch):
@@ -286,27 +311,23 @@
 
 def storage_pass(level, unit_block, unit_lane, delta):
     count, hours, width = delta.shape
-    units = level.shape[1]
     span = 2 * width
     delta[...] = jnp.zeros_like(delta)
 
     def body(c, carry):
         cols = pl.ds(pl.multiple_of(c * span, span), span)
         now = level[:, cols]
-        charge = step_size * (now - earlier(now))
-        high = charge.astype(jnp.bfloat16).astype(jnp.float32)
-        low = charge - high
-        lane = jnp.broadcast_to(unit_lane[:, cols], (width, span))
-        hot = (lane == lax.broadcasted_iota(jnp.int32, (width, span), 0)).astype(jnp.bfloat16)
-        block = jnp.broadcast_to(unit_block[:, cols], (hours, span))
+        charge = high_low(step_size * (now - earlier(now)), 0).astype(jnp.float32)
+        hot = one_hot(unit_lane, cols, width)
+        block = jnp.broadcast_to(unit_block[:, cols], charge.shape)
+        held = jnp.concatenate([jnp.where(block == b, charge, 0.0) for b in range(count)], axis=0)
+        part = lax.dot_general(held.astype(jnp.bfloat16), hot, NT, preferred_element_type=jnp.float32)
         for b in range(count):
-            held = block == b
-            both = jnp.concatenate([jnp.where(held, high, 0.0), jnp.where(held, low, 0.0)], axis=0)
-            part = lax.dot_general(both.astype(jnp.bfloat16), hot, NT, preferred_element_type=jnp.float32)
-            delta[b] = delta[b] + (part[:hours] + part[hours:])
+            high, low = part[2 * b * hours : (2 * b + 1) * hours], part[(2 * b + 1) * hours : (2 * b + 2) * hours]
+            delta[b] = delta[b] + (high + low)
         return carry
 
-    lax.fori_loop(0, units // span, body, 0)
+    lax.fori_loop(0, level.shape[1] // span, body, 0)
 
 
 def storage_kernel(level, unit_block, unit_lane, delta):
@@ -370,12 +391,13 @@
             name=name,
         )(blocks, ptdf_tiles, *operands)
 
-    def small(kernel, name, outs, operands):
+    def small(kernel, name, outs, operands, scratch=(), last=VMEM):
         return pl.pallas_call(
             kernel,
             out_shape=outs,
-            in_specs=[VMEM] * len(operands),
+            in_specs=[VMEM] * (len(operands) - 1) + [last],
             out_specs=[VMEM] * len(outs),
+            scratch_shapes=scratch,
             compiler_params=SMALL,
             cost_estimate=pl.CostEstimate(flops=half_flops, bytes_accessed=4 << 20, transcendentals=0),
             name=name,
@@ -392,10 +414,13 @@
         pack_kernel,
         "pack",
         [jax.ShapeDtypeStruct((devices, hour_rows * rows_in, width), jnp.bfloat16)],
+        [base_injection, soc_init],
         [
-            base_injection.astype(jnp.float32).reshape(hour_rows, bus_count // width, width),
-            soc_init.reshape(hour_rows, unit_rows, width),
+            pltpu.VMEM((devices * hour_rows * rows_in, width), jnp.float32),
+            pltpu.VMEM(soc_init.shape, soc_init.dtype),
+            pltpu.SemaphoreType.DMA,
         ],
+        HBM,
     )
     came = lax.all_to_all(sent, "tm", split_axis=0, concat_axis=0, tiled=True)
     away, base, level = product(

time: 126 us -> 126 us (level)
  Pallas kernels: 51.2 us -> 46.5 us
  waiting for transfers between devices: 16.4 us -> 20.8 us
    all_to_all x2, waiting for transfers between devices: 8.38 us -> 12.8 us  [exchange(): lax.all_to_all(value, 'tm', split_axis=0, concat_axis=0, axis_index_group...]
    pallas_call x4, Pallas kernels: 11.2 us -> 6.98 us  [small(): pl.pallas_call(kernel, out_shape=outs, in_specs=[VMEM] * (len(operands) -...]
  transfers between devices with their start and end apart: 7 -> 7, of which waited for: 3 -> 3; matrix products, arithmetic and copies ran while one was open for 1% -> 1% of each run, Pallas kernels for 24% -> 20%
where the time goes in v7:
time: 126 us; the launch traced here: 125 us
  Pallas kernels  46.5 us (37%)
  blocking collectives  37.1 us (29%)
  waiting for transfers between devices  20.8 us (17%)
  starting transfers between devices  15 us (12%)
  local copies, waits for them, and re-layouts  2.67 us (2%)
  other arithmetic  2.39 us (2%)
    pallas_call x7, Pallas kernels, product(): pl.pallas_call(kernel, out_shape=outs, in_specs=[HBM] * 2 + [VMEM] * len(...  39.5 us
    all_to_all x2, blocking collectives, exchange(): lax.all_to_all(value, 'tm', split_axis=0, concat_axis=0, axis_index_group...  24.5 us
    all_to_all x2, waiting for transfers between devices, exchange(): lax.all_to_all(value, 'tm', split_axis=0, concat_axis=0, axis_index_group...  12.8 us
    all_to_all x1, blocking collectives, shards(): lax.all_to_all(out.reshape(devices, hour_rows * rows_out, width), 'tm', s...  12.6 us
    all_to_all x1, waiting for transfers between devices, shards(): came = lax.all_to_all(sent, 'tm', split_axis=0, concat_axis=0, tiled=True)  7.99 us
    all_to_all x1, starting transfers between devices, shards(): came = lax.all_to_all(sent, 'tm', split_axis=0, concat_axis=0, tiled=True)  7.4 us
    all_to_all x2, starting transfers between devices, exchange(): lax.all_to_all(value, 'tm', split_axis=0, concat_axis=0, axis_index_group...  7 us
    pallas_call x4, Pallas kernels, small(): pl.pallas_call(kernel, out_shape=outs, in_specs=[VMEM] * (len(operands) -...  6.98 us
  transfers between devices with their start and end apart: 7, of which 3 were waited for; matrix products, arithmetic and copies ran while one was open for 1% of the time, Pallas kernels for 20%

profile of v7, /device:TPU:0, one launch (start us, length us, event | category | flops | bytes accessed | tf_op | source)
XLA Modules:
  0.0 125.3 jit_solution(17277594016603278002)
XLA Ops:
  0.6 0.9 copy-done.1
  1.5 0.7 copy-done.2
  2.2 0.8 pack.1
  3.1 7.4 %all-to-all-start = ((bf16[16,48,128]{2,1,0:T(8,128)(2,1)}), bf16[16,48,128]{2,1,0:T(8,128)(2,1)S(1)}, u32[]{:S(2)}, u32[]{:S(2)}) async-start(bf16[16,48,128]{2,1,0:T(8,128)(2,1)} %pack.1), calls=%async_computation | async-start | bytes 393216 | tf_op jit(solution)/shard_map/all_to_all | solution.py:425
  10.5 0.8 copy.10
  11.3 0.2 reshape.63.blocks_hbm
  11.5 8.0 %all-to-all-done = bf16[16,48,128]{2,1,0:T(8,128)(2,1)S(1)} async-done(((bf16[16,48,128]{2,1,0:T(8,128)(2,1)}), bf16[16,48,128]{2,1,0:T(8,128)(2,1)S(1)}, u32[]{:S(2)}, u32[]{:S(2)}) %all-to-all-start) | async-done | bytes 196640 | tf_op jit(solution)/shard_map/all_to_all | solution.py:425
  19.5 5.5 %first_flow.1 = (f32[64,16,128]{2,1,0:T(8,128)S(1)}, bf16[18,16,128]{2,1,0:T(8,128)(2,1)S(1)}, f32[16,2048]{1,0:T(8,128)S(1)}) custom-call(s32[640]{0:T(1024)S(1)} %reshape.63.blocks_hbm, bf16[128,5,128,128]{3,2,1,0:T(8,128)(2,1)} %tiles_hbm.13, bf16[768,128]{1,0:T(8,128)(2,1)S(1)} %bitcast.21), custom_call_target="tpu_custom_call" | custom-call | flops 167772160 | bytes 10485760 | tf_op jit(solution)/shard_map/first_flow/pallas_call | solution.py:381
  25.0 0.1 collective-permute-start
  25.0 5.5 %own_flow.2 = f32[64,16,128]{2,1,0:T(8,128)S(1)} custom-call(s32[640]{0:T(1024)S(1)} %reshape.63.blocks_hbm, bf16[128,5,128,128]{3,2,1,0:T(8,128)(2,1)} %tiles_hbm.13, bf16[18,16,128]{2,1,0:T(8,128)(2,1)S(1)} %get-tuple-element.21.picked.base), custom_call_target="tpu_custom_call" | custom-call | flops 167772160 | bytes 10485760 | tf_op jit(solution)/shard_map/own_flow/pallas_call | solution.py:381
  30.5 0.8 add_convert_fusion.1
  31.3 3.4 %all-to-all-start.1 = ((bf16[8,8,16,128]{3,2,1,0:T(8,128)(2,1)}), bf16[8,8,16,128]{3,2,1,0:T(8,128)(2,1)S(1)}, u32[]{:S(2)}, u32[]{:S(2)}) async-start(bf16[8,8,16,128]{3,2,1,0:T(8,128)(2,1)} %bitcast.1), calls=%async_computation.1 | async-start | bytes 524288 | tf_op jit(solution)/shard_map/all_to_all | solution.py:367
  34.7 0.7 dynamic-slice_bitcast_fusion
  35.4 1.9 %storage.2.delta = f32[18,16,128]{2,1,0:T(8,128)S(1)} custom-call(f32[16,2048]{1,0:T(8,128)S(1)} %get-tuple-element.29.level, s32[1,2048]{1,0:T(1,128)S(1)} %bitcast.26, s32[1,2048]{1,0:T(1,128)S(1)} %bitcast.23), custom_call_target="tpu_custom_call" | custom-call | flops 167772160 | bytes 4194304 | tf_op jit(solution)/shard_map/storage/pallas_call | solution.py:395
  37.3 7.1 %all-to-all-done.1 = bf16[8,8,16,128]{3,2,1,0:T(8,128)(2,1)S(1)} async-done(((bf16[8,8,16,128]{3,2,1,0:T(8,128)(2,1)}), bf16[8,8,16,128]{3,2,1,0:T(8,128)(2,1)S(1)}, u32[]{:S(2)}, u32[]{:S(2)}) %all-to-all-start.1) | async-done | bytes 262176 | tf_op jit(solution)/shard_map/all_to_all | solution.py:367
  44.6 12.5 %all_to_all.30 = bf16[8,8,16,128]{3,2,1,0:T(8,128)(2,1)S(1)} all-to-all(bf16[8,8,16,128]{3,2,1,0:T(8,128)(2,1)S(1)} %broadcast_in_dim.4), channel_id=1, replica_groups={{0,2,4,6,8,10,12,14},{1,3,5,7,9,11,13,15},{16,18,20,22,24,26,28,30},{17..., dimensions={0} | all-to-all | bytes 524288 | tf_op jit(solution)/shard_map/all_to_all | solution.py:367
  57.1 0.0 collective-permute-start.1
  57.1 4.5 %own_price.2.before = f32[18,16,128]{2,1,0:T(8,128)S(1)} custom-call(s32[640]{0:T(1024)S(1)} %reshape.63.blocks_hbm, bf16[128,5,128,128]{3,2,1,0:T(8,128)(2,1)} %tiles_hbm.13, bf16[64,16,128]{2,1,0:T(8,128)(2,1)S(1)} %bitcast.18), custom_call_target="tpu_custom_call" | custom-call | flops 167772160 | bytes 10485760 | tf_op jit(solution)/shard_map/own_price/pallas_call | solution.py:381
  61.6 0.0 copy-start
  61.6 0.0 collective-permute-done.1.dual
  61.6 7.9 %price_then_flow.1 = (f32[18,16,128]{2,1,0:T(8,128)S(1)}, f32[18,16,128]{2,1,0:T(8,128)S(1)}, bf16[18,16,128]{2,1,0:T(8,128)(2,1)S(1)}, f32[64,16,128]{2,1,0:T(8,128)S(1)}) custom-call(s32[640]{0:T(1024)S(1)} %reshape.63.blocks_hbm, bf16[128,5,128,128]{3,2,1,0:T(8,128)(2,1)} %tiles_hbm.13, bf16[64,16,128]{2,1,0:T(8,128)(2,1)S(1)} %collective-permute-done.1.dual, ...), custom_call_target="tpu_custom_call" | custom-call | flops 335544320 | bytes 20971520 | tf_op jit(solution)/shard_map/price_then_flow/pallas_call | solution.py:381
  69.5 0.6 collective-permute-start.2
  70.1 5.4 %own_flow.3 = f32[64,16,128]{2,1,0:T(8,128)S(1)} custom-call(s32[640]{0:T(1024)S(1)} %reshape.63.blocks_hbm, bf16[128,5,128,128]{3,2,1,0:T(8,128)(2,1)} %tiles_hbm.13, bf16[18,16,128]{2,1,0:T(8,128)(2,1)S(1)} %get-tuple-element.26.picked), custom_call_target="tpu_custom_call" | custom-call | flops 167772160 | bytes 10485760 | tf_op jit(solution)/shard_map/own_flow/pallas_call | solution.py:381
  75.5 0.8 add_convert_fusion
  76.3 3.6 %all-to-all-start.3 = ((bf16[8,8,16,128]{3,2,1,0:T(8,128)(2,1)}), bf16[8,8,16,128]{3,2,1,0:T(8,128)(2,1)S(1)}, u32[]{:S(2)}, u32[]{:S(2)}) async-start(bf16[8,8,16,128]{3,2,1,0:T(8,128)(2,1)} %bitcast.8), calls=%async_computation.3 | async-start | bytes 524288 | tf_op jit(solution)/shard_map/all_to_all | solution.py:367
  79.9 3.5 %storage.3 = (f32[16,2048]{1,0:T(8,128)S(1)}, f32[18,16,128]{2,1,0:T(8,128)S(1)}) custom-call(f32[18,16,128]{2,1,0:T(8,128)S(1)} %get-tuple-element.28.price, f32[16,2048]{1,0:T(8,128)S(1)} %get-tuple-element.29.level, s32[1,2048]{1,0:T(1,128)S(1)} %bitcast.27, s32[1,2048]{1,0:T(1,128)S(1)} %bitcast.24, f32[1,2048]{1,0:T(1,128)S(1)} %bitcast.29), custom_call_target="tpu_custom_call" | custom-call | flops 167772160 | bytes 4194304 | tf_op jit(solution)/shard_map/storage/pallas_call | solution.py:395
  83.5 5.6 %all-to-all-done.3 = bf16[8,8,16,128]{3,2,1,0:T(8,128)(2,1)S(1)} async-done(((bf16[8,8,16,128]{3,2,1,0:T(8,128)(2,1)}), bf16[8,8,16,128]{3,2,1,0:T(8,128)(2,1)S(1)}, u32[]{:S(2)}, u32[]{:S(2)}) %all-to-all-start.3) | async-done | bytes 262176 | tf_op jit(solution)/shard_map/all_to_all | solution.py:367
  89.2 12.0 %all_to_all.31 = bf16[8,8,16,128]{3,2,1,0:T(8,128)(2,1)S(1)} all-to-all(bf16[8,8,16,128]{3,2,1,0:T(8,128)(2,1)S(1)} %broadcast_in_dim.5), channel_id=1, replica_groups={{0,2,4,6,8,10,12,14},{1,3,5,7,9,11,13,15},{16,18,20,22,24,26,28,30},{17..., dimensions={0} | all-to-all | bytes 524288 | tf_op jit(solution)/shard_map/all_to_all | solution.py:367
  101.1 4.5 %own_price.3.before = f32[18,16,128]{2,1,0:T(8,128)S(1)} custom-call(s32[640]{0:T(1024)S(1)} %reshape.63.blocks_hbm, bf16[128,5,128,128]{3,2,1,0:T(8,128)(2,1)} %tiles_hbm.13, bf16[64,16,128]{2,1,0:T(8,128)(2,1)S(1)} %bitcast.20), custom_call_target="tpu_custom_call" | custom-call | flops 167772160 | bytes 10485760 | tf_op jit(solution)/shard_map/own_price/pallas_call | solution.py:381
  105.7 6.3 %last_price.1 = bf16[768,128]{1,0:T(8,128)(2,1)S(1)} custom-call(s32[640]{0:T(1024)S(1)} %reshape.63.blocks_hbm, bf16[128,5,128,128]{3,2,1,0:T(8,128)(2,1)} %tiles_hbm.13, bf16[64,16,128]{2,1,0:T(8,128)(2,1)S(1)} %collective-permute-done.3.dual, f32[18,16,128]{2,1,0:T(8,128)S(1)} %own_price.3.before, bf16[18,16,128]{2,1,0:T(8,128)(2,1)S(1)} %get-tuple-element.21.picked.base, ...), custom_call_target="tpu_custom_call" | custom-call | flops 167772160 | bytes 10485760 | tf_op jit(solution)/shard_map/last_price/pallas_call | solution.py:381
  112.0 12.6 %all_to_all.32.back = bf16[16,48,128]{2,1,0:T(8,128)(2,1)S(1)} all-to-all(bf16[16,48,128]{2,1,0:T(8,128)(2,1)S(1)} %bitcast.22), channel_id=1, replica_groups=mesh['scen'=2,'tm'=16] {'tm'}, dimensions={0} | all-to-all | bytes 393216 | tf_op jit(solution)/shard_map/all_to_all | solution.py:478
  124.6 0.7 unpack.1
  (16 shorter events, 0.2 us)
Async XLA Ops:
  0.6 0.9 copy-start.1
  1.5 0.7 copy-start.2
  3.1 16.4 %all-to-all-start = ((bf16[16,48,128]{2,1,0:T(8,128)(2,1)}), bf16[16,48,128]{2,1,0:T(8,128)(2,1)S(1)}, u32[]{:S(2)}, u32[]{:S(2)}) async-start(bf16[16,48,128]{2,1,0:T(8,128)(2,1)} %pack.1), calls=%async_computation | async-start | bytes 393216 | tf_op jit(solution)/shard_map/all_to_all | solution.py:425
  19.5 15.9 %copy-start.3 = (s32[2048]{0:T(1024)S(1)}, s32[2048]{0:T(1024)}, u32[]{:S(2)}) copy-start(s32[2048]{0:T(1024)} %param.11) | copy-start | bytes 24580
  25.0 5.5 %collective-permute-start = (f32[64,16,128]{2,1,0:T(8,128)S(1)}, f32[64,16,128]{2,1,0:T(8,128)S(1)}, u32[]{:S(2)}, u32[]{:S(2)}) collective-permute-start(f32[64,16,128]{2,1,0:T(8,128)S(1)} %get-tuple-element.22), channel_id=1, source_target_pairs={{0,1},{1,0},{2,3},{3,2},{4,5},{5,4},{6,7},{7,6},{8,9},{9,8},{10,11... | collective-permute-start | bytes 1572872 | tf_op jit(solution)/shard_map/ppermute | solution.py:437
  31.3 13.2 %all-to-all-start.1 = ((bf16[8,8,16,128]{3,2,1,0:T(8,128)(2,1)}), bf16[8,8,16,128]{3,2,1,0:T(8,128)(2,1)S(1)}, u32[]{:S(2)}, u32[]{:S(2)}) async-start(bf16[8,8,16,128]{3,2,1,0:T(8,128)(2,1)} %bitcast.1), calls=%async_computation.1 | async-start | bytes 524288 | tf_op jit(solution)/shard_map/all_to_all | solution.py:367
  57.1 4.5 %collective-permute-start.1 = (bf16[64,16,128]{2,1,0:T(8,128)(2,1)S(1)}, bf16[64,16,128]{2,1,0:T(8,128)(2,1)S(1)}, u32[]{:S(2)}, u32[]{:S(2)}) collective-permute-start(bf16[64,16,128]{2,1,0:T(8,128)(2,1)S(1)} %bitcast.17), channel_id=1, source_target_pairs={{0,1},{1,0},{2,3},{3,2},{4,5},{5,4},{6,7},{7,6},{8,9},{9,8},{10,11... | collective-permute-start | bytes 786440 | tf_op jit(solution)/shard_map/ppermute | solution.py:453
  61.6 18.3 %copy-start = (f32[2048]{0:T(1024)S(1)}, f32[2048]{0:T(1024)}, u32[]{:S(2)}) copy-start(f32[2048]{0:T(1024)} %param.12) | copy-start | bytes 24580
  69.5 6.0 %collective-permute-start.2 = (f32[64,16,128]{2,1,0:T(8,128)S(1)}, f32[64,16,128]{2,1,0:T(8,128)S(1)}, u32[]{:S(2)}, u32[]{:S(2)}) collective-permute-start(f32[64,16,128]{2,1,0:T(8,128)S(1)} %get-tuple-element.27), channel_id=1, source_target_pairs={{0,1},{1,0},{2,3},{3,2},{4,5},{5,4},{6,7},{7,6},{8,9},{9,8},{10,11... | collective-permute-start | bytes 1572872 | tf_op jit(solution)/shard_map/ppermute | solution.py:437
  76.3 12.7 %all-to-all-start.3 = ((bf16[8,8,16,128]{3,2,1,0:T(8,128)(2,1)}), bf16[8,8,16,128]{3,2,1,0:T(8,128)(2,1)S(1)}, u32[]{:S(2)}, u32[]{:S(2)}) async-start(bf16[8,8,16,128]{3,2,1,0:T(8,128)(2,1)} %bitcast.8), calls=%async_computation.3 | async-start | bytes 524288 | tf_op jit(solution)/shard_map/all_to_all | solution.py:367
  101.1 4.5 %collective-permute-start.3 = (bf16[64,16,128]{2,1,0:T(8,128)(2,1)S(1)}, bf16[64,16,128]{2,1,0:T(8,128)(2,1)S(1)}, u32[]{:S(2)}, u32[]{:S(2)}) collective-permute-start(bf16[64,16,128]{2,1,0:T(8,128)(2,1)S(1)} %bitcast.19), channel_id=1, source_target_pairs={{0,1},{1,0},{2,3},{3,2},{4,5},{5,4},{6,7},{7,6},{8,9},{9,8},{10,11... | collective-permute-start | bytes 786440 | tf_op jit(solution)/shard_map/ppermute | solution.py:453

commit v8 on v7

--- a/solution.py
+++ b/solution.py
@@ -66,35 +66,34 @@
 
 def flow_pass(picked, half, flows, wait):
     tiles = half.tiles
-    depth, lines = tiles.shape[1], tiles.shape[2]
+    depth = tiles.shape[1]
     hours = picked.shape[1]
+    even = depth - depth % 2
+
+    def side(parts):
+        return jnp.concatenate(parts, axis=1)
 
     def four(base, block):
         rows = [[picked[block(u, k)] for k in range(depth)] for u in range(4)]
         zero = jnp.zeros_like(rows[0][0])
-        totals = [None] * 4
-
-        def add(u, part):
-            totals[u] = part if totals[u] is None else totals[u] + part
-
         for first in (0, 2):
-            for k in range(0, depth - 1, 2):
-                left = wide([[rows[first][k], rows[first][k + 1]], [rows[first + 1][k], rows[first + 1][k + 1]]])
-                g = base + first
-                right = wide([[tiles[g, k], tiles[g, k + 1]], [tiles[g + 1, k], tiles[g + 1, k + 1]]])
+            g = base + first
+            totals = [
+                lax.dot_general(
+                    side(rows[first + u][:even]),
+                    side([tiles[g + u, k] for k in range(even)]),
+                    NT,
+                    preferred_element_type=jnp.float32,
+                )
+                for u in range(2)
+            ]
+            if depth % 2:
+                left = wide([[rows[first][even], zero], [zero, rows[first + 1][even]]])
+                right = side([tiles[g, even], tiles[g + 1, even]])
                 part = lax.dot_general(left, right, NT, preferred_element_type=jnp.float32)
-                add(first, part[:hours, :lines])
-                add(first + 1, part[hours:, lines:])
-        if depth % 2:
-            k = depth - 1
-            left = wide([[rows[0][k], zero], [rows[1][k], zero], [zero, rows[2][k]], [zero, rows[3][k]]])
-            right = wide([[tiles[base, k], tiles[base + 2, k]], [tiles[base + 1, k], tiles[base + 3, k]]])
-            part = lax.dot_general(left, right, NT, preferred_element_type=jnp.float32)
-            for u in range(4):
-                at = (u % 2) * lines
-                add(u, part[u * hours : (u + 1) * hours, at : at + lines])
-        for u in range(4):
-            flows[base + u] = totals[u].astype(flows.dtype)
+                totals = [totals[u] + part[u * hours : (u + 1) * hours] for u in range(2)]
+            for u in range(2):
+                flows[g + u] = totals[u].astype(flows.dtype)
 
     half.each_four(wait, four)
 
@@ -448,8 +447,9 @@
         shifted = jnp.sum(parts.astype(jnp.float32), axis=0) + line_dual
         clipped = jnp.clip(shifted, -own_limits, own_limits)
         line_dual = shifted - clipped
-        dual = exchange(jnp.broadcast_to(line_dual.astype(jnp.bfloat16)[None], (chips, own_groups, hours, lines)))
-        dual = dual.reshape(half_groups, hours, lines)
+        dual = lax.all_gather(
+            line_dual.astype(jnp.bfloat16), "tm", axis=0, axis_index_groups=same_core, tiled=True
+        )
         other = lax.ppermute(dual, "tm", sibling)
         (before,) = product(own_price_kernel, "own_price", [block_shape], [dual], sums)
         if iteration < ITERS - 1:

time: 126 us -> 162 us (1.29)
  blocking collectives: 37.1 us -> 74.1 us
    all_gather x0 -> x2, blocking collectives: none -> 61.7 us  [shards(): lax.all_gather(line_dual.astype(jnp.bfloat16), 'tm', axis=0, axis_index_g...]
    all_to_all x2 -> x0, blocking collectives: 24.5 us -> none  [exchange(): lax.all_to_all(value, 'tm', split_axis=0, concat_axis=0, axis_index_group...]
  transfers between devices with their start and end apart: 7 -> 7, of which waited for: 3 -> 3; matrix products, arithmetic and copies ran while one was open for 1% -> 1% of each run, Pallas kernels for 20% -> 15%
where the time goes in v8:
time: 162 us; the launch traced here: 161 us
  blocking collectives  74.1 us (46%)
  Pallas kernels  45.7 us (28%)
  waiting for transfers between devices  20.8 us (13%)
  starting transfers between devices  15 us (9%)
  local copies, waits for them, and re-layouts  2.6 us (2%)
  other arithmetic  2.39 us (1%)
    all_gather x2, blocking collectives, shards(): lax.all_gather(line_dual.astype(jnp.bfloat16), 'tm', axis=0, axis_index_g...  61.7 us
    pallas_call x7, Pallas kernels, product(): pl.pallas_call(kernel, out_shape=outs, in_specs=[HBM] * 2 + [VMEM] * len(...  38.7 us
    all_to_all x2, waiting for transfers between devices, exchange(): lax.all_to_all(value, 'tm', split_axis=0, concat_axis=0, axis_index_group...  12.8 us
    all_to_all x1, blocking collectives, shards(): lax.all_to_all(out.reshape(devices, hour_rows * rows_out, width), 'tm', s...  12.4 us
    all_to_all x1, waiting for transfers between devices, shards(): came = lax.all_to_all(sent, 'tm', split_axis=0, concat_axis=0, tiled=True)  7.99 us
    all_to_all x1, starting transfers between devices, shards(): came = lax.all_to_all(sent, 'tm', split_axis=0, concat_axis=0, tiled=True)  7.4 us
    pallas_call x4, Pallas kernels, small(): pl.pallas_call(kernel, out_shape=outs, in_specs=[VMEM] * (len(operands) -...  7 us
    all_to_all x2, starting transfers between devices, exchange(): lax.all_to_all(value, 'tm', split_axis=0, concat_axis=0, axis_index_group...  6.98 us
  transfers between devices with their start and end apart: 7, of which 3 were waited for; matrix products, arithmetic and copies ran while one was open for 1% of the time, Pallas kernels for 15%

profile of v8, /device:TPU:0, one launch (start us, length us, event | category | flops | bytes accessed | tf_op | source)
XLA Modules:
  0.0 161.4 jit_solution(95442153769357909)
XLA Ops:
  0.6 0.9 copy-done.1
  1.5 0.7 copy-done.2
  2.2 0.8 pack.1
  3.1 7.4 %all-to-all-start = ((bf16[16,48,128]{2,1,0:T(8,128)(2,1)}), bf16[16,48,128]{2,1,0:T(8,128)(2,1)S(1)}, u32[]{:S(2)}, u32[]{:S(2)}) async-start(bf16[16,48,128]{2,1,0:T(8,128)(2,1)} %pack.1), calls=%async_computation | async-start | bytes 393216 | tf_op jit(solution)/shard_map/all_to_all | solution.py:424
  10.5 0.8 copy.11
  11.3 0.2 reshape.42.blocks_hbm
  11.5 8.0 %all-to-all-done = bf16[16,48,128]{2,1,0:T(8,128)(2,1)S(1)} async-done(((bf16[16,48,128]{2,1,0:T(8,128)(2,1)}), bf16[16,48,128]{2,1,0:T(8,128)(2,1)S(1)}, u32[]{:S(2)}, u32[]{:S(2)}) %all-to-all-start) | async-done | bytes 196640 | tf_op jit(solution)/shard_map/all_to_all | solution.py:424
  19.5 5.2 %first_flow.1 = (f32[64,16,128]{2,1,0:T(8,128)S(1)}, bf16[18,16,128]{2,1,0:T(8,128)(2,1)S(1)}, f32[16,2048]{1,0:T(8,128)S(1)}) custom-call(s32[640]{0:T(1024)S(1)} %reshape.42.blocks_hbm, bf16[128,5,128,128]{3,2,1,0:T(8,128)(2,1)} %tiles_hbm.13, bf16[768,128]{1,0:T(8,128)(2,1)S(1)} %bitcast.15), custom_call_target="tpu_custom_call" | custom-call | flops 167772160 | bytes 10485760 | tf_op jit(solution)/shard_map/first_flow/pallas_call | solution.py:380
  24.7 0.1 collective-permute-start
  24.8 5.2 %own_flow.2 = f32[64,16,128]{2,1,0:T(8,128)S(1)} custom-call(s32[640]{0:T(1024)S(1)} %reshape.42.blocks_hbm, bf16[128,5,128,128]{3,2,1,0:T(8,128)(2,1)} %tiles_hbm.13, bf16[18,16,128]{2,1,0:T(8,128)(2,1)S(1)} %get-tuple-element.21.picked.base), custom_call_target="tpu_custom_call" | custom-call | flops 167772160 | bytes 10485760 | tf_op jit(solution)/shard_map/own_flow/pallas_call | solution.py:380
  30.1 0.8 add_convert_fusion.1
  30.8 3.4 %all-to-all-start.1 = ((bf16[8,8,16,128]{3,2,1,0:T(8,128)(2,1)}), bf16[8,8,16,128]{3,2,1,0:T(8,128)(2,1)S(1)}, u32[]{:S(2)}, u32[]{:S(2)}) async-start(bf16[8,8,16,128]{3,2,1,0:T(8,128)(2,1)} %bitcast.1), calls=%async_computation.1 | async-start | bytes 524288 | tf_op jit(solution)/shard_map/all_to_all | solution.py:366
  34.2 0.7 dynamic-slice_bitcast_fusion
  35.0 1.9 %storage.2.delta = f32[18,16,128]{2,1,0:T(8,128)S(1)} custom-call(f32[16,2048]{1,0:T(8,128)S(1)} %get-tuple-element.29.level, s32[1,2048]{1,0:T(1,128)S(1)} %bitcast.20, s32[1,2048]{1,0:T(1,128)S(1)} %bitcast.17), custom_call_target="tpu_custom_call" | custom-call | flops 167772160 | bytes 4194304 | tf_op jit(solution)/shard_map/storage/pallas_call | solution.py:394
  36.9 7.1 %all-to-all-done.1 = bf16[8,8,16,128]{3,2,1,0:T(8,128)(2,1)S(1)} async-done(((bf16[8,8,16,128]{3,2,1,0:T(8,128)(2,1)}), bf16[8,8,16,128]{3,2,1,0:T(8,128)(2,1)S(1)}, u32[]{:S(2)}, u32[]{:S(2)}) %all-to-all-start.1) | async-done | bytes 262176 | tf_op jit(solution)/shard_map/all_to_all | solution.py:366
  44.1 30.8 %all_gather.6.dual = bf16[64,16,128]{2,1,0:T(8,128)(2,1)S(1)} all-gather(bf16[8,16,128]{2,1,0:T(8,128)(2,1)S(1)} %fusion), channel_id=1, replica_groups={{0,2,4,6,8,10,12,14},{1,3,5,7,9,11,13,15},{16,18,20,22,24,26,28,30},{17..., dimensions={0}, use_global_device_ids=true | all-gather | bytes 294912 | tf_op jit(solution)/shard_map/all_gather | solution.py:450
  74.9 0.0 collective-permute-start.1
  74.9 4.5 %own_price.2.before = f32[18,16,128]{2,1,0:T(8,128)S(1)} custom-call(s32[640]{0:T(1024)S(1)} %reshape.42.blocks_hbm, bf16[128,5,128,128]{3,2,1,0:T(8,128)(2,1)} %tiles_hbm.13, bf16[64,16,128]{2,1,0:T(8,128)(2,1)S(1)} %all_gather.6.dual), custom_call_target="tpu_custom_call" | custom-call | flops 167772160 | bytes 10485760 | tf_op jit(solution)/shard_map/own_price/pallas_call | solution.py:380
  79.4 0.0 copy-start
  79.4 0.0 collective-permute-done.1.dual
  79.4 7.7 %price_then_flow.1 = (f32[18,16,128]{2,1,0:T(8,128)S(1)}, f32[18,16,128]{2,1,0:T(8,128)S(1)}, bf16[18,16,128]{2,1,0:T(8,128)(2,1)S(1)}, f32[64,16,128]{2,1,0:T(8,128)S(1)}) custom-call(s32[640]{0:T(1024)S(1)} %reshape.42.blocks_hbm, bf16[128,5,128,128]{3,2,1,0:T(8,128)(2,1)} %tiles_hbm.13, bf16[64,16,128]{2,1,0:T(8,128)(2,1)S(1)} %collective-permute-done.1.dual, ...), custom_call_target="tpu_custom_call" | custom-call | flops 335544320 | bytes 20971520 | tf_op jit(solution)/shard_map/price_then_flow/pallas_call | solution.py:380
  87.1 0.6 collective-permute-start.2
  87.7 5.2 %own_flow.3 = f32[64,16,128]{2,1,0:T(8,128)S(1)} custom-call(s32[640]{0:T(1024)S(1)} %reshape.42.blocks_hbm, bf16[128,5,128,128]{3,2,1,0:T(8,128)(2,1)} %tiles_hbm.13, bf16[18,16,128]{2,1,0:T(8,128)(2,1)S(1)} %get-tuple-element.26.picked), custom_call_target="tpu_custom_call" | custom-call | flops 167772160 | bytes 10485760 | tf_op jit(solution)/shard_map/own_flow/pallas_call | solution.py:380
  92.9 0.8 add_convert_fusion
  93.7 3.6 %all-to-all-start.2 = ((bf16[8,8,16,128]{3,2,1,0:T(8,128)(2,1)}), bf16[8,8,16,128]{3,2,1,0:T(8,128)(2,1)S(1)}, u32[]{:S(2)}, u32[]{:S(2)}) async-start(bf16[8,8,16,128]{3,2,1,0:T(8,128)(2,1)} %bitcast.7), calls=%async_computation.2 | async-start | bytes 524288 | tf_op jit(solution)/shard_map/all_to_all | solution.py:366
  97.3 3.5 %storage.3 = (f32[16,2048]{1,0:T(8,128)S(1)}, f32[18,16,128]{2,1,0:T(8,128)S(1)}) custom-call(f32[18,16,128]{2,1,0:T(8,128)S(1)} %get-tuple-element.28.price, f32[16,2048]{1,0:T(8,128)S(1)} %get-tuple-element.29.level, s32[1,2048]{1,0:T(1,128)S(1)} %bitcast.21, s32[1,2048]{1,0:T(1,128)S(1)} %bitcast.18, f32[1,2048]{1,0:T(1,128)S(1)} %bitcast.23), custom_call_target="tpu_custom_call" | custom-call | flops 167772160 | bytes 4194304 | tf_op jit(solution)/shard_map/storage/pallas_call | solution.py:394
  100.9 5.6 %all-to-all-done.2 = bf16[8,8,16,128]{3,2,1,0:T(8,128)(2,1)S(1)} async-done(((bf16[8,8,16,128]{3,2,1,0:T(8,128)(2,1)}), bf16[8,8,16,128]{3,2,1,0:T(8,128)(2,1)S(1)}, u32[]{:S(2)}, u32[]{:S(2)}) %all-to-all-start.2) | async-done | bytes 262176 | tf_op jit(solution)/shard_map/all_to_all | solution.py:366
  106.5 30.9 %all_gather.7.dual = bf16[64,16,128]{2,1,0:T(8,128)(2,1)S(1)} all-gather(bf16[8,16,128]{2,1,0:T(8,128)(2,1)S(1)} %get-tuple-element.39), channel_id=1, replica_groups={{0,2,4,6,8,10,12,14},{1,3,5,7,9,11,13,15},{16,18,20,22,24,26,28,30},{17..., dimensions={0}, use_global_device_ids=true | all-gather | bytes 294912 | tf_op jit(solution)/shard_map/all_gather | solution.py:450
  137.4 4.5 %own_price.3.before = f32[18,16,128]{2,1,0:T(8,128)S(1)} custom-call(s32[640]{0:T(1024)S(1)} %reshape.42.blocks_hbm, bf16[128,5,128,128]{3,2,1,0:T(8,128)(2,1)} %tiles_hbm.13, bf16[64,16,128]{2,1,0:T(8,128)(2,1)S(1)} %all_gather.7.dual), custom_call_target="tpu_custom_call" | custom-call | flops 167772160 | bytes 10485760 | tf_op jit(solution)/shard_map/own_price/pallas_call | solution.py:380
  141.9 6.3 %last_price.1 = bf16[768,128]{1,0:T(8,128)(2,1)S(1)} custom-call(s32[640]{0:T(1024)S(1)} %reshape.42.blocks_hbm, bf16[128,5,128,128]{3,2,1,0:T(8,128)(2,1)} %tiles_hbm.13, bf16[64,16,128]{2,1,0:T(8,128)(2,1)S(1)} %collective-permute-done.3.dual, f32[18,16,128]{2,1,0:T(8,128)S(1)} %own_price.3.before, bf16[18,16,128]{2,1,0:T(8,128)(2,1)S(1)} %get-tuple-element.21.picked.base, ...), custom_call_target="tpu_custom_call" | custom-call | flops 167772160 | bytes 10485760 | tf_op jit(solution)/shard_map/last_price/pallas_call | solution.py:380
  148.3 12.4 %all_to_all.20.back = bf16[16,48,128]{2,1,0:T(8,128)(2,1)S(1)} all-to-all(bf16[16,48,128]{2,1,0:T(8,128)(2,1)S(1)} %bitcast.16), channel_id=1, replica_groups=mesh['scen'=2,'tm'=16] {'tm'}, dimensions={0} | all-to-all | bytes 393216 | tf_op jit(solution)/shard_map/all_to_all | solution.py:478
  160.7 0.7 unpack.1
  (14 shorter events, 0.2 us)
Async XLA Ops:
  0.6 0.9 copy-start.1
  1.5 0.7 copy-start.2
  3.1 16.4 %all-to-all-start = ((bf16[16,48,128]{2,1,0:T(8,128)(2,1)}), bf16[16,48,128]{2,1,0:T(8,128)(2,1)S(1)}, u32[]{:S(2)}, u32[]{:S(2)}) async-start(bf16[16,48,128]{2,1,0:T(8,128)(2,1)} %pack.1), calls=%async_computation | async-start | bytes 393216 | tf_op jit(solution)/shard_map/all_to_all | solution.py:424
  19.5 15.5 %copy-start.3 = (s32[2048]{0:T(1024)S(1)}, s32[2048]{0:T(1024)}, u32[]{:S(2)}) copy-start(s32[2048]{0:T(1024)} %param.11) | copy-start | bytes 24580
  24.7 5.3 %collective-permute-start = (f32[64,16,128]{2,1,0:T(8,128)S(1)}, f32[64,16,128]{2,1,0:T(8,128)S(1)}, u32[]{:S(2)}, u32[]{:S(2)}) collective-permute-start(f32[64,16,128]{2,1,0:T(8,128)S(1)} %get-tuple-element.22), channel_id=1, source_target_pairs={{0,1},{1,0},{2,3},{3,2},{4,5},{5,4},{6,7},{7,6},{8,9},{9,8},{10,11... | collective-permute-start | bytes 1572872 | tf_op jit(solution)/shard_map/ppermute | solution.py:436
  30.8 13.2 %all-to-all-start.1 = ((bf16[8,8,16,128]{3,2,1,0:T(8,128)(2,1)}), bf16[8,8,16,128]{3,2,1,0:T(8,128)(2,1)S(1)}, u32[]{:S(2)}, u32[]{:S(2)}) async-start(bf16[8,8,16,128]{3,2,1,0:T(8,128)(2,1)} %bitcast.1), calls=%async_computation.1 | async-start | bytes 524288 | tf_op jit(solution)/shard_map/all_to_all | solution.py:366
  74.9 4.5 %collective-permute-start.1 = (bf16[64,16,128]{2,1,0:T(8,128)(2,1)S(1)}, bf16[64,16,128]{2,1,0:T(8,128)(2,1)S(1)}, u32[]{:S(2)}, u32[]{:S(2)}) collective-permute-start(bf16[64,16,128]{2,1,0:T(8,128)(2,1)S(1)} %all_gather.6.dual), channel_id=1, source_target_pairs={{0,1},{1,0},{2,3},{3,2},{4,5},{5,4},{6,7},{7,6},{8,9},{9,8},{10,11... | collective-permute-start | bytes 786440 | tf_op jit(solution)/shard_map/ppermute | solution.py:453
  79.4 17.9 %copy-start = (f32[2048]{0:T(1024)S(1)}, f32[2048]{0:T(1024)}, u32[]{:S(2)}) copy-start(f32[2048]{0:T(1024)} %param.12) | copy-start | bytes 24580
  87.1 5.8 %collective-permute-start.2 = (f32[64,16,128]{2,1,0:T(8,128)S(1)}, f32[64,16,128]{2,1,0:T(8,128)S(1)}, u32[]{:S(2)}, u32[]{:S(2)}) collective-permute-start(f32[64,16,128]{2,1,0:T(8,128)S(1)} %get-tuple-element.27), channel_id=1, source_target_pairs={{0,1},{1,0},{2,3},{3,2},{4,5},{5,4},{6,7},{7,6},{8,9},{9,8},{10,11... | collective-permute-start | bytes 1572872 | tf_op jit(solution)/shard_map/ppermute | solution.py:436
  93.7 12.7 %all-to-all-start.2 = ((bf16[8,8,16,128]{3,2,1,0:T(8,128)(2,1)}), bf16[8,8,16,128]{3,2,1,0:T(8,128)(2,1)S(1)}, u32[]{:S(2)}, u32[]{:S(2)}) async-start(bf16[8,8,16,128]{3,2,1,0:T(8,128)(2,1)} %bitcast.7), calls=%async_computation.2 | async-start | bytes 524288 | tf_op jit(solution)/shard_map/all_to_all | solution.py:366
  137.4 4.5 %collective-permute-start.3 = (bf16[64,16,128]{2,1,0:T(8,128)(2,1)S(1)}, bf16[64,16,128]{2,1,0:T(8,128)(2,1)S(1)}, u32[]{:S(2)}, u32[]{:S(2)}) collective-permute-start(bf16[64,16,128]{2,1,0:T(8,128)(2,1)S(1)} %all_gather.7.dual), channel_id=1, source_target_pairs={{0,1},{1,0},{2,3},{3,2},{4,5},{5,4},{6,7},{7,6},{8,9},{9,8},{10,11... | collective-permute-start | bytes 786440 | tf_op jit(solution)/shard_map/ppermute | solution.py:453

commit v9 on v8

--- a/solution.py
+++ b/solution.py
@@ -18,19 +18,23 @@
 VMEM = pl.BlockSpec(memory_space=pltpu.VMEM)
 HBM = pl.BlockSpec(memory_space=pl.ANY)
 SMALL = pltpu.CompilerParams(vmem_limit_bytes=12 << 20)
-STRAIGHT = 32
+STRAIGHT = 16
 
 
 class Half:
-    def __init__(self, sibling, blocks_hbm, tiles_hbm, tiles, sems, blocks, block_sem):
+    def __init__(self, sibling, hbm, tiles, blocks, block_sem, sems=None, head=None):
         me = lax.axis_index("tm")
         self.core = 1 - me % 2 if sibling else me % 2
-        self.blocks, self.tiles_hbm, self.tiles, self.sems = blocks, tiles_hbm, tiles, sems
-        self.chunks = sems.shape[0]
-        self.own = tiles.shape[0] // self.chunks
-        for chunk in range(self.chunks):
-            self.fetch(chunk).start()
-        self.block_copy = pltpu.make_async_copy(blocks_hbm, blocks, block_sem)
+        self.tiles, self.head, self.blocks, self.sems = tiles, head, blocks, sems
+        self.blocks_hbm, self.tiles_hbm = hbm
+        self.chunks = lax.axis_size("tm") // 2
+        self.own = self.tiles_hbm.shape[0] // (2 * self.chunks)
+        self.ahead = 0 if head is None else head.shape[0] // self.own
+        self.depth, self.lines, self.width = self.tiles_hbm.shape[1:]
+        if sems is not None:
+            for chunk in range(self.ahead, self.chunks):
+                self.fetch(chunk).start()
+        self.block_copy = pltpu.make_async_copy(self.blocks_hbm, blocks, block_sem)
         self.block_copy.start()
 
     def first_group(self, chunk):
@@ -38,26 +42,48 @@
 
     def fetch(self, chunk):
         there = pl.ds(self.first_group(chunk), self.own)
-        here = pl.ds(chunk * self.own, self.own)
+        here = pl.ds((chunk - self.ahead) * self.own, self.own)
         return pltpu.make_async_copy(self.tiles_hbm.at[there], self.tiles.at[here], self.sems.at[chunk])
 
     def each_four(self, wait, four):
-        depth = self.tiles.shape[1]
+        per = max(1, STRAIGHT // self.own)
+
+        def one(chunk, ref, at):
+            for sub in range(0, self.own, 4):
+                first = (self.first_group(chunk) + sub) * self.depth
+                four(
+                    lambda u, k: ref[at + sub + u, k],
+                    chunk * self.own + sub,
+                    lambda u, k: self.blocks[first + u * self.depth + k],
+                )
+
+        def body(step, carry):
+            for c in range(per):
+                chunk = self.ahead + step * per + c
+                if wait and self.sems is not None:
+                    self.fetch(chunk).wait()
+                one(chunk, self.tiles, (chunk - self.ahead) * self.own)
+            return carry
+
         if wait:
             self.block_copy.wait()
-        per = max(1, STRAIGHT // self.own)
-
-        def body(step, carry):
-            for c in range(per):
-                chunk = step * per + c
-                if wait:
-                    self.fetch(chunk).wait()
-                for sub in range(0, self.own, 4):
-                    first = (self.first_group(chunk) + sub) * depth
-                    four(chunk * self.own + sub, lambda u, k: self.blocks[first + u * depth + k])
-            return carry
-
-        lax.fori_loop(0, self.chunks // per, body, 0)
+        for chunk in range(self.ahead):
+            one(chunk, self.head, chunk * self.own)
+        lax.fori_loop(0, (self.chunks - self.ahead) // per, body, 0)
+
+
+class Ahead:
+    def __init__(self, half, head, sem):
+        self.copies = []
+        for chunk in range(head.shape[0] // half.own):
+            there = pl.ds((2 * chunk + 1 - half.core) * half.own, half.own)
+            here = pl.ds(chunk * half.own, half.own)
+            self.copies.append(pltpu.make_async_copy(half.tiles_hbm.at[there], head.at[here], sem.at[chunk]))
+            self.copies[-1].start()
+
+    def wait(self):
+        for copy in self.copies:
+            copy.wait()
 
 
 def wide(parts):
@@ -65,23 +91,21 @@
 
 
 def flow_pass(picked, half, flows, wait):
-    tiles = half.tiles
-    depth = tiles.shape[1]
+    depth = half.depth
     hours = picked.shape[1]
     even = depth - depth % 2
 
     def side(parts):
         return jnp.concatenate(parts, axis=1)
 
-    def four(base, block):
+    def four(tile, g, block):
         rows = [[picked[block(u, k)] for k in range(depth)] for u in range(4)]
         zero = jnp.zeros_like(rows[0][0])
         for first in (0, 2):
-            g = base + first
             totals = [
                 lax.dot_general(
                     side(rows[first + u][:even]),
-                    side([tiles[g + u, k] for k in range(even)]),
+                    side([tile(first + u, k) for k in range(even)]),
                     NT,
                     preferred_element_type=jnp.float32,
                 )
@@ -89,31 +113,29 @@
             ]
             if depth % 2:
                 left = wide([[rows[first][even], zero], [zero, rows[first + 1][even]]])
-                right = side([tiles[g, even], tiles[g + 1, even]])
+                right = side([tile(first, even), tile(first + 1, even)])
                 part = lax.dot_general(left, right, NT, preferred_element_type=jnp.float32)
                 totals = [totals[u] + part[u * hours : (u + 1) * hours] for u in range(2)]
             for u in range(2):
-                flows[g + u] = totals[u].astype(flows.dtype)
+                flows[g + first + u] = totals[u].astype(flows.dtype)
 
     half.each_four(wait, four)
 
 
 def price_pass(dual, half, sums, wait):
-    tiles = half.tiles
-    depth, width = tiles.shape[1], tiles.shape[3]
+    depth, width = half.depth, half.width
     hours = dual.shape[1]
     for ref in sums:
         ref[...] = jnp.zeros_like(ref)
 
-    def four(base, block):
-        rows = [dual[base + u] for u in range(4)]
+    def four(tile, g, block):
+        rows = [dual[g + u] for u in range(4)]
         zero = jnp.zeros_like(rows[0])
         parts = []
         for first in (0, 2):
             left = wide([[rows[first], zero], [zero, rows[first + 1]]])
             for k in range(0, depth - 1, 2):
-                g = base + first
-                right = wide([[tiles[g, k], tiles[g, k + 1]], [tiles[g + 1, k], tiles[g + 1, k + 1]]])
+                right = wide([[tile(first + u, k), tile(first + u, k + 1)] for u in range(2)])
                 part = jnp.dot(left, right, preferred_element_type=jnp.float32)
                 for u in range(2):
                     for j in range(2):
@@ -122,7 +144,7 @@
         if depth % 2:
             k = depth - 1
             left = wide([[rows[0], zero], [zero, rows[1]], [rows[2], zero], [zero, rows[3]]])
-            right = wide([[tiles[base, k], tiles[base + 2, k]], [tiles[base + 1, k], tiles[base + 3, k]]])
+            right = wide([[tile(0, k), tile(2, k)], [tile(1, k), tile(3, k)]])
             part = jnp.dot(left, right, preferred_element_type=jnp.float32)
             for u in range(4):
                 at = (u // 2) * width
@@ -220,9 +242,11 @@
     out[...] = flat[...].reshape(out.shape).astype(out.dtype)
 
 
-def first_flow_kernel(blocks_hbm, tiles_hbm, came, flows, picked, level, *scratch):
-    stream, (flat,) = (blocks_hbm, tiles_hbm, *scratch[:4]), scratch[4:]
-    half = Half(True, *stream)
+def first_flow_kernel(
+    blocks_hbm, tiles_hbm, came, flows, picked, level, head, blocks, block_sem, tiles, sems, ahead_sem, flat
+):
+    half = Half(True, (blocks_hbm, tiles_hbm), tiles, blocks, block_sem, sems)
+    ahead = Ahead(half, head, ahead_sem)
     count, hours, width = picked.shape
     flat[...] = came[...].astype(jnp.float32)
     rows = flat.shape[0] // hours
@@ -231,27 +255,31 @@
     for c in range(level.shape[1] // width):
         level[:, c * width : (c + 1) * width] = flat[pl.ds(count + c, hours, stride=rows), :]
     flow_pass(picked, half, flows, True)
-
-
-def own_flow_kernel(blocks_hbm, tiles_hbm, picked, flows, *scratch):
-    stream = (blocks_hbm, tiles_hbm, *scratch)
-    half = Half(False, *stream)
-    flow_pass(picked, half, flows, True)
-
-
-def own_price_kernel(blocks_hbm, tiles_hbm, dual, price, *scratch):
-    stream, sums = (blocks_hbm, tiles_hbm, *scratch[:4]), scratch[4:]
-    half = Half(False, *stream)
+    ahead.wait()
+
+
+def own_flow_kernel(blocks_hbm, tiles_hbm, picked, head, flows, blocks, block_sem, tiles, sems):
+    flow_pass(picked, Half(False, (blocks_hbm, tiles_hbm), tiles, blocks, block_sem, sems, head), flows, True)
+
+
+def held_flow_kernel(blocks_hbm, tiles_hbm, picked, tiles, flows, blocks, block_sem):
+    flow_pass(picked, Half(False, (blocks_hbm, tiles_hbm), tiles, blocks, block_sem), flows, True)
+
+
+def own_price_kernel(blocks_hbm, tiles_hbm, dual, price, head, tiles, blocks, block_sem, sems, ahead_sem, *sums):
+    half = Half(False, (blocks_hbm, tiles_hbm), tiles, blocks, block_sem, sems)
+    ahead = Ahead(half, head, ahead_sem)
     price_pass(dual, half, sums, True)
     for b in range(price.shape[0]):
         price[b] = total(sums, b)
+    ahead.wait()
 
 
 def middle_kernel(
-    blocks_hbm, tiles_hbm, dual, before, base, delta, price, inject_out, picked, flows, *scratch
+    blocks_hbm, tiles_hbm, dual, before, base, delta, head, price, inject_out, picked, flows,
+    blocks, block_sem, tiles, sems, *sums
 ):
-    stream, sums = (blocks_hbm, tiles_hbm, *scratch[:4]), scratch[4:]
-    half = Half(True, *stream)
+    half = Half(True, (blocks_hbm, tiles_hbm), tiles, blocks, block_sem, sems, head)
     price_pass(dual, half, sums, True)
 
     def start(b):
@@ -266,11 +294,10 @@
 
 
 def last_kernel(
-    blocks_hbm, tiles_hbm, dual, before, base, inject, delta, level, line_dual, unit_block, unit_lane, gain,
-    out, *scratch
+    blocks_hbm, tiles_hbm, dual, before, base, inject, delta, level, line_dual, unit_block, unit_lane, gain, head,
+    out, blocks, block_sem, tiles, sems, price, level_out, flat, *sums
 ):
-    stream, (price, level_out, flat, *sums) = (blocks_hbm, tiles_hbm, *scratch[:4]), scratch[4:]
-    half = Half(True, *stream)
+    half = Half(True, (blocks_hbm, tiles_hbm), tiles, blocks, block_sem, sems, head)
     count, hours, width = price.shape
     rows = flat.shape[0] // hours
     flat[...] = jnp.zeros_like(flat)
@@ -367,23 +394,30 @@
 
     half_bytes = ptdf_tiles.size
     half_flops = hours * ptdf_tiles.size
-    stream = [pltpu.VMEM((half_groups, *ptdf_tiles.shape[1:]), ptdf_tiles.dtype), pltpu.SemaphoreType.DMA((chips,))]
-    stream += [pltpu.SMEM(blocks.shape, blocks.dtype), pltpu.SemaphoreType.DMA]
-    sums = [pltpu.VMEM((bus_blocks, hours, width), jnp.float32)] * depth
-    large = pltpu.CompilerParams(vmem_limit_bytes=48 << 20)
+    ahead = max(1, chips // 4)
+
+    def tile_shape(chunks):
+        return jax.ShapeDtypeStruct((chunks * own_groups, *ptdf_tiles.shape[1:]), ptdf_tiles.dtype)
+
+    def scratch(shape):
+        return pltpu.VMEM(shape.shape, shape.dtype)
+
     picked_shape = jax.ShapeDtypeStruct((bus_blocks, hours, width), jnp.bfloat16)
     block_shape = jax.ShapeDtypeStruct((bus_blocks, hours, width), jnp.float32)
     level_shape = jax.ShapeDtypeStruct((hours, units), jnp.float32)
     flow_shape = jax.ShapeDtypeStruct((half_groups, hours, lines), jnp.float32)
-
-    def product(kernel, name, outs, operands, scratch, passes=1):
+    head_shape, half_shape, rest_shape = tile_shape(ahead), tile_shape(chips), tile_shape(chips - ahead)
+    sems, ahead_sems = pltpu.SemaphoreType.DMA((chips,)), pltpu.SemaphoreType.DMA((ahead,))
+    sums = [scratch(block_shape)] * depth
+
+    def product(kernel, name, outs, operands, temporary, passes=1, limit=48):
         return pl.pallas_call(
             kernel,
             out_shape=outs,
             in_specs=[HBM] * 2 + [VMEM] * len(operands),
             out_specs=[VMEM] * len(outs),
-            scratch_shapes=stream + scratch,
-            compiler_params=large,
+            scratch_shapes=[pltpu.SMEM(blocks.shape, blocks.dtype), pltpu.SemaphoreType.DMA, *temporary],
+            compiler_params=pltpu.CompilerParams(vmem_limit_bytes=limit << 20),
             cost_estimate=pl.CostEstimate(
                 flops=passes * half_flops, bytes_accessed=passes * half_bytes, transcendentals=0
             ),
@@ -422,19 +456,24 @@
         HBM,
     )
     came = lax.all_to_all(sent, "tm", split_axis=0, concat_axis=0, tiled=True)
-    away, base, level = product(
+    away, base, level, head = product(
         first_flow_kernel,
         "first_flow",
-        [flow_shape, picked_shape, level_shape],
+        [flow_shape, picked_shape, level_shape, head_shape],
         [came.reshape(hours * rows_in, width)],
-        [pltpu.VMEM((hours * rows_in, width), jnp.float32)],
+        [scratch(half_shape), sems, ahead_sems, pltpu.VMEM((hours * rows_in, width), jnp.float32)],
     )
     picked = base
     price = None
     line_dual = jnp.zeros((own_groups, hours, lines), jnp.float32)
     for iteration in range(ITERS):
         arrived = lax.ppermute(away, "tm", sibling)
-        (flows,) = product(own_flow_kernel, "own_flow", [flow_shape], [picked], [])
+        if iteration == 0:
+            (flows,) = product(
+                own_flow_kernel, "own_flow", [flow_shape], [picked, head], [scratch(rest_shape), sems]
+            )
+        else:
+            (flows,) = product(held_flow_kernel, "held_flow", [flow_shape], [picked, held], [], limit=40)
         pair = (flows + arrived).astype(jnp.bfloat16).reshape(chips, own_groups, hours, lines)
         parts = exchange(pair)
         if iteration == 0:
@@ -447,29 +486,45 @@
         shifted = jnp.sum(parts.astype(jnp.float32), axis=0) + line_dual
         clipped = jnp.clip(shifted, -own_limits, own_limits)
         line_dual = shifted - clipped
-        dual = lax.all_gather(
-            line_dual.astype(jnp.bfloat16), "tm", axis=0, axis_index_groups=same_core, tiled=True
-        )
+        dual = exchange(jnp.broadcast_to(line_dual.astype(jnp.bfloat16)[None], (chips, own_groups, hours, lines)))
+        dual = dual.reshape(half_groups, hours, lines)
         other = lax.ppermute(dual, "tm", sibling)
-        (before,) = product(own_price_kernel, "own_price", [block_shape], [dual], sums)
         if iteration < ITERS - 1:
+            before, head, held = product(
+                own_price_kernel,
+                "own_price",
+                [block_shape, head_shape, half_shape],
+                [dual],
+                [sems, ahead_sems] + sums,
+                limit=36,
+            )
             price, inject, picked, away = product(
                 middle_kernel,
                 "price_then_flow",
                 [block_shape, block_shape, picked_shape, flow_shape],
-                [other, before, base, delta],
-                sums,
+                [other, before, base, delta, head],
+                [scratch(rest_shape), sems] + sums,
                 2,
+                limit=36,
             )
         else:
+            before, head = product(
+                lambda *refs: own_price_kernel(*refs[:5], refs[7], *refs[5:7], *refs[8:]),
+                "own_price",
+                [block_shape, head_shape],
+                [dual],
+                [scratch(half_shape), sems, ahead_sems] + sums,
+            )
             (out,) = product(
                 last_kernel,
                 "last_price",
                 [jax.ShapeDtypeStruct((hours * rows_out, width), jnp.bfloat16)],
-                [other, before, base, inject, delta, level, line_dual, unit_block, unit_lane, gain],
+                [other, before, base, inject, delta, level, line_dual, unit_block, unit_lane, gain, head],
                 [
-                    pltpu.VMEM(block_shape.shape, jnp.float32),
-                    pltpu.VMEM(level_shape.shape, jnp.float32),
+                    scratch(rest_shape),
+                    sems,
+                    scratch(block_shape),
+                    scratch(level_shape),
                     pltpu.VMEM((hours * rows_out, width), jnp.float32),
                 ]
                 + sums,

time: 162 us -> 122 us (0.75)
  blocking collectives: 74.1 us -> 37.1 us
  Pallas kernels: 45.7 us -> 43 us
    all_gather x2 -> x0, blocking collectives: 61.7 us -> none  [shards(): lax.all_gather(line_dual.astype(jnp.bfloat16), 'tm', axis=0, axis_index_g...]
    all_to_all x0 -> x2, blocking collectives: none -> 24.5 us  [exchange(): lax.all_to_all(value, 'tm', split_axis=0, concat_axis=0, axis_index_group...]
    pallas_call x7, Pallas kernels: 38.7 us -> 36 us  [product(): pl.pallas_call(kernel, out_shape=outs, in_specs=[HBM] * 2 + [VMEM] * len(...]
  transfers between devices with their start and end apart: 7 -> 7, of which waited for: 3 -> 3; matrix products, arithmetic and copies ran while one was open for 1% -> 1% of each run, Pallas kernels for 15% -> 19%
where the time goes in v9:
time: 122 us
  Pallas kernels  43 us (35%)
  blocking collectives  37.1 us (30%)
  waiting for transfers between devices  20.7 us (17%)
  starting transfers between devices  15 us (12%)
  local copies, waits for them, and re-layouts  2.67 us (2%)
  other arithmetic  2.34 us (2%)
    pallas_call x7, Pallas kernels, product(): pl.pallas_call(kernel, out_shape=outs, in_specs=[HBM] * 2 + [VMEM] * len(...  36 us
    all_to_all x2, blocking collectives, exchange(): lax.all_to_all(value, 'tm', split_axis=0, concat_axis=0, axis_index_group...  24.5 us
    all_to_all x2, waiting for transfers between devices, exchange(): lax.all_to_all(value, 'tm', split_axis=0, concat_axis=0, axis_index_group...  12.7 us
    all_to_all x1, blocking collectives, shards(): lax.all_to_all(out.reshape(devices, hour_rows * rows_out, width), 'tm', s...  12.6 us
    all_to_all x1, waiting for transfers between devices, shards(): came = lax.all_to_all(sent, 'tm', split_axis=0, concat_axis=0, tiled=True)  7.99 us
    all_to_all x1, starting transfers between devices, shards(): came = lax.all_to_all(sent, 'tm', split_axis=0, concat_axis=0, tiled=True)  7.4 us
    all_to_all x2, starting transfers between devices, exchange(): lax.all_to_all(value, 'tm', split_axis=0, concat_axis=0, axis_index_group...  7 us
    pallas_call x4, Pallas kernels, small(): pl.pallas_call(kernel, out_shape=outs, in_specs=[VMEM] * (len(operands) -...  6.97 us
  transfers between devices with their start and end apart: 7, of which 3 were waited for; matrix products, arithmetic and copies ran while one was open for 1% of the time, Pallas kernels for 19%

profile of v9, /device:TPU:0, one launch (start us, length us, event | category | flops | bytes accessed | tf_op | source)
XLA Modules:
  0.0 121.7 jit_solution(9528333307394988844)
XLA Ops:
  0.6 0.9 copy-done.1
  1.5 0.7 copy-done.2
  2.2 0.8 pack.1
  3.1 7.4 %all-to-all-start = ((bf16[16,48,128]{2,1,0:T(8,128)(2,1)}), bf16[16,48,128]{2,1,0:T(8,128)(2,1)S(1)}, u32[]{:S(2)}, u32[]{:S(2)}) async-start(bf16[16,48,128]{2,1,0:T(8,128)(2,1)} %pack.1), calls=%async_computation | async-start | bytes 393216 | tf_op jit(solution)/shard_map/all_to_all | solution.py:458
  10.5 0.8 copy.10
  11.3 0.2 reshape.63.blocks_hbm.refs_0_
  11.5 8.0 %all-to-all-done = bf16[16,48,128]{2,1,0:T(8,128)(2,1)S(1)} async-done(((bf16[16,48,128]{2,1,0:T(8,128)(2,1)}), bf16[16,48,128]{2,1,0:T(8,128)(2,1)S(1)}, u32[]{:S(2)}, u32[]{:S(2)}) %all-to-all-start) | async-done | bytes 196640 | tf_op jit(solution)/shard_map/all_to_all | solution.py:458
  19.5 5.3 %first_flow.1 = (f32[64,16,128]{2,1,0:T(8,128)S(1)}, bf16[18,16,128]{2,1,0:T(8,128)(2,1)S(1)}, f32[16,2048]{1,0:T(8,128)S(1)}, bf16[16,5,128,128]{3,2,1,0:T(8,128)(2,1)S(1)}) custom-call(s32[640]{0:T(1024)S(1)} %reshape.63.blocks_hbm.refs_0_, bf16[128,5,128,128]{3,2,1,0:T(8,128)(2,1)} %tiles_hbm.11, bf16[768,128]{1,0:T(8,128)(2,1)S(1)} %bitcast.21), custom_call_target="tpu_custom_call" | custom-call | flops 167772160 | bytes 10485760 | tf_op jit(solution)/shard_map/first_flow/pallas_call | solution.py:414
  24.7 0.1 collective-permute-start
  24.8 0.0 copy-start.3
  24.8 4.4 %own_flow.1 = f32[64,16,128]{2,1,0:T(8,128)S(1)} custom-call(s32[640]{0:T(1024)S(1)} %reshape.63.blocks_hbm.refs_0_, bf16[128,5,128,128]{3,2,1,0:T(8,128)(2,1)} %tiles_hbm.11, bf16[18,16,128]{2,1,0:T(8,128)(2,1)S(1)} %get-tuple-element.27.picked.base, bf16[16,5,128,128]{3,2,1,0:T(8,128)(2,1)S(1)} %get-tuple-element.28.head), custom_call_target="tpu_custom_call" | custom-call | flops 167772160 | bytes 10485760 | tf_op jit(solution)/shard_map/own_flow/pallas_call | solution.py:414
  29.2 0.0 collective-permute-done
  29.2 0.8 add_convert_fusion.1
  30.0 3.4 %all-to-all-start.1 = ((bf16[8,8,16,128]{3,2,1,0:T(8,128)(2,1)}), bf16[8,8,16,128]{3,2,1,0:T(8,128)(2,1)S(1)}, u32[]{:S(2)}, u32[]{:S(2)}) async-start(bf16[8,8,16,128]{3,2,1,0:T(8,128)(2,1)} %bitcast.1), calls=%async_computation.1 | async-start | bytes 524288 | tf_op jit(solution)/shard_map/all_to_all | solution.py:393
  33.4 0.7 dynamic-slice_bitcast_fusion
  34.1 1.9 %storage.2.delta = f32[18,16,128]{2,1,0:T(8,128)S(1)} custom-call(f32[16,2048]{1,0:T(8,128)S(1)} %get-tuple-element.39.level, s32[1,2048]{1,0:T(1,128)S(1)} %bitcast.26, s32[1,2048]{1,0:T(1,128)S(1)} %bitcast.23), custom_call_target="tpu_custom_call" | custom-call | flops 167772160 | bytes 4194304 | tf_op jit(solution)/shard_map/storage/pallas_call | solution.py:428
  36.0 7.1 %all-to-all-done.1 = bf16[8,8,16,128]{3,2,1,0:T(8,128)(2,1)S(1)} async-done(((bf16[8,8,16,128]{3,2,1,0:T(8,128)(2,1)}), bf16[8,8,16,128]{3,2,1,0:T(8,128)(2,1)S(1)}, u32[]{:S(2)}, u32[]{:S(2)}) %all-to-all-start.1) | async-done | bytes 262176 | tf_op jit(solution)/shard_map/all_to_all | solution.py:393
  43.3 12.5 %all_to_all.30 = bf16[8,8,16,128]{3,2,1,0:T(8,128)(2,1)S(1)} all-to-all(bf16[8,8,16,128]{3,2,1,0:T(8,128)(2,1)S(1)} %broadcast_in_dim.4), channel_id=1, replica_groups={{0,2,4,6,8,10,12,14},{1,3,5,7,9,11,13,15},{16,18,20,22,24,26,28,30},{17..., dimensions={0} | all-to-all | bytes 524288 | tf_op jit(solution)/shard_map/all_to_all | solution.py:393
  55.8 0.0 collective-permute-start.1
  55.8 4.9 %own_price.2 = (f32[18,16,128]{2,1,0:T(8,128)S(1)}, bf16[16,5,128,128]{3,2,1,0:T(8,128)(2,1)S(1)}, bf16[64,5,128,128]{3,2,1,0:T(8,128)(2,1)S(1)}) custom-call(s32[640]{0:T(1024)S(1)} %reshape.63.blocks_hbm.refs_0_, bf16[128,5,128,128]{3,2,1,0:T(8,128)(2,1)} %tiles_hbm.11, bf16[64,16,128]{2,1,0:T(8,128)(2,1)S(1)} %bitcast.18), custom_call_target="tpu_custom_call" | custom-call | flops 167772160 | bytes 10485760 | tf_op jit(solution)/shard_map/own_price/pallas_call | solution.py:414
  60.7 7.1 %price_then_flow.1 = (f32[18,16,128]{2,1,0:T(8,128)S(1)}, f32[18,16,128]{2,1,0:T(8,128)S(1)}, bf16[18,16,128]{2,1,0:T(8,128)(2,1)S(1)}, f32[64,16,128]{2,1,0:T(8,128)S(1)}) custom-call(s32[640]{0:T(1024)S(1)} %reshape.63.blocks_hbm.refs_0_, bf16[128,5,128,128]{3,2,1,0:T(8,128)(2,1)} %tiles_hbm.11, bf16[64,16,128]{2,1,0:T(8,128)(2,1)S(1)} %collective-permute-done.1.dual, ...), custom_call_target="tpu_custom_call" | custom-call | flops 335544320 | bytes 20971520 | tf_op jit(solution)/shard_map/price_then_flow/pallas_call | solution.py:414
  67.8 0.6 collective-permute-start.2
  68.4 3.9 %held_flow.1 = f32[64,16,128]{2,1,0:T(8,128)S(1)} custom-call(s32[640]{0:T(1024)S(1)} %reshape.63.blocks_hbm.refs_0_, bf16[128,5,128,128]{3,2,1,0:T(8,128)(2,1)} %tiles_hbm.11, bf16[18,16,128]{2,1,0:T(8,128)(2,1)S(1)} %get-tuple-element.35.picked, bf16[64,5,128,128]{3,2,1,0:T(8,128)(2,1)S(1)} %get-tuple-element.36.tiles), custom_call_target="tpu_custom_call" | custom-call | flops 167772160 | bytes 10485760 | tf_op jit(solution)/shard_map/held_flow/pallas_call | solution.py:414
  72.4 0.8 add_convert_fusion
  73.1 3.6 %all-to-all-start.3 = ((bf16[8,8,16,128]{3,2,1,0:T(8,128)(2,1)}), bf16[8,8,16,128]{3,2,1,0:T(8,128)(2,1)S(1)}, u32[]{:S(2)}, u32[]{:S(2)}) async-start(bf16[8,8,16,128]{3,2,1,0:T(8,128)(2,1)} %bitcast.8), calls=%async_computation.3 | async-start | bytes 524288 | tf_op jit(solution)/shard_map/all_to_all | solution.py:393
  76.7 3.5 %storage.3 = (f32[16,2048]{1,0:T(8,128)S(1)}, f32[18,16,128]{2,1,0:T(8,128)S(1)}) custom-call(f32[18,16,128]{2,1,0:T(8,128)S(1)} %get-tuple-element.38.price, f32[16,2048]{1,0:T(8,128)S(1)} %get-tuple-element.39.level, s32[1,2048]{1,0:T(1,128)S(1)} %bitcast.27, s32[1,2048]{1,0:T(1,128)S(1)} %bitcast.24, f32[1,2048]{1,0:T(1,128)S(1)} %bitcast.29), custom_call_target="tpu_custom_call" | custom-call | flops 167772160 | bytes 4194304 | tf_op jit(solution)/shard_map/storage/pallas_call | solution.py:428
  80.3 5.6 %all-to-all-done.3 = bf16[8,8,16,128]{3,2,1,0:T(8,128)(2,1)S(1)} async-done(((bf16[8,8,16,128]{3,2,1,0:T(8,128)(2,1)}), bf16[8,8,16,128]{3,2,1,0:T(8,128)(2,1)S(1)}, u32[]{:S(2)}, u32[]{:S(2)}) %all-to-all-start.3) | async-done | bytes 262176 | tf_op jit(solution)/shard_map/all_to_all | solution.py:393
  86.0 12.0 %all_to_all.31 = bf16[8,8,16,128]{3,2,1,0:T(8,128)(2,1)S(1)} all-to-all(bf16[8,8,16,128]{3,2,1,0:T(8,128)(2,1)S(1)} %broadcast_in_dim.5), channel_id=1, replica_groups={{0,2,4,6,8,10,12,14},{1,3,5,7,9,11,13,15},{16,18,20,22,24,26,28,30},{17..., dimensions={0} | all-to-all | bytes 524288 | tf_op jit(solution)/shard_map/all_to_all | solution.py:393
  97.9 4.9 %own_price.3 = (f32[18,16,128]{2,1,0:T(8,128)S(1)}, bf16[16,5,128,128]{3,2,1,0:T(8,128)(2,1)S(1)}) custom-call(s32[640]{0:T(1024)S(1)} %reshape.63.blocks_hbm.refs_0_, bf16[128,5,128,128]{3,2,1,0:T(8,128)(2,1)} %tiles_hbm.11, bf16[64,16,128]{2,1,0:T(8,128)(2,1)S(1)} %bitcast.20), custom_call_target="tpu_custom_call" | custom-call | flops 167772160 | bytes 10485760 | tf_op jit(solution)/shard_map/own_price/pallas_call | solution.py:414
  102.8 5.6 %last_price.1 = bf16[768,128]{1,0:T(8,128)(2,1)S(1)} custom-call(s32[640]{0:T(1024)S(1)} %reshape.63.blocks_hbm.refs_0_, bf16[128,5,128,128]{3,2,1,0:T(8,128)(2,1)} %tiles_hbm.11, bf16[64,16,128]{2,1,0:T(8,128)(2,1)S(1)} %collective-permute-done.3.dual, f32[18,16,128]{2,1,0:T(8,128)S(1)} %get-tuple-element.43.before, ...), custom_call_target="tpu_custom_call" | custom-call | flops 167772160 | bytes 10485760 | tf_op jit(solution)/shard_map/last_price/pallas_call | solution.py:414
  108.4 12.6 %all_to_all.32.back = bf16[16,48,128]{2,1,0:T(8,128)(2,1)S(1)} all-to-all(bf16[16,48,128]{2,1,0:T(8,128)(2,1)S(1)} %bitcast.22), channel_id=1, replica_groups=mesh['scen'=2,'tm'=16] {'tm'}, dimensions={0} | all-to-all | bytes 393216 | tf_op jit(solution)/shard_map/all_to_all | solution.py:533
  121.0 0.7 unpack.1
  (16 shorter events, 0.2 us)
Async XLA Ops:
  0.6 0.9 copy-start.1
  1.5 0.7 copy-start.2
  3.1 16.4 %all-to-all-start = ((bf16[16,48,128]{2,1,0:T(8,128)(2,1)}), bf16[16,48,128]{2,1,0:T(8,128)(2,1)S(1)}, u32[]{:S(2)}, u32[]{:S(2)}) async-start(bf16[16,48,128]{2,1,0:T(8,128)(2,1)} %pack.1), calls=%async_computation | async-start | bytes 393216 | tf_op jit(solution)/shard_map/all_to_all | solution.py:458
  24.7 4.5 %collective-permute-start = (f32[64,16,128]{2,1,0:T(8,128)S(1)}, f32[64,16,128]{2,1,0:T(8,128)S(1)}, u32[]{:S(2)}, u32[]{:S(2)}) collective-permute-start(f32[64,16,128]{2,1,0:T(8,128)S(1)} %get-tuple-element.29), channel_id=1, source_target_pairs={{0,1},{1,0},{2,3},{3,2},{4,5},{5,4},{6,7},{7,6},{8,9},{9,8},{10,11... | collective-permute-start | bytes 1572872 | tf_op jit(solution)/shard_map/ppermute | solution.py:470
  24.8 9.3 %copy-start.3 = (s32[2048]{0:T(1024)S(1)}, s32[2048]{0:T(1024)}, u32[]{:S(2)}) copy-start(s32[2048]{0:T(1024)} %param.11) | copy-start | bytes 24580
  30.0 13.2 %all-to-all-start.1 = ((bf16[8,8,16,128]{3,2,1,0:T(8,128)(2,1)}), bf16[8,8,16,128]{3,2,1,0:T(8,128)(2,1)S(1)}, u32[]{:S(2)}, u32[]{:S(2)}) async-start(bf16[8,8,16,128]{3,2,1,0:T(8,128)(2,1)} %bitcast.1), calls=%async_computation.1 | async-start | bytes 524288 | tf_op jit(solution)/shard_map/all_to_all | solution.py:393
  55.8 4.9 %collective-permute-start.1 = (bf16[64,16,128]{2,1,0:T(8,128)(2,1)S(1)}, bf16[64,16,128]{2,1,0:T(8,128)(2,1)S(1)}, u32[]{:S(2)}, u32[]{:S(2)}) collective-permute-start(bf16[64,16,128]{2,1,0:T(8,128)(2,1)S(1)} %bitcast.17), channel_id=1, source_target_pairs={{0,1},{1,0},{2,3},{3,2},{4,5},{5,4},{6,7},{7,6},{8,9},{9,8},{10,11... | collective-permute-start | bytes 786440 | tf_op jit(solution)/shard_map/ppermute | solution.py:491
  67.8 4.5 %collective-permute-start.2 = (f32[64,16,128]{2,1,0:T(8,128)S(1)}, f32[64,16,128]{2,1,0:T(8,128)S(1)}, u32[]{:S(2)}, u32[]{:S(2)}) collective-permute-start(f32[64,16,128]{2,1,0:T(8,128)S(1)} %get-tuple-element.37), channel_id=1, source_target_pairs={{0,1},{1,0},{2,3},{3,2},{4,5},{5,4},{6,7},{7,6},{8,9},{9,8},{10,11... | collective-permute-start | bytes 1572872 | tf_op jit(solution)/shard_map/ppermute | solution.py:470
  68.4 8.3 %copy-start = (f32[2048]{0:T(1024)S(1)}, f32[2048]{0:T(1024)}, u32[]{:S(2)}) copy-start(f32[2048]{0:T(1024)} %param.12) | copy-start | bytes 24580
  73.1 12.7 %all-to-all-start.3 = ((bf16[8,8,16,128]{3,2,1,0:T(8,128)(2,1)}), bf16[8,8,16,128]{3,2,1,0:T(8,128)(2,1)S(1)}, u32[]{:S(2)}, u32[]{:S(2)}) async-start(bf16[8,8,16,128]{3,2,1,0:T(8,128)(2,1)} %bitcast.8), calls=%async_computation.3 | async-start | bytes 524288 | tf_op jit(solution)/shard_map/all_to_all | solution.py:393
  97.9 4.9 %collective-permute-start.3 = (bf16[64,16,128]{2,1,0:T(8,128)(2,1)S(1)}, bf16[64,16,128]{2,1,0:T(8,128)(2,1)S(1)}, u32[]{:S(2)}, u32[]{:S(2)}) collective-permute-start(bf16[64,16,128]{2,1,0:T(8,128)(2,1)S(1)} %bitcast.19), channel_id=1, source_target_pairs={{0,1},{1,0},{2,3},{3,2},{4,5},{5,4},{6,7},{7,6},{8,9},{9,8},{10,11... | collective-permute-start | bytes 786440 | tf_op jit(solution)/shard_map/ppermute | solution.py:491

commit v10 on v9

--- a/solution.py
+++ b/solution.py
@@ -18,7 +18,7 @@
 VMEM = pl.BlockSpec(memory_space=pltpu.VMEM)
 HBM = pl.BlockSpec(memory_space=pl.ANY)
 SMALL = pltpu.CompilerParams(vmem_limit_bytes=12 << 20)
-STRAIGHT = 16
+STRAIGHT = 64
 
 
 class Half:
@@ -46,7 +46,8 @@
         return pltpu.make_async_copy(self.tiles_hbm.at[there], self.tiles.at[here], self.sems.at[chunk])
 
     def each_four(self, wait, four):
-        per = max(1, STRAIGHT // self.own)
+        rest = self.chunks - self.ahead
+        per = max(n for n in range(1, rest + 1) if rest % n == 0 and n * self.own <= max(STRAIGHT, self.own))
 
         def one(chunk, ref, at):
             for sub in range(0, self.own, 4):
@@ -69,7 +70,10 @@
             self.block_copy.wait()
         for chunk in range(self.ahead):
             one(chunk, self.head, chunk * self.own)
-        lax.fori_loop(0, (self.chunks - self.ahead) // per, body, 0)
+        if per == rest:
+            body(0, 0)
+        else:
+            lax.fori_loop(0, rest // per, body, 0)
 
 
 class Ahead:
@@ -218,6 +222,26 @@
     lax.fori_loop(0, level.shape[1] // span, body, 0)
 
 
+def storage_pass(level, unit_block, unit_lane, delta):
+    count, hours, width = delta.shape
+    span = 2 * width
+    delta[...] = jnp.zeros_like(delta)
+
+    def body(c, carry):
+        cols = pl.ds(pl.multiple_of(c * span, span), span)
+        now = level[:, cols]
+        charge = step_size * (now - earlier(now))
+        hot = one_hot(unit_lane, cols, width)
+        block = jnp.broadcast_to(unit_block[:, cols], (hours, span))
+        held = jnp.concatenate([jnp.where(block == b, charge, 0.0) for b in range(count)], axis=0)
+        part = lax.dot_general(held.astype(jnp.bfloat16), hot, NT, preferred_element_type=jnp.float32)
+        for b in range(count):
+            delta[b] = delta[b] + part[b * hours : (b + 1) * hours]
+        return carry
+
+    lax.fori_loop(0, level.shape[1] // span, body, 0)
+
+
 def pack_kernel(base, soc_hbm, out, flat, soc, sem):
     devices, rows, width = out.shape
     hour_rows = soc.shape[0]
@@ -266,13 +290,32 @@
     flow_pass(picked, Half(False, (blocks_hbm, tiles_hbm), tiles, blocks, block_sem), flows, True)
 
 
-def own_price_kernel(blocks_hbm, tiles_hbm, dual, price, head, tiles, blocks, block_sem, sems, ahead_sem, *sums):
-    half = Half(False, (blocks_hbm, tiles_hbm), tiles, blocks, block_sem, sems)
-    ahead = Ahead(half, head, ahead_sem)
+def own_price(half, ahead, dual, price, sums):
     price_pass(dual, half, sums, True)
     for b in range(price.shape[0]):
         price[b] = total(sums, b)
     ahead.wait()
+
+
+def own_price_kernel(
+    blocks_hbm, tiles_hbm, dual, level, unit_block, unit_lane, before, delta, head, tiles,
+    blocks, block_sem, sems, ahead_sem, *sums
+):
+    half = Half(False, (blocks_hbm, tiles_hbm), tiles, blocks, block_sem, sems)
+    ahead = Ahead(half, head, ahead_sem)
+    storage_pass(level, unit_block, unit_lane, delta)
+    own_price(half, ahead, dual, before, sums)
+
+
+def own_price_level_kernel(
+    blocks_hbm, tiles_hbm, dual, price, level, unit_block, unit_lane, gain, before, level_out, delta, head,
+    blocks, block_sem, tiles, sems, ahead_sem, *sums
+):
+    half = Half(False, (blocks_hbm, tiles_hbm), tiles, blocks, block_sem, sems)
+    ahead = Ahead(half, head, ahead_sem)
+    level_pass(price, level, unit_block, unit_lane, gain, level_out, False)
+    storage_pass(level_out, unit_block, unit_lane, delta)
+    own_price(half, ahead, dual, before, sums)
 
 
 def middle_kernel(
@@ -333,36 +376,6 @@
             part = came[count : count + units]
             sum_levels = part if sum_levels is None else sum_levels + part
         level[r] = sum_levels
-
-
-def storage_pass(level, unit_block, unit_lane, delta):
-    count, hours, width = delta.shape
-    span = 2 * width
-    delta[...] = jnp.zeros_like(delta)
-
-    def body(c, carry):
-        cols = pl.ds(pl.multiple_of(c * span, span), span)
-        now = level[:, cols]
-        charge = high_low(step_size * (now - earlier(now)), 0).astype(jnp.float32)
-        hot = one_hot(unit_lane, cols, width)
-        block = jnp.broadcast_to(unit_block[:, cols], charge.shape)
-        held = jnp.concatenate([jnp.where(block == b, charge, 0.0) for b in range(count)], axis=0)
-        part = lax.dot_general(held.astype(jnp.bfloat16), hot, NT, preferred_element_type=jnp.float32)
-        for b in range(count):
-            high, low = part[2 * b * hours : (2 * b + 1) * hours], part[(2 * b + 1) * hours : (2 * b + 2) * hours]
-            delta[b] = delta[b] + (high + low)
-        return carry
-
-    lax.fori_loop(0, level.shape[1] // span, body, 0)
-
-
-def storage_kernel(level, unit_block, unit_lane, delta):
-    storage_pass(level, unit_block, unit_lane, delta)
-
-
-def level_kernel(price, level, unit_block, unit_lane, gain, level_out, delta):
-    level_pass(price, level, unit_block, unit_lane, gain, level_out, False)
-    storage_pass(level_out, unit_block, unit_lane, delta)
 
 
 def shards(base_injection, ptdf_tiles, tile_block, limits, stor_bus, stor_gain, soc_init):
@@ -456,6 +469,9 @@
         HBM,
     )
     came = lax.all_to_all(sent, "tm", split_axis=0, concat_axis=0, tiled=True)
+    came, own_limits, unit_block, unit_lane, gain, blocks = lax.optimization_barrier(
+        (came, own_limits, unit_block, unit_lane, gain, blocks)
+    )
     away, base, level, head = product(
         first_flow_kernel,
         "first_flow",
@@ -476,13 +492,6 @@
             (flows,) = product(held_flow_kernel, "held_flow", [flow_shape], [picked, held], [], limit=40)
         pair = (flows + arrived).astype(jnp.bfloat16).reshape(chips, own_groups, hours, lines)
         parts = exchange(pair)
-        if iteration == 0:
-            (delta,) = small(storage_kernel, "storage", [block_shape], [level, unit_block, unit_lane])
-        else:
-            level, delta = small(
-                level_kernel, "storage", [level_shape, block_shape], [price, level, unit_block, unit_lane, gain]
-            )
-        parts, level, delta = lax.optimization_barrier((parts, level, delta))
         shifted = jnp.sum(parts.astype(jnp.float32), axis=0) + line_dual
         clipped = jnp.clip(shifted, -own_limits, own_limits)
         line_dual = shifted - clipped
@@ -490,11 +499,11 @@
         dual = dual.reshape(half_groups, hours, lines)
         other = lax.ppermute(dual, "tm", sibling)
         if iteration < ITERS - 1:
-            before, head, held = product(
+            before, delta, head, held = product(
                 own_price_kernel,
                 "own_price",
-                [block_shape, head_shape, half_shape],
-                [dual],
+                [block_shape, block_shape, head_shape, half_shape],
+                [dual, level, unit_block, unit_lane],
                 [sems, ahead_sems] + sums,
                 limit=36,
             )
@@ -508,11 +517,11 @@
                 limit=36,
             )
         else:
-            before, head = product(
-                lambda *refs: own_price_kernel(*refs[:5], refs[7], *refs[5:7], *refs[8:]),
+            before, level, delta, head = product(
+                own_price_level_kernel,
                 "own_price",
-                [block_shape, head_shape],
-                [dual],
+                [block_shape, level_shape, block_shape, head_shape],
+                [dual, price, level, unit_block, unit_lane, gain],
                 [scratch(half_shape), sems, ahead_sems] + sums,
             )
             (out,) = product(

time: 122 us -> 122 us (level)
  blocking collectives: 37.1 us -> 49.5 us
  Pallas kernels: 43 us -> 38.2 us
  waiting for transfers between devices: 20.7 us -> 17 us
  starting transfers between devices: 15 us -> 11.5 us
    all_to_all x2 -> x3, blocking collectives: 24.5 us -> 36.9 us  [exchange(): lax.all_to_all(value, 'tm', split_axis=0, concat_axis=0, axis_index_group...]
    pallas_call x4 -> x2, Pallas kernels: 6.97 us -> 1.54 us  [small(): pl.pallas_call(kernel, out_shape=outs, in_specs=[VMEM] * (len(operands) -...]
    all_to_all x2 -> x1, starting transfers between devices: 7 us -> 3.41 us  [exchange(): lax.all_to_all(value, 'tm', split_axis=0, concat_axis=0, axis_index_group...]
    all_to_all x2 -> x1, waiting for transfers between devices: 12.7 us -> 9.78 us  [exchange(): lax.all_to_all(value, 'tm', split_axis=0, concat_axis=0, axis_index_group...]
  transfers between devices with their start and end apart: 7 -> 6, of which waited for: 3 -> 2; matrix products, arithmetic and copies ran while one was open for 1% -> 1% of each run, Pallas kernels for 19% -> 16%
where the time goes in v10:
time: 122 us; the launch traced here: 121 us
  blocking collectives  49.5 us (41%)
  Pallas kernels  38.2 us (31%)
  waiting for transfers between devices  17 us (14%)
  starting transfers between devices  11.5 us (9%)
  local copies, waits for them, and re-layouts  2.72 us (2%)
  other arithmetic  1.67 us (1%)
    all_to_all x3, blocking collectives, exchange(): lax.all_to_all(value, 'tm', split_axis=0, concat_axis=0, axis_index_group...  36.9 us
    pallas_call x7, Pallas kernels, product(): pl.pallas_call(kernel, out_shape=outs, in_specs=[HBM] * 2 + [VMEM] * len(...  36.7 us
    all_to_all x1, blocking collectives, shards(): lax.all_to_all(out.reshape(devices, hour_rows * rows_out, width), 'tm', s...  12.6 us
    all_to_all x1, waiting for transfers between devices, exchange(): lax.all_to_all(value, 'tm', split_axis=0, concat_axis=0, axis_index_group...  9.78 us
    all_to_all x1, starting transfers between devices, shards(): came = lax.all_to_all(sent, 'tm', split_axis=0, concat_axis=0, tiled=True)  7.4 us
    all_to_all x1, waiting for transfers between devices, shards(): came = lax.all_to_all(sent, 'tm', split_axis=0, concat_axis=0, tiled=True)  7.24 us
    all_to_all x1, starting transfers between devices, exchange(): lax.all_to_all(value, 'tm', split_axis=0, concat_axis=0, axis_index_group...  3.41 us
    unnamed x9, local copies, waits for them, and re-layouts  2.44 us
  transfers between devices with their start and end apart: 6, of which 2 were waited for; matrix products, arithmetic and copies ran while one was open for 1% of the time, Pallas kernels for 16%

profile of v10, /device:TPU:0, one launch (start us, length us, event | category | flops | bytes accessed | tf_op | source)
XLA Modules:
  0.0 121.5 jit_solution(12072630777236103190)
XLA Ops:
  0.6 0.0 copy-start
  0.7 0.9 copy-done.2
  1.6 0.7 copy-done.3
  2.3 0.8 pack.1
  3.1 7.4 %all-to-all-start = ((bf16[16,48,128]{2,1,0:T(8,128)(2,1)}), bf16[16,48,128]{2,1,0:T(8,128)(2,1)S(1)}, u32[]{:S(2)}, u32[]{:S(2)}) async-start(bf16[16,48,128]{2,1,0:T(8,128)(2,1)} %pack.1), calls=%async_computation | async-start | bytes 393216 | tf_op jit(solution)/shard_map/all_to_all | solution.py:471
  10.5 0.8 copy.10
  11.3 0.2 reshape.67.blocks_hbm
  11.6 0.7 add_select_fusion
  12.3 7.2 %all-to-all-done = bf16[16,48,128]{2,1,0:T(8,128)(2,1)S(1)} async-done(((bf16[16,48,128]{2,1,0:T(8,128)(2,1)}), bf16[16,48,128]{2,1,0:T(8,128)(2,1)S(1)}, u32[]{:S(2)}, u32[]{:S(2)}) %all-to-all-start) | async-done | bytes 196640 | tf_op jit(solution)/shard_map/all_to_all | solution.py:471
  19.5 5.3 %first_flow.1 = (f32[64,16,128]{2,1,0:T(8,128)S(1)}, bf16[18,16,128]{2,1,0:T(8,128)(2,1)S(1)}, f32[16,2048]{1,0:T(8,128)S(1)}, bf16[16,5,128,128]{3,2,1,0:T(8,128)(2,1)S(1)}) custom-call(s32[640]{0:T(1024)S(1)} %reshape.67.blocks_hbm, bf16[128,5,128,128]{3,2,1,0:T(8,128)(2,1)} %tiles_hbm.13, bf16[768,128]{1,0:T(8,128)(2,1)S(1)} %bitcast.21), custom_call_target="tpu_custom_call" | custom-call | flops 167772160 | bytes 10485760 | tf_op jit(solution)/shard_map/first_flow/pallas_call | solution.py:427
  24.8 0.1 collective-permute-start
  24.9 4.4 %own_flow.1 = f32[64,16,128]{2,1,0:T(8,128)S(1)} custom-call(s32[640]{0:T(1024)S(1)} %reshape.67.blocks_hbm, bf16[128,5,128,128]{3,2,1,0:T(8,128)(2,1)} %tiles_hbm.13, bf16[18,16,128]{2,1,0:T(8,128)(2,1)S(1)} %get-tuple-element.30.picked.base, bf16[16,5,128,128]{3,2,1,0:T(8,128)(2,1)S(1)} %get-tuple-element.31.head), custom_call_target="tpu_custom_call" | custom-call | flops 167772160 | bytes 10485760 | tf_op jit(solution)/shard_map/own_flow/pallas_call | solution.py:427
  29.2 0.0 collective-permute-done
  29.3 0.8 add_convert_fusion.1
  30.0 3.4 %all-to-all-start.1 = ((bf16[8,8,16,128]{3,2,1,0:T(8,128)(2,1)}), bf16[8,8,16,128]{3,2,1,0:T(8,128)(2,1)S(1)}, u32[]{:S(2)}, u32[]{:S(2)}) async-start(bf16[8,8,16,128]{3,2,1,0:T(8,128)(2,1)} %bitcast.5), calls=%async_computation.1 | async-start | bytes 524288 | tf_op jit(solution)/shard_map/all_to_all | solution.py:406
  33.4 9.8 %all-to-all-done.1 = bf16[8,8,16,128]{3,2,1,0:T(8,128)(2,1)S(1)} async-done(((bf16[8,8,16,128]{3,2,1,0:T(8,128)(2,1)}), bf16[8,8,16,128]{3,2,1,0:T(8,128)(2,1)S(1)}, u32[]{:S(2)}, u32[]{:S(2)}) %all-to-all-start.1) | async-done | bytes 262176 | tf_op jit(solution)/shard_map/all_to_all | solution.py:406
  43.3 12.5 %all_to_all.30 = bf16[8,8,16,128]{3,2,1,0:T(8,128)(2,1)S(1)} all-to-all(bf16[8,8,16,128]{3,2,1,0:T(8,128)(2,1)S(1)} %broadcast_in_dim.4), channel_id=1, replica_groups={{0,2,4,6,8,10,12,14},{1,3,5,7,9,11,13,15},{16,18,20,22,24,26,28,30},{17..., dimensions={0} | all-to-all | bytes 524288 | tf_op jit(solution)/shard_map/all_to_all | solution.py:406
  55.8 0.0 collective-permute-start.1
  55.8 4.9 %own_price.2 = (f32[18,16,128]{2,1,0:T(8,128)S(1)}, f32[18,16,128]{2,1,0:T(8,128)S(1)}, bf16[16,5,128,128]{3,2,1,0:T(8,128)(2,1)S(1)}, bf16[64,5,128,128]{3,2,1,0:T(8,128)(2,1)S(1)}) custom-call(s32[640]{0:T(1024)S(1)} %reshape.67.blocks_hbm, bf16[128,5,128,128]{3,2,1,0:T(8,128)(2,1)} %tiles_hbm.13, bf16[64,16,128]{2,1,0:T(8,128)(2,1)S(1)} %bitcast.20, ...), custom_call_target="tpu_custom_call" | custom-call | flops 167772160 | bytes 10485760 | tf_op jit(solution)/shard_map/own_price/pallas_call | solution.py:427
  60.7 6.8 %price_then_flow.1 = (f32[18,16,128]{2,1,0:T(8,128)S(1)}, f32[18,16,128]{2,1,0:T(8,128)S(1)}, bf16[18,16,128]{2,1,0:T(8,128)(2,1)S(1)}, f32[64,16,128]{2,1,0:T(8,128)S(1)}) custom-call(s32[640]{0:T(1024)S(1)} %reshape.67.blocks_hbm, bf16[128,5,128,128]{3,2,1,0:T(8,128)(2,1)} %tiles_hbm.13, bf16[64,16,128]{2,1,0:T(8,128)(2,1)S(1)} %collective-permute-done.1.dual, ...), custom_call_target="tpu_custom_call" | custom-call | flops 335544320 | bytes 20971520 | tf_op jit(solution)/shard_map/price_then_flow/pallas_call | solution.py:427
  67.5 0.6 collective-permute-start.2
  68.1 3.6 %held_flow.1 = f32[64,16,128]{2,1,0:T(8,128)S(1)} custom-call(s32[640]{0:T(1024)S(1)} %reshape.67.blocks_hbm, bf16[128,5,128,128]{3,2,1,0:T(8,128)(2,1)} %tiles_hbm.13, bf16[18,16,128]{2,1,0:T(8,128)(2,1)S(1)} %get-tuple-element.40.picked, bf16[64,5,128,128]{3,2,1,0:T(8,128)(2,1)S(1)} %get-tuple-element.41.tiles), custom_call_target="tpu_custom_call" | custom-call | flops 167772160 | bytes 10485760 | tf_op jit(solution)/shard_map/held_flow/pallas_call | solution.py:427
  71.7 0.0 copy-start.1
  71.7 0.0 collective-permute-done.2
  71.7 0.1 add_convert_fusion
  71.8 12.5 %all_to_all.31 = bf16[8,8,16,128]{3,2,1,0:T(8,128)(2,1)S(1)} all-to-all(bf16[8,8,16,128]{3,2,1,0:T(8,128)(2,1)S(1)} %bitcast.31), channel_id=1, replica_groups={{0,2,4,6,8,10,12,14},{1,3,5,7,9,11,13,15},{16,18,20,22,24,26,28,30},{17..., dimensions={0} | all-to-all | bytes 524288 | tf_op jit(solution)/shard_map/all_to_all | solution.py:406
  84.4 12.0 %all_to_all.32 = bf16[8,8,16,128]{3,2,1,0:T(8,128)(2,1)S(1)} all-to-all(bf16[8,8,16,128]{3,2,1,0:T(8,128)(2,1)S(1)} %broadcast_in_dim.5), channel_id=1, replica_groups={{0,2,4,6,8,10,12,14},{1,3,5,7,9,11,13,15},{16,18,20,22,24,26,28,30},{17..., dimensions={0} | all-to-all | bytes 524288 | tf_op jit(solution)/shard_map/all_to_all | solution.py:406
  96.3 0.0 collective-permute-start.3
  96.3 6.3 %own_price.3 = (f32[18,16,128]{2,1,0:T(8,128)S(1)}, f32[16,2048]{1,0:T(8,128)S(1)}, f32[18,16,128]{2,1,0:T(8,128)S(1)}, bf16[16,5,128,128]{3,2,1,0:T(8,128)(2,1)S(1)}) custom-call(s32[640]{0:T(1024)S(1)} %reshape.67.blocks_hbm, bf16[128,5,128,128]{3,2,1,0:T(8,128)(2,1)} %tiles_hbm.13, bf16[64,16,128]{2,1,0:T(8,128)(2,1)S(1)} %bitcast.18, ...), custom_call_target="tpu_custom_call" | custom-call | flops 167772160 | bytes 10485760 | tf_op jit(solution)/shard_map/own_price/pallas_call | solution.py:427
  102.6 5.6 %last_price.1 = bf16[768,128]{1,0:T(8,128)(2,1)S(1)} custom-call(s32[640]{0:T(1024)S(1)} %reshape.67.blocks_hbm, bf16[128,5,128,128]{3,2,1,0:T(8,128)(2,1)} %tiles_hbm.13, bf16[64,16,128]{2,1,0:T(8,128)(2,1)S(1)} %collective-permute-done.3.dual, f32[18,16,128]{2,1,0:T(8,128)S(1)} %get-tuple-element.45.before, ...), custom_call_target="tpu_custom_call" | custom-call | flops 167772160 | bytes 10485760 | tf_op jit(solution)/shard_map/last_price/pallas_call | solution.py:427
  108.2 12.6 %all_to_all.33.back = bf16[16,48,128]{2,1,0:T(8,128)(2,1)S(1)} all-to-all(bf16[16,48,128]{2,1,0:T(8,128)(2,1)S(1)} %bitcast.22), channel_id=1, replica_groups=mesh['scen'=2,'tm'=16] {'tm'}, dimensions={0} | all-to-all | bytes 393216 | tf_op jit(solution)/shard_map/all_to_all | solution.py:542
  120.8 0.7 unpack.1
  (14 shorter events, 0.2 us)
Async XLA Ops:
  0.6 10.9 %copy-start = (f32[16384]{0:T(1024)S(1)}, f32[16384]{0:T(1024)}, u32[]{:S(2)}) copy-start(f32[16384]{0:T(1024)} %param.10) | copy-start | bytes 196612
  0.6 0.9 copy-start.2
  1.6 0.7 copy-start.3
  3.1 16.4 %all-to-all-start = ((bf16[16,48,128]{2,1,0:T(8,128)(2,1)}), bf16[16,48,128]{2,1,0:T(8,128)(2,1)S(1)}, u32[]{:S(2)}, u32[]{:S(2)}) async-start(bf16[16,48,128]{2,1,0:T(8,128)(2,1)} %pack.1), calls=%async_computation | async-start | bytes 393216 | tf_op jit(solution)/shard_map/all_to_all | solution.py:471
  24.8 4.5 %collective-permute-start = (f32[64,16,128]{2,1,0:T(8,128)S(1)}, f32[64,16,128]{2,1,0:T(8,128)S(1)}, u32[]{:S(2)}, u32[]{:S(2)}) collective-permute-start(f32[64,16,128]{2,1,0:T(8,128)S(1)} %get-tuple-element.32), channel_id=1, source_target_pairs={{0,1},{1,0},{2,3},{3,2},{4,5},{5,4},{6,7},{7,6},{8,9},{9,8},{10,11... | collective-permute-start | bytes 1572872 | tf_op jit(solution)/shard_map/ppermute | solution.py:486
  30.0 13.2 %all-to-all-start.1 = ((bf16[8,8,16,128]{3,2,1,0:T(8,128)(2,1)}), bf16[8,8,16,128]{3,2,1,0:T(8,128)(2,1)S(1)}, u32[]{:S(2)}, u32[]{:S(2)}) async-start(bf16[8,8,16,128]{3,2,1,0:T(8,128)(2,1)} %bitcast.5), calls=%async_computation.1 | async-start | bytes 524288 | tf_op jit(solution)/shard_map/all_to_all | solution.py:406
  55.8 4.9 %collective-permute-start.1 = (bf16[64,16,128]{2,1,0:T(8,128)(2,1)S(1)}, bf16[64,16,128]{2,1,0:T(8,128)(2,1)S(1)}, u32[]{:S(2)}, u32[]{:S(2)}) collective-permute-start(bf16[64,16,128]{2,1,0:T(8,128)(2,1)S(1)} %bitcast.19), channel_id=1, source_target_pairs={{0,1},{1,0},{2,3},{3,2},{4,5},{5,4},{6,7},{7,6},{8,9},{9,8},{10,11... | collective-permute-start | bytes 786440 | tf_op jit(solution)/shard_map/ppermute | solution.py:500
  67.5 4.2 %collective-permute-start.2 = (f32[64,16,128]{2,1,0:T(8,128)S(1)}, f32[64,16,128]{2,1,0:T(8,128)S(1)}, u32[]{:S(2)}, u32[]{:S(2)}) collective-permute-start(f32[64,16,128]{2,1,0:T(8,128)S(1)} %get-tuple-element.42), channel_id=1, source_target_pairs={{0,1},{1,0},{2,3},{3,2},{4,5},{5,4},{6,7},{7,6},{8,9},{9,8},{10,11... | collective-permute-start | bytes 1572872 | tf_op jit(solution)/shard_map/ppermute | solution.py:486
  71.7 24.7 %copy-start.1 = (f32[2048]{0:T(1024)S(1)}, f32[2048]{0:T(1024)}, u32[]{:S(2)}) copy-start(f32[2048]{0:T(1024)} %param.12) | copy-start | bytes 24580
  96.3 6.3 %collective-permute-start.3 = (bf16[64,16,128]{2,1,0:T(8,128)(2,1)S(1)}, bf16[64,16,128]{2,1,0:T(8,128)(2,1)S(1)}, u32[]{:S(2)}, u32[]{:S(2)}) collective-permute-start(bf16[64,16,128]{2,1,0:T(8,128)(2,1)S(1)} %bitcast.17), channel_id=1, source_target_pairs={{0,1},{1,0},{2,3},{3,2},{4,5},{5,4},{6,7},{7,6},{8,9},{9,8},{10,11... | collective-permute-start | bytes 786440 | tf_op jit(solution)/shard_map/ppermute | solution.py:500

commit v11 on v10

--- a/solution.py
+++ b/solution.py
@@ -199,71 +199,51 @@
     return jnp.concatenate([high, low], axis=axis)
 
 
-def level_pass(price, level, unit_block, unit_lane, gain, out, mine):
-    count, hours, width = price.shape
+def storage_pass(level, unit_block, unit_lane, delta, gain=None, price=None, out=None):
+    hours = level.shape[0]
+    count, _, width = (price if delta is None else delta).shape
     span = 2 * width
-    prices = high_low(jnp.concatenate([price[b] for b in range(count)], axis=0), 1)
+    if price is not None:
+        prices = high_low(jnp.concatenate([price[b] for b in range(count)], axis=0), 1)
+    if delta is not None:
+        delta[...] = jnp.zeros_like(delta)
 
     def body(c, carry):
         cols = pl.ds(pl.multiple_of(c * span, span), span)
         hot = one_hot(unit_lane, cols, width)
-        picked = jnp.dot(prices, jnp.concatenate([hot, hot], axis=0), preferred_element_type=jnp.float32)
         block = jnp.broadcast_to(unit_block[:, cols], (hours, span))
-        found = jnp.zeros((hours, span), jnp.float32)
-        for b in range(count):
-            found = jnp.where(block == b, picked[b * hours : (b + 1) * hours], found)
+        here = [block == b for b in range(count)]
         now = level[:, cols]
-        new = 0.5 * (now + earlier(now)) - gain[:, cols] * found
-        if mine:
-            new = jnp.where((block >= 0) & (block < count), new, 0.0)
-        out[:, cols] = new
+        if price is not None:
+            picked = jnp.dot(prices, jnp.concatenate([hot, hot], axis=0), preferred_element_type=jnp.float32)
+            found = jnp.zeros((hours, span), jnp.float32)
+            for b in range(count):
+                found = jnp.where(here[b], picked[b * hours : (b + 1) * hours], found)
+            now = 0.5 * (now + earlier(now)) - gain[:, cols] * found
+            if delta is None:
+                now = jnp.where((block >= 0) & (block < count), now, 0.0)
+            out[:, cols] = now
+        if delta is not None:
+            charge = step_size * (now - earlier(now))
+            held = jnp.concatenate([jnp.where(here[b], charge, 0.0) for b in range(count)], axis=0)
+            part = lax.dot_general(held.astype(jnp.bfloat16), hot, NT, preferred_element_type=jnp.float32)
+            for b in range(count):
+                delta[b] = delta[b] + part[b * hours : (b + 1) * hours]
         return carry
 
     lax.fori_loop(0, level.shape[1] // span, body, 0)
 
 
-def storage_pass(level, unit_block, unit_lane, delta):
-    count, hours, width = delta.shape
-    span = 2 * width
-    delta[...] = jnp.zeros_like(delta)
-
-    def body(c, carry):
-        cols = pl.ds(pl.multiple_of(c * span, span), span)
-        now = level[:, cols]
-        charge = step_size * (now - earlier(now))
-        hot = one_hot(unit_lane, cols, width)
-        block = jnp.broadcast_to(unit_block[:, cols], (hours, span))
-        held = jnp.concatenate([jnp.where(block == b, charge, 0.0) for b in range(count)], axis=0)
-        part = lax.dot_general(held.astype(jnp.bfloat16), hot, NT, preferred_element_type=jnp.float32)
-        for b in range(count):
-            delta[b] = delta[b] + part[b * hours : (b + 1) * hours]
-        return carry
-
-    lax.fori_loop(0, level.shape[1] // span, body, 0)
-
-
-def pack_kernel(base, soc_hbm, out, flat, soc, sem):
+def pack_kernel(joined, out, *, units):
     devices, rows, width = out.shape
-    hour_rows = soc.shape[0]
-    rows = rows // hour_rows
-    count = base.shape[1] // (devices * width)
-    units = soc.shape[1] // width
-    copy = pltpu.make_async_copy(soc_hbm, soc, sem)
-    copy.start()
-    flat[...] = jnp.zeros_like(flat)
-    for r in range(hour_rows):
-        for d in range(devices):
-            at = (d * hour_rows + r) * rows
-            for b in range(count):
-                first = (d * count + b) * width
-                flat[at + b : at + b + 1, :] = base[r : r + 1, first : first + width].astype(jnp.float32)
-    copy.wait()
-    for r in range(hour_rows):
-        levels = jnp.concatenate([soc[r : r + 1, c * width : (c + 1) * width] for c in range(units)], axis=0)
-        for d in range(devices):
-            at = (d * hour_rows + r) * rows
-            flat[at + count : at + count + units, :] = levels
-    out[...] = flat[...].reshape(out.shape).astype(out.dtype)
+    hour_rows = joined.shape[0]
+    count = (joined.shape[1] - units) // devices
+    pad = jnp.zeros((rows // hour_rows - count - units, width), jnp.float32)
+    for d in range(devices):
+        parts = []
+        for r in range(hour_rows):
+            parts += [joined[r, d * count : (d + 1) * count], joined[r, devices * count :], pad]
+        out[d] = jnp.concatenate(parts, axis=0).astype(out.dtype)
 
 
 def first_flow_kernel(
@@ -313,8 +293,7 @@
 ):
     half = Half(False, (blocks_hbm, tiles_hbm), tiles, blocks, block_sem, sems)
     ahead = Ahead(half, head, ahead_sem)
-    level_pass(price, level, unit_block, unit_lane, gain, level_out, False)
-    storage_pass(level_out, unit_block, unit_lane, delta)
+    storage_pass(level, unit_block, unit_lane, delta, gain, price, level_out)
     own_price(half, ahead, dual, before, sums)
 
 
@@ -356,7 +335,7 @@
         flat[pl.ds(b, hours, stride=rows), :] = new
 
     update_pass(sums, before, lambda b: inject[b], start, delta, price, write)
-    level_pass(price, level, unit_block, unit_lane, gain, level_out, True)
+    storage_pass(level, unit_block, unit_lane, None, gain, price, level_out)
     for c in range(units):
         flat[pl.ds(count + c, hours, stride=rows), :] = level_out[:, c * width : (c + 1) * width]
     out[...] = flat[...].astype(out.dtype)
@@ -437,13 +416,12 @@
             name=name,
         )(blocks, ptdf_tiles, *operands)
 
-    def small(kernel, name, outs, operands, scratch=(), last=VMEM):
+    def small(kernel, name, outs, operands):
         return pl.pallas_call(
             kernel,
             out_shape=outs,
-            in_specs=[VMEM] * (len(operands) - 1) + [last],
+            in_specs=[VMEM] * len(operands),
             out_specs=[VMEM] * len(outs),
-            scratch_shapes=scratch,
             compiler_params=SMALL,
             cost_estimate=pl.CostEstimate(flops=half_flops, bytes_accessed=4 << 20, transcendentals=0),
             name=name,
@@ -456,21 +434,16 @@
 
     rows_in = whole_tiles(bus_blocks + unit_rows)
     rows_out = whole_tiles(bus_blocks + unit_rows + own_groups)
+    joined = jnp.concatenate([base_injection.astype(jnp.float32), soc_init], axis=1)
     (sent,) = small(
-        pack_kernel,
+        functools.partial(pack_kernel, units=unit_rows),
         "pack",
         [jax.ShapeDtypeStruct((devices, hour_rows * rows_in, width), jnp.bfloat16)],
-        [base_injection, soc_init],
-        [
-            pltpu.VMEM((devices * hour_rows * rows_in, width), jnp.float32),
-            pltpu.VMEM(soc_init.shape, soc_init.dtype),
-            pltpu.SemaphoreType.DMA,
-        ],
-        HBM,
+        [joined.reshape(hour_rows, (bus_count + units) // width, width)],
     )
     came = lax.all_to_all(sent, "tm", split_axis=0, concat_axis=0, tiled=True)
-    came, own_limits, unit_block, unit_lane, gain, blocks = lax.optimization_barrier(
-        (came, own_limits, unit_block, unit_lane, gain, blocks)
+    came, high, low, unit_block, unit_lane, gain, blocks = lax.optimization_barrier(
+        (came, own_limits, -own_limits, unit_block, unit_lane, gain, blocks)
     )
     away, base, level, head = product(
         first_flow_kernel,
@@ -493,7 +466,7 @@
         pair = (flows + arrived).astype(jnp.bfloat16).reshape(chips, own_groups, hours, lines)
         parts = exchange(pair)
         shifted = jnp.sum(parts.astype(jnp.float32), axis=0) + line_dual
-        clipped = jnp.clip(shifted, -own_limits, own_limits)
+        clipped = jnp.clip(shifted, low, high)
         line_dual = shifted - clipped
         dual = exchange(jnp.broadcast_to(line_dual.astype(jnp.bfloat16)[None], (chips, own_groups, hours, lines)))
         dual = dual.reshape(half_groups, hours, lines)

time: 122 us -> 121 us (level)
  blocking collectives: 49.5 us -> 61.8 us
  waiting for transfers between devices: 17 us -> 6.59 us
  starting transfers between devices: 11.5 us -> 8.03 us
  other arithmetic: 1.67 us -> 3.56 us
  local copies, waits for them, and re-layouts: 2.72 us -> 1.07 us
    all_to_all x3 -> x4, blocking collectives: 36.9 us -> 49.2 us  [exchange(): lax.all_to_all(value, 'tm', split_axis=0, concat_axis=0, axis_index_group...]
    all_to_all x1 -> x0, waiting for transfers between devices: 9.78 us -> none  [exchange(): lax.all_to_all(value, 'tm', split_axis=0, concat_axis=0, axis_index_group...]
    all_to_all x1 -> x0, starting transfers between devices: 3.41 us -> none  [exchange(): lax.all_to_all(value, 'tm', split_axis=0, concat_axis=0, axis_index_group...]
    unnamed x9 -> x3, local copies, waits for them, and re-layouts: 2.44 us -> 0.8 us
  transfers between devices with their start and end apart: 6 -> 5, of which waited for: 2 -> 1; matrix products, arithmetic and copies ran while one was open for 1% -> 2% of each run, Pallas kernels for 16% -> 16%
where the time goes in v11:
time: 121 us; the launch traced here: 120 us
  blocking collectives  61.8 us (51%)
  Pallas kernels  38.2 us (32%)
  starting transfers between devices  8.03 us (7%)
  waiting for transfers between devices  6.59 us (5%)
  other arithmetic  3.56 us (3%)
    all_to_all x4, blocking collectives, exchange(): lax.all_to_all(value, 'tm', split_axis=0, concat_axis=0, axis_index_group...  49.2 us
    pallas_call x7, Pallas kernels, product(): pl.pallas_call(kernel, out_shape=outs, in_specs=[HBM] * 2 + [VMEM] * len(...  36.8 us
    all_to_all x1, blocking collectives, shards(): lax.all_to_all(out.reshape(devices, hour_rows * rows_out, width), 'tm', s...  12.6 us
    all_to_all x1, starting transfers between devices, shards(): came = lax.all_to_all(sent, 'tm', split_axis=0, concat_axis=0, tiled=True)  7.39 us
    all_to_all x1, waiting for transfers between devices, shards(): came = lax.all_to_all(sent, 'tm', split_axis=0, concat_axis=0, tiled=True)  6.58 us
  transfers between devices with their start and end apart: 5, of which 1 were waited for; matrix products, arithmetic and copies ran while one was open for 2% of the time, Pallas kernels for 16%

profile of v11, /device:TPU:0, one launch (start us, length us, event | category | flops | bytes accessed | tf_op | source)
XLA Modules:
  0.0 120.1 jit_solution(5392725492137751060)
XLA Ops:
  0.6 1.1 convert_element_type.29
  1.7 0.8 pad_maximum_fusion
  2.5 0.7 pack.1
  3.2 7.4 %all-to-all-start = ((bf16[16,48,128]{2,1,0:T(8,128)(2,1)}), bf16[16,48,128]{2,1,0:T(8,128)(2,1)S(1)}, u32[]{:S(2)}, u32[]{:S(2)}) async-start(bf16[16,48,128]{2,1,0:T(8,128)(2,1)} %pack.1), calls=%async_computation | async-start | bytes 393216 | tf_op jit(solution)/shard_map/all_to_all | solution.py:444
  10.6 0.8 copy.10
  11.4 0.2 reshape.71.blocks_hbm
  11.6 0.7 fusion.5
  12.3 0.7 add_select_fusion
  13.0 6.6 %all-to-all-done = bf16[16,48,128]{2,1,0:T(8,128)(2,1)S(1)} async-done(((bf16[16,48,128]{2,1,0:T(8,128)(2,1)}), bf16[16,48,128]{2,1,0:T(8,128)(2,1)S(1)}, u32[]{:S(2)}, u32[]{:S(2)}) %all-to-all-start) | async-done | bytes 196640 | tf_op jit(solution)/shard_map/all_to_all | solution.py:444
  19.6 5.2 %first_flow.1 = (f32[64,16,128]{2,1,0:T(8,128)S(1)}, bf16[18,16,128]{2,1,0:T(8,128)(2,1)S(1)}, f32[16,2048]{1,0:T(8,128)S(1)}, bf16[16,5,128,128]{3,2,1,0:T(8,128)(2,1)S(1)}) custom-call(s32[640]{0:T(1024)S(1)} %reshape.71.blocks_hbm, bf16[128,5,128,128]{3,2,1,0:T(8,128)(2,1)} %tiles_hbm.13, bf16[768,128]{1,0:T(8,128)(2,1)S(1)} %bitcast.20), custom_call_target="tpu_custom_call" | custom-call | flops 167772160 | bytes 10485760 | tf_op jit(solution)/shard_map/first_flow/pallas_call | solution.py:406
  24.9 0.1 collective-permute-start
  24.9 4.4 %own_flow.1 = f32[64,16,128]{2,1,0:T(8,128)S(1)} custom-call(s32[640]{0:T(1024)S(1)} %reshape.71.blocks_hbm, bf16[128,5,128,128]{3,2,1,0:T(8,128)(2,1)} %tiles_hbm.13, bf16[18,16,128]{2,1,0:T(8,128)(2,1)S(1)} %get-tuple-element.31.picked.base, bf16[16,5,128,128]{3,2,1,0:T(8,128)(2,1)S(1)} %get-tuple-element.32.head), custom_call_target="tpu_custom_call" | custom-call | flops 167772160 | bytes 10485760 | tf_op jit(solution)/shard_map/own_flow/pallas_call | solution.py:406
  29.3 0.0 collective-permute-done
  29.3 0.1 add_convert_fusion.1
  29.4 12.3 %all_to_all.30 = bf16[8,8,16,128]{3,2,1,0:T(8,128)(2,1)S(1)} all-to-all(bf16[8,8,16,128]{3,2,1,0:T(8,128)(2,1)S(1)} %bitcast.31), channel_id=1, replica_groups={{0,2,4,6,8,10,12,14},{1,3,5,7,9,11,13,15},{16,18,20,22,24,26,28,30},{17..., dimensions={0} | all-to-all | bytes 524288 | tf_op jit(solution)/shard_map/all_to_all | solution.py:385
  41.8 12.5 %all_to_all.31 = bf16[8,8,16,128]{3,2,1,0:T(8,128)(2,1)S(1)} all-to-all(bf16[8,8,16,128]{3,2,1,0:T(8,128)(2,1)S(1)} %broadcast_in_dim.4), channel_id=1, replica_groups={{0,2,4,6,8,10,12,14},{1,3,5,7,9,11,13,15},{16,18,20,22,24,26,28,30},{17..., dimensions={0} | all-to-all | bytes 524288 | tf_op jit(solution)/shard_map/all_to_all | solution.py:385
  54.3 0.0 collective-permute-start.1
  54.3 4.9 %own_price.2 = (f32[18,16,128]{2,1,0:T(8,128)S(1)}, f32[18,16,128]{2,1,0:T(8,128)S(1)}, bf16[16,5,128,128]{3,2,1,0:T(8,128)(2,1)S(1)}, bf16[64,5,128,128]{3,2,1,0:T(8,128)(2,1)S(1)}) custom-call(s32[640]{0:T(1024)S(1)} %reshape.71.blocks_hbm, bf16[128,5,128,128]{3,2,1,0:T(8,128)(2,1)} %tiles_hbm.13, bf16[64,16,128]{2,1,0:T(8,128)(2,1)S(1)} %bitcast.19, ...), custom_call_target="tpu_custom_call" | custom-call | flops 167772160 | bytes 10485760 | tf_op jit(solution)/shard_map/own_price/pallas_call | solution.py:406
  59.2 0.0 collective-permute-done.1.dual
  59.2 6.8 %price_then_flow.1 = (f32[18,16,128]{2,1,0:T(8,128)S(1)}, f32[18,16,128]{2,1,0:T(8,128)S(1)}, bf16[18,16,128]{2,1,0:T(8,128)(2,1)S(1)}, f32[64,16,128]{2,1,0:T(8,128)S(1)}) custom-call(s32[640]{0:T(1024)S(1)} %reshape.71.blocks_hbm, bf16[128,5,128,128]{3,2,1,0:T(8,128)(2,1)} %tiles_hbm.13, bf16[64,16,128]{2,1,0:T(8,128)(2,1)S(1)} %collective-permute-done.1.dual, ...), custom_call_target="tpu_custom_call" | custom-call | flops 335544320 | bytes 20971520 | tf_op jit(solution)/shard_map/price_then_flow/pallas_call | solution.py:406
  66.0 0.6 collective-permute-start.2
  66.6 3.6 %held_flow.1 = f32[64,16,128]{2,1,0:T(8,128)S(1)} custom-call(s32[640]{0:T(1024)S(1)} %reshape.71.blocks_hbm, bf16[128,5,128,128]{3,2,1,0:T(8,128)(2,1)} %tiles_hbm.13, bf16[18,16,128]{2,1,0:T(8,128)(2,1)S(1)} %get-tuple-element.42.picked, bf16[64,5,128,128]{3,2,1,0:T(8,128)(2,1)S(1)} %get-tuple-element.43.tiles), custom_call_target="tpu_custom_call" | custom-call | flops 167772160 | bytes 10485760 | tf_op jit(solution)/shard_map/held_flow/pallas_call | solution.py:406
  70.1 0.0 copy-start
  70.2 0.0 collective-permute-done.2
  70.2 0.1 add_convert_fusion
  70.2 12.5 %all_to_all.32 = bf16[8,8,16,128]{3,2,1,0:T(8,128)(2,1)S(1)} all-to-all(bf16[8,8,16,128]{3,2,1,0:T(8,128)(2,1)S(1)} %bitcast.32), channel_id=1, replica_groups={{0,2,4,6,8,10,12,14},{1,3,5,7,9,11,13,15},{16,18,20,22,24,26,28,30},{17..., dimensions={0} | all-to-all | bytes 524288 | tf_op jit(solution)/shard_map/all_to_all | solution.py:385
  82.8 12.0 %all_to_all.33 = bf16[8,8,16,128]{3,2,1,0:T(8,128)(2,1)S(1)} all-to-all(bf16[8,8,16,128]{3,2,1,0:T(8,128)(2,1)S(1)} %broadcast_in_dim.5), channel_id=1, replica_groups={{0,2,4,6,8,10,12,14},{1,3,5,7,9,11,13,15},{16,18,20,22,24,26,28,30},{17..., dimensions={0} | all-to-all | bytes 524288 | tf_op jit(solution)/shard_map/all_to_all | solution.py:385
  94.8 0.0 collective-permute-start.3
  94.8 6.4 %own_price.3 = (f32[18,16,128]{2,1,0:T(8,128)S(1)}, f32[16,2048]{1,0:T(8,128)S(1)}, f32[18,16,128]{2,1,0:T(8,128)S(1)}, bf16[16,5,128,128]{3,2,1,0:T(8,128)(2,1)S(1)}) custom-call(s32[640]{0:T(1024)S(1)} %reshape.71.blocks_hbm, bf16[128,5,128,128]{3,2,1,0:T(8,128)(2,1)} %tiles_hbm.13, bf16[64,16,128]{2,1,0:T(8,128)(2,1)S(1)} %bitcast.17, ...), custom_call_target="tpu_custom_call" | custom-call | flops 167772160 | bytes 10485760 | tf_op jit(solution)/shard_map/own_price/pallas_call | solution.py:406
  101.2 5.6 %last_price.1 = bf16[768,128]{1,0:T(8,128)(2,1)S(1)} custom-call(s32[640]{0:T(1024)S(1)} %reshape.71.blocks_hbm, bf16[128,5,128,128]{3,2,1,0:T(8,128)(2,1)} %tiles_hbm.13, bf16[64,16,128]{2,1,0:T(8,128)(2,1)S(1)} %collective-permute-done.3.dual, f32[18,16,128]{2,1,0:T(8,128)S(1)} %get-tuple-element.47.before, ...), custom_call_target="tpu_custom_call" | custom-call | flops 167772160 | bytes 10485760 | tf_op jit(solution)/shard_map/last_price/pallas_call | solution.py:406
  106.8 12.6 %all_to_all.34.back = bf16[16,48,128]{2,1,0:T(8,128)(2,1)S(1)} all-to-all(bf16[16,48,128]{2,1,0:T(8,128)(2,1)S(1)} %bitcast.21), channel_id=1, replica_groups=mesh['scen'=2,'tm'=16] {'tm'}, dimensions={0} | all-to-all | bytes 393216 | tf_op jit(solution)/shard_map/all_to_all | solution.py:515
  119.4 0.7 unpack.1
  (8 shorter events, 0.2 us)
Async XLA Ops:
  3.2 16.4 %all-to-all-start = ((bf16[16,48,128]{2,1,0:T(8,128)(2,1)}), bf16[16,48,128]{2,1,0:T(8,128)(2,1)S(1)}, u32[]{:S(2)}, u32[]{:S(2)}) async-start(bf16[16,48,128]{2,1,0:T(8,128)(2,1)} %pack.1), calls=%async_computation | async-start | bytes 393216 | tf_op jit(solution)/shard_map/all_to_all | solution.py:444
  24.9 4.5 %collective-permute-start = (f32[64,16,128]{2,1,0:T(8,128)S(1)}, f32[64,16,128]{2,1,0:T(8,128)S(1)}, u32[]{:S(2)}, u32[]{:S(2)}) collective-permute-start(f32[64,16,128]{2,1,0:T(8,128)S(1)} %get-tuple-element.33), channel_id=1, source_target_pairs={{0,1},{1,0},{2,3},{3,2},{4,5},{5,4},{6,7},{7,6},{8,9},{9,8},{10,11... | collective-permute-start | bytes 1572872 | tf_op jit(solution)/shard_map/ppermute | solution.py:459
  54.3 4.9 %collective-permute-start.1 = (bf16[64,16,128]{2,1,0:T(8,128)(2,1)S(1)}, bf16[64,16,128]{2,1,0:T(8,128)(2,1)S(1)}, u32[]{:S(2)}, u32[]{:S(2)}) collective-permute-start(bf16[64,16,128]{2,1,0:T(8,128)(2,1)S(1)} %bitcast.18), channel_id=1, source_target_pairs={{0,1},{1,0},{2,3},{3,2},{4,5},{5,4},{6,7},{7,6},{8,9},{9,8},{10,11... | collective-permute-start | bytes 786440 | tf_op jit(solution)/shard_map/ppermute | solution.py:473
  66.0 4.2 %collective-permute-start.2 = (f32[64,16,128]{2,1,0:T(8,128)S(1)}, f32[64,16,128]{2,1,0:T(8,128)S(1)}, u32[]{:S(2)}, u32[]{:S(2)}) collective-permute-start(f32[64,16,128]{2,1,0:T(8,128)S(1)} %get-tuple-element.44), channel_id=1, source_target_pairs={{0,1},{1,0},{2,3},{3,2},{4,5},{5,4},{6,7},{7,6},{8,9},{9,8},{10,11... | collective-permute-start | bytes 1572872 | tf_op jit(solution)/shard_map/ppermute | solution.py:459
  70.1 24.7 %copy-start = (f32[2048]{0:T(1024)S(1)}, f32[2048]{0:T(1024)}, u32[]{:S(2)}) copy-start(f32[2048]{0:T(1024)} %param.12) | copy-start | bytes 24580
  94.8 6.4 %collective-permute-start.3 = (bf16[64,16,128]{2,1,0:T(8,128)(2,1)S(1)}, bf16[64,16,128]{2,1,0:T(8,128)(2,1)S(1)}, u32[]{:S(2)}, u32[]{:S(2)}) collective-permute-start(bf16[64,16,128]{2,1,0:T(8,128)(2,1)S(1)} %bitcast.16), channel_id=1, source_target_pairs={{0,1},{1,0},{2,3},{3,2},{4,5},{5,4},{6,7},{7,6},{8,9},{9,8},{10,11... | collective-permute-start | bytes 786440 | tf_op jit(solution)/shard_map/ppermute | solution.py:473

commit v12 on v11

--- a/solution.py
+++ b/solution.py
@@ -28,9 +28,10 @@
         self.tiles, self.head, self.blocks, self.sems = tiles, head, blocks, sems
         self.blocks_hbm, self.tiles_hbm = hbm
         self.chunks = lax.axis_size("tm") // 2
-        self.own = self.tiles_hbm.shape[0] // (2 * self.chunks)
-        self.ahead = 0 if head is None else head.shape[0] // self.own
-        self.depth, self.lines, self.width = self.tiles_hbm.shape[1:]
+        ahead_groups = 0 if head is None else head.shape[0]
+        self.own = (ahead_groups + tiles.shape[0]) // self.chunks
+        self.ahead = ahead_groups // self.own
+        self.depth, self.lines, self.width = tiles.shape[1:]
         if sems is not None:
             for chunk in range(self.ahead, self.chunks):
                 self.fetch(chunk).start()
@@ -129,30 +130,24 @@
 def price_pass(dual, half, sums, wait):
     depth, width = half.depth, half.width
     hours = dual.shape[1]
+    even = depth - depth % 2
     for ref in sums:
         ref[...] = jnp.zeros_like(ref)
 
     def four(tile, g, block):
         rows = [dual[g + u] for u in range(4)]
-        zero = jnp.zeros_like(rows[0])
         parts = []
         for first in (0, 2):
-            left = wide([[rows[first], zero], [zero, rows[first + 1]]])
-            for k in range(0, depth - 1, 2):
-                right = wide([[tile(first + u, k), tile(first + u, k + 1)] for u in range(2)])
+            for u in (first, first + 1):
+                right = jnp.concatenate([tile(u, k) for k in range(even)], axis=1)
+                part = jnp.dot(rows[u], right, preferred_element_type=jnp.float32)
+                parts += [(u, k, part[:, k * width : (k + 1) * width]) for k in range(even)]
+            if depth % 2:
+                left = jnp.concatenate(rows[first : first + 2], axis=0)
+                right = jnp.concatenate([tile(first, even), tile(first + 1, even)], axis=1)
                 part = jnp.dot(left, right, preferred_element_type=jnp.float32)
                 for u in range(2):
-                    for j in range(2):
-                        piece = part[u * hours : (u + 1) * hours, j * width : (j + 1) * width]
-                        parts.append((first + u, k + j, piece))
-        if depth % 2:
-            k = depth - 1
-            left = wide([[rows[0], zero], [zero, rows[1]], [rows[2], zero], [zero, rows[3]]])
-            right = wide([[tile(0, k), tile(2, k)], [tile(1, k), tile(3, k)]])
-            part = jnp.dot(left, right, preferred_element_type=jnp.float32)
-            for u in range(4):
-                at = (u // 2) * width
-                parts.append((u, k, part[u * hours : (u + 1) * hours, at : at + width]))
+                    parts.append((first + u, even, part[u * hours : (u + 1) * hours, u * width : (u + 1) * width]))
         for u, k, part in parts:
             at = block(u, k)
             sums[k][at] = sums[k][at] + part
@@ -234,20 +229,28 @@
     lax.fori_loop(0, level.shape[1] // span, body, 0)
 
 
-def pack_kernel(joined, out, *, units):
+def pack_kernel(joined, out, flat, *, units):
     devices, rows, width = out.shape
     hour_rows = joined.shape[0]
-    count = (joined.shape[1] - units) // devices
-    pad = jnp.zeros((rows // hour_rows - count - units, width), jnp.float32)
-    for d in range(devices):
-        parts = []
-        for r in range(hour_rows):
-            parts += [joined[r, d * count : (d + 1) * count], joined[r, devices * count :], pad]
-        out[d] = jnp.concatenate(parts, axis=0).astype(out.dtype)
+    rows = rows // hour_rows
+    count = (joined.shape[1] // width - units) // devices
+    flat[...] = jnp.zeros_like(flat)
+
+    def row(r, at):
+        return joined[r : r + 1, at * width : (at + 1) * width].astype(jnp.float32)
+
+    for r in range(hour_rows):
+        levels = jnp.concatenate([row(r, devices * count + c) for c in range(units)], axis=0)
+        for d in range(devices):
+            at = (d * hour_rows + r) * rows
+            for b in range(count):
+                flat[at + b : at + b + 1, :] = row(r, d * count + b)
+            flat[at + count : at + count + units, :] = levels
+    out[...] = flat[...].reshape(out.shape).astype(out.dtype)
 
 
 def first_flow_kernel(
-    blocks_hbm, tiles_hbm, came, flows, picked, level, head, blocks, block_sem, tiles, sems, ahead_sem, flat
+    blocks_hbm, tiles_hbm, came, flows, picked, level, head, tiles, blocks, block_sem, sems, ahead_sem, flat
 ):
     half = Half(True, (blocks_hbm, tiles_hbm), tiles, blocks, block_sem, sems)
     ahead = Ahead(half, head, ahead_sem)
@@ -262,46 +265,41 @@
     ahead.wait()
 
 
-def own_flow_kernel(blocks_hbm, tiles_hbm, picked, head, flows, blocks, block_sem, tiles, sems):
+def own_flow_kernel(blocks_hbm, tiles_hbm, picked, head, flows, tiles, blocks, block_sem, sems):
     flow_pass(picked, Half(False, (blocks_hbm, tiles_hbm), tiles, blocks, block_sem, sems, head), flows, True)
 
 
-def held_flow_kernel(blocks_hbm, tiles_hbm, picked, tiles, flows, blocks, block_sem):
-    flow_pass(picked, Half(False, (blocks_hbm, tiles_hbm), tiles, blocks, block_sem), flows, True)
-
-
-def own_price(half, ahead, dual, price, sums):
+def held_flow_kernel(blocks_hbm, head, tiles, picked, flows, blocks, block_sem):
+    flow_pass(picked, Half(False, (blocks_hbm, None), tiles, blocks, block_sem, head=head), flows, True)
+
+
+def own_price(half, dual, price, sums):
     price_pass(dual, half, sums, True)
     for b in range(price.shape[0]):
         price[b] = total(sums, b)
-    ahead.wait()
 
 
 def own_price_kernel(
-    blocks_hbm, tiles_hbm, dual, level, unit_block, unit_lane, before, delta, head, tiles,
-    blocks, block_sem, sems, ahead_sem, *sums
+    blocks_hbm, head, tiles, dual, level, unit_block, unit_lane, before, delta, blocks, block_sem, *sums
 ):
-    half = Half(False, (blocks_hbm, tiles_hbm), tiles, blocks, block_sem, sems)
-    ahead = Ahead(half, head, ahead_sem)
+    half = Half(False, (blocks_hbm, None), tiles, blocks, block_sem, head=head)
     storage_pass(level, unit_block, unit_lane, delta)
-    own_price(half, ahead, dual, before, sums)
+    own_price(half, dual, before, sums)
 
 
 def own_price_level_kernel(
-    blocks_hbm, tiles_hbm, dual, price, level, unit_block, unit_lane, gain, before, level_out, delta, head,
-    blocks, block_sem, tiles, sems, ahead_sem, *sums
+    blocks_hbm, head, tiles, dual, price, level, unit_block, unit_lane, gain, before, level_out, delta,
+    blocks, block_sem, *sums
 ):
-    half = Half(False, (blocks_hbm, tiles_hbm), tiles, blocks, block_sem, sems)
-    ahead = Ahead(half, head, ahead_sem)
+    half = Half(False, (blocks_hbm, None), tiles, blocks, block_sem, head=head)
     storage_pass(level, unit_block, unit_lane, delta, gain, price, level_out)
-    own_price(half, ahead, dual, before, sums)
+    own_price(half, dual, before, sums)
 
 
 def middle_kernel(
-    blocks_hbm, tiles_hbm, dual, before, base, delta, head, price, inject_out, picked, flows,
-    blocks, block_sem, tiles, sems, *sums
+    blocks_hbm, tiles, dual, before, base, delta, price, inject_out, picked, flows, blocks, block_sem, *sums
 ):
-    half = Half(True, (blocks_hbm, tiles_hbm), tiles, blocks, block_sem, sems, head)
+    half = Half(True, (blocks_hbm, None), tiles, blocks, block_sem)
     price_pass(dual, half, sums, True)
 
     def start(b):
@@ -316,10 +314,10 @@
 
 
 def last_kernel(
-    blocks_hbm, tiles_hbm, dual, before, base, inject, delta, level, line_dual, unit_block, unit_lane, gain, head,
-    out, blocks, block_sem, tiles, sems, price, level_out, flat, *sums
+    blocks_hbm, tiles, dual, before, base, inject, delta, level, line_dual, unit_block, unit_lane, gain,
+    out, blocks, block_sem, price, level_out, flat, *sums
 ):
-    half = Half(True, (blocks_hbm, tiles_hbm), tiles, blocks, block_sem, sems, head)
+    half = Half(True, (blocks_hbm, None), tiles, blocks, block_sem)
     count, hours, width = price.shape
     rows = flat.shape[0] // hours
     flat[...] = jnp.zeros_like(flat)
@@ -402,11 +400,11 @@
     sems, ahead_sems = pltpu.SemaphoreType.DMA((chips,)), pltpu.SemaphoreType.DMA((ahead,))
     sums = [scratch(block_shape)] * depth
 
-    def product(kernel, name, outs, operands, temporary, passes=1, limit=48):
+    def product(kernel, name, outs, operands, temporary, passes=1, hbm=(), limit=16):
         return pl.pallas_call(
             kernel,
             out_shape=outs,
-            in_specs=[HBM] * 2 + [VMEM] * len(operands),
+            in_specs=[HBM] * (1 + len(hbm)) + [VMEM] * len(operands),
             out_specs=[VMEM] * len(outs),
             scratch_shapes=[pltpu.SMEM(blocks.shape, blocks.dtype), pltpu.SemaphoreType.DMA, *temporary],
             compiler_params=pltpu.CompilerParams(vmem_limit_bytes=limit << 20),
@@ -414,14 +412,15 @@
                 flops=passes * half_flops, bytes_accessed=passes * half_bytes, transcendentals=0
             ),
             name=name,
-        )(blocks, ptdf_tiles, *operands)
-
-    def small(kernel, name, outs, operands):
+        )(blocks, *hbm, *operands)
+
+    def small(kernel, name, outs, operands, temporary=()):
         return pl.pallas_call(
             kernel,
             out_shape=outs,
             in_specs=[VMEM] * len(operands),
             out_specs=[VMEM] * len(outs),
+            scratch_shapes=temporary,
             compiler_params=SMALL,
             cost_estimate=pl.CostEstimate(flops=half_flops, bytes_accessed=4 << 20, transcendentals=0),
             name=name,
@@ -434,23 +433,26 @@
 
     rows_in = whole_tiles(bus_blocks + unit_rows)
     rows_out = whole_tiles(bus_blocks + unit_rows + own_groups)
-    joined = jnp.concatenate([base_injection.astype(jnp.float32), soc_init], axis=1)
+    joined = jnp.concatenate([base_injection, soc_init.astype(jnp.bfloat16)], axis=1)
     (sent,) = small(
         functools.partial(pack_kernel, units=unit_rows),
         "pack",
         [jax.ShapeDtypeStruct((devices, hour_rows * rows_in, width), jnp.bfloat16)],
-        [joined.reshape(hour_rows, (bus_count + units) // width, width)],
+        [joined],
+        [pltpu.VMEM((devices * hour_rows * rows_in, width), jnp.float32)],
     )
     came = lax.all_to_all(sent, "tm", split_axis=0, concat_axis=0, tiled=True)
     came, high, low, unit_block, unit_lane, gain, blocks = lax.optimization_barrier(
         (came, own_limits, -own_limits, unit_block, unit_lane, gain, blocks)
     )
-    away, base, level, head = product(
+    away, base, level, head, other_half = product(
         first_flow_kernel,
         "first_flow",
-        [flow_shape, picked_shape, level_shape, head_shape],
+        [flow_shape, picked_shape, level_shape, head_shape, half_shape],
         [came.reshape(hours * rows_in, width)],
-        [scratch(half_shape), sems, ahead_sems, pltpu.VMEM((hours * rows_in, width), jnp.float32)],
+        [sems, ahead_sems, pltpu.VMEM((hours * rows_in, width), jnp.float32)],
+        hbm=[ptdf_tiles],
+        limit=36,
     )
     picked = base
     price = None
@@ -458,11 +460,17 @@
     for iteration in range(ITERS):
         arrived = lax.ppermute(away, "tm", sibling)
         if iteration == 0:
-            (flows,) = product(
-                own_flow_kernel, "own_flow", [flow_shape], [picked, head], [scratch(rest_shape), sems]
+            flows, rest = product(
+                own_flow_kernel,
+                "own_flow",
+                [flow_shape, rest_shape],
+                [picked, head],
+                [sems],
+                hbm=[ptdf_tiles],
+                limit=28,
             )
         else:
-            (flows,) = product(held_flow_kernel, "held_flow", [flow_shape], [picked, held], [], limit=40)
+            (flows,) = product(held_flow_kernel, "held_flow", [flow_shape], [head, rest, picked], [])
         pair = (flows + arrived).astype(jnp.bfloat16).reshape(chips, own_groups, hours, lines)
         parts = exchange(pair)
         shifted = jnp.sum(parts.astype(jnp.float32), axis=0) + line_dual
@@ -472,39 +480,35 @@
         dual = dual.reshape(half_groups, hours, lines)
         other = lax.ppermute(dual, "tm", sibling)
         if iteration < ITERS - 1:
-            before, delta, head, held = product(
+            before, delta = product(
                 own_price_kernel,
                 "own_price",
-                [block_shape, block_shape, head_shape, half_shape],
-                [dual, level, unit_block, unit_lane],
-                [sems, ahead_sems] + sums,
-                limit=36,
+                [block_shape, block_shape],
+                [head, rest, dual, level, unit_block, unit_lane],
+                sums,
             )
             price, inject, picked, away = product(
                 middle_kernel,
                 "price_then_flow",
                 [block_shape, block_shape, picked_shape, flow_shape],
-                [other, before, base, delta, head],
-                [scratch(rest_shape), sems] + sums,
+                [other_half, other, before, base, delta],
+                sums,
                 2,
-                limit=36,
             )
         else:
-            before, level, delta, head = product(
+            before, level, delta = product(
                 own_price_level_kernel,
                 "own_price",
-                [block_shape, level_shape, block_shape, head_shape],
-                [dual, price, level, unit_block, unit_lane, gain],
-                [scratch(half_shape), sems, ahead_sems] + sums,
+                [block_shape, level_shape, block_shape],
+                [head, rest, dual, price, level, unit_block, unit_lane, gain],
+                sums,
             )
             (out,) = product(
                 last_kernel,
                 "last_price",
                 [jax.ShapeDtypeStruct((hours * rows_out, width), jnp.bfloat16)],
-                [other, before, base, inject, delta, level, line_dual, unit_block, unit_lane, gain, head],
+                [other_half, other, before, base, inject, delta, level, line_dual, unit_block, unit_lane, gain],
                 [
-                    scratch(rest_shape),
-                    sems,
                     scratch(block_shape),
                     scratch(level_shape),
                     pltpu.VMEM((hours * rows_out, width), jnp.float32),

time: 121 us -> 114 us (0.942)
  Pallas kernels: 38.2 us -> 32.1 us
    pallas_call x7, Pallas kernels: 36.8 us -> 30.6 us  [product(): pl.pallas_call(kernel, out_shape=outs, in_specs=[HBM] * (1 + len(hbm)) +...]
  transfers between devices with their start and end apart: 5 -> 5, of which waited for: 1 -> 1; matrix products, arithmetic and copies ran while one was open for 2% -> 2% of each run, Pallas kernels for 16% -> 14%
where the time goes in v12:
time: 114 us
  blocking collectives  61.8 us (54%)
  Pallas kernels  32.1 us (28%)
  starting transfers between devices  8.04 us (7%)
  waiting for transfers between devices  6.59 us (6%)
  other arithmetic  3.44 us (3%)
    all_to_all x4, blocking collectives, exchange(): lax.all_to_all(value, 'tm', split_axis=0, concat_axis=0, axis_index_group...  49.2 us
    pallas_call x7, Pallas kernels, product(): pl.pallas_call(kernel, out_shape=outs, in_specs=[HBM] * (1 + len(hbm)) +...  30.6 us
    all_to_all x1, blocking collectives, shards(): lax.all_to_all(out.reshape(devices, hour_rows * rows_out, width), 'tm', s...  12.6 us
    all_to_all x1, starting transfers between devices, shards(): came = lax.all_to_all(sent, 'tm', split_axis=0, concat_axis=0, tiled=True)  7.39 us
    all_to_all x1, waiting for transfers between devices, shards(): came = lax.all_to_all(sent, 'tm', split_axis=0, concat_axis=0, tiled=True)  6.58 us
  transfers between devices with their start and end apart: 5, of which 1 were waited for; matrix products, arithmetic and copies ran while one was open for 2% of the time, Pallas kernels for 14%

profile of v12, /device:TPU:0, one launch (start us, length us, event | category | flops | bytes accessed | tf_op | source)
XLA Modules:
  0.0 113.9 jit_solution(4481719869533566048)
XLA Ops:
  0.6 0.7 convert_element_type.29
  1.3 1.1 pad_maximum_fusion.joined
  2.4 0.8 pack.1
  3.2 7.4 %all-to-all-start = ((bf16[16,48,128]{2,1,0:T(8,128)(2,1)}), bf16[16,48,128]{2,1,0:T(8,128)(2,1)S(1)}, u32[]{:S(2)}, u32[]{:S(2)}) async-start(bf16[16,48,128]{2,1,0:T(8,128)(2,1)} %pack.1), calls=%async_computation | async-start | bytes 393216 | tf_op jit(solution)/shard_map/all_to_all | solution.py:444
  10.6 0.8 copy.10
  11.4 0.2 reshape.67.blocks_hbm
  11.6 0.7 fusion.5
  12.3 0.7 add_select_fusion
  13.0 6.6 %all-to-all-done = bf16[16,48,128]{2,1,0:T(8,128)(2,1)S(1)} async-done(((bf16[16,48,128]{2,1,0:T(8,128)(2,1)}), bf16[16,48,128]{2,1,0:T(8,128)(2,1)S(1)}, u32[]{:S(2)}, u32[]{:S(2)}) %all-to-all-start) | async-done | bytes 196640 | tf_op jit(solution)/shard_map/all_to_all | solution.py:444
  19.6 5.2 %first_flow.1 = (f32[64,16,128]{2,1,0:T(8,128)S(1)}, bf16[18,16,128]{2,1,0:T(8,128)(2,1)S(1)}, f32[16,2048]{1,0:T(8,128)S(1)}, bf16[16,5,128,128]{3,2,1,0:T(8,128)(2,1)S(1)}, bf16[64,5,128,128]{3,2,1,0:T(8,128)(2,1)S(1)}) custom-call(s32[640]{0:T(1024)S(1)} %reshape.67.blocks_hbm, bf16[128,5,128,128]{3,2,1,0:T(8,128)(2,1)} %tiles_hbm.3, ...), custom_call_target="tpu_custom_call" | custom-call | flops 167772160 | bytes 10485760 | tf_op jit(solution)/shard_map/first_flow/pallas_call | solution.py:404
  24.9 0.1 collective-permute-start
  24.9 4.4 %own_flow.1 = (f32[64,16,128]{2,1,0:T(8,128)S(1)}, bf16[48,5,128,128]{3,2,1,0:T(8,128)(2,1)S(1)}) custom-call(s32[640]{0:T(1024)S(1)} %reshape.67.blocks_hbm, bf16[128,5,128,128]{3,2,1,0:T(8,128)(2,1)} %tiles_hbm.3, bf16[18,16,128]{2,1,0:T(8,128)(2,1)S(1)} %get-tuple-element.33.picked.base, bf16[16,5,128,128]{3,2,1,0:T(8,128)(2,1)S(1)} %get-tuple-element.32.head), custom_call_target="tpu_custom_call" | custom-call | flops 167772160 | bytes 10485760 | tf_op jit(solution)/shard_map/own_flow/pallas_call | solution.py:404
  29.3 0.0 collective-permute-done
  29.3 0.1 add_convert_fusion.1
  29.4 12.3 %all_to_all.30 = bf16[8,8,16,128]{3,2,1,0:T(8,128)(2,1)S(1)} all-to-all(bf16[8,8,16,128]{3,2,1,0:T(8,128)(2,1)S(1)} %bitcast.29), channel_id=1, replica_groups={{0,2,4,6,8,10,12,14},{1,3,5,7,9,11,13,15},{16,18,20,22,24,26,28,30},{17..., dimensions={0} | all-to-all | bytes 524288 | tf_op jit(solution)/shard_map/all_to_all | solution.py:383
  41.8 12.5 %all_to_all.31 = bf16[8,8,16,128]{3,2,1,0:T(8,128)(2,1)S(1)} all-to-all(bf16[8,8,16,128]{3,2,1,0:T(8,128)(2,1)S(1)} %broadcast_in_dim.4), channel_id=1, replica_groups={{0,2,4,6,8,10,12,14},{1,3,5,7,9,11,13,15},{16,18,20,22,24,26,28,30},{17..., dimensions={0} | all-to-all | bytes 524288 | tf_op jit(solution)/shard_map/all_to_all | solution.py:383
  54.3 0.0 collective-permute-start.1
  54.3 3.2 %own_price.2 = (f32[18,16,128]{2,1,0:T(8,128)S(1)}, f32[18,16,128]{2,1,0:T(8,128)S(1)}) custom-call(s32[640]{0:T(1024)S(1)} %reshape.67.blocks_hbm, bf16[16,5,128,128]{3,2,1,0:T(8,128)(2,1)S(1)} %get-tuple-element.32.head, bf16[48,5,128,128]{3,2,1,0:T(8,128)(2,1)S(1)} %get-tuple-element.34.tiles, bf16[64,16,128]{2,1,0:T(8,128)(2,1)S(1)} %bitcast.18, ...), custom_call_target="tpu_custom_call" | custom-call | flops 167772160 | bytes 10485760 | tf_op jit(solution)/shard_map/own_price/pallas_call | solution.py:404
  57.5 0.0 collective-permute-done.1.dual
  57.5 0.0 copy-start
  57.5 5.2 %price_then_flow.1 = (f32[18,16,128]{2,1,0:T(8,128)S(1)}, f32[18,16,128]{2,1,0:T(8,128)S(1)}, bf16[18,16,128]{2,1,0:T(8,128)(2,1)S(1)}, f32[64,16,128]{2,1,0:T(8,128)S(1)}) custom-call(s32[640]{0:T(1024)S(1)} %reshape.67.blocks_hbm, bf16[64,5,128,128]{3,2,1,0:T(8,128)(2,1)S(1)} %get-tuple-element.31.tiles, ...), custom_call_target="tpu_custom_call" | custom-call | flops 335544320 | bytes 20971520 | tf_op jit(solution)/shard_map/price_then_flow/pallas_call | solution.py:404
  62.7 0.6 collective-permute-start.2
  63.3 3.6 %held_flow.1 = f32[64,16,128]{2,1,0:T(8,128)S(1)} custom-call(s32[640]{0:T(1024)S(1)} %reshape.67.blocks_hbm, bf16[16,5,128,128]{3,2,1,0:T(8,128)(2,1)S(1)} %get-tuple-element.32.head, bf16[48,5,128,128]{3,2,1,0:T(8,128)(2,1)S(1)} %get-tuple-element.34.tiles, bf16[18,16,128]{2,1,0:T(8,128)(2,1)S(1)} %get-tuple-element.44.picked), custom_call_target="tpu_custom_call" | custom-call | flops 167772160 | bytes 10485760 | tf_op jit(solution)/shard_map/held_flow/pallas_call | solution.py:404
  66.9 0.1 add_convert_fusion
  67.0 12.5 %all_to_all.32 = bf16[8,8,16,128]{3,2,1,0:T(8,128)(2,1)S(1)} all-to-all(bf16[8,8,16,128]{3,2,1,0:T(8,128)(2,1)S(1)} %bitcast.30), channel_id=1, replica_groups={{0,2,4,6,8,10,12,14},{1,3,5,7,9,11,13,15},{16,18,20,22,24,26,28,30},{17..., dimensions={0} | all-to-all | bytes 524288 | tf_op jit(solution)/shard_map/all_to_all | solution.py:383
  79.6 12.0 %all_to_all.33 = bf16[8,8,16,128]{3,2,1,0:T(8,128)(2,1)S(1)} all-to-all(bf16[8,8,16,128]{3,2,1,0:T(8,128)(2,1)S(1)} %broadcast_in_dim.5), channel_id=1, replica_groups={{0,2,4,6,8,10,12,14},{1,3,5,7,9,11,13,15},{16,18,20,22,24,26,28,30},{17..., dimensions={0} | all-to-all | bytes 524288 | tf_op jit(solution)/shard_map/all_to_all | solution.py:383
  91.5 0.0 collective-permute-start.3
  91.5 5.0 %own_price.3 = (f32[18,16,128]{2,1,0:T(8,128)S(1)}, f32[16,2048]{1,0:T(8,128)S(1)}, f32[18,16,128]{2,1,0:T(8,128)S(1)}) custom-call(s32[640]{0:T(1024)S(1)} %reshape.67.blocks_hbm, bf16[16,5,128,128]{3,2,1,0:T(8,128)(2,1)S(1)} %get-tuple-element.32.head, bf16[48,5,128,128]{3,2,1,0:T(8,128)(2,1)S(1)} %get-tuple-element.34.tiles, ...), custom_call_target="tpu_custom_call" | custom-call | flops 167772160 | bytes 10485760 | tf_op jit(solution)/shard_map/own_price/pallas_call | solution.py:404
  96.6 0.0 collective-permute-done.3.dual
  96.6 4.0 %last_price.1 = bf16[768,128]{1,0:T(8,128)(2,1)S(1)} custom-call(s32[640]{0:T(1024)S(1)} %reshape.67.blocks_hbm, bf16[64,5,128,128]{3,2,1,0:T(8,128)(2,1)S(1)} %get-tuple-element.31.tiles, bf16[64,16,128]{2,1,0:T(8,128)(2,1)S(1)} %collective-permute-done.3.dual, f32[18,16,128]{2,1,0:T(8,128)S(1)} %get-tuple-element.48.before, ...), custom_call_target="tpu_custom_call" | custom-call | flops 167772160 | bytes 10485760 | tf_op jit(solution)/shard_map/last_price/pallas_call | solution.py:404
  100.6 12.6 %all_to_all.34.back = bf16[16,48,128]{2,1,0:T(8,128)(2,1)S(1)} all-to-all(bf16[16,48,128]{2,1,0:T(8,128)(2,1)S(1)} %bitcast.20), channel_id=1, replica_groups=mesh['scen'=2,'tm'=16] {'tm'}, dimensions={0} | all-to-all | bytes 393216 | tf_op jit(solution)/shard_map/all_to_all | solution.py:519
  113.2 0.7 unpack.1
  (8 shorter events, 0.2 us)
Async XLA Ops:
  3.2 16.4 %all-to-all-start = ((bf16[16,48,128]{2,1,0:T(8,128)(2,1)}), bf16[16,48,128]{2,1,0:T(8,128)(2,1)S(1)}, u32[]{:S(2)}, u32[]{:S(2)}) async-start(bf16[16,48,128]{2,1,0:T(8,128)(2,1)} %pack.1), calls=%async_computation | async-start | bytes 393216 | tf_op jit(solution)/shard_map/all_to_all | solution.py:444
  24.9 4.5 %collective-permute-start = (f32[64,16,128]{2,1,0:T(8,128)S(1)}, f32[64,16,128]{2,1,0:T(8,128)S(1)}, u32[]{:S(2)}, u32[]{:S(2)}) collective-permute-start(f32[64,16,128]{2,1,0:T(8,128)S(1)} %get-tuple-element.36), channel_id=1, source_target_pairs={{0,1},{1,0},{2,3},{3,2},{4,5},{5,4},{6,7},{7,6},{8,9},{9,8},{10,11... | collective-permute-start | bytes 1572872 | tf_op jit(solution)/shard_map/ppermute | solution.py:461
  54.3 3.2 %collective-permute-start.1 = (bf16[64,16,128]{2,1,0:T(8,128)(2,1)S(1)}, bf16[64,16,128]{2,1,0:T(8,128)(2,1)S(1)}, u32[]{:S(2)}, u32[]{:S(2)}) collective-permute-start(bf16[64,16,128]{2,1,0:T(8,128)(2,1)S(1)} %bitcast.17), channel_id=1, source_target_pairs={{0,1},{1,0},{2,3},{3,2},{4,5},{5,4},{6,7},{7,6},{8,9},{9,8},{10,11... | collective-permute-start | bytes 786440 | tf_op jit(solution)/shard_map/ppermute | solution.py:481
  57.5 34.0 %copy-start = (f32[2048]{0:T(1024)S(1)}, f32[2048]{0:T(1024)}, u32[]{:S(2)}) copy-start(f32[2048]{0:T(1024)} %param.12) | copy-start | bytes 24580
  62.7 4.2 %collective-permute-start.2 = (f32[64,16,128]{2,1,0:T(8,128)S(1)}, f32[64,16,128]{2,1,0:T(8,128)S(1)}, u32[]{:S(2)}, u32[]{:S(2)}) collective-permute-start(f32[64,16,128]{2,1,0:T(8,128)S(1)} %get-tuple-element.45), channel_id=1, source_target_pairs={{0,1},{1,0},{2,3},{3,2},{4,5},{5,4},{6,7},{7,6},{8,9},{9,8},{10,11... | collective-permute-start | bytes 1572872 | tf_op jit(solution)/shard_map/ppermute | solution.py:461
  91.5 5.0 %collective-permute-start.3 = (bf16[64,16,128]{2,1,0:T(8,128)(2,1)S(1)}, bf16[64,16,128]{2,1,0:T(8,128)(2,1)S(1)}, u32[]{:S(2)}, u32[]{:S(2)}) collective-permute-start(bf16[64,16,128]{2,1,0:T(8,128)(2,1)S(1)} %bitcast.15), channel_id=1, source_target_pairs={{0,1},{1,0},{2,3},{3,2},{4,5},{5,4},{6,7},{7,6},{8,9},{9,8},{10,11... | collective-permute-start | bytes 786440 | tf_op jit(solution)/shard_map/ppermute | solution.py:481

commit v13 on v12

--- a/solution.py
+++ b/solution.py
@@ -203,8 +203,8 @@
     if delta is not None:
         delta[...] = jnp.zeros_like(delta)
 
-    def body(c, carry):
-        cols = pl.ds(pl.multiple_of(c * span, span), span)
+    for c in range(level.shape[1] // span):
+        cols = pl.ds(c * span, span)
         hot = one_hot(unit_lane, cols, width)
         block = jnp.broadcast_to(unit_block[:, cols], (hours, span))
         here = [block == b for b in range(count)]
@@ -224,9 +224,6 @@
             part = lax.dot_general(held.astype(jnp.bfloat16), hot, NT, preferred_element_type=jnp.float32)
             for b in range(count):
                 delta[b] = delta[b] + part[b * hours : (b + 1) * hours]
-        return carry
-
-    lax.fori_loop(0, level.shape[1] // span, body, 0)
 
 
 def pack_kernel(joined, out, flat, *, units):

time: 114 us -> 110 us (0.965)
  Pallas kernels: 32.1 us -> 27.9 us
    pallas_call x7, Pallas kernels: 30.6 us -> 26.4 us  [product(): pl.pallas_call(kernel, out_shape=outs, in_specs=[HBM] * (1 + len(hbm)) +...]
  transfers between devices with their start and end apart: 5 -> 5, of which waited for: 1 -> 1; matrix products, arithmetic and copies ran while one was open for 2% -> 2% of each run, Pallas kernels for 14% -> 12%
where the time goes in v13:
time: 110 us
  blocking collectives  61.8 us (56%)
  Pallas kernels  27.9 us (25%)
  starting transfers between devices  8.03 us (7%)
  waiting for transfers between devices  6.59 us (6%)
  other arithmetic  3.44 us (3%)
    all_to_all x4, blocking collectives, exchange(): lax.all_to_all(value, 'tm', split_axis=0, concat_axis=0, axis_index_group...  49.2 us
    pallas_call x7, Pallas kernels, product(): pl.pallas_call(kernel, out_shape=outs, in_specs=[HBM] * (1 + len(hbm)) +...  26.4 us
    all_to_all x1, blocking collectives, shards(): lax.all_to_all(out.reshape(devices, hour_rows * rows_out, width), 'tm', s...  12.6 us
    all_to_all x1, starting transfers between devices, shards(): came = lax.all_to_all(sent, 'tm', split_axis=0, concat_axis=0, tiled=True)  7.39 us
    all_to_all x1, waiting for transfers between devices, shards(): came = lax.all_to_all(sent, 'tm', split_axis=0, concat_axis=0, tiled=True)  6.58 us
  transfers between devices with their start and end apart: 5, of which 1 were waited for; matrix products, arithmetic and copies ran while one was open for 2% of the time, Pallas kernels for 12%

profile of v13, /device:TPU:0, one launch (start us, length us, event | category | flops | bytes accessed | tf_op | source)
XLA Modules:
  0.0 109.7 jit_solution(9417161995517056822)
XLA Ops:
  0.6 0.7 convert_element_type.29
  1.3 1.1 pad_maximum_fusion.joined
  2.4 0.8 pack.1
  3.2 7.4 %all-to-all-start = ((bf16[16,48,128]{2,1,0:T(8,128)(2,1)}), bf16[16,48,128]{2,1,0:T(8,128)(2,1)S(1)}, u32[]{:S(2)}, u32[]{:S(2)}) async-start(bf16[16,48,128]{2,1,0:T(8,128)(2,1)} %pack.1), calls=%async_computation | async-start | bytes 393216 | tf_op jit(solution)/shard_map/all_to_all | solution.py:441
  10.6 0.8 copy.10
  11.4 0.2 reshape.67.blocks_hbm
  11.6 0.7 fusion.5
  12.3 0.7 add_select_fusion
  13.0 6.6 %all-to-all-done = bf16[16,48,128]{2,1,0:T(8,128)(2,1)S(1)} async-done(((bf16[16,48,128]{2,1,0:T(8,128)(2,1)}), bf16[16,48,128]{2,1,0:T(8,128)(2,1)S(1)}, u32[]{:S(2)}, u32[]{:S(2)}) %all-to-all-start) | async-done | bytes 196640 | tf_op jit(solution)/shard_map/all_to_all | solution.py:441
  19.6 5.3 %first_flow.1 = (f32[64,16,128]{2,1,0:T(8,128)S(1)}, bf16[18,16,128]{2,1,0:T(8,128)(2,1)S(1)}, f32[16,2048]{1,0:T(8,128)S(1)}, bf16[16,5,128,128]{3,2,1,0:T(8,128)(2,1)S(1)}, bf16[64,5,128,128]{3,2,1,0:T(8,128)(2,1)S(1)}) custom-call(s32[640]{0:T(1024)S(1)} %reshape.67.blocks_hbm, bf16[128,5,128,128]{3,2,1,0:T(8,128)(2,1)} %tiles_hbm.3, ...), custom_call_target="tpu_custom_call" | custom-call | flops 167772160 | bytes 10485760 | tf_op jit(solution)/shard_map/first_flow/pallas_call | solution.py:401
  24.9 0.1 collective-permute-start
  25.0 4.4 %own_flow.1 = (f32[64,16,128]{2,1,0:T(8,128)S(1)}, bf16[48,5,128,128]{3,2,1,0:T(8,128)(2,1)S(1)}) custom-call(s32[640]{0:T(1024)S(1)} %reshape.67.blocks_hbm, bf16[128,5,128,128]{3,2,1,0:T(8,128)(2,1)} %tiles_hbm.3, bf16[18,16,128]{2,1,0:T(8,128)(2,1)S(1)} %get-tuple-element.33.picked.base, bf16[16,5,128,128]{3,2,1,0:T(8,128)(2,1)S(1)} %get-tuple-element.32.head), custom_call_target="tpu_custom_call" | custom-call | flops 167772160 | bytes 10485760 | tf_op jit(solution)/shard_map/own_flow/pallas_call | solution.py:401
  29.3 0.0 collective-permute-done
  29.3 0.1 add_convert_fusion.1
  29.4 12.3 %all_to_all.30 = bf16[8,8,16,128]{3,2,1,0:T(8,128)(2,1)S(1)} all-to-all(bf16[8,8,16,128]{3,2,1,0:T(8,128)(2,1)S(1)} %bitcast.29), channel_id=1, replica_groups={{0,2,4,6,8,10,12,14},{1,3,5,7,9,11,13,15},{16,18,20,22,24,26,28,30},{17..., dimensions={0} | all-to-all | bytes 524288 | tf_op jit(solution)/shard_map/all_to_all | solution.py:380
  41.8 12.5 %all_to_all.31 = bf16[8,8,16,128]{3,2,1,0:T(8,128)(2,1)S(1)} all-to-all(bf16[8,8,16,128]{3,2,1,0:T(8,128)(2,1)S(1)} %broadcast_in_dim.4), channel_id=1, replica_groups={{0,2,4,6,8,10,12,14},{1,3,5,7,9,11,13,15},{16,18,20,22,24,26,28,30},{17..., dimensions={0} | all-to-all | bytes 524288 | tf_op jit(solution)/shard_map/all_to_all | solution.py:380
  54.3 0.0 collective-permute-start.1
  54.3 2.6 %own_price.2 = (f32[18,16,128]{2,1,0:T(8,128)S(1)}, f32[18,16,128]{2,1,0:T(8,128)S(1)}) custom-call(s32[640]{0:T(1024)S(1)} %reshape.67.blocks_hbm, bf16[16,5,128,128]{3,2,1,0:T(8,128)(2,1)S(1)} %get-tuple-element.32.head, bf16[48,5,128,128]{3,2,1,0:T(8,128)(2,1)S(1)} %get-tuple-element.34.tiles, bf16[64,16,128]{2,1,0:T(8,128)(2,1)S(1)} %bitcast.18, ...), custom_call_target="tpu_custom_call" | custom-call | flops 167772160 | bytes 10485760 | tf_op jit(solution)/shard_map/own_price/pallas_call | solution.py:401
  57.0 0.0 collective-permute-done.1.dual
  57.0 0.0 copy-start
  57.0 5.2 %price_then_flow.1 = (f32[18,16,128]{2,1,0:T(8,128)S(1)}, f32[18,16,128]{2,1,0:T(8,128)S(1)}, bf16[18,16,128]{2,1,0:T(8,128)(2,1)S(1)}, f32[64,16,128]{2,1,0:T(8,128)S(1)}) custom-call(s32[640]{0:T(1024)S(1)} %reshape.67.blocks_hbm, bf16[64,5,128,128]{3,2,1,0:T(8,128)(2,1)S(1)} %get-tuple-element.31.tiles, ...), custom_call_target="tpu_custom_call" | custom-call | flops 335544320 | bytes 20971520 | tf_op jit(solution)/shard_map/price_then_flow/pallas_call | solution.py:401
  62.2 0.6 collective-permute-start.2
  62.7 3.6 %held_flow.1 = f32[64,16,128]{2,1,0:T(8,128)S(1)} custom-call(s32[640]{0:T(1024)S(1)} %reshape.67.blocks_hbm, bf16[16,5,128,128]{3,2,1,0:T(8,128)(2,1)S(1)} %get-tuple-element.32.head, bf16[48,5,128,128]{3,2,1,0:T(8,128)(2,1)S(1)} %get-tuple-element.34.tiles, bf16[18,16,128]{2,1,0:T(8,128)(2,1)S(1)} %get-tuple-element.44.picked), custom_call_target="tpu_custom_call" | custom-call | flops 167772160 | bytes 10485760 | tf_op jit(solution)/shard_map/held_flow/pallas_call | solution.py:401
  66.3 0.0 collective-permute-done.2
  66.4 0.1 add_convert_fusion
  66.4 12.5 %all_to_all.32 = bf16[8,8,16,128]{3,2,1,0:T(8,128)(2,1)S(1)} all-to-all(bf16[8,8,16,128]{3,2,1,0:T(8,128)(2,1)S(1)} %bitcast.30), channel_id=1, replica_groups={{0,2,4,6,8,10,12,14},{1,3,5,7,9,11,13,15},{16,18,20,22,24,26,28,30},{17..., dimensions={0} | all-to-all | bytes 524288 | tf_op jit(solution)/shard_map/all_to_all | solution.py:380
  79.0 12.0 %all_to_all.33 = bf16[8,8,16,128]{3,2,1,0:T(8,128)(2,1)S(1)} all-to-all(bf16[8,8,16,128]{3,2,1,0:T(8,128)(2,1)S(1)} %broadcast_in_dim.5), channel_id=1, replica_groups={{0,2,4,6,8,10,12,14},{1,3,5,7,9,11,13,15},{16,18,20,22,24,26,28,30},{17..., dimensions={0} | all-to-all | bytes 524288 | tf_op jit(solution)/shard_map/all_to_all | solution.py:380
  91.0 0.0 collective-permute-start.3
  91.0 2.6 %own_price.3 = (f32[18,16,128]{2,1,0:T(8,128)S(1)}, f32[16,2048]{1,0:T(8,128)S(1)}, f32[18,16,128]{2,1,0:T(8,128)S(1)}) custom-call(s32[640]{0:T(1024)S(1)} %reshape.67.blocks_hbm, bf16[16,5,128,128]{3,2,1,0:T(8,128)(2,1)S(1)} %get-tuple-element.32.head, bf16[48,5,128,128]{3,2,1,0:T(8,128)(2,1)S(1)} %get-tuple-element.34.tiles, ...), custom_call_target="tpu_custom_call" | custom-call | flops 167772160 | bytes 10485760 | tf_op jit(solution)/shard_map/own_price/pallas_call | solution.py:401
  93.6 2.7 %last_price.1 = bf16[768,128]{1,0:T(8,128)(2,1)S(1)} custom-call(s32[640]{0:T(1024)S(1)} %reshape.67.blocks_hbm, bf16[64,5,128,128]{3,2,1,0:T(8,128)(2,1)S(1)} %get-tuple-element.31.tiles, bf16[64,16,128]{2,1,0:T(8,128)(2,1)S(1)} %collective-permute-done.3.dual, f32[18,16,128]{2,1,0:T(8,128)S(1)} %get-tuple-element.48.before, ...), custom_call_target="tpu_custom_call" | custom-call | flops 167772160 | bytes 10485760 | tf_op jit(solution)/shard_map/last_price/pallas_call | solution.py:401
  96.4 12.6 %all_to_all.34.back = bf16[16,48,128]{2,1,0:T(8,128)(2,1)S(1)} all-to-all(bf16[16,48,128]{2,1,0:T(8,128)(2,1)S(1)} %bitcast.20), channel_id=1, replica_groups=mesh['scen'=2,'tm'=16] {'tm'}, dimensions={0} | all-to-all | bytes 393216 | tf_op jit(solution)/shard_map/all_to_all | solution.py:516
  109.0 0.7 unpack.1
  (8 shorter events, 0.2 us)
Async XLA Ops:
  3.2 16.4 %all-to-all-start = ((bf16[16,48,128]{2,1,0:T(8,128)(2,1)}), bf16[16,48,128]{2,1,0:T(8,128)(2,1)S(1)}, u32[]{:S(2)}, u32[]{:S(2)}) async-start(bf16[16,48,128]{2,1,0:T(8,128)(2,1)} %pack.1), calls=%async_computation | async-start | bytes 393216 | tf_op jit(solution)/shard_map/all_to_all | solution.py:441
  24.9 4.5 %collective-permute-start = (f32[64,16,128]{2,1,0:T(8,128)S(1)}, f32[64,16,128]{2,1,0:T(8,128)S(1)}, u32[]{:S(2)}, u32[]{:S(2)}) collective-permute-start(f32[64,16,128]{2,1,0:T(8,128)S(1)} %get-tuple-element.36), channel_id=1, source_target_pairs={{0,1},{1,0},{2,3},{3,2},{4,5},{5,4},{6,7},{7,6},{8,9},{9,8},{10,11... | collective-permute-start | bytes 1572872 | tf_op jit(solution)/shard_map/ppermute | solution.py:458
  54.3 2.7 %collective-permute-start.1 = (bf16[64,16,128]{2,1,0:T(8,128)(2,1)S(1)}, bf16[64,16,128]{2,1,0:T(8,128)(2,1)S(1)}, u32[]{:S(2)}, u32[]{:S(2)}) collective-permute-start(bf16[64,16,128]{2,1,0:T(8,128)(2,1)S(1)} %bitcast.17), channel_id=1, source_target_pairs={{0,1},{1,0},{2,3},{3,2},{4,5},{5,4},{6,7},{7,6},{8,9},{9,8},{10,11... | collective-permute-start | bytes 786440 | tf_op jit(solution)/shard_map/ppermute | solution.py:478
  57.0 34.0 %copy-start = (f32[2048]{0:T(1024)S(1)}, f32[2048]{0:T(1024)}, u32[]{:S(2)}) copy-start(f32[2048]{0:T(1024)} %param.12) | copy-start | bytes 24580
  62.2 4.2 %collective-permute-start.2 = (f32[64,16,128]{2,1,0:T(8,128)S(1)}, f32[64,16,128]{2,1,0:T(8,128)S(1)}, u32[]{:S(2)}, u32[]{:S(2)}) collective-permute-start(f32[64,16,128]{2,1,0:T(8,128)S(1)} %get-tuple-element.45), channel_id=1, source_target_pairs={{0,1},{1,0},{2,3},{3,2},{4,5},{5,4},{6,7},{7,6},{8,9},{9,8},{10,11... | collective-permute-start | bytes 1572872 | tf_op jit(solution)/shard_map/ppermute | solution.py:458
  91.0 2.6 %collective-permute-start.3 = (bf16[64,16,128]{2,1,0:T(8,128)(2,1)S(1)}, bf16[64,16,128]{2,1,0:T(8,128)(2,1)S(1)}, u32[]{:S(2)}, u32[]{:S(2)}) collective-permute-start(bf16[64,16,128]{2,1,0:T(8,128)(2,1)S(1)} %bitcast.15), channel_id=1, source_target_pairs={{0,1},{1,0},{2,3},{3,2},{4,5},{5,4},{6,7},{7,6},{8,9},{9,8},{10,11... | collective-permute-start | bytes 786440 | tf_op jit(solution)/shard_map/ppermute | solution.py:478

commit v14 on v13

--- a/solution.py
+++ b/solution.py
@@ -1,5 +1,3 @@
-import functools
-
 import jax
 import jax.numpy as jnp
 from jax import lax
@@ -226,24 +224,16 @@
                 delta[b] = delta[b] + part[b * hours : (b + 1) * hours]
 
 
-def pack_kernel(joined, out, flat, *, units):
+def pack_kernel(base, soc, out):
     devices, rows, width = out.shape
-    hour_rows = joined.shape[0]
-    rows = rows // hour_rows
-    count = (joined.shape[1] // width - units) // devices
-    flat[...] = jnp.zeros_like(flat)
-
-    def row(r, at):
-        return joined[r : r + 1, at * width : (at + 1) * width].astype(jnp.float32)
-
-    for r in range(hour_rows):
-        levels = jnp.concatenate([row(r, devices * count + c) for c in range(units)], axis=0)
-        for d in range(devices):
-            at = (d * hour_rows + r) * rows
-            for b in range(count):
-                flat[at + b : at + b + 1, :] = row(r, d * count + b)
-            flat[at + count : at + count + units, :] = levels
-    out[...] = flat[...].reshape(out.shape).astype(out.dtype)
+    hour_rows, units = soc.shape[0], soc.shape[1]
+    count = base.shape[1] // devices
+    pad = jnp.zeros((rows // hour_rows - count - units, width), jnp.float32)
+    for d in range(devices):
+        parts = []
+        for r in range(hour_rows):
+            parts += [base[r, d * count : (d + 1) * count], soc[r], pad]
+        out[d] = jnp.concatenate(parts, axis=0).astype(out.dtype)
 
 
 def first_flow_kernel(
@@ -411,13 +401,12 @@
             name=name,
         )(blocks, *hbm, *operands)
 
-    def small(kernel, name, outs, operands, temporary=()):
+    def small(kernel, name, outs, operands):
         return pl.pallas_call(
             kernel,
             out_shape=outs,
             in_specs=[VMEM] * len(operands),
             out_specs=[VMEM] * len(outs),
-            scratch_shapes=temporary,
             compiler_params=SMALL,
             cost_estimate=pl.CostEstimate(flops=half_flops, bytes_accessed=4 << 20, transcendentals=0),
             name=name,
@@ -430,13 +419,14 @@
 
     rows_in = whole_tiles(bus_blocks + unit_rows)
     rows_out = whole_tiles(bus_blocks + unit_rows + own_groups)
-    joined = jnp.concatenate([base_injection, soc_init.astype(jnp.bfloat16)], axis=1)
     (sent,) = small(
-        functools.partial(pack_kernel, units=unit_rows),
+        pack_kernel,
         "pack",
         [jax.ShapeDtypeStruct((devices, hour_rows * rows_in, width), jnp.bfloat16)],
-        [joined],
-        [pltpu.VMEM((devices * hour_rows * rows_in, width), jnp.float32)],
+        [
+            base_injection.astype(jnp.float32).reshape(hour_rows, bus_count // width, width),
+            soc_init.reshape(hour_rows, unit_rows, width),
+        ],
     )
     came = lax.all_to_all(sent, "tm", split_axis=0, concat_axis=0, tiled=True)
     came, high, low, unit_block, unit_lane, gain, blocks = lax.optimization_barrier(

time: 110 us -> 110 us (level)
  no operation moved by 1% of the time
where the time goes in v14:
time: 110 us
  blocking collectives  61.8 us (56%)
  Pallas kernels  27.8 us (25%)
  starting transfers between devices  8.02 us (7%)
  waiting for transfers between devices  6.59 us (6%)
  other arithmetic  2.73 us (2%)
  local copies, waits for them, and re-layouts  1.76 us (2%)
    all_to_all x4, blocking collectives, exchange(): lax.all_to_all(value, 'tm', split_axis=0, concat_axis=0, axis_index_group...  49.3 us
    pallas_call x7, Pallas kernels, product(): pl.pallas_call(kernel, out_shape=outs, in_specs=[HBM] * (1 + len(hbm)) +...  26.4 us
    all_to_all x1, blocking collectives, shards(): lax.all_to_all(out.reshape(devices, hour_rows * rows_out, width), 'tm', s...  12.6 us
    all_to_all x1, starting transfers between devices, shards(): came = lax.all_to_all(sent, 'tm', split_axis=0, concat_axis=0, tiled=True)  7.39 us
    all_to_all x1, waiting for transfers between devices, shards(): came = lax.all_to_all(sent, 'tm', split_axis=0, concat_axis=0, tiled=True)  6.58 us
  transfers between devices with their start and end apart: 5, of which 1 were waited for; matrix products, arithmetic and copies ran while one was open for 2% of the time, Pallas kernels for 12%

profile of v14, /device:TPU:0, one launch (start us, length us, event | category | flops | bytes accessed | tf_op | source)
XLA Modules:
  0.0 109.5 jit_solution(16446246015210908815)
XLA Ops:
  0.6 1.1 reshape.88
  1.7 0.0 copy-start.1
  1.7 0.7 copy-done.1
  2.4 0.7 pack.1
  3.1 7.4 %all-to-all-start = ((bf16[16,48,128]{2,1,0:T(8,128)(2,1)}), bf16[16,48,128]{2,1,0:T(8,128)(2,1)S(1)}, u32[]{:S(2)}, u32[]{:S(2)}) async-start(bf16[16,48,128]{2,1,0:T(8,128)(2,1)} %pack.1), calls=%async_computation | async-start | bytes 393216 | tf_op jit(solution)/shard_map/all_to_all | solution.py:431
  10.5 0.8 copy.10
  11.3 0.2 reshape.78.blocks_hbm
  11.5 0.7 fusion.5
  12.2 0.7 add_select_fusion
  12.9 6.6 %all-to-all-done = bf16[16,48,128]{2,1,0:T(8,128)(2,1)S(1)} async-done(((bf16[16,48,128]{2,1,0:T(8,128)(2,1)}), bf16[16,48,128]{2,1,0:T(8,128)(2,1)S(1)}, u32[]{:S(2)}, u32[]{:S(2)}) %all-to-all-start) | async-done | bytes 196640 | tf_op jit(solution)/shard_map/all_to_all | solution.py:431
  19.5 5.2 %first_flow.1 = (f32[64,16,128]{2,1,0:T(8,128)S(1)}, bf16[18,16,128]{2,1,0:T(8,128)(2,1)S(1)}, f32[16,2048]{1,0:T(8,128)S(1)}, bf16[16,5,128,128]{3,2,1,0:T(8,128)(2,1)S(1)}, bf16[64,5,128,128]{3,2,1,0:T(8,128)(2,1)S(1)}) custom-call(s32[640]{0:T(1024)S(1)} %reshape.78.blocks_hbm, bf16[128,5,128,128]{3,2,1,0:T(8,128)(2,1)} %tiles_hbm.3, ...), custom_call_target="tpu_custom_call" | custom-call | flops 167772160 | bytes 10485760 | tf_op jit(solution)/shard_map/first_flow/pallas_call | solution.py:391
  24.7 0.1 collective-permute-start
  24.8 4.4 %own_flow.1 = (f32[64,16,128]{2,1,0:T(8,128)S(1)}, bf16[48,5,128,128]{3,2,1,0:T(8,128)(2,1)S(1)}) custom-call(s32[640]{0:T(1024)S(1)} %reshape.78.blocks_hbm, bf16[128,5,128,128]{3,2,1,0:T(8,128)(2,1)} %tiles_hbm.3, bf16[18,16,128]{2,1,0:T(8,128)(2,1)S(1)} %get-tuple-element.33.picked.base, bf16[16,5,128,128]{3,2,1,0:T(8,128)(2,1)S(1)} %get-tuple-element.32.head), custom_call_target="tpu_custom_call" | custom-call | flops 167772160 | bytes 10485760 | tf_op jit(solution)/shard_map/own_flow/pallas_call | solution.py:391
  29.2 0.0 collective-permute-done
  29.2 0.1 add_convert_fusion.1
  29.3 12.3 %all_to_all.30 = bf16[8,8,16,128]{3,2,1,0:T(8,128)(2,1)S(1)} all-to-all(bf16[8,8,16,128]{3,2,1,0:T(8,128)(2,1)S(1)} %bitcast.33), channel_id=1, replica_groups={{0,2,4,6,8,10,12,14},{1,3,5,7,9,11,13,15},{16,18,20,22,24,26,28,30},{17..., dimensions={0} | all-to-all | bytes 524288 | tf_op jit(solution)/shard_map/all_to_all | solution.py:370
  41.7 12.5 %all_to_all.31 = bf16[8,8,16,128]{3,2,1,0:T(8,128)(2,1)S(1)} all-to-all(bf16[8,8,16,128]{3,2,1,0:T(8,128)(2,1)S(1)} %broadcast_in_dim.4), channel_id=1, replica_groups={{0,2,4,6,8,10,12,14},{1,3,5,7,9,11,13,15},{16,18,20,22,24,26,28,30},{17..., dimensions={0} | all-to-all | bytes 524288 | tf_op jit(solution)/shard_map/all_to_all | solution.py:370
  54.2 0.0 collective-permute-start.1
  54.2 2.6 %own_price.2 = (f32[18,16,128]{2,1,0:T(8,128)S(1)}, f32[18,16,128]{2,1,0:T(8,128)S(1)}) custom-call(s32[640]{0:T(1024)S(1)} %reshape.78.blocks_hbm, bf16[16,5,128,128]{3,2,1,0:T(8,128)(2,1)S(1)} %get-tuple-element.32.head, bf16[48,5,128,128]{3,2,1,0:T(8,128)(2,1)S(1)} %get-tuple-element.34.tiles, bf16[64,16,128]{2,1,0:T(8,128)(2,1)S(1)} %bitcast.20, ...), custom_call_target="tpu_custom_call" | custom-call | flops 167772160 | bytes 10485760 | tf_op jit(solution)/shard_map/own_price/pallas_call | solution.py:391
  56.8 0.0 collective-permute-done.1.dual
  56.9 0.0 copy-start
  56.9 5.2 %price_then_flow.1 = (f32[18,16,128]{2,1,0:T(8,128)S(1)}, f32[18,16,128]{2,1,0:T(8,128)S(1)}, bf16[18,16,128]{2,1,0:T(8,128)(2,1)S(1)}, f32[64,16,128]{2,1,0:T(8,128)S(1)}) custom-call(s32[640]{0:T(1024)S(1)} %reshape.78.blocks_hbm, bf16[64,5,128,128]{3,2,1,0:T(8,128)(2,1)S(1)} %get-tuple-element.31.tiles, ...), custom_call_target="tpu_custom_call" | custom-call | flops 335544320 | bytes 20971520 | tf_op jit(solution)/shard_map/price_then_flow/pallas_call | solution.py:391
  62.0 0.6 collective-permute-start.2
  62.6 3.6 %held_flow.1 = f32[64,16,128]{2,1,0:T(8,128)S(1)} custom-call(s32[640]{0:T(1024)S(1)} %reshape.78.blocks_hbm, bf16[16,5,128,128]{3,2,1,0:T(8,128)(2,1)S(1)} %get-tuple-element.32.head, bf16[48,5,128,128]{3,2,1,0:T(8,128)(2,1)S(1)} %get-tuple-element.34.tiles, bf16[18,16,128]{2,1,0:T(8,128)(2,1)S(1)} %get-tuple-element.44.picked), custom_call_target="tpu_custom_call" | custom-call | flops 167772160 | bytes 10485760 | tf_op jit(solution)/shard_map/held_flow/pallas_call | solution.py:391
  66.2 0.0 collective-permute-done.2
  66.2 0.1 add_convert_fusion
  66.3 12.5 %all_to_all.32 = bf16[8,8,16,128]{3,2,1,0:T(8,128)(2,1)S(1)} all-to-all(bf16[8,8,16,128]{3,2,1,0:T(8,128)(2,1)S(1)} %bitcast.34), channel_id=1, replica_groups={{0,2,4,6,8,10,12,14},{1,3,5,7,9,11,13,15},{16,18,20,22,24,26,28,30},{17..., dimensions={0} | all-to-all | bytes 524288 | tf_op jit(solution)/shard_map/all_to_all | solution.py:370
  78.9 12.0 %all_to_all.33 = bf16[8,8,16,128]{3,2,1,0:T(8,128)(2,1)S(1)} all-to-all(bf16[8,8,16,128]{3,2,1,0:T(8,128)(2,1)S(1)} %broadcast_in_dim.5), channel_id=1, replica_groups={{0,2,4,6,8,10,12,14},{1,3,5,7,9,11,13,15},{16,18,20,22,24,26,28,30},{17..., dimensions={0} | all-to-all | bytes 524288 | tf_op jit(solution)/shard_map/all_to_all | solution.py:370
  90.9 2.6 %own_price.3 = (f32[18,16,128]{2,1,0:T(8,128)S(1)}, f32[16,2048]{1,0:T(8,128)S(1)}, f32[18,16,128]{2,1,0:T(8,128)S(1)}) custom-call(s32[640]{0:T(1024)S(1)} %reshape.78.blocks_hbm, bf16[16,5,128,128]{3,2,1,0:T(8,128)(2,1)S(1)} %get-tuple-element.32.head, bf16[48,5,128,128]{3,2,1,0:T(8,128)(2,1)S(1)} %get-tuple-element.34.tiles, ...), custom_call_target="tpu_custom_call" | custom-call | flops 167772160 | bytes 10485760 | tf_op jit(solution)/shard_map/own_price/pallas_call | solution.py:391
  93.5 2.7 %last_price.1 = bf16[768,128]{1,0:T(8,128)(2,1)S(1)} custom-call(s32[640]{0:T(1024)S(1)} %reshape.78.blocks_hbm, bf16[64,5,128,128]{3,2,1,0:T(8,128)(2,1)S(1)} %get-tuple-element.31.tiles, bf16[64,16,128]{2,1,0:T(8,128)(2,1)S(1)} %collective-permute-done.3.dual, f32[18,16,128]{2,1,0:T(8,128)S(1)} %get-tuple-element.48.before, ...), custom_call_target="tpu_custom_call" | custom-call | flops 167772160 | bytes 10485760 | tf_op jit(solution)/shard_map/last_price/pallas_call | solution.py:391
  96.2 12.6 %all_to_all.34.back = bf16[16,48,128]{2,1,0:T(8,128)(2,1)S(1)} all-to-all(bf16[16,48,128]{2,1,0:T(8,128)(2,1)S(1)} %bitcast.22), channel_id=1, replica_groups=mesh['scen'=2,'tm'=16] {'tm'}, dimensions={0} | all-to-all | bytes 393216 | tf_op jit(solution)/shard_map/all_to_all | solution.py:506
  108.8 0.7 unpack.1
  (9 shorter events, 0.2 us)
Async XLA Ops:
  1.7 0.7 copy-start.1
  3.1 16.4 %all-to-all-start = ((bf16[16,48,128]{2,1,0:T(8,128)(2,1)}), bf16[16,48,128]{2,1,0:T(8,128)(2,1)S(1)}, u32[]{:S(2)}, u32[]{:S(2)}) async-start(bf16[16,48,128]{2,1,0:T(8,128)(2,1)} %pack.1), calls=%async_computation | async-start | bytes 393216 | tf_op jit(solution)/shard_map/all_to_all | solution.py:431
  24.7 4.5 %collective-permute-start = (f32[64,16,128]{2,1,0:T(8,128)S(1)}, f32[64,16,128]{2,1,0:T(8,128)S(1)}, u32[]{:S(2)}, u32[]{:S(2)}) collective-permute-start(f32[64,16,128]{2,1,0:T(8,128)S(1)} %get-tuple-element.36), channel_id=1, source_target_pairs={{0,1},{1,0},{2,3},{3,2},{4,5},{5,4},{6,7},{7,6},{8,9},{9,8},{10,11... | collective-permute-start | bytes 1572872 | tf_op jit(solution)/shard_map/ppermute | solution.py:448
  54.2 2.7 %collective-permute-start.1 = (bf16[64,16,128]{2,1,0:T(8,128)(2,1)S(1)}, bf16[64,16,128]{2,1,0:T(8,128)(2,1)S(1)}, u32[]{:S(2)}, u32[]{:S(2)}) collective-permute-start(bf16[64,16,128]{2,1,0:T(8,128)(2,1)S(1)} %bitcast.19), channel_id=1, source_target_pairs={{0,1},{1,0},{2,3},{3,2},{4,5},{5,4},{6,7},{7,6},{8,9},{9,8},{10,11... | collective-permute-start | bytes 786440 | tf_op jit(solution)/shard_map/ppermute | solution.py:468
  56.9 34.0 %copy-start = (f32[2048]{0:T(1024)S(1)}, f32[2048]{0:T(1024)}, u32[]{:S(2)}) copy-start(f32[2048]{0:T(1024)} %param.12) | copy-start | bytes 24580
  62.0 4.1 %collective-permute-start.2 = (f32[64,16,128]{2,1,0:T(8,128)S(1)}, f32[64,16,128]{2,1,0:T(8,128)S(1)}, u32[]{:S(2)}, u32[]{:S(2)}) collective-permute-start(f32[64,16,128]{2,1,0:T(8,128)S(1)} %get-tuple-element.45), channel_id=1, source_target_pairs={{0,1},{1,0},{2,3},{3,2},{4,5},{5,4},{6,7},{7,6},{8,9},{9,8},{10,11... | collective-permute-start | bytes 1572872 | tf_op jit(solution)/shard_map/ppermute | solution.py:448
  90.8 2.7 %collective-permute-start.3 = (bf16[64,16,128]{2,1,0:T(8,128)(2,1)S(1)}, bf16[64,16,128]{2,1,0:T(8,128)(2,1)S(1)}, u32[]{:S(2)}, u32[]{:S(2)}) collective-permute-start(bf16[64,16,128]{2,1,0:T(8,128)(2,1)S(1)} %bitcast.17), channel_id=1, source_target_pairs={{0,1},{1,0},{2,3},{3,2},{4,5},{5,4},{6,7},{7,6},{8,9},{9,8},{10,11... | collective-permute-start | bytes 786440 | tf_op jit(solution)/shard_map/ppermute | solution.py:468

commit v15 on v14

--- a/solution.py
+++ b/solution.py
@@ -371,7 +371,7 @@
 
     half_bytes = ptdf_tiles.size
     half_flops = hours * ptdf_tiles.size
-    ahead = max(1, chips // 4)
+    ahead = max(1, 3 * chips // 8)
 
     def tile_shape(chunks):
         return jax.ShapeDtypeStruct((chunks * own_groups, *ptdf_tiles.shape[1:]), ptdf_tiles.dtype)

time: 110 us -> 110 us (level)
  no operation moved by 1% of the time
where the time goes in v15:
time: 110 us
  blocking collectives  61.8 us (56%)
  Pallas kernels  27.8 us (25%)
  starting transfers between devices  8.04 us (7%)
  waiting for transfers between devices  6.59 us (6%)
  other arithmetic  2.73 us (2%)
  local copies, waits for them, and re-layouts  1.76 us (2%)
    all_to_all x4, blocking collectives, exchange(): lax.all_to_all(value, 'tm', split_axis=0, concat_axis=0, axis_index_group...  49.2 us
    pallas_call x7, Pallas kernels, product(): pl.pallas_call(kernel, out_shape=outs, in_specs=[HBM] * (1 + len(hbm)) +...  26.5 us
    all_to_all x1, blocking collectives, shards(): lax.all_to_all(out.reshape(devices, hour_rows * rows_out, width), 'tm', s...  12.6 us
    all_to_all x1, starting transfers between devices, shards(): came = lax.all_to_all(sent, 'tm', split_axis=0, concat_axis=0, tiled=True)  7.39 us
    all_to_all x1, waiting for transfers between devices, shards(): came = lax.all_to_all(sent, 'tm', split_axis=0, concat_axis=0, tiled=True)  6.58 us
  transfers between devices with their start and end apart: 5, of which 1 were waited for; matrix products, arithmetic and copies ran while one was open for 2% of the time, Pallas kernels for 12%

profile of v15, /device:TPU:0, one launch (start us, length us, event | category | flops | bytes accessed | tf_op | source)
XLA Modules:
  0.0 109.6 jit_solution(10990969976224466466)
XLA Ops:
  0.6 1.1 reshape.88
  1.7 0.0 copy-start.1
  1.7 0.7 copy-done.1
  2.4 0.7 pack.1
  3.1 7.4 %all-to-all-start = ((bf16[16,48,128]{2,1,0:T(8,128)(2,1)}), bf16[16,48,128]{2,1,0:T(8,128)(2,1)S(1)}, u32[]{:S(2)}, u32[]{:S(2)}) async-start(bf16[16,48,128]{2,1,0:T(8,128)(2,1)} %pack.1), calls=%async_computation | async-start | bytes 393216 | tf_op jit(solution)/shard_map/all_to_all | solution.py:431
  10.5 0.8 copy.10
  11.3 0.2 reshape.78.blocks_hbm
  11.5 0.7 fusion.5
  12.2 0.7 add_select_fusion
  12.9 6.6 %all-to-all-done = bf16[16,48,128]{2,1,0:T(8,128)(2,1)S(1)} async-done(((bf16[16,48,128]{2,1,0:T(8,128)(2,1)}), bf16[16,48,128]{2,1,0:T(8,128)(2,1)S(1)}, u32[]{:S(2)}, u32[]{:S(2)}) %all-to-all-start) | async-done | bytes 196640 | tf_op jit(solution)/shard_map/all_to_all | solution.py:431
  19.5 5.5 %first_flow.1 = (f32[64,16,128]{2,1,0:T(8,128)S(1)}, bf16[18,16,128]{2,1,0:T(8,128)(2,1)S(1)}, f32[16,2048]{1,0:T(8,128)S(1)}, bf16[24,5,128,128]{3,2,1,0:T(8,128)(2,1)S(1)}, bf16[64,5,128,128]{3,2,1,0:T(8,128)(2,1)S(1)}) custom-call(s32[640]{0:T(1024)S(1)} %reshape.78.blocks_hbm, bf16[128,5,128,128]{3,2,1,0:T(8,128)(2,1)} %tiles_hbm.3, ...), custom_call_target="tpu_custom_call" | custom-call | flops 167772160 | bytes 10485760 | tf_op jit(solution)/shard_map/first_flow/pallas_call | solution.py:391
  25.0 0.1 collective-permute-start
  25.0 4.2 %own_flow.1 = (f32[64,16,128]{2,1,0:T(8,128)S(1)}, bf16[40,5,128,128]{3,2,1,0:T(8,128)(2,1)S(1)}) custom-call(s32[640]{0:T(1024)S(1)} %reshape.78.blocks_hbm, bf16[128,5,128,128]{3,2,1,0:T(8,128)(2,1)} %tiles_hbm.3, bf16[18,16,128]{2,1,0:T(8,128)(2,1)S(1)} %get-tuple-element.33.picked.base, bf16[24,5,128,128]{3,2,1,0:T(8,128)(2,1)S(1)} %get-tuple-element.32.head), custom_call_target="tpu_custom_call" | custom-call | flops 167772160 | bytes 10485760 | tf_op jit(solution)/shard_map/own_flow/pallas_call | solution.py:391
  29.3 0.0 collective-permute-done
  29.3 0.1 add_convert_fusion.1
  29.4 12.3 %all_to_all.30 = bf16[8,8,16,128]{3,2,1,0:T(8,128)(2,1)S(1)} all-to-all(bf16[8,8,16,128]{3,2,1,0:T(8,128)(2,1)S(1)} %bitcast.33), channel_id=1, replica_groups={{0,2,4,6,8,10,12,14},{1,3,5,7,9,11,13,15},{16,18,20,22,24,26,28,30},{17..., dimensions={0} | all-to-all | bytes 524288 | tf_op jit(solution)/shard_map/all_to_all | solution.py:370
  41.8 12.5 %all_to_all.31 = bf16[8,8,16,128]{3,2,1,0:T(8,128)(2,1)S(1)} all-to-all(bf16[8,8,16,128]{3,2,1,0:T(8,128)(2,1)S(1)} %broadcast_in_dim.4), channel_id=1, replica_groups={{0,2,4,6,8,10,12,14},{1,3,5,7,9,11,13,15},{16,18,20,22,24,26,28,30},{17..., dimensions={0} | all-to-all | bytes 524288 | tf_op jit(solution)/shard_map/all_to_all | solution.py:370
  54.3 0.0 collective-permute-start.1
  54.3 2.6 %own_price.2 = (f32[18,16,128]{2,1,0:T(8,128)S(1)}, f32[18,16,128]{2,1,0:T(8,128)S(1)}) custom-call(s32[640]{0:T(1024)S(1)} %reshape.78.blocks_hbm, bf16[24,5,128,128]{3,2,1,0:T(8,128)(2,1)S(1)} %get-tuple-element.32.head, bf16[40,5,128,128]{3,2,1,0:T(8,128)(2,1)S(1)} %get-tuple-element.34.tiles, bf16[64,16,128]{2,1,0:T(8,128)(2,1)S(1)} %bitcast.20, ...), custom_call_target="tpu_custom_call" | custom-call | flops 167772160 | bytes 10485760 | tf_op jit(solution)/shard_map/own_price/pallas_call | solution.py:391
  56.9 0.0 collective-permute-done.1.dual
  57.0 0.0 copy-start
  57.0 5.2 %price_then_flow.1 = (f32[18,16,128]{2,1,0:T(8,128)S(1)}, f32[18,16,128]{2,1,0:T(8,128)S(1)}, bf16[18,16,128]{2,1,0:T(8,128)(2,1)S(1)}, f32[64,16,128]{2,1,0:T(8,128)S(1)}) custom-call(s32[640]{0:T(1024)S(1)} %reshape.78.blocks_hbm, bf16[64,5,128,128]{3,2,1,0:T(8,128)(2,1)S(1)} %get-tuple-element.31.tiles, ...), custom_call_target="tpu_custom_call" | custom-call | flops 335544320 | bytes 20971520 | tf_op jit(solution)/shard_map/price_then_flow/pallas_call | solution.py:391
  62.1 0.6 collective-permute-start.2
  62.7 3.6 %held_flow.1 = f32[64,16,128]{2,1,0:T(8,128)S(1)} custom-call(s32[640]{0:T(1024)S(1)} %reshape.78.blocks_hbm, bf16[24,5,128,128]{3,2,1,0:T(8,128)(2,1)S(1)} %get-tuple-element.32.head, bf16[40,5,128,128]{3,2,1,0:T(8,128)(2,1)S(1)} %get-tuple-element.34.tiles, bf16[18,16,128]{2,1,0:T(8,128)(2,1)S(1)} %get-tuple-element.44.picked), custom_call_target="tpu_custom_call" | custom-call | flops 167772160 | bytes 10485760 | tf_op jit(solution)/shard_map/held_flow/pallas_call | solution.py:391
  66.3 0.1 add_convert_fusion
  66.4 12.5 %all_to_all.32 = bf16[8,8,16,128]{3,2,1,0:T(8,128)(2,1)S(1)} all-to-all(bf16[8,8,16,128]{3,2,1,0:T(8,128)(2,1)S(1)} %bitcast.34), channel_id=1, replica_groups={{0,2,4,6,8,10,12,14},{1,3,5,7,9,11,13,15},{16,18,20,22,24,26,28,30},{17..., dimensions={0} | all-to-all | bytes 524288 | tf_op jit(solution)/shard_map/all_to_all | solution.py:370
  79.0 12.0 %all_to_all.33 = bf16[8,8,16,128]{3,2,1,0:T(8,128)(2,1)S(1)} all-to-all(bf16[8,8,16,128]{3,2,1,0:T(8,128)(2,1)S(1)} %broadcast_in_dim.5), channel_id=1, replica_groups={{0,2,4,6,8,10,12,14},{1,3,5,7,9,11,13,15},{16,18,20,22,24,26,28,30},{17..., dimensions={0} | all-to-all | bytes 524288 | tf_op jit(solution)/shard_map/all_to_all | solution.py:370
  91.0 2.6 %own_price.3 = (f32[18,16,128]{2,1,0:T(8,128)S(1)}, f32[16,2048]{1,0:T(8,128)S(1)}, f32[18,16,128]{2,1,0:T(8,128)S(1)}) custom-call(s32[640]{0:T(1024)S(1)} %reshape.78.blocks_hbm, bf16[24,5,128,128]{3,2,1,0:T(8,128)(2,1)S(1)} %get-tuple-element.32.head, bf16[40,5,128,128]{3,2,1,0:T(8,128)(2,1)S(1)} %get-tuple-element.34.tiles, ...), custom_call_target="tpu_custom_call" | custom-call | flops 167772160 | bytes 10485760 | tf_op jit(solution)/shard_map/own_price/pallas_call | solution.py:391
  93.6 0.0 collective-permute-done.3.dual
  93.6 2.7 %last_price.1 = bf16[768,128]{1,0:T(8,128)(2,1)S(1)} custom-call(s32[640]{0:T(1024)S(1)} %reshape.78.blocks_hbm, bf16[64,5,128,128]{3,2,1,0:T(8,128)(2,1)S(1)} %get-tuple-element.31.tiles, bf16[64,16,128]{2,1,0:T(8,128)(2,1)S(1)} %collective-permute-done.3.dual, f32[18,16,128]{2,1,0:T(8,128)S(1)} %get-tuple-element.48.before, ...), custom_call_target="tpu_custom_call" | custom-call | flops 167772160 | bytes 10485760 | tf_op jit(solution)/shard_map/last_price/pallas_call | solution.py:391
  96.3 12.6 %all_to_all.34.back = bf16[16,48,128]{2,1,0:T(8,128)(2,1)S(1)} all-to-all(bf16[16,48,128]{2,1,0:T(8,128)(2,1)S(1)} %bitcast.22), channel_id=1, replica_groups=mesh['scen'=2,'tm'=16] {'tm'}, dimensions={0} | all-to-all | bytes 393216 | tf_op jit(solution)/shard_map/all_to_all | solution.py:506
  108.9 0.7 unpack.1
  (9 shorter events, 0.2 us)
Async XLA Ops:
  1.7 0.7 copy-start.1
  3.1 16.4 %all-to-all-start = ((bf16[16,48,128]{2,1,0:T(8,128)(2,1)}), bf16[16,48,128]{2,1,0:T(8,128)(2,1)S(1)}, u32[]{:S(2)}, u32[]{:S(2)}) async-start(bf16[16,48,128]{2,1,0:T(8,128)(2,1)} %pack.1), calls=%async_computation | async-start | bytes 393216 | tf_op jit(solution)/shard_map/all_to_all | solution.py:431
  25.0 4.3 %collective-permute-start = (f32[64,16,128]{2,1,0:T(8,128)S(1)}, f32[64,16,128]{2,1,0:T(8,128)S(1)}, u32[]{:S(2)}, u32[]{:S(2)}) collective-permute-start(f32[64,16,128]{2,1,0:T(8,128)S(1)} %get-tuple-element.36), channel_id=1, source_target_pairs={{0,1},{1,0},{2,3},{3,2},{4,5},{5,4},{6,7},{7,6},{8,9},{9,8},{10,11... | collective-permute-start | bytes 1572872 | tf_op jit(solution)/shard_map/ppermute | solution.py:448
  54.3 2.7 %collective-permute-start.1 = (bf16[64,16,128]{2,1,0:T(8,128)(2,1)S(1)}, bf16[64,16,128]{2,1,0:T(8,128)(2,1)S(1)}, u32[]{:S(2)}, u32[]{:S(2)}) collective-permute-start(bf16[64,16,128]{2,1,0:T(8,128)(2,1)S(1)} %bitcast.19), channel_id=1, source_target_pairs={{0,1},{1,0},{2,3},{3,2},{4,5},{5,4},{6,7},{7,6},{8,9},{9,8},{10,11... | collective-permute-start | bytes 786440 | tf_op jit(solution)/shard_map/ppermute | solution.py:468
  57.0 34.0 %copy-start = (f32[2048]{0:T(1024)S(1)}, f32[2048]{0:T(1024)}, u32[]{:S(2)}) copy-start(f32[2048]{0:T(1024)} %param.12) | copy-start | bytes 24580
  62.1 4.2 %collective-permute-start.2 = (f32[64,16,128]{2,1,0:T(8,128)S(1)}, f32[64,16,128]{2,1,0:T(8,128)S(1)}, u32[]{:S(2)}, u32[]{:S(2)}) collective-permute-start(f32[64,16,128]{2,1,0:T(8,128)S(1)} %get-tuple-element.45), channel_id=1, source_target_pairs={{0,1},{1,0},{2,3},{3,2},{4,5},{5,4},{6,7},{7,6},{8,9},{9,8},{10,11... | collective-permute-start | bytes 1572872 | tf_op jit(solution)/shard_map/ppermute | solution.py:448
  90.9 2.6 %collective-permute-start.3 = (bf16[64,16,128]{2,1,0:T(8,128)(2,1)S(1)}, bf16[64,16,128]{2,1,0:T(8,128)(2,1)S(1)}, u32[]{:S(2)}, u32[]{:S(2)}) collective-permute-start(bf16[64,16,128]{2,1,0:T(8,128)(2,1)S(1)} %bitcast.17), channel_id=1, source_target_pairs={{0,1},{1,0},{2,3},{3,2},{4,5},{5,4},{6,7},{7,6},{8,9},{9,8},{10,11... | collective-permute-start | bytes 786440 | tf_op jit(solution)/shard_map/ppermute | solution.py:468
